TPU v7x, 256 devices: a whole 4x4x8 slice. The times are simulated.
256 devices in a mesh: dom: 16 (over z, x_hi), orb: 16 (over x_lo, y, core).
Axes of the slice: x: 4 (x_hi: 2, x_lo: 2; x = x_hi * 2 + x_lo), y: 4, z: 8, core: 2. Of those that a mesh axis runs over, the one named last changes fastest.
Arguments:
- rhs: float32 [128, 32, 32, 128], P('orb', 'dom'), may hold values from -6 to 6
- potential: float32 [32, 32, 128], P('dom'), may hold values from 0.5 to 2
- eigen_table: float32 [4096], replicated, may hold values from -1 to -0.1
- win_index: int32 [128], P('orb'), may hold values from 0 to 4095
- occupied: bfloat16 [32, 128, 32, 32, 128], P('orb', None, 'dom'), may hold values from -6 to 6
- block_ids: int32 [4], replicated, may hold values from 0 to 31, as said below
- psi_win: bfloat16 [128, 32, 32, 128], P('orb', 'dom'), may hold values from -6 to 6
- smoother: float32 [32, 32], replicated, may hold values from -1 to 1
Outputs:
- solution: float32 [128, 32, 32, 128], P('orb', 'dom')
- correlations: float32 [4, 128, 128], P(None, None, 'orb')
- gradient: float32 [32, 32, 128], P(None, 'dom', 'orb')
Inputs may be any that keep to these rules, and one draw needn't show every extreme that they name: `block_ids`: distinct block numbers; block 0 and block 31 are always among them.
All inputs are finite; a program needn't handle non-finite values.
Results may differ from a plain program's by a relative error of at most 0.0047.
Values may be sent and summed in bfloat16 or wider, within the bound.
No kernel may reach another device: no remote copies, remote signals or barrier semaphores. Data moves between devices by JAX's collectives and lax.ppermute only.
A program may use at most 64 MiB of HBM per device.

v0:
```python
import functools
import math

import jax
import jax.numpy as jnp
from jax import lax
from jax.experimental import pallas as pl
from jax.experimental.pallas import tpu as pltpu
from jax.sharding import PartitionSpec as P

ITERS = 3
VMEM_LIMIT = 16 * 1024 * 1024
NT = (((1,), (1,)), ((), ()))
SMEM = pl.BlockSpec(memory_space=pltpu.SMEM)
ANY = pl.BlockSpec(memory_space=pl.ANY)
VMEM = pl.BlockSpec(memory_space=pltpu.VMEM)

MID, CHIP, SAME, SLOT, CORE, DEV, TABLE = 0, 2, 4, 5, 6, 7, 8


def shape(dims, dtype=jnp.float32):
    return jax.ShapeDtypeStruct(dims, dtype)


def plan(per_dev, n_orb, ids_ref, dev_ref, out_ref):
    nproj = ids_ref.shape[0]
    chips = n_orb // 2
    ring = chips // 2
    last = per_dev * n_orb - 1
    dev = dev_ref[0]
    chip = dev // 2
    seen = jnp.int32(0)
    mids = [jnp.int32(0)] * (nproj - 2)
    order = []
    for j in range(nproj):
        block = ids_ref[j]
        middle = jnp.logical_and(block != 0, block != last)
        for k in range(nproj - 2):
            mids[k] = jnp.where(jnp.logical_and(middle, seen == k), block, mids[k])
        order.append(jnp.where(block == 0, 0, jnp.where(block == last, 1, 2 + seen)))
        seen = seen + jnp.where(middle, 1, 0)
    owners = [mid // (2 * per_dev) for mid in mids]
    for k in range(nproj - 2):
        out_ref[MID + k] = mids[k]
        out_ref[CHIP + k] = owners[k]
    out_ref[SAME] = jnp.where(owners[0] == owners[1], 1, 0)
    offer = jnp.where(chip == owners[0], mids[0], mids[1])
    out_ref[SLOT] = offer % per_dev
    out_ref[CORE] = (offer // per_dev) % 2
    out_ref[DEV] = dev
    y, x = chip % ring, chip // ring
    for j in range(nproj):
        for q in range(chips):
            down = (q // 2 + ring - y) % ring
            first = jnp.where(down == 1, 4, jnp.where(down == 3, 8, jnp.where(down == 2, 12, 0)))
            first = first + (order[j] + x) % 2 * 2 + q % 2
            down = (q % ring + ring - y) % ring
            side = (q // ring + x) % 2
            second = jnp.where(down == 1, 4, jnp.where(down == 3, 2, 0)) + side * 6
            second = 14 + jnp.where(down == 2, 12 + side * 2, second) + order[j]
            out_ref[TABLE + j * chips + q] = jnp.where(order[j] < 2, first, second)


def copies(source, target, sem):
    parts = sem.shape[0]
    rows = target.shape[0] // parts
    return [
        pltpu.make_async_copy(source(k * rows, rows), target.at[pl.ds(k * rows, rows)], sem.at[k])
        for k in range(parts)
    ]


def run(started):
    for copy in started:
        copy.start()
    for copy in started:
        copy.wait()


def offer_kernel(per_dev, n_orb, ids_ref, dev_ref, occupied_ref, plan_ref, offer_ref, sem):
    plan(per_dev, n_orb, ids_ref, dev_ref, plan_ref)
    core = plan_ref[DEV] % 2
    run(copies(lambda at, n: occupied_ref.at[plan_ref[SLOT], pl.ds(at, n), 1 - core], offer_ref, sem))


def fixed_kernel(plan_ref, occupied_ref, fixed_ref, sem):
    core = plan_ref[DEV] % 2
    slot = core * (occupied_ref.shape[0] - 1)
    run(copies(lambda at, n: occupied_ref.at[slot, pl.ds(at, n), 1 - core], fixed_ref, sem))


def pick_kernel(plan_ref, occupied_ref, offer_ref, out_ref, sem):
    core = plan_ref[DEV] % 2

    @pl.when(plan_ref[CORE] == core)
    def _():
        run(copies(lambda at, n: occupied_ref.at[plan_ref[SLOT], pl.ds(at, n), core], out_ref, sem))

    @pl.when(plan_ref[CORE] != core)
    def _():
        step = 16

        @pl.loop(0, out_ref.shape[0] // step)
        def _(k):
            here = pl.ds(k * step, step)
            out_ref[here] = offer_ref[here]


def pieces_kernel(n_orb, plan_ref, occupied_ref, fixed_ref, *refs):
    *piece_refs, sem = refs
    dev = plan_ref[DEV]
    core = dev % 2
    last = occupied_ref.shape[0] - 1
    ring = len(piece_refs)
    rows = piece_refs[0].shape[0]

    def at(s):
        return pl.ds(jnp.where(dev < n_orb // 2, s, (ring - 1 + s) % ring) * rows, rows)

    @pl.when(jnp.logical_or(dev == 0, dev == n_orb - 1))
    def _():
        run([
            pltpu.make_async_copy(occupied_ref.at[core * last, at(s), core], ref, sem.at[s])
            for s, ref in enumerate(piece_refs)
        ])

    @pl.when(jnp.logical_or(dev == 1, dev == n_orb - 2))
    def _():
        for s, ref in enumerate(piece_refs):
            ref[...] = fixed_ref[at(s)]


def share_kernel(plan_ref, *refs):
    *piece_refs, out_ref = refs
    ring = len(piece_refs)
    chip = plan_ref[DEV] // 2
    y, x = chip % ring, chip // ring
    away = (y + x) % ring
    for s, ref in enumerate(piece_refs):

        @pl.when(away == s)
        def _(ref=ref):
            out_ref[...] = ref[...]


def core_mask(low_ref, width):
    return jnp.concatenate([low_ref[...]] * (width // low_ref.shape[1]), axis=1) > 0.5


def split(low_ref, value, mine_ref, other_ref):
    half = value.shape[0] // 2
    low = core_mask(low_ref, value.shape[1])
    first, second = value[:half], value[half:]
    mine_ref[...] = jnp.where(low, first, second)
    other_ref[...] = jnp.where(low, second, first)


def project(scale, low_ref, resid_b, block_refs, mine_ref, other_ref):
    parts = [
        lax.dot_general(resid_b, ref[...], NT, preferred_element_type=jnp.float32) for ref in block_refs
    ]
    split(low_ref, jnp.concatenate(parts, axis=1) * scale, mine_ref, other_ref)


def fields_kernel(low_ref, field_ref, mine_ref, other_ref, *all_refs):
    rows_y, rows_z = field_ref.shape[2:]
    low = low_ref[...] > 0.5
    half = field_ref.shape[0]
    for y in range(rows_y):
        first, second = field_ref[:, 0, y, :], field_ref[:, 1, y, :]
        here = slice(y * rows_z, (y + 1) * rows_z)
        mine_ref[:, here] = jnp.where(low, first, second)
        other_ref[:, here] = jnp.where(low, second, first)
    if all_refs:
        (all_ref,) = all_refs
        wide = all_ref.shape[2]
        step = rows_y * rows_z // wide
        for plane in range(2):
            for y in range(rows_y // step):
                parts = [field_ref[:, plane, y + k * (rows_y // step), :] for k in range(step)]
                rows = jnp.concatenate(parts, axis=0).astype(jnp.bfloat16)
                for d in range(plane, all_ref.shape[0], 2):
                    all_ref[d, :, y * rows_z : (y + 1) * rows_z] = rows


def shares_kernel(scale, all_ref, ends_ref, mids_ref, out_ref):
    sources, rows, wide = all_ref.shape
    every = all_ref[...].reshape(sources * rows, wide)
    parts = rows // out_ref.shape[1]
    for at, ref in ((0, ends_ref), (ends_ref.shape[0], mids_ref)):
        n = ref.shape[0]
        total = 0.0
        for k in range(parts):
            cells = ref[:, k * wide : (k + 1) * wide]
            got = lax.dot_general(every, cells, NT, preferred_element_type=jnp.float32)
            got = got.reshape(sources, parts, rows // parts, n)
            total = total + got[:, k]
        out_ref[:, :, at : at + n] = total * scale


def spread_shares_kernel(parts_ref, out_ref):
    total = jnp.concatenate(
        [parts_ref[k] + parts_ref[k + 1] for k in range(0, parts_ref.shape[0], 2)], axis=1
    )
    for d in range(out_ref.shape[0]):
        out_ref[d] = total


def resid_kernel(
    scale, row, low_ref, x_ref, sib_ref, off_ref, rhs_ref, diag_ref, first_ref, second_ref,
    resid_ref, mine_ref, other_ref, rb_ref,
):
    cells = x_ref.shape[1]
    lane = lax.broadcasted_iota(jnp.int32, (x_ref.shape[0], row), 1)
    for at in range(0, cells, row):
        here = slice(at, at + row)
        x = x_ref[:, here]
        beside = sib_ref[:, here] + off_ref[:, here].astype(jnp.float32)
        if at > 0:
            beside = beside + x_ref[:, at - row : at]
        if at + row < cells:
            beside = beside + x_ref[:, at + row : at + 2 * row]
        beside = beside + jnp.where(lane == 0, 0.0, pltpu.roll(x, 1, 1))
        beside = beside + jnp.where(lane == row - 1, 0.0, pltpu.roll(x, row - 1, 1))
        resid = rhs_ref[:, here] - (diag_ref[:, here] * x - 0.5 * beside)
        resid_ref[:, here] = resid
        rb_ref[:, here] = resid.astype(jnp.bfloat16)
    project(scale, low_ref, rb_ref[...], (first_ref, second_ref), mine_ref, other_ref)


def stacked(value):
    half = value.shape[1] // 2
    return jnp.concatenate([value[:, :half], value[:, half:]], axis=0)


def unstacked(value):
    half = value.shape[0] // 2
    return jnp.concatenate([value[:half], value[half:]], axis=1)


def spread_kernel(mine_ref, other_ref, out_ref):
    total = mine_ref[...] + other_ref[...]
    for d in range(out_ref.shape[0]):
        out_ref[d] = total


def total_kernel(parts_ref, *out_refs):
    total = parts_ref[0]
    for d in range(1, parts_ref.shape[0]):
        total = total + parts_ref[d]
    out_refs[0][...] = stacked(total).astype(jnp.bfloat16)
    if len(out_refs) > 1:
        out_refs[1][...] = total


def update_kernel(scale, tile, has_x, last, root, low_ref, mine_ref, other_ref, resid_ref, diag_ref, *refs):
    refs = list(refs)
    x_ref = refs.pop(0) if has_x else None
    move_ref = None if has_x else refs.pop(0)
    psi_ref = refs.pop(0) if last else None
    first_ref, second_ref, *outs = refs
    low = core_mask(low_ref, 2 * mine_ref.shape[1])
    mine = unstacked(mine_ref[...].astype(jnp.float32))
    other = unstacked(other_ref[...].astype(jnp.float32))
    coeff = jnp.concatenate([jnp.where(low, mine, other), jnp.where(low, other, mine)], axis=0)
    coeff = coeff.astype(jnp.bfloat16)
    if not has_x:
        coeff = jnp.dot(coeff, move_ref[...], preferred_element_type=jnp.float32).astype(jnp.bfloat16)
    cells = resid_ref.shape[1]
    for at in range(0, cells, tile):
        here = slice(at, at + tile)
        corr = 0.0
        start = 0
        for ref in (first_ref, second_ref):
            rows = ref.shape[0]
            some = coeff[:, start : start + rows]
            corr = corr + jnp.dot(some, ref[:, here], preferred_element_type=jnp.float32)
            start += rows
        x = (resid_ref[:, here] - corr * scale) / diag_ref[:, here]
        if has_x:
            x = x + x_ref[:, here]
        if last:
            half = x.shape[0] // 2
            low = core_mask(low_ref, tile)
            outs[0][:, here] = jnp.where(low, x[:half], x[half:])
            outs[1][:, here] = jnp.where(low, x[half:], x[:half])
            raw = jnp.sum(x * psi_ref[:, here].astype(jnp.float32), axis=0, keepdims=True) / root
            rows, wide = outs[2].shape[2:]
            for k in range(tile // wide):
                row = raw[:, k * wide : (k + 1) * wide]
                spot = at // wide + k
                outs[2][spot // rows, :, spot % rows, :] = jnp.broadcast_to(row, (outs[2].shape[1], wide))
        else:
            outs[0][:, here] = x
            outs[1][:, here] = x.astype(jnp.bfloat16)


def table_kernel(plan_ref, coeff_ref, out_ref, rows_ref):
    rows_ref[...] = coeff_ref[...].T
    share = 16
    for j in range(out_ref.shape[0] // share):
        at = pl.multiple_of(plan_ref[TABLE + j] * share, share)
        out_ref[j * share : (j + 1) * share] = rows_ref[pl.ds(at, share)]


def finish_kernel(weights_ref, pick_ref, terms_ref, out_ref):
    def product(one, two):
        return lax.dot_general(
            one, two, (((1,), (0,)), ((), ())),
            precision=lax.Precision.HIGHEST, preferred_element_type=jnp.float32,
        )

    for k in range(terms_ref.shape[1]):
        out_ref[:, k, :] = product(product(weights_ref[...], terms_ref[:, k, :]), pick_ref[...])


def call(kernel, out_shape, in_specs=None, out_specs=None, scratch=()):
    specs = {}
    if in_specs is not None:
        specs["in_specs"] = in_specs
    if out_specs is not None:
        specs["out_specs"] = out_specs
    return pl.pallas_call(
        kernel,
        out_shape=out_shape,
        scratch_shapes=scratch,
        compiler_params=pltpu.CompilerParams(vmem_limit_bytes=VMEM_LIMIT),
        **specs,
    )


def per_device(rhs, potential, eigen_table, win_index, occupied, block_ids, psi_win, smoother):
    local_orbs, planes, rows_y, rows_z = rhs.shape
    n_dom = lax.axis_size("dom")
    n_orb = lax.axis_size("orb")
    cells = rows_y * rows_z
    wide = 2 * local_orbs
    width = local_orbs * n_orb
    scale = 1.0 / math.sqrt(planes * n_dom * rows_y * rows_z)
    n_occ = eigen_table.shape[0]
    per_dev, blk_rows = occupied.shape[:2]
    nproj = block_ids.shape[0]
    chips = n_orb // 2
    ring = chips // 2
    share = blk_rows // chips
    n_rows = nproj * blk_rows
    o = lax.axis_index("orb")
    core = o % 2
    low = core == 0
    groups = [[2 * k + c for k in range(chips)] for c in range(2)]

    def chip_perm(target):
        return [(2 * k + c, 2 * target(k) + c) for k in range(chips) for c in range(2)]

    swap_core = [(i, i ^ 1) for i in range(n_orb)]
    swap_x = chip_perm(lambda k: (k + ring) % chips)
    up_y = chip_perm(lambda k: k // ring * ring + (k + 1) % ring)
    down_y = chip_perm(lambda k: k // ring * ring + (k - 1) % ring)

    def permute(value, pairs):
        return lax.ppermute(value, "orb", pairs)

    def pair(own, other):
        return jnp.concatenate([jnp.where(low, own, other), jnp.where(low, other, own)], axis=0)

    low_mask = jnp.broadcast_to(jnp.where(low, 1.0, 0.0), (local_orbs, 128))
    four = (pltpu.SemaphoreType.DMA((4,)),)

    plane_shape = shape((blk_rows, rows_y, rows_z), jnp.bfloat16)
    piece_shape = shape((2 * share, rows_y, rows_z), jnp.bfloat16)
    plan, offer = call(
        functools.partial(offer_kernel, per_dev, n_orb),
        (shape((TABLE + nproj * chips,), jnp.int32), plane_shape),
        [SMEM, SMEM, ANY],
        (SMEM, VMEM),
        four,
    )(block_ids, o.astype(jnp.int32).reshape(1), occupied)
    offer = permute(offer, swap_core)

    flat_field = shape((local_orbs, cells))
    rhs_mine, rhs_other, rhs_all = call(
        fields_kernel, (flat_field, flat_field, shape((n_orb, 2 * local_orbs, cells // 2), jnp.bfloat16))
    )(low_mask, rhs)
    rhs_all = lax.all_to_all(rhs_all, "orb", 0, 0, tiled=True)
    rhs_wide = pair(rhs_mine, permute(rhs_other, swap_core))

    offer = call(pick_kernel, plane_shape, [SMEM, ANY, VMEM], VMEM, four)(plan, occupied, offer)
    fixed = call(fixed_kernel, plane_shape, [SMEM, ANY], VMEM, four)(plan, occupied)
    fixed = permute(fixed, [(0, 1), (n_orb - 1, n_orb - 2)])
    pieces = call(
        functools.partial(pieces_kernel, n_orb),
        [piece_shape] * ring,
        [SMEM, ANY, VMEM],
        [VMEM] * ring,
        (pltpu.SemaphoreType.DMA((ring,)),),
    )(plan, occupied, fixed)

    got = [pieces[0]]
    for s in range(1, ring):
        pairs = [(c, 2 * s + c) for c in range(2)]
        pairs += [(n_orb - 2 + c, 2 * (ring + (ring - 1 + s) % ring) + c) for c in range(2)]
        got.append(permute(pieces[s], pairs))
    fixed = call(share_kernel, piece_shape, [SMEM] + [VMEM] * ring, VMEM)(plan, *got)

    def scatter(value):
        value = value.reshape(chips, share, rows_y, rows_z)
        return lax.all_to_all(value, "orb", 0, 0, axis_index_groups=groups, tiled=True)

    def take(value, owner):
        return lax.dynamic_index_in_dim(value, owner, 0, keepdims=False)

    def apart(plan, occupied):
        return jnp.zeros((share, rows_y, rows_z), jnp.bfloat16)

    def together(plan, occupied):
        def plane_of(slot, plane):
            dims = (1, blk_rows, 1, rows_y, rows_z)
            return lax.dynamic_slice(occupied, (slot, 0, plane, 0, 0), dims).reshape(plane_shape.shape)

        mid = plan[MID + 1]
        other = permute(plane_of(mid % per_dev, 1 - core), swap_core)
        here = (mid // per_dev) % 2 == core
        again = scatter(jnp.where(here, plane_of(mid % per_dev, core), other))
        return take(again, plan[CHIP + 1])

    same = plan[SAME] == 1
    offered = scatter(offer)
    later, _ = lax.optimization_barrier((plan, got[1]))
    second = lax.cond(later[SAME] == 1, together, apart, later, occupied)
    second = jnp.where(same, second, take(offered, plan[CHIP + 1]))
    mids = jnp.concatenate([take(offered, plan[CHIP]), second], axis=0)

    xs = fixed.reshape(2 * share, cells)
    ys = mids.reshape(2 * share, cells)
    xs, ys = lax.optimization_barrier((xs, ys))
    xs_x = permute(xs, swap_x)
    ys_up = permute(ys, up_y)
    ys_down = permute(ys, down_y)
    xs_x, ys_up, ys_down = lax.optimization_barrier((xs_x, ys_up, ys_down))
    own = jnp.concatenate([xs, xs_x], axis=0)
    line = jnp.concatenate([ys, ys_up, ys_down], axis=0)
    line_x = permute(line, swap_x)
    above = permute(own, up_y)
    below = permute(own, down_y)
    far_up = permute(ys_up[:share], up_y)
    far_down = permute(ys_down[share:], down_y)
    line_x, above, below, far_up, far_down = lax.optimization_barrier(
        (line_x, above, below, far_up, far_down)
    )
    far = jnp.concatenate([far_up, far_down], axis=0)
    far_x = permute(far, swap_x)
    own_up = permute(above[: 2 * share], up_y)
    own_down = permute(below[2 * share :], down_y)
    blocks = [
        jnp.concatenate([own, below, above, own_up, own_down], axis=0),
        jnp.concatenate([line, line_x, far, far_x], axis=0),
    ]

    picks = win_index[:, None] == jnp.arange(n_occ, dtype=jnp.int32)[None, :]
    eps = jnp.sum(jnp.where(picks, eigen_table[None, :], 0.0), axis=1)[:, None]
    eps = pair(eps, permute(eps, swap_core))
    plane_pot = lax.dynamic_index_in_dim(potential, core, 0, keepdims=True).reshape(1, cells)
    diag = 3.0 + plane_pot - eps
    psi_mine, psi_other = call(fields_kernel, (flat_field, flat_field))(
        low_mask, psi_win.astype(jnp.float32)
    )
    psi_other = permute(psi_other.astype(jnp.bfloat16), swap_core)
    psi_wide = pair(psi_mine.astype(jnp.bfloat16), psi_other)

    half_shape = shape((local_orbs, n_rows))
    spread_shape = shape((n_dom, local_orbs, n_rows))
    field_shape = shape((wide, cells))
    flat_shape = (wide, n_rows // 2)

    def total(spread, outs):
        parts = lax.all_to_all(spread, "dom", 0, 0, tiled=True)
        coeff_b, *coeff = call(total_kernel, outs)(parts)
        return coeff, coeff_b, permute(coeff_b, swap_core)

    own_rows = 4 * share
    share_parts = call(
        functools.partial(shares_kernel, scale), shape((n_orb, local_orbs, own_rows))
    )(rhs_all, xs, ys)
    share_parts = lax.all_to_all(share_parts, "orb", 0, 0, tiled=True)
    first_spread = call(spread_shares_kernel, spread_shape)(share_parts)
    row = jnp.arange(n_rows)
    within = row % (2 * share)
    down = jnp.array([0, 0, 1, 1, 3, 3, 2, 2, 0, 3, 1, 0, 3, 1, 2, 2])
    side = jnp.array([0, 1, 0, 1, 0, 1, 0, 1, 0, 0, 0, 1, 1, 1, 0, 1])
    chip = o // 2
    chip_from = (chip // ring + side) % 2 * ring + (chip % ring + down) % ring
    at = chip_from * own_rows + jnp.where(jnp.arange(16) < 8, 0, 2 * share)
    at = jnp.repeat(at, 2 * share) + within
    move = (row[:, None] == at[None, :]).astype(jnp.bfloat16)

    across = []
    for d in range(n_dom - 1):
        for k in range(chips):
            left, right = d * n_orb + 2 * k + 1, (d + 1) * n_orb + 2 * k
            across += [(left, right), (right, left)]

    x = None
    for step in range(ITERS):
        final = step == ITERS - 1
        sums = [shape(flat_shape, jnp.bfloat16)] + ([half_shape] if final else [])
        if step == 0:
            resid, spread = rhs_wide, first_spread
        else:
            sib = permute(x, swap_core)
            off = lax.ppermute(x_b, ("dom", "orb"), across)
            resid, mine, other = call(
                functools.partial(resid_kernel, scale, rows_z),
                (field_shape, half_shape, half_shape),
                scratch=(pltpu.VMEM((wide, cells), jnp.bfloat16),),
            )(low_mask, x, sib, off, rhs_wide, diag, *blocks)
            spread = call(spread_kernel, spread_shape)(mine, permute(other, swap_core))
        coeff, coeff_b, coeff_o = total(spread, sums)
        extra = ([x] if step else [move]) + ([psi_wide] if final else [])
        outs = [field_shape, shape((wide, cells), jnp.bfloat16)]
        if final:
            outs = [shape((local_orbs, cells))] * 2 + [shape((n_dom, n_orb, rows_y // n_dom, rows_z))]
        x, x_b, *rest = call(
            functools.partial(update_kernel, scale, 512, step > 0, final, math.sqrt(width)),
            outs,
        )(low_mask, coeff_b, coeff_o, resid, diag, *extra, *blocks)
    other, raw = x_b, rest[0]

    weights = jnp.broadcast_to(
        smoother.reshape(2 * n_dom, n_dom, 1, 2), (2 * n_dom, n_dom, chips, 2)
    ).reshape(2 * n_dom, n_dom * n_orb)
    terms = lax.all_to_all(
        raw.reshape((n_dom * n_orb,) + raw.shape[2:]), ("dom", "orb"), 0, 0, tiled=True
    )
    z_part = rows_z // n_orb
    z_mine = o * z_part + jnp.arange(z_part)[None, :]
    pick = (jnp.arange(rows_z)[:, None] == z_mine).astype(jnp.float32)
    gradient = call(finish_kernel, shape((2 * n_dom, rows_y // n_dom, z_part)))(weights, pick, terms)

    other = permute(other, swap_core)
    solution = jnp.stack([jnp.where(low, x, other), jnp.where(low, other, x)], axis=1)
    solution = solution.reshape(rhs.shape)

    coeff, raw = lax.optimization_barrier((coeff[0], raw))
    correlations = call(
        table_kernel,
        shape((n_rows, local_orbs)),
        [SMEM, VMEM],
        scratch=(pltpu.VMEM((n_rows, local_orbs), jnp.float32),),
    )(plan, coeff).reshape(nproj, blk_rows, local_orbs)
    return (solution, correlations, gradient)


def solution(mesh):
    return jax.shard_map(
        per_device,
        mesh=mesh,
        in_specs=(
            P("orb", "dom", None, None),
            P("dom", None, None),
            P(),
            P("orb"),
            P("orb", None, "dom", None, None),
            P(),
            P("orb", "dom", None, None),
            P(),
        ),
        out_specs=(P("orb", "dom", None, None), P(None, None, "orb"), P(None, "dom", "orb")),
        check_vma=False,
    )
```

profile of v0, /device:TPU:1, one launch (start us, length us, event | category | flops | bytes accessed | tf_op | source)
XLA Modules:
  0.0 237.2 jit_solution(13807601009673674072)
XLA Ops:
  1.3 3.2 %shard_map.122 = (s32[40]{0:T(128)S(1)}, bf16[128,32,128]{2,1,0:T(8,128)(2,1)}) custom-call(s32[4]{0:T(128)S(1)} %copy-done.10, s32[1]{0:T(128)} %bitcast.6.dev_ref, bf16[2,128,2,32,128]{4,3,2,1,0:T(8,128)(2,1)} %occupied_ref.7), custom_call_target="tpu_custom_call" | custom-call | tf_op jit(solution)/shard_map/pallas_call | solution.py:371
  5.2 1.3 collective-permute-start.1
  6.5 3.4 %collective-permute-start.5 = (bf16[128,32,128]{2,1,0:T(8,128)(2,1)}, bf16[128,32,128]{2,1,0:T(8,128)(2,1)S(1)}, u32[]{:S(2)}, u32[]{:S(2)}) collective-permute-start(bf16[128,32,128]{2,1,0:T(8,128)(2,1)} %get-tuple-element.59), channel_id=1, source_target_pairs={{0,1},{1,0},{2,3},{3,2},{4,5},{5,4},{6,7},{7,6},{8,9},{9,8},{10,11... | collective-permute-start | bytes 3145736 | tf_op jit(solution)/shard_map/ppermute | solution.py:361
  9.9 1.5 shard_map.121
  13.8 1.3 add_bitcast_fusion
  16.7 1.3 collective-permute-start.2
  23.4 2.7 %shard_map.126 = bf16[128,32,128]{2,1,0:T(8,128)(2,1)} custom-call(s32[40]{0:T(128)S(1)} %get-tuple-element.60.plan_ref, bf16[2,128,2,32,128]{4,3,2,1,0:T(8,128)(2,1)} %occupied_ref.7, bf16[128,32,128]{2,1,0:T(8,128)(2,1)S(1)} %collective-permute-done.5.offer_ref), custom_call_target="tpu_custom_call" | custom-call | tf_op jit(solution)/shard_map/pallas_call | solution.py:387
  27.6 5.0 %all-to-all-start.2 = ((bf16[8,16,32,128]{3,2,1,0:T(8,128)(2,1)}), bf16[8,16,32,128]{3,2,1,0:T(8,128)(2,1)S(1)}, u32[]{:S(2)}, u32[]{:S(2)}) async-start(bf16[8,16,32,128]{3,2,1,0:T(8,128)(2,1)} %bitcast.7), calls=%async_computation.2 | async-start | bytes 2097152 | tf_op jit(solution)/shard_map/all_to_all | solution.py:407
  32.6 1.6 broadcast_select_fusion.3
  34.2 5.0 %collective-permute-start.3 = (bf16[32,32,128]{2,1,0:T(8,128)(2,1)S(1)}, bf16[32,32,128]{2,1,0:T(8,128)(2,1)S(1)}, u32[]{:S(2)}, u32[]{:S(2)}) collective-permute-start(bf16[32,32,128]{2,1,0:T(8,128)(2,1)S(1)} %get-tuple-element.57), channel_id=1, source_target_pairs={{0,4},{1,5},{14,10},{15,11},{16,20},{17,21},{30,26},{31,27},{32,36... | collective-permute-start | bytes 786440 | tf_op jit(solution)/shard_map/ppermute | solution.py:361
  39.2 1.3 collective-permute-start.4
  40.5 6.3 %all-to-all-done.2 = bf16[8,16,32,128]{3,2,1,0:T(8,128)(2,1)S(1)} async-done(((bf16[8,16,32,128]{3,2,1,0:T(8,128)(2,1)}), bf16[8,16,32,128]{3,2,1,0:T(8,128)(2,1)S(1)}, u32[]{:S(2)}, u32[]{:S(2)}) %all-to-all-start.2) | async-done | bytes 1048608 | tf_op jit(solution)/shard_map/all_to_all | solution.py:407
  47.8 4.3 %all-to-all-start.1 = ((bf16[16,16,2048]{2,1,0:T(8,128)(2,1)}), bf16[16,16,2048]{2,1,0:T(8,128)(2,1)S(1)}, u32[]{:S(2)}, u32[]{:S(2)}) async-start(bf16[16,16,2048]{2,1,0:T(8,128)(2,1)} %get-tuple-element.53), calls=%async_computation.1 | async-start | bytes 2097152 | tf_op jit(solution)/shard_map/all_to_all | solution.py:384
  55.7 1.5 collective-permute-start.10
  57.2 1.3 collective-permute-start.11
  58.5 6.1 %collective-permute-start.9 = (bf16[32,4096]{1,0:T(8,128)(2,1)S(1)}, bf16[32,4096]{1,0:T(8,128)(2,1)}, u32[]{:S(2)}, u32[]{:S(2)}) collective-permute-start(bf16[32,4096]{1,0:T(8,128)(2,1)S(1)} %bitcast.45), channel_id=1, source_target_pairs={{0,8},{1,9},{2,10},{3,11},{4,12},{5,13},{6,14},{7,15},{8,0},{9,1},... | collective-permute-start | bytes 786440 | tf_op jit(solution)/shard_map/ppermute | solution.py:361
  64.6 3.3 %all-to-all-done.1.all_ref = bf16[16,16,2048]{2,1,0:T(8,128)(2,1)S(1)} async-done(((bf16[16,16,2048]{2,1,0:T(8,128)(2,1)}), bf16[16,16,2048]{2,1,0:T(8,128)(2,1)S(1)}, u32[]{:S(2)}, u32[]{:S(2)}) %all-to-all-start.1) | async-done | bytes 1048608 | tf_op jit(solution)/shard_map/all_to_all | solution.py:384
  67.9 1.3 shard_map.127
  69.9 5.8 %all-to-all-start.3 = ((f32[16,1,512]{2,1,0:T(1,128)}), f32[16,1,512]{2,1,0:T(1,128)S(1)}, u32[]{:S(2)}, u32[]{:S(2)}) async-start(f32[16,1,512]{2,1,0:T(1,128)} %reshape.92), calls=%async_computation.3 | async-start | bytes 65536 | tf_op jit(solution)/shard_map/all_to_all | solution.py:484
  76.6 4.9 %all-to-all-done.3 = f32[16,1,512]{2,1,0:T(1,128)S(1)} async-done(((f32[16,1,512]{2,1,0:T(1,128)}), f32[16,1,512]{2,1,0:T(1,128)S(1)}, u32[]{:S(2)}, u32[]{:S(2)}) %all-to-all-start.3) | async-done | bytes 32800 | tf_op jit(solution)/shard_map/all_to_all | solution.py:484
  83.7 10.5 %all-to-all-start.4 = ((f32[16,8,512]{2,1,0:T(8,128)}), f32[16,8,512]{2,1,0:T(8,128)S(1)}, u32[]{:S(2)}, u32[]{:S(2)}) async-start(f32[16,8,512]{2,1,0:T(8,128)} %shard_map.128), calls=%async_computation.4 | async-start | bytes 524288 | tf_op jit(solution)/shard_map/all_to_all | solution.py:476
  94.2 1.8 constant_dynamic-update-slice_fusion
  96.2 2.4 %collective-permute-start.14 = (bf16[64,4096]{1,0:T(8,128)(2,1)}, bf16[64,4096]{1,0:T(8,128)(2,1)}, u32[]{:S(2)}, u32[]{:S(2)}) collective-permute-start(bf16[64,4096]{1,0:T(8,128)(2,1)} %get-tuple-element.104), channel_id=1, source_target_pairs={{0,6},{1,7},{2,0},{3,1},{4,2},{5,3},{6,4},{7,5},{8,14},{9,15},{10,... | collective-permute-start | bytes 1572872 | tf_op jit(solution)/shard_map/ppermute | solution.py:361
  99.6 2.0 pad_maximum_fusion
  102.8 2.7 %collective-permute-start.16 = (bf16[16,4096]{1,0:T(8,128)(2,1)S(1)}, bf16[16,4096]{1,0:T(8,128)(2,1)S(1)}, u32[]{:S(2)}, u32[]{:S(2)}) collective-permute-start(bf16[16,4096]{1,0:T(8,128)(2,1)S(1)} %slice.35), channel_id=1, source_target_pairs={{0,6},{1,7},{2,0},{3,1},{4,2},{5,3},{6,4},{7,5},{8,14},{9,15},{10,... | collective-permute-start | bytes 393224 | tf_op jit(solution)/shard_map/ppermute | solution.py:361
  107.5 5.5 %collective-permute-done.15 = bf16[16,4096]{1,0:T(8,128)(2,1)S(1)} collective-permute-done((bf16[16,4096]{1,0:T(8,128)(2,1)S(1)}, bf16[16,4096]{1,0:T(8,128)(2,1)S(1)}, u32[]{:S(2)}, u32[]{:S(2)}) %collective-permute-start.15) | collective-permute-done | bytes 131104 | tf_op jit(solution)/shard_map/ppermute | solution.py:361
  113.0 1.5 collective-permute-start.6
  114.5 6.1 %collective-permute-done.12 = bf16[96,4096]{1,0:T(8,128)(2,1)} collective-permute-done((bf16[96,4096]{1,0:T(8,128)(2,1)}, bf16[96,4096]{1,0:T(8,128)(2,1)}, u32[]{:S(2)}, u32[]{:S(2)}) %collective-permute-start.12) | collective-permute-done | bytes 786464 | tf_op jit(solution)/shard_map/ppermute | solution.py:361
  127.0 2.7 %collective-permute-start.18 = (bf16[32,4096]{1,0:T(8,128)(2,1)S(1)}, bf16[32,4096]{1,0:T(8,128)(2,1)S(1)}, u32[]{:S(2)}, u32[]{:S(2)}) collective-permute-start(bf16[32,4096]{1,0:T(8,128)(2,1)S(1)} %slice.37), channel_id=1, source_target_pairs={{0,6},{1,7},{2,0},{3,1},{4,2},{5,3},{6,4},{7,5},{8,14},{9,15},{10,... | collective-permute-start | bytes 786440 | tf_op jit(solution)/shard_map/ppermute | solution.py:361
  129.7 4.3 %collective-permute-done.17 = bf16[32,4096]{1,0:T(8,128)(2,1)S(1)} collective-permute-done((bf16[32,4096]{1,0:T(8,128)(2,1)S(1)}, bf16[32,4096]{1,0:T(8,128)(2,1)S(1)}, u32[]{:S(2)}, u32[]{:S(2)}) %collective-permute-start.17) | collective-permute-done | bytes 262176 | tf_op jit(solution)/shard_map/ppermute | solution.py:361
  134.9 2.9 %collective-permute-start.20 = (f32[16,4096]{1,0:T(8,128)S(1)}, f32[16,4096]{1,0:T(8,128)S(1)}, u32[]{:S(2)}, u32[]{:S(2)}) collective-permute-start(f32[16,4096]{1,0:T(8,128)S(1)} %get-tuple-element.73.x_ref.refs_0_), channel_id=1, source_target_pairs={{0,1},{1,0},{2,3},{3,2},{4,5},{5,4},{6,7},{7,6},{8,9},{9,8},{10,11... | collective-permute-start | bytes 786440 | tf_op jit(solution)/shard_map/ppermute | solution.py:361
  137.8 4.5 %collective-permute-start.21 = (bf16[16,4096]{1,0:T(8,128)(2,1)S(1)}, bf16[16,4096]{1,0:T(8,128)(2,1)S(1)}, u32[]{:S(2)}, u32[]{:S(2)}) collective-permute-start(bf16[16,4096]{1,0:T(8,128)(2,1)S(1)} %get-tuple-element.74), channel_id=1, source_target_pairs={{1,16},{16,1},{3,18},{18,3},{5,20},{20,5},{7,22},{22,7},{9,24},{24... | collective-permute-start | bytes 393224 | tf_op jit(solution)/shard_map/ppermute | solution.py:510
  142.4 3.2 %collective-permute-done.21.off_ref = bf16[16,4096]{1,0:T(8,128)(2,1)S(1)} collective-permute-done((bf16[16,4096]{1,0:T(8,128)(2,1)S(1)}, bf16[16,4096]{1,0:T(8,128)(2,1)S(1)}, u32[]{:S(2)}, u32[]{:S(2)}) %collective-permute-start.21) | collective-permute-done | bytes 131104 | tf_op jit(solution)/shard_map/ppermute | solution.py:510
  145.6 1.2 shard_map.131
  148.1 22.3 %all_to_all.39.parts_ref = f32[16,8,512]{2,1,0:T(8,128)S(1)} all-to-all(f32[16,8,512]{2,1,0:T(8,128)S(1)} %shard_map.132), channel_id=1, replica_groups=mesh['dom'=16,'orb'=16] {'dom'}, dimensions={0} | all-to-all | bytes 524288 | tf_op jit(solution)/shard_map/all_to_all | solution.py:476
  170.4 1.7 collective-permute-start.23
  172.9 1.3 shard_map.134
  174.6 2.3 collective-permute-start.25
  177.7 4.8 %collective-permute-done.25.off_ref = bf16[16,4096]{1,0:T(8,128)(2,1)S(1)} collective-permute-done((bf16[16,4096]{1,0:T(8,128)(2,1)}, bf16[16,4096]{1,0:T(8,128)(2,1)S(1)}, u32[]{:S(2)}, u32[]{:S(2)}) %collective-permute-start.25) | collective-permute-done | bytes 131104 | tf_op jit(solution)/shard_map/ppermute | solution.py:510
  183.2 1.6 copy-done.2
  185.7 1.8 shard_map.135
  191.0 4.5 %all-to-all-start.6 = ((f32[16,8,512]{2,1,0:T(8,128)}), f32[16,8,512]{2,1,0:T(8,128)S(1)}, u32[]{:S(2)}, u32[]{:S(2)}) async-start(f32[16,8,512]{2,1,0:T(8,128)} %shard_map.136), calls=%async_computation.6 | async-start | bytes 524288 | tf_op jit(solution)/shard_map/all_to_all | solution.py:476
  196.4 12.0 %all-to-all-done.6.parts_ref = f32[16,8,512]{2,1,0:T(8,128)S(1)} async-done(((f32[16,8,512]{2,1,0:T(8,128)}), f32[16,8,512]{2,1,0:T(8,128)S(1)}, u32[]{:S(2)}, u32[]{:S(2)}) %all-to-all-start.6) | async-done | bytes 262176 | tf_op jit(solution)/shard_map/all_to_all | solution.py:476
  208.4 1.9 collective-permute-start.27
  211.1 1.6 copy-done.3
  212.7 1.4 shard_map.139
  214.5 6.2 %all-to-all-start.7 = ((f32[256,2,128]{2,1,0:T(2,128)}), f32[256,2,128]{2,1,0:T(2,128)S(1)}, u32[]{:S(2)}, u32[]{:S(2)}) async-start(f32[256,2,128]{2,1,0:T(2,128)} %bitcast.21), calls=%async_computation.7 | async-start | bytes 524288 | tf_op jit(solution)/shard_map/all_to_all | solution.py:531
  222.9 13.0 %all-to-all-done.7.terms_ref = f32[256,2,128]{2,1,0:T(2,128)S(1)} async-done(((f32[256,2,128]{2,1,0:T(2,128)}), f32[256,2,128]{2,1,0:T(2,128)S(1)}, u32[]{:S(2)}, u32[]{:S(2)}) %all-to-all-start.7) | async-done | bytes 262176 | tf_op jit(solution)/shard_map/all_to_all | solution.py:531
  (139 shorter events, 40.3 us)
Async XLA Ops:
  1.3 3.2 %copy-start.11 = (bf16[2,128,2,32,128]{4,3,2,1,0:T(8,128)(2,1)S(1)}, bf16[2,128,2,32,128]{4,3,2,1,0:T(8,128)(2,1)}, u32[]{:S(2)}) copy-start(bf16[2,128,2,32,128]{4,3,2,1,0:T(8,128)(2,1)} %occupied_ref.7) | copy-start | bytes 12582916
  4.5 5.4 %copy-start.5 = (f32[8,2,32,128]{3,2,1,0:T(8,128)S(1)}, f32[8,2,32,128]{3,2,1,0:T(8,128)}, u32[]{:S(2)}) copy-start(f32[8,2,32,128]{3,2,1,0:T(8,128)} %field_ref.1) | copy-start | bytes 786436
  4.5 6.9 %copy-start.17 = (s32[8]{0:T(128)S(1)}, s32[8]{0:T(128)}, u32[]{:S(2)}) copy-start(s32[8]{0:T(128)} %param.15) | copy-start | bytes 100
  5.2 10.8 %collective-permute-start.1 = (bf16[128,32,128]{2,1,0:T(8,128)(2,1)S(1)}, bf16[128,32,128]{2,1,0:T(8,128)(2,1)S(1)}, u32[]{:S(2)}, u32[]{:S(2)}) collective-permute-start(bf16[128,32,128]{2,1,0:T(8,128)(2,1)S(1)} %shard_map.123), channel_id=1, source_target_pairs={{0,1},{15,14},{16,17},{31,30},{32,33},{47,46},{48,49},{63,62},{64,... | collective-permute-start | bytes 3145736 | tf_op jit(solution)/shard_map/ppermute | solution.py:361
  6.5 16.9 %collective-permute-start.5 = (bf16[128,32,128]{2,1,0:T(8,128)(2,1)}, bf16[128,32,128]{2,1,0:T(8,128)(2,1)S(1)}, u32[]{:S(2)}, u32[]{:S(2)}) collective-permute-start(bf16[128,32,128]{2,1,0:T(8,128)(2,1)} %get-tuple-element.59), channel_id=1, source_target_pairs={{0,1},{1,0},{2,3},{3,2},{4,5},{5,4},{6,7},{7,6},{8,9},{9,8},{10,11... | collective-permute-start | bytes 3145736 | tf_op jit(solution)/shard_map/ppermute | solution.py:361
  11.4 21.2 %collective-permute-start.7 = (f32[8,4096]{1,0:T(8,128)}, f32[8,4096]{1,0:T(8,128)}, u32[]{:S(2)}, u32[]{:S(2)}) collective-permute-start(f32[8,4096]{1,0:T(8,128)} %get-tuple-element.64), channel_id=1, source_target_pairs={{0,1},{1,0},{2,3},{3,2},{4,5},{5,4},{6,7},{7,6},{8,9},{9,8},{10,11... | collective-permute-start | bytes 393224 | tf_op jit(solution)/shard_map/ppermute | solution.py:361
  12.4 11.0 %collective-permute-start.8 = (f32[8,1]{0,1:T(1,128)S(1)}, f32[8,1]{0,1:T(1,128)S(1)}, u32[]{:S(2)}, u32[]{:S(2)}) collective-permute-start(f32[8,1]{0,1:T(1,128)S(1)} %bitcast.56), channel_id=1, source_target_pairs={{0,1},{1,0},{2,3},{3,2},{4,5},{5,4},{6,7},{7,6},{8,9},{9,8},{10,11... | collective-permute-start | bytes 104 | tf_op jit(solution)/shard_map/ppermute | solution.py:361
  16.7 9.4 %collective-permute-start.2 = (bf16[32,32,128]{2,1,0:T(8,128)(2,1)S(1)}, bf16[32,32,128]{2,1,0:T(8,128)(2,1)S(1)}, u32[]{:S(2)}, u32[]{:S(2)}) collective-permute-start(bf16[32,32,128]{2,1,0:T(8,128)(2,1)S(1)} %get-tuple-element.56), channel_id=1, source_target_pairs={{0,2},{1,3},{14,8},{15,9},{16,18},{17,19},{30,24},{31,25},{32,34},... | collective-permute-start | bytes 786440 | tf_op jit(solution)/shard_map/ppermute | solution.py:361
  27.6 20.3 %copy-start.13 = (bf16[16,32,128]{2,1,0:T(8,128)(2,1)}, bf16[16,32,128]{2,1,0:T(8,128)(2,1)S(1)}, u32[]{:S(2)}) copy-start(bf16[16,32,128]{2,1,0:T(8,128)(2,1)S(1)} %get-tuple-element.120) | copy-start | bytes 393220
  27.6 19.3 %all-to-all-start.2 = ((bf16[8,16,32,128]{3,2,1,0:T(8,128)(2,1)}), bf16[8,16,32,128]{3,2,1,0:T(8,128)(2,1)S(1)}, u32[]{:S(2)}, u32[]{:S(2)}) async-start(bf16[8,16,32,128]{3,2,1,0:T(8,128)(2,1)} %bitcast.7), calls=%async_computation.2 | async-start | bytes 2097152 | tf_op jit(solution)/shard_map/all_to_all | solution.py:407
  34.2 17.9 %copy-start.15 = (f32[8,4096]{1,0:T(8,128)S(1)}, f32[8,4096]{1,0:T(8,128)}, u32[]{:S(2)}) copy-start(f32[8,4096]{1,0:T(8,128)} %get-tuple-element.109) | copy-start | bytes 393220
  34.2 18.7 %collective-permute-start.3 = (bf16[32,32,128]{2,1,0:T(8,128)(2,1)S(1)}, bf16[32,32,128]{2,1,0:T(8,128)(2,1)S(1)}, u32[]{:S(2)}, u32[]{:S(2)}) collective-permute-start(bf16[32,32,128]{2,1,0:T(8,128)(2,1)S(1)} %get-tuple-element.57), channel_id=1, source_target_pairs={{0,4},{1,5},{14,10},{15,11},{16,20},{17,21},{30,26},{31,27},{32,36... | collective-permute-start | bytes 786440 | tf_op jit(solution)/shard_map/ppermute | solution.py:361
  39.2 13.7 %collective-permute-start.4 = (bf16[32,32,128]{2,1,0:T(8,128)(2,1)S(1)}, bf16[32,32,128]{2,1,0:T(8,128)(2,1)S(1)}, u32[]{:S(2)}, u32[]{:S(2)}) collective-permute-start(bf16[32,32,128]{2,1,0:T(8,128)(2,1)S(1)} %get-tuple-element.58), channel_id=1, source_target_pairs={{0,6},{1,7},{14,12},{15,13},{16,22},{17,23},{30,28},{31,29},{32,38... | collective-permute-start | bytes 786440 | tf_op jit(solution)/shard_map/ppermute | solution.py:361
  46.9 1.0 copy-start.12
  47.8 20.1 %all-to-all-start.1 = ((bf16[16,16,2048]{2,1,0:T(8,128)(2,1)}), bf16[16,16,2048]{2,1,0:T(8,128)(2,1)S(1)}, u32[]{:S(2)}, u32[]{:S(2)}) async-start(bf16[16,16,2048]{2,1,0:T(8,128)(2,1)} %get-tuple-element.53), calls=%async_computation.1 | async-start | bytes 2097152 | tf_op jit(solution)/shard_map/all_to_all | solution.py:384
  52.1 1.6 copy-start.14
  55.7 38.4 %collective-permute-start.10 = (bf16[32,4096]{1,0:T(8,128)(2,1)S(1)}, bf16[32,4096]{1,0:T(8,128)(2,1)}, u32[]{:S(2)}, u32[]{:S(2)}) collective-permute-start(bf16[32,4096]{1,0:T(8,128)(2,1)S(1)} %pad_maximum_fusion.1.mids_ref), channel_id=1, source_target_pairs={{0,2},{1,3},{2,4},{3,5},{4,6},{5,7},{6,0},{7,1},{8,10},{9,11},{10,... | collective-permute-start | bytes 786440 | tf_op jit(solution)/shard_map/ppermute | solution.py:361
  57.2 37.0 %collective-permute-start.11 = (bf16[32,4096]{1,0:T(8,128)(2,1)S(1)}, bf16[32,4096]{1,0:T(8,128)(2,1)}, u32[]{:S(2)}, u32[]{:S(2)}) collective-permute-start(bf16[32,4096]{1,0:T(8,128)(2,1)S(1)} %pad_maximum_fusion.1.mids_ref), channel_id=1, source_target_pairs={{0,6},{1,7},{2,0},{3,1},{4,2},{5,3},{6,4},{7,5},{8,14},{9,15},{10,... | collective-permute-start | bytes 786440 | tf_op jit(solution)/shard_map/ppermute | solution.py:361
  58.5 35.7 %collective-permute-start.9 = (bf16[32,4096]{1,0:T(8,128)(2,1)S(1)}, bf16[32,4096]{1,0:T(8,128)(2,1)}, u32[]{:S(2)}, u32[]{:S(2)}) collective-permute-start(bf16[32,4096]{1,0:T(8,128)(2,1)S(1)} %bitcast.45), channel_id=1, source_target_pairs={{0,8},{1,9},{2,10},{3,11},{4,12},{5,13},{6,14},{7,15},{8,0},{9,1},... | collective-permute-start | bytes 786440 | tf_op jit(solution)/shard_map/ppermute | solution.py:361
  69.9 11.6 %all-to-all-start.3 = ((f32[16,1,512]{2,1,0:T(1,128)}), f32[16,1,512]{2,1,0:T(1,128)S(1)}, u32[]{:S(2)}, u32[]{:S(2)}) async-start(f32[16,1,512]{2,1,0:T(1,128)} %reshape.92), calls=%async_computation.3 | async-start | bytes 65536 | tf_op jit(solution)/shard_map/all_to_all | solution.py:484
  83.7 23.8 %all-to-all-start.4 = ((f32[16,8,512]{2,1,0:T(8,128)}), f32[16,8,512]{2,1,0:T(8,128)S(1)}, u32[]{:S(2)}, u32[]{:S(2)}) async-start(f32[16,8,512]{2,1,0:T(8,128)} %shard_map.128), calls=%async_computation.4 | async-start | bytes 524288 | tf_op jit(solution)/shard_map/all_to_all | solution.py:476
  96.0 18.6 %collective-permute-start.13 = (bf16[64,4096]{1,0:T(8,128)(2,1)}, bf16[64,4096]{1,0:T(8,128)(2,1)}, u32[]{:S(2)}, u32[]{:S(2)}) collective-permute-start(bf16[64,4096]{1,0:T(8,128)(2,1)} %get-tuple-element.104), channel_id=1, source_target_pairs={{0,2},{1,3},{2,4},{3,5},{4,6},{5,7},{6,0},{7,1},{8,10},{9,11},{10,... | collective-permute-start | bytes 1572872 | tf_op jit(solution)/shard_map/ppermute | solution.py:361
  96.2 18.3 %collective-permute-start.14 = (bf16[64,4096]{1,0:T(8,128)(2,1)}, bf16[64,4096]{1,0:T(8,128)(2,1)}, u32[]{:S(2)}, u32[]{:S(2)}) collective-permute-start(bf16[64,4096]{1,0:T(8,128)(2,1)} %get-tuple-element.104), channel_id=1, source_target_pairs={{0,6},{1,7},{2,0},{3,1},{4,2},{5,3},{6,4},{7,5},{8,14},{9,15},{10,... | collective-permute-start | bytes 1572872 | tf_op jit(solution)/shard_map/ppermute | solution.py:361
  102.5 18.2 %collective-permute-start.12 = (bf16[96,4096]{1,0:T(8,128)(2,1)}, bf16[96,4096]{1,0:T(8,128)(2,1)}, u32[]{:S(2)}, u32[]{:S(2)}) collective-permute-start(bf16[96,4096]{1,0:T(8,128)(2,1)} %pad_maximum_fusion), channel_id=1, source_target_pairs={{0,8},{1,9},{2,10},{3,11},{4,12},{5,13},{6,14},{7,15},{8,0},{9,1},... | collective-permute-start | bytes 2359304 | tf_op jit(solution)/shard_map/ppermute | solution.py:361
  102.6 10.4 %collective-permute-start.15 = (bf16[16,4096]{1,0:T(8,128)(2,1)S(1)}, bf16[16,4096]{1,0:T(8,128)(2,1)S(1)}, u32[]{:S(2)}, u32[]{:S(2)}) collective-permute-start(bf16[16,4096]{1,0:T(8,128)(2,1)S(1)} %slice.34), channel_id=1, source_target_pairs={{0,2},{1,3},{2,4},{3,5},{4,6},{5,7},{6,0},{7,1},{8,10},{9,11},{10,... | collective-permute-start | bytes 393224 | tf_op jit(solution)/shard_map/ppermute | solution.py:361
  102.8 11.7 %collective-permute-start.16 = (bf16[16,4096]{1,0:T(8,128)(2,1)S(1)}, bf16[16,4096]{1,0:T(8,128)(2,1)S(1)}, u32[]{:S(2)}, u32[]{:S(2)}) collective-permute-start(bf16[16,4096]{1,0:T(8,128)(2,1)S(1)} %slice.35), channel_id=1, source_target_pairs={{0,6},{1,7},{2,0},{3,1},{4,2},{5,3},{6,4},{7,5},{8,14},{9,15},{10,... | collective-permute-start | bytes 393224 | tf_op jit(solution)/shard_map/ppermute | solution.py:361
  107.4 16.2 %copy-start = (bf16[256,4096]{1,0:T(8,128)(2,1)S(1)}, bf16[256,4096]{1,0:T(8,128)(2,1)}, u32[]{:S(2)}) copy-start(bf16[256,4096]{1,0:T(8,128)(2,1)} %get-tuple-element.105) | copy-start | bytes 6291460
  113.0 21.1 %collective-permute-start.6 = (bf16[16,256]{1,0:T(8,128)(2,1)S(1)}, bf16[16,256]{1,0:T(8,128)(2,1)S(1)}, u32[]{:S(2)}, u32[]{:S(2)}) collective-permute-start(bf16[16,256]{1,0:T(8,128)(2,1)S(1)} %shard_map.129.mine_ref), channel_id=1, source_target_pairs={{0,1},{1,0},{2,3},{3,2},{4,5},{5,4},{6,7},{7,6},{8,9},{9,8},{10,11... | collective-permute-start | bytes 24584 | tf_op jit(solution)/shard_map/ppermute | solution.py:361
  120.7 9.0 %collective-permute-start.19 = (bf16[32,4096]{1,0:T(8,128)(2,1)S(1)}, bf16[32,4096]{1,0:T(8,128)(2,1)S(1)}, u32[]{:S(2)}, u32[]{:S(2)}) collective-permute-start(bf16[32,4096]{1,0:T(8,128)(2,1)S(1)} %pad_maximum_fusion.3), channel_id=1, source_target_pairs={{0,8},{1,9},{2,10},{3,11},{4,12},{5,13},{6,14},{7,15},{8,0},{9,1},... | collective-permute-start | bytes 786440 | tf_op jit(solution)/shard_map/ppermute | solution.py:361
  123.7 10.4 %copy-start.4 = (bf16[512,512]{1,0:T(8,128)(2,1)S(1)}, bf16[512,512]{1,0:T(8,128)(2,1)}, u32[]{:S(2)}) copy-start(bf16[512,512]{1,0:T(8,128)(2,1)} %fusion.refs_0_) | copy-start | bytes 1572868
  126.9 7.2 %collective-permute-start.17 = (bf16[32,4096]{1,0:T(8,128)(2,1)S(1)}, bf16[32,4096]{1,0:T(8,128)(2,1)S(1)}, u32[]{:S(2)}, u32[]{:S(2)}) collective-permute-start(bf16[32,4096]{1,0:T(8,128)(2,1)S(1)} %slice.36), channel_id=1, source_target_pairs={{0,2},{1,3},{2,4},{3,5},{4,6},{5,7},{6,0},{7,1},{8,10},{9,11},{10,... | collective-permute-start | bytes 786440 | tf_op jit(solution)/shard_map/ppermute | solution.py:361
  127.0 7.1 %collective-permute-start.18 = (bf16[32,4096]{1,0:T(8,128)(2,1)S(1)}, bf16[32,4096]{1,0:T(8,128)(2,1)S(1)}, u32[]{:S(2)}, u32[]{:S(2)}) collective-permute-start(bf16[32,4096]{1,0:T(8,128)(2,1)S(1)} %slice.37), channel_id=1, source_target_pairs={{0,6},{1,7},{2,0},{3,1},{4,2},{5,3},{6,4},{7,5},{8,14},{9,15},{10,... | collective-permute-start | bytes 786440 | tf_op jit(solution)/shard_map/ppermute | solution.py:361
  134.1 38.8 %copy-start.1 = (bf16[256,4096]{1,0:T(8,128)(2,1)}, bf16[256,4096]{1,0:T(8,128)(2,1)S(1)}, u32[]{:S(2)}) copy-start(bf16[256,4096]{1,0:T(8,128)(2,1)S(1)} %constant_dynamic-update-slice_fusion.2.refs_1_.first_ref.refs_2_) | copy-start | bytes 6291460
  134.9 10.7 %collective-permute-start.20 = (f32[16,4096]{1,0:T(8,128)S(1)}, f32[16,4096]{1,0:T(8,128)S(1)}, u32[]{:S(2)}, u32[]{:S(2)}) collective-permute-start(f32[16,4096]{1,0:T(8,128)S(1)} %get-tuple-element.73.x_ref.refs_0_), channel_id=1, source_target_pairs={{0,1},{1,0},{2,3},{3,2},{4,5},{5,4},{6,7},{7,6},{8,9},{9,8},{10,11... | collective-permute-start | bytes 786440 | tf_op jit(solution)/shard_map/ppermute | solution.py:361
  137.8 7.8 %collective-permute-start.21 = (bf16[16,4096]{1,0:T(8,128)(2,1)S(1)}, bf16[16,4096]{1,0:T(8,128)(2,1)S(1)}, u32[]{:S(2)}, u32[]{:S(2)}) collective-permute-start(bf16[16,4096]{1,0:T(8,128)(2,1)S(1)} %get-tuple-element.74), channel_id=1, source_target_pairs={{1,16},{16,1},{3,18},{18,3},{5,20},{20,5},{7,22},{22,7},{9,24},{24... | collective-permute-start | bytes 393224 | tf_op jit(solution)/shard_map/ppermute | solution.py:510
  146.8 1.2 collective-permute-start.22
  170.4 2.5 %collective-permute-start.23 = (bf16[16,256]{1,0:T(8,128)(2,1)S(1)}, bf16[16,256]{1,0:T(8,128)(2,1)S(1)}, u32[]{:S(2)}, u32[]{:S(2)}) collective-permute-start(bf16[16,256]{1,0:T(8,128)(2,1)S(1)} %shard_map.133.mine_ref), channel_id=1, source_target_pairs={{0,1},{1,0},{2,3},{3,2},{4,5},{5,4},{6,7},{7,6},{8,9},{9,8},{10,11... | collective-permute-start | bytes 24584 | tf_op jit(solution)/shard_map/ppermute | solution.py:361
  172.9 4.0 %copy-start.16 = (bf16[8,2,32,128]{3,2,1,0:T(8,128)(2,1)S(1)}, bf16[8,2,32,128]{3,2,1,0:T(8,128)(2,1)}, u32[]{:S(2)}) copy-start(bf16[8,2,32,128]{3,2,1,0:T(8,128)(2,1)} %param.18) | copy-start | bytes 393220
  174.2 9.0 %collective-permute-start.24 = (f32[16,4096]{1,0:T(8,128)S(1)}, f32[16,4096]{1,0:T(8,128)S(1)}, u32[]{:S(2)}, u32[]{:S(2)}) collective-permute-start(f32[16,4096]{1,0:T(8,128)S(1)} %get-tuple-element.78.x_ref.refs_0_), channel_id=1, source_target_pairs={{0,1},{1,0},{2,3},{3,2},{4,5},{5,4},{6,7},{7,6},{8,9},{9,8},{10,11... | collective-permute-start | bytes 786440 | tf_op jit(solution)/shard_map/ppermute | solution.py:361
  174.6 8.0 %collective-permute-start.25 = (bf16[16,4096]{1,0:T(8,128)(2,1)}, bf16[16,4096]{1,0:T(8,128)(2,1)S(1)}, u32[]{:S(2)}, u32[]{:S(2)}) collective-permute-start(bf16[16,4096]{1,0:T(8,128)(2,1)} %get-tuple-element.79), channel_id=1, source_target_pairs={{1,16},{16,1},{3,18},{18,3},{5,20},{20,5},{7,22},{22,7},{9,24},{24... | collective-permute-start | bytes 393224 | tf_op jit(solution)/shard_map/ppermute | solution.py:510
  177.7 17.8 %collective-permute-start.28 = (bf16[8,4096]{1,0:T(8,128)(2,1)}, bf16[8,4096]{1,0:T(8,128)(2,1)}, u32[]{:S(2)}, u32[]{:S(2)}) collective-permute-start(bf16[8,4096]{1,0:T(8,128)(2,1)} %convert_element_type.26), channel_id=1, source_target_pairs={{0,1},{1,0},{2,3},{3,2},{4,5},{5,4},{6,7},{7,6},{8,9},{9,8},{10,11... | collective-permute-start | bytes 196616 | tf_op jit(solution)/shard_map/ppermute | solution.py:361
  183.2 1.6 copy-start.2
  188.2 1.4 collective-permute-start.26
  191.0 17.3 %all-to-all-start.6 = ((f32[16,8,512]{2,1,0:T(8,128)}), f32[16,8,512]{2,1,0:T(8,128)S(1)}, u32[]{:S(2)}, u32[]{:S(2)}) async-start(f32[16,8,512]{2,1,0:T(8,128)} %shard_map.136), calls=%async_computation.6 | async-start | bytes 524288 | tf_op jit(solution)/shard_map/all_to_all | solution.py:476
  208.4 2.7 %collective-permute-start.27 = (bf16[16,256]{1,0:T(8,128)(2,1)S(1)}, bf16[16,256]{1,0:T(8,128)(2,1)S(1)}, u32[]{:S(2)}, u32[]{:S(2)}) collective-permute-start(bf16[16,256]{1,0:T(8,128)(2,1)S(1)} %get-tuple-element.82.mine_ref), channel_id=1, source_target_pairs={{0,1},{1,0},{2,3},{3,2},{4,5},{5,4},{6,7},{7,6},{8,9},{9,8},{10,11... | collective-permute-start | bytes 24584 | tf_op jit(solution)/shard_map/ppermute | solution.py:361
  211.1 1.6 copy-start.3
  214.1 8.0 %collective-permute-start.29 = (f32[8,4096]{1,0:T(8,128)S(1)}, f32[8,4096]{1,0:T(8,128)S(1)}, u32[]{:S(2)}, u32[]{:S(2)}) collective-permute-start(f32[8,4096]{1,0:T(8,128)S(1)} %get-tuple-element.87), channel_id=1, source_target_pairs={{0,1},{1,0},{2,3},{3,2},{4,5},{5,4},{6,7},{7,6},{8,9},{9,8},{10,11... | collective-permute-start | bytes 393224 | tf_op jit(solution)/shard_map/ppermute | solution.py:361
  214.5 21.5 %all-to-all-start.7 = ((f32[256,2,128]{2,1,0:T(2,128)}), f32[256,2,128]{2,1,0:T(2,128)S(1)}, u32[]{:S(2)}, u32[]{:S(2)}) async-start(f32[256,2,128]{2,1,0:T(2,128)} %bitcast.21), calls=%async_computation.7 | async-start | bytes 524288 | tf_op jit(solution)/shard_map/all_to_all | solution.py:531
  (5 other events, 3.5 us)
where the time goes:
time: 239 us; the launch traced here: 237 us
  starting transfers between devices  82.8 us (35%)
  waiting for transfers between devices  66.9 us (28%)
  local copies, waits for them, and re-layouts  25.9 us (11%)
  blocking collectives  22.3 us (9%)
  Pallas kernels  20.3 us (8%)
  other arithmetic  12.3 us (5%)
  between operations  6.62 us (3%)
    ppermute x27, starting transfers between devices, permute(): return lax.ppermute(value, 'orb', pairs)  39.7 us
    all_to_all x1, blocking collectives, total(): parts = lax.all_to_all(spread, 'dom', 0, 0, tiled=True)  22.3 us
    ppermute x27, waiting for transfers between devices, permute(): return lax.ppermute(value, 'orb', pairs)  19.4 us
    unnamed x53, local copies, waits for them, and re-layouts  17.2 us
    all_to_all x2, starting transfers between devices, total(): parts = lax.all_to_all(spread, 'dom', 0, 0, tiled=True)  15 us
    all_to_all x1, waiting for transfers between devices, per_device(): lax.all_to_all(raw.reshape((n_dom * n_orb,) + raw.shape[2:]), ('dom', 'or...  13 us
    all_to_all x2, waiting for transfers between devices, total(): parts = lax.all_to_all(spread, 'dom', 0, 0, tiled=True)  12 us
    ppermute x2, waiting for transfers between devices, per_device(): off = lax.ppermute(x_b, ('dom', 'orb'), across)  8.07 us
  transfers between devices with their start and end apart: 35, of which 14 were waited for; matrix products, arithmetic and copies ran while one was open for 13% of the time, Pallas kernels for 5%

commit v1 on v0

--- a/solution.py
+++ b/solution.py
@@ -77,8 +77,9 @@
         copy.wait()
 
 
-def offer_kernel(per_dev, n_orb, ids_ref, dev_ref, occupied_ref, plan_ref, offer_ref, sem):
+def offer_kernel(per_dev, n_orb, ids_ref, dev_ref, occupied_ref, plan_ref, same_ref, offer_ref, sem):
     plan(per_dev, n_orb, ids_ref, dev_ref, plan_ref)
+    same_ref[0] = plan_ref[SAME]
     core = plan_ref[DEV] % 2
     run(copies(lambda at, n: occupied_ref.at[plan_ref[SLOT], pl.ds(at, n), 1 - core], offer_ref, sem))
 
@@ -162,40 +163,48 @@
     split(low_ref, jnp.concatenate(parts, axis=1) * scale, mine_ref, other_ref)
 
 
-def fields_kernel(low_ref, field_ref, mine_ref, other_ref, *all_refs):
+def fields_kernel(low_ref, field_ref, mine_ref, other_ref, *both_refs):
     rows_y, rows_z = field_ref.shape[2:]
     low = low_ref[...] > 0.5
-    half = field_ref.shape[0]
     for y in range(rows_y):
         first, second = field_ref[:, 0, y, :], field_ref[:, 1, y, :]
         here = slice(y * rows_z, (y + 1) * rows_z)
         mine_ref[:, here] = jnp.where(low, first, second)
         other_ref[:, here] = jnp.where(low, second, first)
-    if all_refs:
-        (all_ref,) = all_refs
-        wide = all_ref.shape[2]
-        step = rows_y * rows_z // wide
-        for plane in range(2):
-            for y in range(rows_y // step):
-                parts = [field_ref[:, plane, y + k * (rows_y // step), :] for k in range(step)]
-                rows = jnp.concatenate(parts, axis=0).astype(jnp.bfloat16)
-                for d in range(plane, all_ref.shape[0], 2):
-                    all_ref[d, :, y * rows_z : (y + 1) * rows_z] = rows
-
-
-def shares_kernel(scale, all_ref, ends_ref, mids_ref, out_ref):
-    sources, rows, wide = all_ref.shape
-    every = all_ref[...].reshape(sources * rows, wide)
-    parts = rows // out_ref.shape[1]
+        for ref in both_refs:
+            ref[:, here] = jnp.concatenate([first, second], axis=0).astype(jnp.bfloat16)
+
+
+def pair_kernel(low_ref, mine_ref, other_ref, out_ref):
+    half = mine_ref.shape[0]
+    low = core_mask(low_ref, mine_ref.shape[1])
+    mine, other = mine_ref[...], other_ref[...]
+    out_ref[:half] = jnp.where(low, mine, other)
+    out_ref[half:] = jnp.where(low, other, mine)
+
+
+def take_kernel(plan_ref, offered_ref, second_ref, out_ref):
+    rows = offered_ref.shape[1]
+    out_ref[:rows] = offered_ref[plan_ref[CHIP]]
+
+    @pl.when(plan_ref[SAME] == 1)
+    def _():
+        out_ref[rows:] = second_ref[...]
+
+    @pl.when(plan_ref[SAME] != 1)
+    def _():
+        out_ref[rows:] = offered_ref[plan_ref[CHIP + 1]]
+
+
+def shares_kernel(scale, low_ref, all_ref, ends_ref, mids_ref, out_ref):
+    devices, orbs = out_ref.shape[:2]
+    low = low_ref[0:1, 0:1] > 0.5
     for at, ref in ((0, ends_ref), (ends_ref.shape[0], mids_ref)):
         n = ref.shape[0]
-        total = 0.0
-        for k in range(parts):
-            cells = ref[:, k * wide : (k + 1) * wide]
-            got = lax.dot_general(every, cells, NT, preferred_element_type=jnp.float32)
-            got = got.reshape(sources, parts, rows // parts, n)
-            total = total + got[:, k]
-        out_ref[:, :, at : at + n] = total * scale
+        got = lax.dot_general(all_ref[...], ref[...], NT, preferred_element_type=jnp.float32)
+        got = got.reshape(devices, 2 * orbs, n)
+        got = jnp.where(low[None], got[:, :orbs], got[:, orbs:])
+        out_ref[:, :, at : at + n] = got * scale
 
 
 def spread_shares_kernel(parts_ref, out_ref):
@@ -253,12 +262,27 @@
         out_refs[1][...] = total
 
 
-def update_kernel(scale, tile, has_x, last, root, low_ref, mine_ref, other_ref, resid_ref, diag_ref, *refs):
+def pack_kernel(splits, *refs):
+    pieces, outs = refs[: sum(splits)], refs[sum(splits) :]
+    for count, out_ref in zip(splits, outs):
+        at = 0
+        for ref in pieces[:count]:
+            rows = ref.shape[0]
+            out_ref[at : at + rows] = ref[...]
+            at += rows
+        pieces = pieces[count:]
+
+
+def update_kernel(scale, tile, has_x, last, root, splits, low_ref, mine_ref, other_ref, resid_ref, diag_ref, *refs):
     refs = list(refs)
     x_ref = refs.pop(0) if has_x else None
     move_ref = None if has_x else refs.pop(0)
     psi_ref = refs.pop(0) if last else None
-    first_ref, second_ref, *outs = refs
+    if has_x:
+        first_ref, second_ref, *outs = refs
+    else:
+        *refs, x_out, x_b_out, first_ref, second_ref = refs
+        outs = [x_out, x_b_out]
     low = core_mask(low_ref, 2 * mine_ref.shape[1])
     mine = unstacked(mine_ref[...].astype(jnp.float32))
     other = unstacked(other_ref[...].astype(jnp.float32))
@@ -266,6 +290,7 @@
     coeff = coeff.astype(jnp.bfloat16)
     if not has_x:
         coeff = jnp.dot(coeff, move_ref[...], preferred_element_type=jnp.float32).astype(jnp.bfloat16)
+        pack_kernel(splits, *refs, first_ref, second_ref)
     cells = resid_ref.shape[1]
     for at in range(0, cells, tile):
         here = slice(at, at + tile)
@@ -368,25 +393,27 @@
 
     plane_shape = shape((blk_rows, rows_y, rows_z), jnp.bfloat16)
     piece_shape = shape((2 * share, rows_y, rows_z), jnp.bfloat16)
-    plan, offer = call(
+    plan, same, offer = call(
         functools.partial(offer_kernel, per_dev, n_orb),
-        (shape((TABLE + nproj * chips,), jnp.int32), plane_shape),
+        (shape((TABLE + nproj * chips,), jnp.int32), shape((1,), jnp.int32), plane_shape),
         [SMEM, SMEM, ANY],
-        (SMEM, VMEM),
+        (SMEM, SMEM, VMEM),
         four,
     )(block_ids, o.astype(jnp.int32).reshape(1), occupied)
     offer = permute(offer, swap_core)
 
     flat_field = shape((local_orbs, cells))
-    rhs_mine, rhs_other, rhs_all = call(
-        fields_kernel, (flat_field, flat_field, shape((n_orb, 2 * local_orbs, cells // 2), jnp.bfloat16))
+    field_shape = shape((wide, cells))
+    rhs_mine, rhs_other, rhs_b = call(
+        fields_kernel, (flat_field, flat_field, shape((wide, cells), jnp.bfloat16))
     )(low_mask, rhs)
-    rhs_all = lax.all_to_all(rhs_all, "orb", 0, 0, tiled=True)
-    rhs_wide = pair(rhs_mine, permute(rhs_other, swap_core))
+    rhs_all = lax.all_gather(rhs_b, "orb", tiled=True)
+    rhs_wide = call(pair_kernel, field_shape)(low_mask, rhs_mine, permute(rhs_other, swap_core))
 
     offer = call(pick_kernel, plane_shape, [SMEM, ANY, VMEM], VMEM, four)(plan, occupied, offer)
     fixed = call(fixed_kernel, plane_shape, [SMEM, ANY], VMEM, four)(plan, occupied)
     fixed = permute(fixed, [(0, 1), (n_orb - 1, n_orb - 2)])
+    offer, fixed = lax.optimization_barrier((offer, fixed))
     pieces = call(
         functools.partial(pieces_kernel, n_orb),
         [piece_shape] * ring,
@@ -423,12 +450,11 @@
         again = scatter(jnp.where(here, plane_of(mid % per_dev, core), other))
         return take(again, plan[CHIP + 1])
 
-    same = plan[SAME] == 1
     offered = scatter(offer)
-    later, _ = lax.optimization_barrier((plan, got[1]))
-    second = lax.cond(later[SAME] == 1, together, apart, later, occupied)
-    second = jnp.where(same, second, take(offered, plan[CHIP + 1]))
-    mids = jnp.concatenate([take(offered, plan[CHIP]), second], axis=0)
+    second = lax.cond(same[0] == 1, together, apart, plan, occupied)
+    mids = call(
+        take_kernel, shape((2 * share, rows_y, rows_z), jnp.bfloat16), [SMEM, VMEM, VMEM], VMEM
+    )(plan, offered, second)
 
     xs = fixed.reshape(2 * share, cells)
     ys = mids.reshape(2 * share, cells)
@@ -436,25 +462,35 @@
     xs_x = permute(xs, swap_x)
     ys_up = permute(ys, up_y)
     ys_down = permute(ys, down_y)
-    xs_x, ys_up, ys_down = lax.optimization_barrier((xs_x, ys_up, ys_down))
-    own = jnp.concatenate([xs, xs_x], axis=0)
-    line = jnp.concatenate([ys, ys_up, ys_down], axis=0)
+    own_rows = 4 * share
+    half_shape = shape((local_orbs, n_rows))
+    spread_shape = shape((n_dom, local_orbs, n_rows))
+    parts = call(functools.partial(shares_kernel, scale), shape((n_orb, local_orbs, own_rows)))(
+        low_mask, rhs_all, xs, ys
+    )
+    parts = lax.all_to_all(parts, "orb", 0, 0, tiled=True)
+    xs_x, ys_up, ys_down, parts = lax.optimization_barrier((xs_x, ys_up, ys_down, parts))
+    own, line = call(
+        functools.partial(pack_kernel, (2, 3)),
+        (shape((4 * share, cells), jnp.bfloat16), shape((6 * share, cells), jnp.bfloat16)),
+    )(xs, xs_x, ys, ys_up, ys_down)
     line_x = permute(line, swap_x)
     above = permute(own, up_y)
     below = permute(own, down_y)
     far_up = permute(ys_up[:share], up_y)
     far_down = permute(ys_down[share:], down_y)
-    line_x, above, below, far_up, far_down = lax.optimization_barrier(
-        (line_x, above, below, far_up, far_down)
+    first_parts = lax.all_to_all(
+        call(spread_shares_kernel, spread_shape)(parts), "dom", 0, 0, tiled=True
+    )
+    line_x, above, below, far_up, far_down, first_parts = lax.optimization_barrier(
+        (line_x, above, below, far_up, far_down, first_parts)
     )
     far = jnp.concatenate([far_up, far_down], axis=0)
     far_x = permute(far, swap_x)
     own_up = permute(above[: 2 * share], up_y)
     own_down = permute(below[2 * share :], down_y)
-    blocks = [
-        jnp.concatenate([own, below, above, own_up, own_down], axis=0),
-        jnp.concatenate([line, line_x, far, far_x], axis=0),
-    ]
+    pieces = [own, below, above, own_up, own_down, line, line_x, far, far_x]
+    blocks_shape = [shape((n_rows // 2, cells), jnp.bfloat16)] * 2
 
     picks = win_index[:, None] == jnp.arange(n_occ, dtype=jnp.int32)[None, :]
     eps = jnp.sum(jnp.where(picks, eigen_table[None, :], 0.0), axis=1)[:, None]
@@ -464,25 +500,15 @@
     psi_mine, psi_other = call(fields_kernel, (flat_field, flat_field))(
         low_mask, psi_win.astype(jnp.float32)
     )
-    psi_other = permute(psi_other.astype(jnp.bfloat16), swap_core)
-    psi_wide = pair(psi_mine.astype(jnp.bfloat16), psi_other)
-
-    half_shape = shape((local_orbs, n_rows))
-    spread_shape = shape((n_dom, local_orbs, n_rows))
-    field_shape = shape((wide, cells))
+    psi_wide = call(pair_kernel, field_shape)(
+        low_mask, psi_mine, permute(psi_other.astype(jnp.bfloat16), swap_core).astype(jnp.float32)
+    )
     flat_shape = (wide, n_rows // 2)
 
-    def total(spread, outs):
-        parts = lax.all_to_all(spread, "dom", 0, 0, tiled=True)
+    def total(parts, outs):
         coeff_b, *coeff = call(total_kernel, outs)(parts)
         return coeff, coeff_b, permute(coeff_b, swap_core)
 
-    own_rows = 4 * share
-    share_parts = call(
-        functools.partial(shares_kernel, scale), shape((n_orb, local_orbs, own_rows))
-    )(rhs_all, xs, ys)
-    share_parts = lax.all_to_all(share_parts, "orb", 0, 0, tiled=True)
-    first_spread = call(spread_shares_kernel, spread_shape)(share_parts)
     row = jnp.arange(n_rows)
     within = row % (2 * share)
     down = jnp.array([0, 0, 1, 1, 3, 3, 2, 2, 0, 3, 1, 0, 3, 1, 2, 2])
@@ -504,7 +530,7 @@
         final = step == ITERS - 1
         sums = [shape(flat_shape, jnp.bfloat16)] + ([half_shape] if final else [])
         if step == 0:
-            resid, spread = rhs_wide, first_spread
+            resid, parts = rhs_wide, first_parts
         else:
             sib = permute(x, swap_core)
             off = lax.ppermute(x_b, ("dom", "orb"), across)
@@ -514,15 +540,20 @@
                 scratch=(pltpu.VMEM((wide, cells), jnp.bfloat16),),
             )(low_mask, x, sib, off, rhs_wide, diag, *blocks)
             spread = call(spread_kernel, spread_shape)(mine, permute(other, swap_core))
-        coeff, coeff_b, coeff_o = total(spread, sums)
+            parts = lax.all_to_all(spread, "dom", 0, 0, tiled=True)
+        coeff, coeff_b, coeff_o = total(parts, sums)
         extra = ([x] if step else [move]) + ([psi_wide] if final else [])
         outs = [field_shape, shape((wide, cells), jnp.bfloat16)]
         if final:
             outs = [shape((local_orbs, cells))] * 2 + [shape((n_dom, n_orb, rows_y // n_dom, rows_z))]
+        if step == 0:
+            outs, blocks = outs + blocks_shape, pieces
         x, x_b, *rest = call(
-            functools.partial(update_kernel, scale, 512, step > 0, final, math.sqrt(width)),
+            functools.partial(update_kernel, scale, 512, step > 0, final, math.sqrt(width), (5, 4)),
             outs,
         )(low_mask, coeff_b, coeff_o, resid, diag, *extra, *blocks)
+        if step == 0:
+            blocks = rest
     other, raw = x_b, rest[0]
 
     weights = jnp.broadcast_to(

time: 239 us -> 227 us (0.950)
  local copies, waits for them, and re-layouts: 25.9 us -> 15.9 us
  between operations: 6.62 us -> 15.4 us
  starting transfers between devices: 82.8 us -> 75.1 us
  other arithmetic: 12.3 us -> 4.72 us
  waiting for transfers between devices: 66.9 us -> 69.9 us
  Pallas kernels: 20.3 us -> 22.8 us
    ppermute x27, waiting for transfers between devices: 19.4 us -> 29.9 us  [permute(): return lax.ppermute(value, 'orb', pairs)]
    all_to_all x1, waiting for transfers between devices: 6.32 us -> 0.01 us  [scatter(): lax.all_to_all(value, 'orb', 0, 0, axis_index_groups=groups, tiled=True)]
    all_to_all x4 -> x3, starting transfers between devices: 25 us -> 19.6 us  [the longest x1 9.85 us: per_device(): lax.all_to_all(call(spread_shares_kernel, spread_shape)(parts), 'dom', 0,...]
    unnamed x53 -> x47, local copies, waits for them, and re-layouts: 17.2 us -> 12 us
    concatenate x5 -> x0, other arithmetic: 2.88 us -> none  [the longest x1 1.99 us: per_device(): line = jnp.concatenate([ys, ys_up, ys_down], axis=0)]
    all_to_all x4 -> x3, waiting for transfers between devices: 20.2 us -> 17.9 us  [the longest x1 12.1 us: per_device(): parts = lax.all_to_all(spread, 'dom', 0, 0, tiled=True)]
  transfers between devices with their start and end apart: 35 -> 35, of which waited for: 14 -> 13; matrix products, arithmetic and copies ran while one was open for 13% -> 5% of each run, Pallas kernels for 5% -> 6%
where the time goes in v1:
time: 227 us; the launch traced here: 226 us
  starting transfers between devices  75.1 us (33%)
  waiting for transfers between devices  69.9 us (31%)
  Pallas kernels  22.8 us (10%)
  blocking collectives  22.1 us (10%)
  local copies, waits for them, and re-layouts  15.9 us (7%)
  between operations  15.4 us (7%)
  other arithmetic  4.72 us (2%)
    ppermute x27, starting transfers between devices, permute(): return lax.ppermute(value, 'orb', pairs)  39.3 us
    ppermute x27, waiting for transfers between devices, permute(): return lax.ppermute(value, 'orb', pairs)  29.9 us
    all_to_all x1, blocking collectives, per_device(): parts = lax.all_to_all(spread, 'dom', 0, 0, tiled=True)  22.1 us
    all_to_all x1, waiting for transfers between devices, per_device(): lax.all_to_all(raw.reshape((n_dom * n_orb,) + raw.shape[2:]), ('dom', 'or...  13 us
    all_to_all x1, waiting for transfers between devices, per_device(): parts = lax.all_to_all(spread, 'dom', 0, 0, tiled=True)  12.1 us
    unnamed x47, local copies, waits for them, and re-layouts  12 us
    all_to_all x1, starting transfers between devices, per_device(): lax.all_to_all(call(spread_shares_kernel, spread_shape)(parts), 'dom', 0,...  9.85 us
    ppermute x2, waiting for transfers between devices, per_device(): off = lax.ppermute(x_b, ('dom', 'orb'), across)  9.08 us
  transfers between devices with their start and end apart: 35, of which 13 were waited for; matrix products, arithmetic and copies ran while one was open for 5% of the time, Pallas kernels for 6%

profile of v1, /device:TPU:1, one launch (start us, length us, event | category | flops | bytes accessed | tf_op | source)
XLA Modules:
  0.0 225.9 jit_solution(11019019482658070689)
XLA Ops:
  10.3 2.9 %shard_map.121 = (s32[40]{0:T(128)S(1)}, s32[1]{0:T(128)}, bf16[128,32,128]{2,1,0:T(8,128)(2,1)}) custom-call(s32[4]{0:T(128)S(1)} %copy-done.12, s32[1]{0:T(128)} %bitcast.6.dev_ref, bf16[2,128,2,32,128]{4,3,2,1,0:T(8,128)(2,1)} %occupied_ref.7), custom_call_target="tpu_custom_call" | custom-call | tf_op jit(solution)/shard_map/pallas_call | solution.py:396
  13.2 3.3 %collective-permute-start.1 = (bf16[128,32,128]{2,1,0:T(8,128)(2,1)}, bf16[128,32,128]{2,1,0:T(8,128)(2,1)S(1)}, u32[]{:S(2)}, u32[]{:S(2)}) collective-permute-start(bf16[128,32,128]{2,1,0:T(8,128)(2,1)} %get-tuple-element.62), channel_id=1, source_target_pairs={{0,1},{1,0},{2,3},{3,2},{4,5},{5,4},{6,7},{7,6},{8,9},{9,8},{10,11... | collective-permute-start | bytes 3145736 | tf_op jit(solution)/shard_map/ppermute | solution.py:386
  16.6 1.8 shard_map.123
  18.4 1.3 collective-permute-start.2
  20.4 2.8 %shard_map.122 = bf16[128,32,128]{2,1,0:T(8,128)(2,1)} custom-call(s32[40]{0:T(128)S(1)} %get-tuple-element.61.plan_ref, bf16[2,128,2,32,128]{4,3,2,1,0:T(8,128)(2,1)} %occupied_ref.7, bf16[128,32,128]{2,1,0:T(8,128)(2,1)S(1)} %collective-permute-done.1.offer_ref), custom_call_target="tpu_custom_call" | custom-call | tf_op jit(solution)/shard_map/pallas_call | solution.py:413
  23.2 3.9 %all-to-all-start.1 = ((bf16[8,16,32,128]{3,2,1,0:T(8,128)(2,1)}), bf16[8,16,32,128]{3,2,1,0:T(8,128)(2,1)S(1)}, u32[]{:S(2)}, u32[]{:S(2)}) async-start(bf16[8,16,32,128]{3,2,1,0:T(8,128)(2,1)} %bitcast.7), calls=%async_computation.1 | async-start | bytes 2097152 | tf_op jit(solution)/shard_map/all_to_all | solution.py:434
  27.8 3.3 %collective-permute-start.3 = (bf16[32,32,128]{2,1,0:T(8,128)(2,1)S(1)}, bf16[32,32,128]{2,1,0:T(8,128)(2,1)S(1)}, u32[]{:S(2)}, u32[]{:S(2)}) collective-permute-start(bf16[32,32,128]{2,1,0:T(8,128)(2,1)S(1)} %get-tuple-element.65), channel_id=1, source_target_pairs={{0,2},{1,3},{14,8},{15,9},{16,18},{17,19},{30,24},{31,25},{32,34},... | collective-permute-start | bytes 786440 | tf_op jit(solution)/shard_map/ppermute | solution.py:386
  31.1 2.2 collective-permute-start.4
  33.3 1.3 collective-permute-start.5
  34.6 16.7 %collective-permute-done.3.refs_1_ = bf16[32,32,128]{2,1,0:T(8,128)(2,1)S(1)} collective-permute-done((bf16[32,32,128]{2,1,0:T(8,128)(2,1)S(1)}, bf16[32,32,128]{2,1,0:T(8,128)(2,1)S(1)}, u32[]{:S(2)}, u32[]{:S(2)}) %collective-permute-start.3) | collective-permute-done | bytes 262176 | tf_op jit(solution)/shard_map/ppermute | solution.py:386
  51.3 7.4 %collective-permute-done.4.refs_2_ = bf16[32,32,128]{2,1,0:T(8,128)(2,1)S(1)} collective-permute-done((bf16[32,32,128]{2,1,0:T(8,128)(2,1)S(1)}, bf16[32,32,128]{2,1,0:T(8,128)(2,1)S(1)}, u32[]{:S(2)}, u32[]{:S(2)}) %collective-permute-start.4) | collective-permute-done | bytes 262176 | tf_op jit(solution)/shard_map/ppermute | solution.py:386
  60.2 2.7 %collective-permute-start.8 = (bf16[32,4096]{1,0:T(8,128)(2,1)S(1)}, bf16[32,4096]{1,0:T(8,128)(2,1)S(1)}, u32[]{:S(2)}, u32[]{:S(2)}) collective-permute-start(bf16[32,4096]{1,0:T(8,128)(2,1)S(1)} %get-tuple-element.71.mids_ref.refs_2_), channel_id=1, source_target_pairs={{0,6},{1,7},{2,0},{3,1},{4,2},{5,3},{6,4},{7,5},{8,14},{9,15},{10,... | collective-permute-start | bytes 786440 | tf_op jit(solution)/shard_map/ppermute | solution.py:386
  62.8 1.2 collective-permute-start.6
  64.3 1.1 collective-permute-start.16
  65.4 1.6 copy-done.2
  66.9 1.3 shard_map.128
  69.0 5.3 %all-to-all-start.2 = ((f32[16,1,512]{2,1,0:T(1,128)}), f32[16,1,512]{2,1,0:T(1,128)S(1)}, u32[]{:S(2)}, u32[]{:S(2)}) async-start(f32[16,1,512]{2,1,0:T(1,128)} %reshape.90), calls=%async_computation.2 | async-start | bytes 65536 | tf_op jit(solution)/shard_map/all_to_all | solution.py:471
  74.4 5.6 %all-to-all-done.2 = f32[16,1,512]{2,1,0:T(1,128)S(1)} async-done(((f32[16,1,512]{2,1,0:T(1,128)}), f32[16,1,512]{2,1,0:T(1,128)S(1)}, u32[]{:S(2)}, u32[]{:S(2)}) %all-to-all-start.2) | async-done | bytes 32800 | tf_op jit(solution)/shard_map/all_to_all | solution.py:471
  82.9 2.4 %collective-permute-start.11 = (bf16[64,4096]{1,0:T(8,128)(2,1)}, bf16[64,4096]{1,0:T(8,128)(2,1)S(1)}, u32[]{:S(2)}, u32[]{:S(2)}) collective-permute-start(bf16[64,4096]{1,0:T(8,128)(2,1)} %get-tuple-element.77.refs_1_), channel_id=1, source_target_pairs={{0,6},{1,7},{2,0},{3,1},{4,2},{5,3},{6,4},{7,5},{8,14},{9,15},{10,... | collective-permute-start | bytes 1572872 | tf_op jit(solution)/shard_map/ppermute | solution.py:386
  86.1 9.9 %all-to-all-start.3 = ((f32[16,8,512]{2,1,0:T(8,128)}), f32[16,8,512]{2,1,0:T(8,128)S(1)}, u32[]{:S(2)}, u32[]{:S(2)}) async-start(f32[16,8,512]{2,1,0:T(8,128)} %shard_map.130), calls=%async_computation.3 | async-start | bytes 524288 | tf_op jit(solution)/shard_map/all_to_all | solution.py:482
  96.1 1.3 add_bitcast_fusion
  99.4 2.7 %collective-permute-start.13 = (bf16[16,4096]{1,0:T(8,128)(2,1)S(1)}, bf16[16,4096]{1,0:T(8,128)(2,1)}, u32[]{:S(2)}, u32[]{:S(2)}) collective-permute-start(bf16[16,4096]{1,0:T(8,128)(2,1)S(1)} %slice.19), channel_id=1, source_target_pairs={{0,6},{1,7},{2,0},{3,1},{4,2},{5,3},{6,4},{7,5},{8,14},{9,15},{10,... | collective-permute-start | bytes 393224 | tf_op jit(solution)/shard_map/ppermute | solution.py:386
  102.7 1.9 collective-permute-done.12
  104.7 2.4 %collective-permute-start.15 = (f32[8,4096]{1,0:T(8,128)}, f32[8,4096]{1,0:T(8,128)}, u32[]{:S(2)}, u32[]{:S(2)}) collective-permute-start(f32[8,4096]{1,0:T(8,128)} %copy-done.13), channel_id=1, source_target_pairs={{0,1},{1,0},{2,3},{3,2},{4,5},{5,4},{6,7},{7,6},{8,9},{9,8},{10,11... | collective-permute-start | bytes 393224 | tf_op jit(solution)/shard_map/ppermute | solution.py:386
  107.3 1.1 constant_dynamic-update-slice_fusion.1
  110.1 2.7 %collective-permute-start.18 = (bf16[32,4096]{1,0:T(8,128)(2,1)S(1)}, bf16[32,4096]{1,0:T(8,128)(2,1)S(1)}, u32[]{:S(2)}, u32[]{:S(2)}) collective-permute-start(bf16[32,4096]{1,0:T(8,128)(2,1)S(1)} %slice.21), channel_id=1, source_target_pairs={{0,6},{1,7},{2,0},{3,1},{4,2},{5,3},{6,4},{7,5},{8,14},{9,15},{10,... | collective-permute-start | bytes 786440 | tf_op jit(solution)/shard_map/ppermute | solution.py:386
  112.9 4.2 %collective-permute-start.14 = (bf16[16,256]{1,0:T(8,128)(2,1)S(1)}, bf16[16,256]{1,0:T(8,128)(2,1)S(1)}, u32[]{:S(2)}, u32[]{:S(2)}) collective-permute-start(bf16[16,256]{1,0:T(8,128)(2,1)S(1)} %shard_map.131.mine_ref), channel_id=1, source_target_pairs={{0,1},{1,0},{2,3},{3,2},{4,5},{5,4},{6,7},{7,6},{8,9},{9,8},{10,11... | collective-permute-start | bytes 24584 | tf_op jit(solution)/shard_map/ppermute | solution.py:386
  119.9 1.1 copy-done.6
  121.1 1.1 copy-done.8
  122.2 1.9 shard_map.133
  124.1 2.4 %collective-permute-start.20 = (f32[16,4096]{1,0:T(8,128)S(1)}, f32[16,4096]{1,0:T(8,128)S(1)}, u32[]{:S(2)}, u32[]{:S(2)}) collective-permute-start(f32[16,4096]{1,0:T(8,128)S(1)} %get-tuple-element.87.x_ref.refs_0_), channel_id=1, source_target_pairs={{0,1},{1,0},{2,3},{3,2},{4,5},{5,4},{6,7},{7,6},{8,9},{9,8},{10,11... | collective-permute-start | bytes 786440 | tf_op jit(solution)/shard_map/ppermute | solution.py:386
  126.6 4.1 %collective-permute-start.21 = (bf16[16,4096]{1,0:T(8,128)(2,1)S(1)}, bf16[16,4096]{1,0:T(8,128)(2,1)S(1)}, u32[]{:S(2)}, u32[]{:S(2)}) collective-permute-start(bf16[16,4096]{1,0:T(8,128)(2,1)S(1)} %get-tuple-element.88), channel_id=1, source_target_pairs={{1,16},{16,1},{3,18},{18,3},{5,20},{20,5},{7,22},{22,7},{9,24},{24... | collective-permute-start | bytes 393224 | tf_op jit(solution)/shard_map/ppermute | solution.py:536
  130.7 3.6 %collective-permute-done.21.off_ref = bf16[16,4096]{1,0:T(8,128)(2,1)S(1)} collective-permute-done((bf16[16,4096]{1,0:T(8,128)(2,1)S(1)}, bf16[16,4096]{1,0:T(8,128)(2,1)S(1)}, u32[]{:S(2)}, u32[]{:S(2)}) %collective-permute-start.21) | collective-permute-done | bytes 131104 | tf_op jit(solution)/shard_map/ppermute | solution.py:536
  134.3 1.2 shard_map.134
  135.6 1.2 collective-permute-done.22.other_ref
  136.8 22.1 %all_to_all.34.parts_ref = f32[16,8,512]{2,1,0:T(8,128)S(1)} all-to-all(f32[16,8,512]{2,1,0:T(8,128)S(1)} %shard_map.135), channel_id=1, replica_groups=mesh['dom'=16,'orb'=16] {'dom'}, dimensions={0} | all-to-all | bytes 524288 | tf_op jit(solution)/shard_map/all_to_all | solution.py:543
  158.9 1.7 collective-permute-start.23
  162.5 2.3 %collective-permute-start.25 = (bf16[16,4096]{1,0:T(8,128)(2,1)S(1)}, bf16[16,4096]{1,0:T(8,128)(2,1)S(1)}, u32[]{:S(2)}, u32[]{:S(2)}) collective-permute-start(bf16[16,4096]{1,0:T(8,128)(2,1)S(1)} %get-tuple-element.95), channel_id=1, source_target_pairs={{1,16},{16,1},{3,18},{18,3},{5,20},{20,5},{7,22},{22,7},{9,24},{24... | collective-permute-start | bytes 393224 | tf_op jit(solution)/shard_map/ppermute | solution.py:536
  164.8 5.4 %collective-permute-done.25.off_ref = bf16[16,4096]{1,0:T(8,128)(2,1)S(1)} collective-permute-done((bf16[16,4096]{1,0:T(8,128)(2,1)S(1)}, bf16[16,4096]{1,0:T(8,128)(2,1)S(1)}, u32[]{:S(2)}, u32[]{:S(2)}) %collective-permute-start.25) | collective-permute-done | bytes 131104 | tf_op jit(solution)/shard_map/ppermute | solution.py:536
  170.3 1.2 shard_map.138
  171.5 1.2 collective-permute-done.26.other_ref
  173.5 4.5 %all-to-all-start.5 = ((f32[16,8,512]{2,1,0:T(8,128)}), f32[16,8,512]{2,1,0:T(8,128)S(1)}, u32[]{:S(2)}, u32[]{:S(2)}) async-start(f32[16,8,512]{2,1,0:T(8,128)} %shard_map.139), calls=%async_computation.5 | async-start | bytes 524288 | tf_op jit(solution)/shard_map/all_to_all | solution.py:543
  178.7 12.1 %all-to-all-done.5.parts_ref = f32[16,8,512]{2,1,0:T(8,128)S(1)} async-done(((f32[16,8,512]{2,1,0:T(8,128)}), f32[16,8,512]{2,1,0:T(8,128)S(1)}, u32[]{:S(2)}, u32[]{:S(2)}) %all-to-all-start.5) | async-done | bytes 262176 | tf_op jit(solution)/shard_map/all_to_all | solution.py:543
  190.8 1.7 collective-permute-start.27
  193.3 1.6 copy-done.1
  194.9 1.4 shard_map.143
  196.7 5.8 %all-to-all-start.6 = ((f32[256,2,128]{2,1,0:T(2,128)}), f32[256,2,128]{2,1,0:T(2,128)S(1)}, u32[]{:S(2)}, u32[]{:S(2)}) async-start(f32[256,2,128]{2,1,0:T(2,128)} %bitcast.17), calls=%async_computation.6 | async-start | bytes 524288 | tf_op jit(solution)/shard_map/all_to_all | solution.py:562
  204.8 13.0 %all-to-all-done.6.terms_ref = f32[256,2,128]{2,1,0:T(2,128)S(1)} async-done(((f32[256,2,128]{2,1,0:T(2,128)}), f32[256,2,128]{2,1,0:T(2,128)S(1)}, u32[]{:S(2)}, u32[]{:S(2)}) %all-to-all-start.6) | async-done | bytes 262176 | tf_op jit(solution)/shard_map/all_to_all | solution.py:562
  (129 shorter events, 25.6 us)
Async XLA Ops:
  7.2 58.2 %all-gather.2.cloned.1.call-start = ((), (), s32[]{:S(2)}) async-start(), calls=%async_computation.7 | async-start | bytes 2228224 | tf_op jit(solution)/shard_map/all_gather | solution.py:410
  13.2 7.1 %collective-permute-start.1 = (bf16[128,32,128]{2,1,0:T(8,128)(2,1)}, bf16[128,32,128]{2,1,0:T(8,128)(2,1)S(1)}, u32[]{:S(2)}, u32[]{:S(2)}) collective-permute-start(bf16[128,32,128]{2,1,0:T(8,128)(2,1)} %get-tuple-element.62), channel_id=1, source_target_pairs={{0,1},{1,0},{2,3},{3,2},{4,5},{5,4},{6,7},{7,6},{8,9},{9,8},{10,11... | collective-permute-start | bytes 3145736 | tf_op jit(solution)/shard_map/ppermute | solution.py:386
  18.4 4.8 %collective-permute-start.2 = (bf16[128,32,128]{2,1,0:T(8,128)(2,1)S(1)}, bf16[128,32,128]{2,1,0:T(8,128)(2,1)S(1)}, u32[]{:S(2)}, u32[]{:S(2)}) collective-permute-start(bf16[128,32,128]{2,1,0:T(8,128)(2,1)S(1)} %shard_map.123), channel_id=1, source_target_pairs={{0,1},{15,14},{16,17},{31,30},{32,33},{47,46},{48,49},{63,62},{64,... | collective-permute-start | bytes 3145736 | tf_op jit(solution)/shard_map/ppermute | solution.py:386
  23.2 36.1 %all-to-all-start.1 = ((bf16[8,16,32,128]{3,2,1,0:T(8,128)(2,1)}), bf16[8,16,32,128]{3,2,1,0:T(8,128)(2,1)S(1)}, u32[]{:S(2)}, u32[]{:S(2)}) async-start(bf16[8,16,32,128]{3,2,1,0:T(8,128)(2,1)} %bitcast.7), calls=%async_computation.1 | async-start | bytes 2097152 | tf_op jit(solution)/shard_map/all_to_all | solution.py:434
  27.1 37.0 %copy-start.16 = (f32[4096]{0:T(1024)S(1)}, f32[4096]{0:T(1024)}, u32[]{:S(2)}) copy-start(f32[4096]{0:T(1024)} %param.14) | copy-start | bytes 49156
  27.1 37.0 %copy-start.18 = (s32[8]{0:T(128)S(1)}, s32[8]{0:T(128)}, u32[]{:S(2)}) copy-start(s32[8]{0:T(128)} %param.15) | copy-start | bytes 100
  27.8 46.4 %copy-start.19 = (s32[16]{0:T(128)S(1)}, s32[16]{0:T(128)}, u32[]{:S(2)}) copy-start(s32[16]{0:T(128)} %constant.135.clone) | copy-start | bytes 196
  27.8 46.4 %copy-start.20 = (s32[16]{0:T(128)S(1)}, s32[16]{0:T(128)}, u32[]{:S(2)}) copy-start(s32[16]{0:T(128)} %constant.136.clone) | copy-start | bytes 196
  27.8 23.5 %collective-permute-start.3 = (bf16[32,32,128]{2,1,0:T(8,128)(2,1)S(1)}, bf16[32,32,128]{2,1,0:T(8,128)(2,1)S(1)}, u32[]{:S(2)}, u32[]{:S(2)}) collective-permute-start(bf16[32,32,128]{2,1,0:T(8,128)(2,1)S(1)} %get-tuple-element.65), channel_id=1, source_target_pairs={{0,2},{1,3},{14,8},{15,9},{16,18},{17,19},{30,24},{31,25},{32,34},... | collective-permute-start | bytes 786440 | tf_op jit(solution)/shard_map/ppermute | solution.py:386
  31.1 27.6 %collective-permute-start.4 = (bf16[32,32,128]{2,1,0:T(8,128)(2,1)S(1)}, bf16[32,32,128]{2,1,0:T(8,128)(2,1)S(1)}, u32[]{:S(2)}, u32[]{:S(2)}) collective-permute-start(bf16[32,32,128]{2,1,0:T(8,128)(2,1)S(1)} %get-tuple-element.66), channel_id=1, source_target_pairs={{0,4},{1,5},{14,10},{15,11},{16,20},{17,21},{30,26},{31,27},{32,36... | collective-permute-start | bytes 786440 | tf_op jit(solution)/shard_map/ppermute | solution.py:386
  33.3 25.4 %collective-permute-start.5 = (bf16[32,32,128]{2,1,0:T(8,128)(2,1)S(1)}, bf16[32,32,128]{2,1,0:T(8,128)(2,1)S(1)}, u32[]{:S(2)}, u32[]{:S(2)}) collective-permute-start(bf16[32,32,128]{2,1,0:T(8,128)(2,1)S(1)} %get-tuple-element.67), channel_id=1, source_target_pairs={{0,6},{1,7},{14,12},{15,13},{16,22},{17,23},{30,28},{31,29},{32,38... | collective-permute-start | bytes 786440 | tf_op jit(solution)/shard_map/ppermute | solution.py:386
  60.1 21.3 %collective-permute-start.7 = (bf16[32,4096]{1,0:T(8,128)(2,1)S(1)}, bf16[32,4096]{1,0:T(8,128)(2,1)S(1)}, u32[]{:S(2)}, u32[]{:S(2)}) collective-permute-start(bf16[32,4096]{1,0:T(8,128)(2,1)S(1)} %get-tuple-element.71.mids_ref.refs_2_), channel_id=1, source_target_pairs={{0,2},{1,3},{2,4},{3,5},{4,6},{5,7},{6,0},{7,1},{8,10},{9,11},{10,... | collective-permute-start | bytes 786440 | tf_op jit(solution)/shard_map/ppermute | solution.py:386
  60.2 21.2 %collective-permute-start.8 = (bf16[32,4096]{1,0:T(8,128)(2,1)S(1)}, bf16[32,4096]{1,0:T(8,128)(2,1)S(1)}, u32[]{:S(2)}, u32[]{:S(2)}) collective-permute-start(bf16[32,4096]{1,0:T(8,128)(2,1)S(1)} %get-tuple-element.71.mids_ref.refs_2_), channel_id=1, source_target_pairs={{0,6},{1,7},{2,0},{3,1},{4,2},{5,3},{6,4},{7,5},{8,14},{9,15},{10,... | collective-permute-start | bytes 786440 | tf_op jit(solution)/shard_map/ppermute | solution.py:386
  62.8 18.5 %collective-permute-start.6 = (bf16[32,4096]{1,0:T(8,128)(2,1)S(1)}, bf16[32,4096]{1,0:T(8,128)(2,1)S(1)}, u32[]{:S(2)}, u32[]{:S(2)}) collective-permute-start(bf16[32,4096]{1,0:T(8,128)(2,1)S(1)} %get-tuple-element.70.ends_ref.refs_0_), channel_id=1, source_target_pairs={{0,8},{1,9},{2,10},{3,11},{4,12},{5,13},{6,14},{7,15},{8,0},{9,1},... | collective-permute-start | bytes 786440 | tf_op jit(solution)/shard_map/ppermute | solution.py:386
  64.3 35.1 %collective-permute-start.16 = (f32[8,1]{0,1:T(1,128)S(1)}, f32[8,1]{0,1:T(1,128)}, u32[]{:S(2)}, u32[]{:S(2)}) collective-permute-start(f32[8,1]{0,1:T(1,128)S(1)} %bitcast.39), channel_id=1, source_target_pairs={{0,1},{1,0},{2,3},{3,2},{4,5},{5,4},{6,7},{7,6},{8,9},{9,8},{10,11... | collective-permute-start | bytes 104 | tf_op jit(solution)/shard_map/ppermute | solution.py:386
  65.4 1.6 copy-start.2
  69.0 11.1 %all-to-all-start.2 = ((f32[16,1,512]{2,1,0:T(1,128)}), f32[16,1,512]{2,1,0:T(1,128)S(1)}, u32[]{:S(2)}, u32[]{:S(2)}) async-start(f32[16,1,512]{2,1,0:T(1,128)} %reshape.90), calls=%async_computation.2 | async-start | bytes 65536 | tf_op jit(solution)/shard_map/all_to_all | solution.py:471
  81.4 4.8 %copy-start.9 = (bf16[32,4096]{1,0:T(8,128)(2,1)}, bf16[32,4096]{1,0:T(8,128)(2,1)S(1)}, u32[]{:S(2)}) copy-start(bf16[32,4096]{1,0:T(8,128)(2,1)S(1)} %collective-permute-done.7.refs_3_) | copy-start | bytes 786436
  82.3 36.5 %copy-start.5 = (bf16[96,4096]{1,0:T(8,128)(2,1)}, bf16[96,4096]{1,0:T(8,128)(2,1)S(1)}, u32[]{:S(2)}) copy-start(bf16[96,4096]{1,0:T(8,128)(2,1)S(1)} %get-tuple-element.76.refs_6_) | copy-start | bytes 2359300
  82.3 25.0 %collective-permute-start.9 = (bf16[96,4096]{1,0:T(8,128)(2,1)S(1)}, bf16[96,4096]{1,0:T(8,128)(2,1)S(1)}, u32[]{:S(2)}, u32[]{:S(2)}) collective-permute-start(bf16[96,4096]{1,0:T(8,128)(2,1)S(1)} %get-tuple-element.76.refs_6_), channel_id=1, source_target_pairs={{0,8},{1,9},{2,10},{3,11},{4,12},{5,13},{6,14},{7,15},{8,0},{9,1},... | collective-permute-start | bytes 2359304 | tf_op jit(solution)/shard_map/ppermute | solution.py:386
  82.6 24.7 %collective-permute-start.10 = (bf16[64,4096]{1,0:T(8,128)(2,1)}, bf16[64,4096]{1,0:T(8,128)(2,1)S(1)}, u32[]{:S(2)}, u32[]{:S(2)}) collective-permute-start(bf16[64,4096]{1,0:T(8,128)(2,1)} %get-tuple-element.77.refs_1_), channel_id=1, source_target_pairs={{0,2},{1,3},{2,4},{3,5},{4,6},{5,7},{6,0},{7,1},{8,10},{9,11},{10,... | collective-permute-start | bytes 1572872 | tf_op jit(solution)/shard_map/ppermute | solution.py:386
  82.9 24.4 %collective-permute-start.11 = (bf16[64,4096]{1,0:T(8,128)(2,1)}, bf16[64,4096]{1,0:T(8,128)(2,1)S(1)}, u32[]{:S(2)}, u32[]{:S(2)}) collective-permute-start(bf16[64,4096]{1,0:T(8,128)(2,1)} %get-tuple-element.77.refs_1_), channel_id=1, source_target_pairs={{0,6},{1,7},{2,0},{3,1},{4,2},{5,3},{6,4},{7,5},{8,14},{9,15},{10,... | collective-permute-start | bytes 1572872 | tf_op jit(solution)/shard_map/ppermute | solution.py:386
  86.1 21.2 %all-to-all-start.3 = ((f32[16,8,512]{2,1,0:T(8,128)}), f32[16,8,512]{2,1,0:T(8,128)S(1)}, u32[]{:S(2)}, u32[]{:S(2)}) async-start(f32[16,8,512]{2,1,0:T(8,128)} %shard_map.130), calls=%async_computation.3 | async-start | bytes 524288 | tf_op jit(solution)/shard_map/all_to_all | solution.py:482
  99.3 5.4 %collective-permute-start.12 = (bf16[16,4096]{1,0:T(8,128)(2,1)S(1)}, bf16[16,4096]{1,0:T(8,128)(2,1)S(1)}, u32[]{:S(2)}, u32[]{:S(2)}) collective-permute-start(bf16[16,4096]{1,0:T(8,128)(2,1)S(1)} %slice.18), channel_id=1, source_target_pairs={{0,2},{1,3},{2,4},{3,5},{4,6},{5,7},{6,0},{7,1},{8,10},{9,11},{10,... | collective-permute-start | bytes 393224 | tf_op jit(solution)/shard_map/ppermute | solution.py:386
  99.4 7.7 %collective-permute-start.13 = (bf16[16,4096]{1,0:T(8,128)(2,1)S(1)}, bf16[16,4096]{1,0:T(8,128)(2,1)}, u32[]{:S(2)}, u32[]{:S(2)}) collective-permute-start(bf16[16,4096]{1,0:T(8,128)(2,1)S(1)} %slice.19), channel_id=1, source_target_pairs={{0,6},{1,7},{2,0},{3,1},{4,2},{5,3},{6,4},{7,5},{8,14},{9,15},{10,... | collective-permute-start | bytes 393224 | tf_op jit(solution)/shard_map/ppermute | solution.py:386
  104.7 2.4 %copy-start.15 = (bf16[16,4096]{1,0:T(8,128)(2,1)}, bf16[16,4096]{1,0:T(8,128)(2,1)S(1)}, u32[]{:S(2)}) copy-start(bf16[16,4096]{1,0:T(8,128)(2,1)S(1)} %collective-permute-done.12) | copy-start | bytes 393220
  104.7 13.2 %collective-permute-start.15 = (f32[8,4096]{1,0:T(8,128)}, f32[8,4096]{1,0:T(8,128)}, u32[]{:S(2)}, u32[]{:S(2)}) collective-permute-start(f32[8,4096]{1,0:T(8,128)} %copy-done.13), channel_id=1, source_target_pairs={{0,1},{1,0},{2,3},{3,2},{4,5},{5,4},{6,7},{7,6},{8,9},{9,8},{10,11... | collective-permute-start | bytes 393224 | tf_op jit(solution)/shard_map/ppermute | solution.py:386
  107.3 11.6 %copy-start.3 = (bf16[64,4096]{1,0:T(8,128)(2,1)}, bf16[64,4096]{1,0:T(8,128)(2,1)S(1)}, u32[]{:S(2)}) copy-start(bf16[64,4096]{1,0:T(8,128)(2,1)S(1)} %collective-permute-done.11.refs_2_) | copy-start | bytes 1572868
  107.3 5.6 %copy-start.7 = (bf16[96,4096]{1,0:T(8,128)(2,1)}, bf16[96,4096]{1,0:T(8,128)(2,1)S(1)}, u32[]{:S(2)}) copy-start(bf16[96,4096]{1,0:T(8,128)(2,1)S(1)} %collective-permute-done.9.refs_7_) | copy-start | bytes 2359300
  109.3 9.5 %collective-permute-start.19 = (bf16[32,4096]{1,0:T(8,128)(2,1)S(1)}, bf16[32,4096]{1,0:T(8,128)(2,1)S(1)}, u32[]{:S(2)}, u32[]{:S(2)}) collective-permute-start(bf16[32,4096]{1,0:T(8,128)(2,1)S(1)} %constant_dynamic-update-slice_fusion.refs_8_), channel_id=1, source_target_pairs={{0,8},{1,9},{2,10},{3,11},{4,12},{5,13},{6,14},{7,15},{8,0},{9,1},... | collective-permute-start | bytes 786440 | tf_op jit(solution)/shard_map/ppermute | solution.py:386
  110.0 8.9 %collective-permute-start.17 = (bf16[32,4096]{1,0:T(8,128)(2,1)S(1)}, bf16[32,4096]{1,0:T(8,128)(2,1)S(1)}, u32[]{:S(2)}, u32[]{:S(2)}) collective-permute-start(bf16[32,4096]{1,0:T(8,128)(2,1)S(1)} %slice.20), channel_id=1, source_target_pairs={{0,2},{1,3},{2,4},{3,5},{4,6},{5,7},{6,0},{7,1},{8,10},{9,11},{10,... | collective-permute-start | bytes 786440 | tf_op jit(solution)/shard_map/ppermute | solution.py:386
  110.1 8.8 %collective-permute-start.18 = (bf16[32,4096]{1,0:T(8,128)(2,1)S(1)}, bf16[32,4096]{1,0:T(8,128)(2,1)S(1)}, u32[]{:S(2)}, u32[]{:S(2)}) collective-permute-start(bf16[32,4096]{1,0:T(8,128)(2,1)S(1)} %slice.21), channel_id=1, source_target_pairs={{0,6},{1,7},{2,0},{3,1},{4,2},{5,3},{6,4},{7,5},{8,14},{9,15},{10,... | collective-permute-start | bytes 786440 | tf_op jit(solution)/shard_map/ppermute | solution.py:386
  112.9 6.0 %collective-permute-start.14 = (bf16[16,256]{1,0:T(8,128)(2,1)S(1)}, bf16[16,256]{1,0:T(8,128)(2,1)S(1)}, u32[]{:S(2)}, u32[]{:S(2)}) collective-permute-start(bf16[16,256]{1,0:T(8,128)(2,1)S(1)} %shard_map.131.mine_ref), channel_id=1, source_target_pairs={{0,1},{1,0},{2,3},{3,2},{4,5},{5,4},{6,7},{7,6},{8,9},{9,8},{10,11... | collective-permute-start | bytes 24584 | tf_op jit(solution)/shard_map/ppermute | solution.py:386
  124.1 46.2 %copy-start = (bf16[256,4096]{1,0:T(8,128)(2,1)}, bf16[256,4096]{1,0:T(8,128)(2,1)S(1)}, u32[]{:S(2)}) copy-start(bf16[256,4096]{1,0:T(8,128)(2,1)S(1)} %get-tuple-element.90.second_ref.refs_2_.refs_3_) | copy-start | bytes 6291460
  124.1 10.2 %collective-permute-start.20 = (f32[16,4096]{1,0:T(8,128)S(1)}, f32[16,4096]{1,0:T(8,128)S(1)}, u32[]{:S(2)}, u32[]{:S(2)}) collective-permute-start(f32[16,4096]{1,0:T(8,128)S(1)} %get-tuple-element.87.x_ref.refs_0_), channel_id=1, source_target_pairs={{0,1},{1,0},{2,3},{3,2},{4,5},{5,4},{6,7},{7,6},{8,9},{9,8},{10,11... | collective-permute-start | bytes 786440 | tf_op jit(solution)/shard_map/ppermute | solution.py:386
  126.6 7.8 %collective-permute-start.21 = (bf16[16,4096]{1,0:T(8,128)(2,1)S(1)}, bf16[16,4096]{1,0:T(8,128)(2,1)S(1)}, u32[]{:S(2)}, u32[]{:S(2)}) collective-permute-start(bf16[16,4096]{1,0:T(8,128)(2,1)S(1)} %get-tuple-element.88), channel_id=1, source_target_pairs={{1,16},{16,1},{3,18},{18,3},{5,20},{20,5},{7,22},{22,7},{9,24},{24... | collective-permute-start | bytes 393224 | tf_op jit(solution)/shard_map/ppermute | solution.py:536
  135.6 1.2 collective-permute-start.22
  158.9 2.5 %collective-permute-start.23 = (bf16[16,256]{1,0:T(8,128)(2,1)S(1)}, bf16[16,256]{1,0:T(8,128)(2,1)S(1)}, u32[]{:S(2)}, u32[]{:S(2)}) collective-permute-start(bf16[16,256]{1,0:T(8,128)(2,1)S(1)} %shard_map.136.mine_ref), channel_id=1, source_target_pairs={{0,1},{1,0},{2,3},{3,2},{4,5},{5,4},{6,7},{7,6},{8,9},{9,8},{10,11... | collective-permute-start | bytes 24584 | tf_op jit(solution)/shard_map/ppermute | solution.py:386
  162.1 15.9 %copy-start.14 = (bf16[8,2,32,128]{3,2,1,0:T(8,128)(2,1)S(1)}, bf16[8,2,32,128]{3,2,1,0:T(8,128)(2,1)}, u32[]{:S(2)}) copy-start(bf16[8,2,32,128]{3,2,1,0:T(8,128)(2,1)} %param.18) | copy-start | bytes 393220
  162.1 30.4 %copy-start.17 = (f32[32,32]{1,0:T(8,128)S(1)}, f32[32,32]{1,0:T(8,128)}, u32[]{:S(2)}) copy-start(f32[32,32]{1,0:T(8,128)} %param.19) | copy-start | bytes 12292
  162.1 8.2 %collective-permute-start.24 = (f32[16,4096]{1,0:T(8,128)S(1)}, f32[16,4096]{1,0:T(8,128)S(1)}, u32[]{:S(2)}, u32[]{:S(2)}) collective-permute-start(f32[16,4096]{1,0:T(8,128)S(1)} %get-tuple-element.94.x_ref.refs_0_), channel_id=1, source_target_pairs={{0,1},{1,0},{2,3},{3,2},{4,5},{5,4},{6,7},{7,6},{8,9},{9,8},{10,11... | collective-permute-start | bytes 786440 | tf_op jit(solution)/shard_map/ppermute | solution.py:386
  162.5 7.8 %collective-permute-start.25 = (bf16[16,4096]{1,0:T(8,128)(2,1)S(1)}, bf16[16,4096]{1,0:T(8,128)(2,1)S(1)}, u32[]{:S(2)}, u32[]{:S(2)}) collective-permute-start(bf16[16,4096]{1,0:T(8,128)(2,1)S(1)} %get-tuple-element.95), channel_id=1, source_target_pairs={{1,16},{16,1},{3,18},{18,3},{5,20},{20,5},{7,22},{22,7},{9,24},{24... | collective-permute-start | bytes 393224 | tf_op jit(solution)/shard_map/ppermute | solution.py:536
  171.5 1.2 collective-permute-start.26
  173.5 17.3 %all-to-all-start.5 = ((f32[16,8,512]{2,1,0:T(8,128)}), f32[16,8,512]{2,1,0:T(8,128)S(1)}, u32[]{:S(2)}, u32[]{:S(2)}) async-start(f32[16,8,512]{2,1,0:T(8,128)} %shard_map.139), calls=%async_computation.5 | async-start | bytes 524288 | tf_op jit(solution)/shard_map/all_to_all | solution.py:543
  178.2 14.5 %collective-permute-start.28 = (bf16[8,4096]{1,0:T(8,128)(2,1)S(1)}, bf16[8,4096]{1,0:T(8,128)(2,1)S(1)}, u32[]{:S(2)}, u32[]{:S(2)}) collective-permute-start(bf16[8,4096]{1,0:T(8,128)(2,1)S(1)} %convert_element_type.25), channel_id=1, source_target_pairs={{0,1},{1,0},{2,3},{3,2},{4,5},{5,4},{6,7},{7,6},{8,9},{9,8},{10,11... | collective-permute-start | bytes 196616 | tf_op jit(solution)/shard_map/ppermute | solution.py:386
  190.8 2.5 %collective-permute-start.27 = (bf16[16,256]{1,0:T(8,128)(2,1)S(1)}, bf16[16,256]{1,0:T(8,128)(2,1)S(1)}, u32[]{:S(2)}, u32[]{:S(2)}) collective-permute-start(bf16[16,256]{1,0:T(8,128)(2,1)S(1)} %get-tuple-element.98.mine_ref), channel_id=1, source_target_pairs={{0,1},{1,0},{2,3},{3,2},{4,5},{5,4},{6,7},{7,6},{8,9},{9,8},{10,11... | collective-permute-start | bytes 24584 | tf_op jit(solution)/shard_map/ppermute | solution.py:386
  196.4 7.6 %collective-permute-start.29 = (f32[8,4096]{1,0:T(8,128)S(1)}, f32[8,4096]{1,0:T(8,128)S(1)}, u32[]{:S(2)}, u32[]{:S(2)}) collective-permute-start(f32[8,4096]{1,0:T(8,128)S(1)} %get-tuple-element.103), channel_id=1, source_target_pairs={{0,1},{1,0},{2,3},{3,2},{4,5},{5,4},{6,7},{7,6},{8,9},{9,8},{10,11... | collective-permute-start | bytes 393224 | tf_op jit(solution)/shard_map/ppermute | solution.py:386
  196.7 21.1 %all-to-all-start.6 = ((f32[256,2,128]{2,1,0:T(2,128)}), f32[256,2,128]{2,1,0:T(2,128)S(1)}, u32[]{:S(2)}, u32[]{:S(2)}) async-start(f32[256,2,128]{2,1,0:T(2,128)} %bitcast.17), calls=%async_computation.6 | async-start | bytes 524288 | tf_op jit(solution)/shard_map/all_to_all | solution.py:562
  (8 other events, 8.1 us)
Sparse Core Ops, SparseCore 0:
  10.4 50.6 all-gather.1

commit v2 on v1

--- a/solution.py
+++ b/solution.py
@@ -14,6 +14,7 @@
 SMEM = pl.BlockSpec(memory_space=pltpu.SMEM)
 ANY = pl.BlockSpec(memory_space=pl.ANY)
 VMEM = pl.BlockSpec(memory_space=pltpu.VMEM)
+HBM = pl.BlockSpec(memory_space=pltpu.HBM)
 
 MID, CHIP, SAME, SLOT, CORE, DEV, TABLE = 0, 2, 4, 5, 6, 7, 8
 
@@ -163,7 +164,7 @@
     split(low_ref, jnp.concatenate(parts, axis=1) * scale, mine_ref, other_ref)
 
 
-def fields_kernel(low_ref, field_ref, mine_ref, other_ref, *both_refs):
+def fields_kernel(low_ref, field_ref, mine_ref, other_ref):
     rows_y, rows_z = field_ref.shape[2:]
     low = low_ref[...] > 0.5
     for y in range(rows_y):
@@ -171,16 +172,16 @@
         here = slice(y * rows_z, (y + 1) * rows_z)
         mine_ref[:, here] = jnp.where(low, first, second)
         other_ref[:, here] = jnp.where(low, second, first)
-        for ref in both_refs:
-            ref[:, here] = jnp.concatenate([first, second], axis=0).astype(jnp.bfloat16)
-
-
-def pair_kernel(low_ref, mine_ref, other_ref, out_ref):
+
+
+def pair_kernel(low_ref, mine_ref, other_ref, out_ref, *rounded_refs):
     half = mine_ref.shape[0]
     low = core_mask(low_ref, mine_ref.shape[1])
     mine, other = mine_ref[...], other_ref[...]
-    out_ref[:half] = jnp.where(low, mine, other)
-    out_ref[half:] = jnp.where(low, other, mine)
+    both = jnp.concatenate([jnp.where(low, mine, other), jnp.where(low, other, mine)], axis=0)
+    out_ref[...] = both
+    for ref in rounded_refs:
+        ref[...] = both.astype(jnp.bfloat16)
 
 
 def take_kernel(plan_ref, offered_ref, second_ref, out_ref):
@@ -196,20 +197,32 @@
         out_ref[rows:] = offered_ref[plan_ref[CHIP + 1]]
 
 
-def shares_kernel(scale, low_ref, all_ref, ends_ref, mids_ref, out_ref):
-    devices, orbs = out_ref.shape[:2]
-    low = low_ref[0:1, 0:1] > 0.5
-    for at, ref in ((0, ends_ref), (ends_ref.shape[0], mids_ref)):
-        n = ref.shape[0]
-        got = lax.dot_general(all_ref[...], ref[...], NT, preferred_element_type=jnp.float32)
-        got = got.reshape(devices, 2 * orbs, n)
-        got = jnp.where(low[None], got[:, :orbs], got[:, orbs:])
-        out_ref[:, :, at : at + n] = got * scale
+def shares_kernel(scale, places, plan_ref, *refs):
+    *field_refs, ends_ref, mids_ref, out_ref = refs
+    devices, orbs, lanes = out_ref.shape
+    ring = devices // 4
+    chip = plan_ref[DEV] // 2
+    y, x = chip % ring, chip // ring
+    spare = lanes - ends_ref.shape[0] - mids_ref.shape[0]
+    for down, field_ref in zip(places, field_refs):
+        field = field_ref[...]
+        got = [
+            lax.dot_general(field, ref[...], NT, preferred_element_type=jnp.float32)
+            for ref in (ends_ref, mids_ref)
+        ]
+        rows = jnp.concatenate(got + [jnp.zeros((field.shape[0], spare), jnp.float32)], axis=1) * scale
+        for k in range(rows.shape[0] // (2 * orbs)):
+            side = down[1] + k
+            to = 2 * ((x + side) % 2 * ring + (y + down[0]) % ring)
+            at = k * 2 * orbs
+            out_ref[pl.ds(to, 1)] = rows[at : at + orbs][None]
+            out_ref[pl.ds(to + 1, 1)] = rows[at + orbs : at + 2 * orbs][None]
 
 
 def spread_shares_kernel(parts_ref, out_ref):
+    rows = out_ref.shape[2] * 2 // parts_ref.shape[0]
     total = jnp.concatenate(
-        [parts_ref[k] + parts_ref[k + 1] for k in range(0, parts_ref.shape[0], 2)], axis=1
+        [(parts_ref[k] + parts_ref[k + 1])[:, :rows] for k in range(0, parts_ref.shape[0], 2)], axis=1
     )
     for d in range(out_ref.shape[0]):
         out_ref[d] = total
@@ -273,6 +286,20 @@
         pieces = pieces[count:]
 
 
+def packed(splits, *refs):
+    *refs, sem = refs
+    pieces, outs = refs[: sum(splits)], refs[sum(splits) :]
+    moves = []
+    for count, out_ref in zip(splits, outs):
+        at = 0
+        for ref in pieces[:count]:
+            rows = ref.shape[0]
+            moves.append(pltpu.make_async_copy(ref, out_ref.at[pl.ds(at, rows)], sem.at[len(moves)]))
+            at += rows
+        pieces = pieces[count:]
+    return moves
+
+
 def update_kernel(scale, tile, has_x, last, root, splits, low_ref, mine_ref, other_ref, resid_ref, diag_ref, *refs):
     refs = list(refs)
     x_ref = refs.pop(0) if has_x else None
@@ -281,7 +308,7 @@
     if has_x:
         first_ref, second_ref, *outs = refs
     else:
-        *refs, x_out, x_b_out, first_ref, second_ref = refs
+        *refs, x_out, x_b_out, first_ref, second_ref, sem = refs
         outs = [x_out, x_b_out]
     low = core_mask(low_ref, 2 * mine_ref.shape[1])
     mine = unstacked(mine_ref[...].astype(jnp.float32))
@@ -290,7 +317,7 @@
     coeff = coeff.astype(jnp.bfloat16)
     if not has_x:
         coeff = jnp.dot(coeff, move_ref[...], preferred_element_type=jnp.float32).astype(jnp.bfloat16)
-        pack_kernel(splits, *refs, first_ref, second_ref)
+        run(packed(splits, *refs, first_ref, second_ref, sem))
     cells = resid_ref.shape[1]
     for at in range(0, cells, tile):
         here = slice(at, at + tile)
@@ -404,11 +431,12 @@
 
     flat_field = shape((local_orbs, cells))
     field_shape = shape((wide, cells))
-    rhs_mine, rhs_other, rhs_b = call(
-        fields_kernel, (flat_field, flat_field, shape((wide, cells), jnp.bfloat16))
-    )(low_mask, rhs)
-    rhs_all = lax.all_gather(rhs_b, "orb", tiled=True)
-    rhs_wide = call(pair_kernel, field_shape)(low_mask, rhs_mine, permute(rhs_other, swap_core))
+    rhs_mine, rhs_other = call(fields_kernel, (flat_field, flat_field))(low_mask, rhs)
+    rhs_wide, rhs_b = call(pair_kernel, (field_shape, shape((wide, cells), jnp.bfloat16)))(
+        low_mask, rhs_mine, permute(rhs_other, swap_core)
+    )
+    rhs_own = jnp.concatenate([rhs_b, permute(rhs_b, swap_x)], axis=0)
+    offer, rhs_own = lax.optimization_barrier((offer, rhs_own))
 
     offer = call(pick_kernel, plane_shape, [SMEM, ANY, VMEM], VMEM, four)(plan, occupied, offer)
     fixed = call(fixed_kernel, plane_shape, [SMEM, ANY], VMEM, four)(plan, occupied)
@@ -427,6 +455,9 @@
         pairs = [(c, 2 * s + c) for c in range(2)]
         pairs += [(n_orb - 2 + c, 2 * (ring + (ring - 1 + s) % ring) + c) for c in range(2)]
         got.append(permute(pieces[s], pairs))
+    rhs_up, rhs_down = permute(rhs_own, up_y), permute(rhs_own, down_y)
+    rhs_up, rhs_down, *got = lax.optimization_barrier((rhs_up, rhs_down, *got))
+    rhs_far_up, rhs_far_down = permute(rhs_up[:wide], up_y), permute(rhs_down[wide:], down_y)
     fixed = call(share_kernel, piece_shape, [SMEM] + [VMEM] * ring, VMEM)(plan, *got)
 
     def scatter(value):
@@ -465,9 +496,12 @@
     own_rows = 4 * share
     half_shape = shape((local_orbs, n_rows))
     spread_shape = shape((n_dom, local_orbs, n_rows))
-    parts = call(functools.partial(shares_kernel, scale), shape((n_orb, local_orbs, own_rows)))(
-        low_mask, rhs_all, xs, ys
-    )
+    rhs_places = ((0, 0), (ring - 1, 0), (1, 0), (2, 0), (2, 1))
+    parts = call(
+        functools.partial(shares_kernel, scale, rhs_places),
+        shape((n_orb, local_orbs, 128)),
+        [SMEM] + [VMEM] * 7,
+    )(plan, rhs_own, rhs_up, rhs_down, rhs_far_up, rhs_far_down, xs, ys)
     parts = lax.all_to_all(parts, "orb", 0, 0, tiled=True)
     xs_x, ys_up, ys_down, parts = lax.optimization_barrier((xs_x, ys_up, ys_down, parts))
     own, line = call(
@@ -485,11 +519,11 @@
     line_x, above, below, far_up, far_down, first_parts = lax.optimization_barrier(
         (line_x, above, below, far_up, far_down, first_parts)
     )
-    far = jnp.concatenate([far_up, far_down], axis=0)
-    far_x = permute(far, swap_x)
+    far_up_x, far_down_x = permute(far_up, swap_x), permute(far_down, swap_x)
     own_up = permute(above[: 2 * share], up_y)
     own_down = permute(below[2 * share :], down_y)
-    pieces = [own, below, above, own_up, own_down, line, line_x, far, far_x]
+    pieces = [own, below, above, own_up, own_down]
+    pieces += [line, line_x, far_up, far_down, far_up_x, far_down_x]
     blocks_shape = [shape((n_rows // 2, cells), jnp.bfloat16)] * 2
 
     picks = win_index[:, None] == jnp.arange(n_occ, dtype=jnp.int32)[None, :]
@@ -548,9 +582,15 @@
             outs = [shape((local_orbs, cells))] * 2 + [shape((n_dom, n_orb, rows_y // n_dom, rows_z))]
         if step == 0:
             outs, blocks = outs + blocks_shape, pieces
+            specs = [VMEM] * 6 + [HBM] * len(pieces), [VMEM] * 4
+            sems = (pltpu.SemaphoreType.DMA((len(pieces),)),)
+        else:
+            specs, sems = (None, None), ()
         x, x_b, *rest = call(
-            functools.partial(update_kernel, scale, 512, step > 0, final, math.sqrt(width), (5, 4)),
+            functools.partial(update_kernel, scale, 512, step > 0, final, math.sqrt(width), (5, 6)),
             outs,
+            *specs,
+            sems,
         )(low_mask, coeff_b, coeff_o, resid, diag, *extra, *blocks)
         if step == 0:
             blocks = rest

time: 227 us -> 213 us (0.938)
  between operations: 15.4 us -> 1.92 us
  starting transfers between devices: 75.1 us -> 81.6 us
  local copies, waits for them, and re-layouts: 15.9 us -> 9.51 us
  blocking collectives: 22.1 us -> 17.8 us
  waiting for transfers between devices: 69.9 us -> 73.9 us
    ppermute x27 -> x33, starting transfers between devices: 39.3 us -> 50 us  [permute(): return lax.ppermute(value, 'orb', pairs)]
    all_to_all x1, waiting for transfers between devices: 0.23 us -> 5.14 us  [per_device(): lax.all_to_all(call(spread_shares_kernel, spread_shape)(parts), 'dom', 0,...]
    unnamed x47 -> x27, local copies, waits for them, and re-layouts: 12 us -> 7.64 us
    all_to_all x1, blocking collectives: 22.1 us -> 17.8 us  [per_device(): parts = lax.all_to_all(spread, 'dom', 0, 0, tiled=True)]
    ppermute x27 -> x33, waiting for transfers between devices: 29.9 us -> 27.1 us  [permute(): return lax.ppermute(value, 'orb', pairs)]
    ppermute x2, starting transfers between devices: 6.46 us -> 4.14 us  [per_device(): off = lax.ppermute(x_b, ('dom', 'orb'), across)]
    ppermute x2, waiting for transfers between devices: 9.08 us -> 11.4 us  [per_device(): off = lax.ppermute(x_b, ('dom', 'orb'), across)]
  transfers between devices with their start and end apart: 35 -> 40, of which waited for: 13 -> 16; matrix products, arithmetic and copies ran while one was open for 5% -> 3% of each run, Pallas kernels for 6% -> 6%
where the time goes in v2:
time: 213 us; the launch traced here: 212 us
  starting transfers between devices  81.6 us (38%)
  waiting for transfers between devices  73.9 us (35%)
  Pallas kernels  23.3 us (11%)
  blocking collectives  17.8 us (8%)
  local copies, waits for them, and re-layouts  9.51 us (4%)
  other arithmetic  3.46 us (2%)
    ppermute x33, starting transfers between devices, permute(): return lax.ppermute(value, 'orb', pairs)  50 us
    ppermute x33, waiting for transfers between devices, permute(): return lax.ppermute(value, 'orb', pairs)  27.1 us
    all_to_all x1, blocking collectives, per_device(): parts = lax.all_to_all(spread, 'dom', 0, 0, tiled=True)  17.8 us
    all_to_all x1, waiting for transfers between devices, per_device(): lax.all_to_all(raw.reshape((n_dom * n_orb,) + raw.shape[2:]), ('dom', 'or...  13.1 us
    all_to_all x1, waiting for transfers between devices, per_device(): parts = lax.all_to_all(spread, 'dom', 0, 0, tiled=True)  12.1 us
    ppermute x2, waiting for transfers between devices, per_device(): off = lax.ppermute(x_b, ('dom', 'orb'), across)  11.4 us
    all_to_all x1, starting transfers between devices, per_device(): lax.all_to_all(call(spread_shares_kernel, spread_shape)(parts), 'dom', 0,...  9.96 us
    unnamed x27, local copies, waits for them, and re-layouts  7.64 us
  transfers between devices with their start and end apart: 40, of which 16 were waited for; matrix products, arithmetic and copies ran while one was open for 3% of the time, Pallas kernels for 6%

profile of v2, /device:TPU:1, one launch (start us, length us, event | category | flops | bytes accessed | tf_op | source)
XLA Modules:
  0.0 211.5 jit_solution(2105548127589488033)
XLA Ops:
  1.3 2.9 %shard_map.121 = (s32[40]{0:T(128)S(1)}, s32[1]{0:T(128)}, bf16[128,32,128]{2,1,0:T(8,128)(2,1)}) custom-call(s32[4]{0:T(128)S(1)} %copy-done.9, s32[1]{0:T(128)} %bitcast.6.dev_ref, bf16[2,128,2,32,128]{4,3,2,1,0:T(8,128)(2,1)} %occupied_ref.7), custom_call_target="tpu_custom_call" | custom-call | tf_op jit(solution)/shard_map/pallas_call | solution.py:423
  4.2 3.3 %collective-permute-start.1 = (bf16[128,32,128]{2,1,0:T(8,128)(2,1)}, bf16[128,32,128]{2,1,0:T(8,128)(2,1)S(1)}, u32[]{:S(2)}, u32[]{:S(2)}) collective-permute-start(bf16[128,32,128]{2,1,0:T(8,128)(2,1)} %get-tuple-element.71), channel_id=1, source_target_pairs={{0,1},{1,0},{2,3},{3,2},{4,5},{5,4},{6,7},{7,6},{8,9},{9,8},{10,11... | collective-permute-start | bytes 3145736 | tf_op jit(solution)/shard_map/ppermute | solution.py:413
  7.5 2.8 %shard_map.125 = bf16[128,32,128]{2,1,0:T(8,128)(2,1)} custom-call(s32[40]{0:T(128)S(1)} %get-tuple-element.70.plan_ref, bf16[2,128,2,32,128]{4,3,2,1,0:T(8,128)(2,1)} %occupied_ref.7), custom_call_target="tpu_custom_call" | custom-call | tf_op jit(solution)/shard_map/pallas_call | solution.py:442
  10.3 1.3 collective-permute-start.6
  11.8 2.2 %collective-permute-start.2 = (f32[8,4096]{1,0:T(8,128)S(1)}, f32[8,4096]{1,0:T(8,128)S(1)}, u32[]{:S(2)}, u32[]{:S(2)}) collective-permute-start(f32[8,4096]{1,0:T(8,128)S(1)} %get-tuple-element.73), channel_id=1, source_target_pairs={{0,1},{1,0},{2,3},{3,2},{4,5},{5,4},{6,7},{7,6},{8,9},{9,8},{10,11... | collective-permute-start | bytes 393224 | tf_op jit(solution)/shard_map/ppermute | solution.py:413
  15.9 4.1 %collective-permute-done.3 = bf16[16,4096]{1,0:T(8,128)(2,1)S(1)} collective-permute-done((bf16[16,4096]{1,0:T(8,128)(2,1)S(1)}, bf16[16,4096]{1,0:T(8,128)(2,1)S(1)}, u32[]{:S(2)}, u32[]{:S(2)}) %collective-permute-start.3) | collective-permute-done | bytes 131104 | tf_op jit(solution)/shard_map/ppermute | solution.py:413
  20.0 1.7 shard_map.124
  21.7 3.6 %all-to-all-start.1 = ((bf16[8,16,32,128]{3,2,1,0:T(8,128)(2,1)}), bf16[8,16,32,128]{3,2,1,0:T(8,128)(2,1)S(1)}, u32[]{:S(2)}, u32[]{:S(2)}) async-start(bf16[8,16,32,128]{3,2,1,0:T(8,128)(2,1)} %bitcast.7), calls=%async_computation.1 | async-start | bytes 2097152 | tf_op jit(solution)/shard_map/all_to_all | solution.py:465
  25.3 1.4 shard_map.126
  26.7 3.2 %collective-permute-start.7 = (bf16[32,32,128]{2,1,0:T(8,128)(2,1)S(1)}, bf16[32,32,128]{2,1,0:T(8,128)(2,1)S(1)}, u32[]{:S(2)}, u32[]{:S(2)}) collective-permute-start(bf16[32,32,128]{2,1,0:T(8,128)(2,1)S(1)} %get-tuple-element.79), channel_id=1, source_target_pairs={{0,2},{1,3},{14,8},{15,9},{16,18},{17,19},{30,24},{31,25},{32,34},... | collective-permute-start | bytes 786440 | tf_op jit(solution)/shard_map/ppermute | solution.py:413
  29.9 2.2 %collective-permute-start.8 = (bf16[32,32,128]{2,1,0:T(8,128)(2,1)S(1)}, bf16[32,32,128]{2,1,0:T(8,128)(2,1)S(1)}, u32[]{:S(2)}, u32[]{:S(2)}) collective-permute-start(bf16[32,32,128]{2,1,0:T(8,128)(2,1)S(1)} %get-tuple-element.80), channel_id=1, source_target_pairs={{0,4},{1,5},{14,10},{15,11},{16,20},{17,21},{30,26},{31,27},{32,36... | collective-permute-start | bytes 786440 | tf_op jit(solution)/shard_map/ppermute | solution.py:413
  32.1 1.3 collective-permute-start.9
  33.5 2.7 %collective-permute-start.5 = (bf16[32,4096]{1,0:T(8,128)(2,1)S(1)}, bf16[32,4096]{1,0:T(8,128)(2,1)S(1)}, u32[]{:S(2)}, u32[]{:S(2)}) collective-permute-start(bf16[32,4096]{1,0:T(8,128)(2,1)S(1)} %pad_maximum_fusion.refs_0_), channel_id=1, source_target_pairs={{0,6},{1,7},{2,0},{3,1},{4,2},{5,3},{6,4},{7,5},{8,14},{9,15},{10,... | collective-permute-start | bytes 786440 | tf_op jit(solution)/shard_map/ppermute | solution.py:413
  36.2 4.3 %collective-permute-done.7.refs_1_ = bf16[32,32,128]{2,1,0:T(8,128)(2,1)S(1)} collective-permute-done((bf16[32,32,128]{2,1,0:T(8,128)(2,1)S(1)}, bf16[32,32,128]{2,1,0:T(8,128)(2,1)S(1)}, u32[]{:S(2)}, u32[]{:S(2)}) %collective-permute-start.7) | collective-permute-done | bytes 262176 | tf_op jit(solution)/shard_map/ppermute | solution.py:413
  40.5 5.6 %collective-permute-done.8.refs_2_ = bf16[32,32,128]{2,1,0:T(8,128)(2,1)S(1)} collective-permute-done((bf16[32,32,128]{2,1,0:T(8,128)(2,1)S(1)}, bf16[32,32,128]{2,1,0:T(8,128)(2,1)S(1)}, u32[]{:S(2)}, u32[]{:S(2)}) %collective-permute-start.8) | collective-permute-done | bytes 262176 | tf_op jit(solution)/shard_map/ppermute | solution.py:413
  46.1 5.6 %collective-permute-done.4.refs_1_ = bf16[32,4096]{1,0:T(8,128)(2,1)S(1)} collective-permute-done((bf16[32,4096]{1,0:T(8,128)(2,1)S(1)}, bf16[32,4096]{1,0:T(8,128)(2,1)S(1)}, u32[]{:S(2)}, u32[]{:S(2)}) %collective-permute-start.4) | collective-permute-done | bytes 262176 | tf_op jit(solution)/shard_map/ppermute | solution.py:413
  52.4 2.2 %collective-permute-start.13 = (bf16[16,4096]{1,0:T(8,128)(2,1)}, bf16[16,4096]{1,0:T(8,128)(2,1)S(1)}, u32[]{:S(2)}, u32[]{:S(2)}) collective-permute-start(bf16[16,4096]{1,0:T(8,128)(2,1)} %slice.24), channel_id=1, source_target_pairs={{0,2},{1,3},{2,4},{3,5},{4,6},{5,7},{6,0},{7,1},{8,10},{9,11},{10,... | collective-permute-start | bytes 393224 | tf_op jit(solution)/shard_map/ppermute | solution.py:413
  58.1 1.7 collective-permute-start.12
  59.8 3.4 %collective-permute-start.10 = (bf16[32,4096]{1,0:T(8,128)(2,1)S(1)}, bf16[32,4096]{1,0:T(8,128)(2,1)S(1)}, u32[]{:S(2)}, u32[]{:S(2)}) collective-permute-start(bf16[32,4096]{1,0:T(8,128)(2,1)S(1)} %get-tuple-element.88.refs_5_.refs_0_), channel_id=1, source_target_pairs={{0,8},{1,9},{2,10},{3,11},{4,12},{5,13},{6,14},{7,15},{8,0},{9,1},... | collective-permute-start | bytes 786440 | tf_op jit(solution)/shard_map/ppermute | solution.py:413
  64.2 1.7 collective-permute-start.21
  65.9 2.4 %shard_map.129 = f32[16,8,128]{2,1,0:T(8,128)} custom-call(s32[40]{0:T(128)S(1)} %get-tuple-element.70.plan_ref, bf16[32,4096]{1,0:T(8,128)(2,1)S(1)} %pad_maximum_fusion.refs_0_, bf16[32,4096]{1,0:T(8,128)(2,1)S(1)} %collective-permute-done.4.refs_1_, bf16[32,4096]{1,0:T(8,128)(2,1)S(1)} %collective-permute-done.5.refs_2_, ...), custom_call_target="tpu_custom_call" | custom-call | tf_op jit(solution)/shard_map/pallas_call | solution.py:500
  68.3 4.1 %all-to-all-start.2 = ((f32[16,8,128]{2,1,0:T(8,128)}), f32[16,8,128]{2,1,0:T(8,128)S(1)}, u32[]{:S(2)}, u32[]{:S(2)}) async-start(f32[16,8,128]{2,1,0:T(8,128)} %shard_map.129), calls=%async_computation.2 | async-start | bytes 131072 | tf_op jit(solution)/shard_map/all_to_all | solution.py:505
  73.3 5.0 %all-to-all-done.2.parts_ref = f32[16,8,128]{2,1,0:T(8,128)S(1)} async-done(((f32[16,8,128]{2,1,0:T(8,128)}), f32[16,8,128]{2,1,0:T(8,128)S(1)}, u32[]{:S(2)}, u32[]{:S(2)}) %all-to-all-start.2) | async-done | bytes 65568 | tf_op jit(solution)/shard_map/all_to_all | solution.py:505
  79.9 2.3 %collective-permute-start.17 = (bf16[64,4096]{1,0:T(8,128)(2,1)}, bf16[64,4096]{1,0:T(8,128)(2,1)S(1)}, u32[]{:S(2)}, u32[]{:S(2)}) collective-permute-start(bf16[64,4096]{1,0:T(8,128)(2,1)} %get-tuple-element.96.refs_1_), channel_id=1, source_target_pairs={{0,6},{1,7},{2,0},{3,1},{4,2},{5,3},{6,4},{7,5},{8,14},{9,15},{10,... | collective-permute-start | bytes 1572872 | tf_op jit(solution)/shard_map/ppermute | solution.py:413
  83.0 10.0 %all-to-all-start.3 = ((f32[16,8,512]{2,1,0:T(8,128)}), f32[16,8,512]{2,1,0:T(8,128)S(1)}, u32[]{:S(2)}, u32[]{:S(2)}) async-start(f32[16,8,512]{2,1,0:T(8,128)} %shard_map.131), calls=%async_computation.3 | async-start | bytes 524288 | tf_op jit(solution)/shard_map/all_to_all | solution.py:516
  94.0 2.7 %collective-permute-start.19 = (bf16[16,4096]{1,0:T(8,128)(2,1)S(1)}, bf16[16,4096]{1,0:T(8,128)(2,1)S(1)}, u32[]{:S(2)}, u32[]{:S(2)}) collective-permute-start(bf16[16,4096]{1,0:T(8,128)(2,1)S(1)} %slice.27), channel_id=1, source_target_pairs={{0,6},{1,7},{2,0},{3,1},{4,2},{5,3},{6,4},{7,5},{8,14},{9,15},{10,... | collective-permute-start | bytes 393224 | tf_op jit(solution)/shard_map/ppermute | solution.py:413
  96.7 2.4 %collective-permute-done.18.refs_8_ = bf16[16,4096]{1,0:T(8,128)(2,1)S(1)} collective-permute-done((bf16[16,4096]{1,0:T(8,128)(2,1)S(1)}, bf16[16,4096]{1,0:T(8,128)(2,1)S(1)}, u32[]{:S(2)}, u32[]{:S(2)}) %collective-permute-start.18) | collective-permute-done | bytes 131104 | tf_op jit(solution)/shard_map/ppermute | solution.py:413
  99.1 5.1 %all-to-all-done.3.parts_ref = f32[16,8,512]{2,1,0:T(8,128)S(1)} async-done(((f32[16,8,512]{2,1,0:T(8,128)}), f32[16,8,512]{2,1,0:T(8,128)S(1)}, u32[]{:S(2)}, u32[]{:S(2)}) %all-to-all-start.3) | async-done | bytes 262176 | tf_op jit(solution)/shard_map/all_to_all | solution.py:516
  104.5 2.7 %collective-permute-start.23 = (bf16[32,4096]{1,0:T(8,128)(2,1)S(1)}, bf16[32,4096]{1,0:T(8,128)(2,1)S(1)}, u32[]{:S(2)}, u32[]{:S(2)}) collective-permute-start(bf16[32,4096]{1,0:T(8,128)(2,1)S(1)} %slice.29), channel_id=1, source_target_pairs={{0,6},{1,7},{2,0},{3,1},{4,2},{5,3},{6,4},{7,5},{8,14},{9,15},{10,... | collective-permute-start | bytes 786440 | tf_op jit(solution)/shard_map/ppermute | solution.py:413
  108.7 4.5 %collective-permute-start.20 = (bf16[16,256]{1,0:T(8,128)(2,1)S(1)}, bf16[16,256]{1,0:T(8,128)(2,1)S(1)}, u32[]{:S(2)}, u32[]{:S(2)}) collective-permute-start(bf16[16,256]{1,0:T(8,128)(2,1)S(1)} %shard_map.132.mine_ref), channel_id=1, source_target_pairs={{0,1},{1,0},{2,3},{3,2},{4,5},{5,4},{6,7},{7,6},{8,9},{9,8},{10,11... | collective-permute-start | bytes 24584 | tf_op jit(solution)/shard_map/ppermute | solution.py:413
  117.3 2.3 %shard_map.133 = (f32[16,4096]{1,0:T(8,128)S(1)}, bf16[16,4096]{1,0:T(8,128)(2,1)S(1)}, bf16[256,4096]{1,0:T(8,128)(2,1)S(1)}, bf16[256,4096]{1,0:T(8,128)(2,1)S(1)}) custom-call(f32[8,128]{1,0:T(8,128)S(1)} %broadcast_in_dim.41.low_ref, bf16[16,256]{1,0:T(8,128)(2,1)S(1)} %shard_map.132.mine_ref, bf16[16,256]{1,0:T(8,128)(2,1)S(1)} %collective-permute-done.20.other_ref, ...), custom_call_target="tpu_custom_call" | custom-call | tf_op jit(solution)/shard_map/pallas_call | solution.py:589
  119.6 3.5 %collective-permute-start.26 = (f32[16,4096]{1,0:T(8,128)S(1)}, f32[16,4096]{1,0:T(8,128)S(1)}, u32[]{:S(2)}, u32[]{:S(2)}) collective-permute-start(f32[16,4096]{1,0:T(8,128)S(1)} %get-tuple-element.105.x_ref.refs_0_), channel_id=1, source_target_pairs={{0,1},{1,0},{2,3},{3,2},{4,5},{5,4},{6,7},{7,6},{8,9},{9,8},{10,11... | collective-permute-start | bytes 786440 | tf_op jit(solution)/shard_map/ppermute | solution.py:413
  123.1 2.0 collective-permute-start.27
  125.1 5.8 %collective-permute-done.27.off_ref = bf16[16,4096]{1,0:T(8,128)(2,1)S(1)} collective-permute-done((bf16[16,4096]{1,0:T(8,128)(2,1)S(1)}, bf16[16,4096]{1,0:T(8,128)(2,1)S(1)}, u32[]{:S(2)}, u32[]{:S(2)}) %collective-permute-start.27) | collective-permute-done | bytes 131104 | tf_op jit(solution)/shard_map/ppermute | solution.py:570
  130.9 1.2 shard_map.134
  132.1 1.2 collective-permute-done.28.other_ref
  133.4 17.8 %all_to_all.34.parts_ref = f32[16,8,512]{2,1,0:T(8,128)S(1)} all-to-all(f32[16,8,512]{2,1,0:T(8,128)S(1)} %shard_map.135), channel_id=1, replica_groups=mesh['dom'=16,'orb'=16] {'dom'}, dimensions={0} | all-to-all | bytes 524288 | tf_op jit(solution)/shard_map/all_to_all | solution.py:577
  151.2 2.0 collective-permute-start.29
  155.2 2.1 %collective-permute-start.31 = (bf16[16,4096]{1,0:T(8,128)(2,1)S(1)}, bf16[16,4096]{1,0:T(8,128)(2,1)S(1)}, u32[]{:S(2)}, u32[]{:S(2)}) collective-permute-start(bf16[16,4096]{1,0:T(8,128)(2,1)S(1)} %get-tuple-element.113), channel_id=1, source_target_pairs={{1,16},{16,1},{3,18},{18,3},{5,20},{20,5},{7,22},{22,7},{9,24},{24... | collective-permute-start | bytes 393224 | tf_op jit(solution)/shard_map/ppermute | solution.py:570
  157.3 5.6 %collective-permute-done.31.off_ref = bf16[16,4096]{1,0:T(8,128)(2,1)S(1)} collective-permute-done((bf16[16,4096]{1,0:T(8,128)(2,1)S(1)}, bf16[16,4096]{1,0:T(8,128)(2,1)S(1)}, u32[]{:S(2)}, u32[]{:S(2)}) %collective-permute-start.31) | collective-permute-done | bytes 131104 | tf_op jit(solution)/shard_map/ppermute | solution.py:570
  162.9 1.2 shard_map.138
  166.3 4.5 %all-to-all-start.5 = ((f32[16,8,512]{2,1,0:T(8,128)}), f32[16,8,512]{2,1,0:T(8,128)S(1)}, u32[]{:S(2)}, u32[]{:S(2)}) async-start(f32[16,8,512]{2,1,0:T(8,128)} %shard_map.139), calls=%async_computation.5 | async-start | bytes 524288 | tf_op jit(solution)/shard_map/all_to_all | solution.py:577
  171.5 12.1 %all-to-all-done.5.parts_ref = f32[16,8,512]{2,1,0:T(8,128)S(1)} async-done(((f32[16,8,512]{2,1,0:T(8,128)}), f32[16,8,512]{2,1,0:T(8,128)S(1)}, u32[]{:S(2)}, u32[]{:S(2)}) %all-to-all-start.5) | async-done | bytes 262176 | tf_op jit(solution)/shard_map/all_to_all | solution.py:577
  183.6 1.7 collective-permute-start.33
  186.3 1.6 copy-done.1
  187.9 1.4 shard_map.143
  189.5 5.3 %all-to-all-start.6 = ((f32[256,2,128]{2,1,0:T(2,128)}), f32[256,2,128]{2,1,0:T(2,128)S(1)}, u32[]{:S(2)}, u32[]{:S(2)}) async-start(f32[256,2,128]{2,1,0:T(2,128)} %bitcast.17), calls=%async_computation.6 | async-start | bytes 524288 | tf_op jit(solution)/shard_map/all_to_all | solution.py:602
  197.1 13.1 %all-to-all-done.6.terms_ref = f32[256,2,128]{2,1,0:T(2,128)S(1)} async-done(((f32[256,2,128]{2,1,0:T(2,128)}), f32[256,2,128]{2,1,0:T(2,128)S(1)}, u32[]{:S(2)}, u32[]{:S(2)}) %all-to-all-start.6) | async-done | bytes 262176 | tf_op jit(solution)/shard_map/all_to_all | solution.py:602
  (117 shorter events, 26.7 us)
Async XLA Ops:
  1.3 10.4 %copy-start.8 = (f32[8,2,32,128]{3,2,1,0:T(8,128)S(1)}, f32[8,2,32,128]{3,2,1,0:T(8,128)}, u32[]{:S(2)}) copy-start(f32[8,2,32,128]{3,2,1,0:T(8,128)} %field_ref.1) | copy-start | bytes 786436
  4.2 15.8 %collective-permute-start.1 = (bf16[128,32,128]{2,1,0:T(8,128)(2,1)}, bf16[128,32,128]{2,1,0:T(8,128)(2,1)S(1)}, u32[]{:S(2)}, u32[]{:S(2)}) collective-permute-start(bf16[128,32,128]{2,1,0:T(8,128)(2,1)} %get-tuple-element.71), channel_id=1, source_target_pairs={{0,1},{1,0},{2,3},{3,2},{4,5},{5,4},{6,7},{7,6},{8,9},{9,8},{10,11... | collective-permute-start | bytes 3145736 | tf_op jit(solution)/shard_map/ppermute | solution.py:413
  10.3 11.4 %collective-permute-start.6 = (bf16[128,32,128]{2,1,0:T(8,128)(2,1)}, bf16[128,32,128]{2,1,0:T(8,128)(2,1)}, u32[]{:S(2)}, u32[]{:S(2)}) collective-permute-start(bf16[128,32,128]{2,1,0:T(8,128)(2,1)} %shard_map.125), channel_id=1, source_target_pairs={{0,1},{15,14},{16,17},{31,30},{32,33},{47,46},{48,49},{63,62},{64,... | collective-permute-start | bytes 3145736 | tf_op jit(solution)/shard_map/ppermute | solution.py:413
  11.8 3.3 %collective-permute-start.2 = (f32[8,4096]{1,0:T(8,128)S(1)}, f32[8,4096]{1,0:T(8,128)S(1)}, u32[]{:S(2)}, u32[]{:S(2)}) collective-permute-start(f32[8,4096]{1,0:T(8,128)S(1)} %get-tuple-element.73), channel_id=1, source_target_pairs={{0,1},{1,0},{2,3},{3,2},{4,5},{5,4},{6,7},{7,6},{8,9},{9,8},{10,11... | collective-permute-start | bytes 393224 | tf_op jit(solution)/shard_map/ppermute | solution.py:413
  15.1 4.9 %collective-permute-start.3 = (bf16[16,4096]{1,0:T(8,128)(2,1)S(1)}, bf16[16,4096]{1,0:T(8,128)(2,1)S(1)}, u32[]{:S(2)}, u32[]{:S(2)}) collective-permute-start(bf16[16,4096]{1,0:T(8,128)(2,1)S(1)} %get-tuple-element.74), channel_id=1, source_target_pairs={{0,8},{1,9},{2,10},{3,11},{4,12},{5,13},{6,14},{7,15},{8,0},{9,1},... | collective-permute-start | bytes 393224 | tf_op jit(solution)/shard_map/ppermute | solution.py:413
  21.7 34.5 %all-to-all-start.1 = ((bf16[8,16,32,128]{3,2,1,0:T(8,128)(2,1)}), bf16[8,16,32,128]{3,2,1,0:T(8,128)(2,1)S(1)}, u32[]{:S(2)}, u32[]{:S(2)}) async-start(bf16[8,16,32,128]{3,2,1,0:T(8,128)(2,1)} %bitcast.7), calls=%async_computation.1 | async-start | bytes 2097152 | tf_op jit(solution)/shard_map/all_to_all | solution.py:465
  25.3 37.9 %copy-start.11 = (s32[8]{0:T(128)S(1)}, s32[8]{0:T(128)}, u32[]{:S(2)}) copy-start(s32[8]{0:T(128)} %param.15) | copy-start | bytes 100
  26.7 13.7 %collective-permute-start.7 = (bf16[32,32,128]{2,1,0:T(8,128)(2,1)S(1)}, bf16[32,32,128]{2,1,0:T(8,128)(2,1)S(1)}, u32[]{:S(2)}, u32[]{:S(2)}) collective-permute-start(bf16[32,32,128]{2,1,0:T(8,128)(2,1)S(1)} %get-tuple-element.79), channel_id=1, source_target_pairs={{0,2},{1,3},{14,8},{15,9},{16,18},{17,19},{30,24},{31,25},{32,34},... | collective-permute-start | bytes 786440 | tf_op jit(solution)/shard_map/ppermute | solution.py:413
  29.9 16.1 %collective-permute-start.8 = (bf16[32,32,128]{2,1,0:T(8,128)(2,1)S(1)}, bf16[32,32,128]{2,1,0:T(8,128)(2,1)S(1)}, u32[]{:S(2)}, u32[]{:S(2)}) collective-permute-start(bf16[32,32,128]{2,1,0:T(8,128)(2,1)S(1)} %get-tuple-element.80), channel_id=1, source_target_pairs={{0,4},{1,5},{14,10},{15,11},{16,20},{17,21},{30,26},{31,27},{32,36... | collective-permute-start | bytes 786440 | tf_op jit(solution)/shard_map/ppermute | solution.py:413
  32.1 13.9 %collective-permute-start.9 = (bf16[32,32,128]{2,1,0:T(8,128)(2,1)S(1)}, bf16[32,32,128]{2,1,0:T(8,128)(2,1)S(1)}, u32[]{:S(2)}, u32[]{:S(2)}) collective-permute-start(bf16[32,32,128]{2,1,0:T(8,128)(2,1)S(1)} %get-tuple-element.81), channel_id=1, source_target_pairs={{0,6},{1,7},{14,12},{15,13},{16,22},{17,23},{30,28},{31,29},{32,38... | collective-permute-start | bytes 786440 | tf_op jit(solution)/shard_map/ppermute | solution.py:413
  33.4 18.2 %collective-permute-start.4 = (bf16[32,4096]{1,0:T(8,128)(2,1)S(1)}, bf16[32,4096]{1,0:T(8,128)(2,1)S(1)}, u32[]{:S(2)}, u32[]{:S(2)}) collective-permute-start(bf16[32,4096]{1,0:T(8,128)(2,1)S(1)} %pad_maximum_fusion.refs_0_), channel_id=1, source_target_pairs={{0,2},{1,3},{2,4},{3,5},{4,6},{5,7},{6,0},{7,1},{8,10},{9,11},{10,... | collective-permute-start | bytes 786440 | tf_op jit(solution)/shard_map/ppermute | solution.py:413
  33.5 18.2 %collective-permute-start.5 = (bf16[32,4096]{1,0:T(8,128)(2,1)S(1)}, bf16[32,4096]{1,0:T(8,128)(2,1)S(1)}, u32[]{:S(2)}, u32[]{:S(2)}) collective-permute-start(bf16[32,4096]{1,0:T(8,128)(2,1)S(1)} %pad_maximum_fusion.refs_0_), channel_id=1, source_target_pairs={{0,6},{1,7},{2,0},{3,1},{4,2},{5,3},{6,4},{7,5},{8,14},{9,15},{10,... | collective-permute-start | bytes 786440 | tf_op jit(solution)/shard_map/ppermute | solution.py:413
  52.4 11.8 %collective-permute-start.13 = (bf16[16,4096]{1,0:T(8,128)(2,1)}, bf16[16,4096]{1,0:T(8,128)(2,1)S(1)}, u32[]{:S(2)}, u32[]{:S(2)}) collective-permute-start(bf16[16,4096]{1,0:T(8,128)(2,1)} %slice.24), channel_id=1, source_target_pairs={{0,2},{1,3},{2,4},{3,5},{4,6},{5,7},{6,0},{7,1},{8,10},{9,11},{10,... | collective-permute-start | bytes 393224 | tf_op jit(solution)/shard_map/ppermute | solution.py:413
  55.2 10.7 %collective-permute-start.14 = (bf16[16,4096]{1,0:T(8,128)(2,1)}, bf16[16,4096]{1,0:T(8,128)(2,1)}, u32[]{:S(2)}, u32[]{:S(2)}) collective-permute-start(bf16[16,4096]{1,0:T(8,128)(2,1)} %slice.25), channel_id=1, source_target_pairs={{0,6},{1,7},{2,0},{3,1},{4,2},{5,3},{6,4},{7,5},{8,14},{9,15},{10,... | collective-permute-start | bytes 393224 | tf_op jit(solution)/shard_map/ppermute | solution.py:413
  57.0 21.3 %collective-permute-start.11 = (bf16[32,4096]{1,0:T(8,128)(2,1)S(1)}, bf16[32,4096]{1,0:T(8,128)(2,1)S(1)}, u32[]{:S(2)}, u32[]{:S(2)}) collective-permute-start(bf16[32,4096]{1,0:T(8,128)(2,1)S(1)} %get-tuple-element.89.refs_6_.refs_2_), channel_id=1, source_target_pairs={{0,2},{1,3},{2,4},{3,5},{4,6},{5,7},{6,0},{7,1},{8,10},{9,11},{10,... | collective-permute-start | bytes 786440 | tf_op jit(solution)/shard_map/ppermute | solution.py:413
  58.1 20.2 %collective-permute-start.12 = (bf16[32,4096]{1,0:T(8,128)(2,1)S(1)}, bf16[32,4096]{1,0:T(8,128)(2,1)S(1)}, u32[]{:S(2)}, u32[]{:S(2)}) collective-permute-start(bf16[32,4096]{1,0:T(8,128)(2,1)S(1)} %get-tuple-element.89.refs_6_.refs_2_), channel_id=1, source_target_pairs={{0,6},{1,7},{2,0},{3,1},{4,2},{5,3},{6,4},{7,5},{8,14},{9,15},{10,... | collective-permute-start | bytes 786440 | tf_op jit(solution)/shard_map/ppermute | solution.py:413
  59.8 18.5 %collective-permute-start.10 = (bf16[32,4096]{1,0:T(8,128)(2,1)S(1)}, bf16[32,4096]{1,0:T(8,128)(2,1)S(1)}, u32[]{:S(2)}, u32[]{:S(2)}) collective-permute-start(bf16[32,4096]{1,0:T(8,128)(2,1)S(1)} %get-tuple-element.88.refs_5_.refs_0_), channel_id=1, source_target_pairs={{0,8},{1,9},{2,10},{3,11},{4,12},{5,13},{6,14},{7,15},{8,0},{9,1},... | collective-permute-start | bytes 786440 | tf_op jit(solution)/shard_map/ppermute | solution.py:413
  64.2 29.8 %collective-permute-start.21 = (f32[8,1]{0,1:T(1,128)S(1)}, f32[8,1]{0,1:T(1,128)S(1)}, u32[]{:S(2)}, u32[]{:S(2)}) collective-permute-start(f32[8,1]{0,1:T(1,128)S(1)} %bitcast.38), channel_id=1, source_target_pairs={{0,1},{1,0},{2,3},{3,2},{4,5},{5,4},{6,7},{7,6},{8,9},{9,8},{10,11... | collective-permute-start | bytes 104 | tf_op jit(solution)/shard_map/ppermute | solution.py:413
  68.3 10.0 %all-to-all-start.2 = ((f32[16,8,128]{2,1,0:T(8,128)}), f32[16,8,128]{2,1,0:T(8,128)S(1)}, u32[]{:S(2)}, u32[]{:S(2)}) async-start(f32[16,8,128]{2,1,0:T(8,128)} %shard_map.129), calls=%async_computation.2 | async-start | bytes 131072 | tf_op jit(solution)/shard_map/all_to_all | solution.py:505
  79.2 34.8 %copy-start.6 = (bf16[96,4096]{1,0:T(8,128)(2,1)}, bf16[96,4096]{1,0:T(8,128)(2,1)S(1)}, u32[]{:S(2)}) copy-start(bf16[96,4096]{1,0:T(8,128)(2,1)S(1)} %get-tuple-element.95.refs_6_) | copy-start | bytes 2359300
  79.2 25.1 %collective-permute-start.15 = (bf16[96,4096]{1,0:T(8,128)(2,1)S(1)}, bf16[96,4096]{1,0:T(8,128)(2,1)}, u32[]{:S(2)}, u32[]{:S(2)}) collective-permute-start(bf16[96,4096]{1,0:T(8,128)(2,1)S(1)} %get-tuple-element.95.refs_6_), channel_id=1, source_target_pairs={{0,8},{1,9},{2,10},{3,11},{4,12},{5,13},{6,14},{7,15},{8,0},{9,1},... | collective-permute-start | bytes 2359304 | tf_op jit(solution)/shard_map/ppermute | solution.py:413
  79.5 24.7 %collective-permute-start.16 = (bf16[64,4096]{1,0:T(8,128)(2,1)}, bf16[64,4096]{1,0:T(8,128)(2,1)S(1)}, u32[]{:S(2)}, u32[]{:S(2)}) collective-permute-start(bf16[64,4096]{1,0:T(8,128)(2,1)} %get-tuple-element.96.refs_1_), channel_id=1, source_target_pairs={{0,2},{1,3},{2,4},{3,5},{4,6},{5,7},{6,0},{7,1},{8,10},{9,11},{10,... | collective-permute-start | bytes 1572872 | tf_op jit(solution)/shard_map/ppermute | solution.py:413
  79.9 24.4 %collective-permute-start.17 = (bf16[64,4096]{1,0:T(8,128)(2,1)}, bf16[64,4096]{1,0:T(8,128)(2,1)S(1)}, u32[]{:S(2)}, u32[]{:S(2)}) collective-permute-start(bf16[64,4096]{1,0:T(8,128)(2,1)} %get-tuple-element.96.refs_1_), channel_id=1, source_target_pairs={{0,6},{1,7},{2,0},{3,1},{4,2},{5,3},{6,4},{7,5},{8,14},{9,15},{10,... | collective-permute-start | bytes 1572872 | tf_op jit(solution)/shard_map/ppermute | solution.py:413
  83.0 21.3 %all-to-all-start.3 = ((f32[16,8,512]{2,1,0:T(8,128)}), f32[16,8,512]{2,1,0:T(8,128)S(1)}, u32[]{:S(2)}, u32[]{:S(2)}) async-start(f32[16,8,512]{2,1,0:T(8,128)} %shard_map.131), calls=%async_computation.3 | async-start | bytes 524288 | tf_op jit(solution)/shard_map/all_to_all | solution.py:516
  93.9 5.2 %collective-permute-start.18 = (bf16[16,4096]{1,0:T(8,128)(2,1)S(1)}, bf16[16,4096]{1,0:T(8,128)(2,1)S(1)}, u32[]{:S(2)}, u32[]{:S(2)}) collective-permute-start(bf16[16,4096]{1,0:T(8,128)(2,1)S(1)} %slice.26), channel_id=1, source_target_pairs={{0,2},{1,3},{2,4},{3,5},{4,6},{5,7},{6,0},{7,1},{8,10},{9,11},{10,... | collective-permute-start | bytes 393224 | tf_op jit(solution)/shard_map/ppermute | solution.py:413
  94.0 5.1 %collective-permute-start.19 = (bf16[16,4096]{1,0:T(8,128)(2,1)S(1)}, bf16[16,4096]{1,0:T(8,128)(2,1)S(1)}, u32[]{:S(2)}, u32[]{:S(2)}) collective-permute-start(bf16[16,4096]{1,0:T(8,128)(2,1)S(1)} %slice.27), channel_id=1, source_target_pairs={{0,6},{1,7},{2,0},{3,1},{4,2},{5,3},{6,4},{7,5},{8,14},{9,15},{10,... | collective-permute-start | bytes 393224 | tf_op jit(solution)/shard_map/ppermute | solution.py:413
  104.3 9.8 %copy-start.2 = (bf16[64,4096]{1,0:T(8,128)(2,1)}, bf16[64,4096]{1,0:T(8,128)(2,1)S(1)}, u32[]{:S(2)}) copy-start(bf16[64,4096]{1,0:T(8,128)(2,1)S(1)} %collective-permute-done.16.refs_3_) | copy-start | bytes 1572868
  104.3 9.8 %copy-start.4 = (bf16[64,4096]{1,0:T(8,128)(2,1)}, bf16[64,4096]{1,0:T(8,128)(2,1)S(1)}, u32[]{:S(2)}) copy-start(bf16[64,4096]{1,0:T(8,128)(2,1)S(1)} %collective-permute-done.17.refs_2_) | copy-start | bytes 1572868
  104.3 9.7 %collective-permute-start.22 = (bf16[32,4096]{1,0:T(8,128)(2,1)S(1)}, bf16[32,4096]{1,0:T(8,128)(2,1)S(1)}, u32[]{:S(2)}, u32[]{:S(2)}) collective-permute-start(bf16[32,4096]{1,0:T(8,128)(2,1)S(1)} %slice.28), channel_id=1, source_target_pairs={{0,2},{1,3},{2,4},{3,5},{4,6},{5,7},{6,0},{7,1},{8,10},{9,11},{10,... | collective-permute-start | bytes 786440 | tf_op jit(solution)/shard_map/ppermute | solution.py:413
  104.5 9.6 %collective-permute-start.23 = (bf16[32,4096]{1,0:T(8,128)(2,1)S(1)}, bf16[32,4096]{1,0:T(8,128)(2,1)S(1)}, u32[]{:S(2)}, u32[]{:S(2)}) collective-permute-start(bf16[32,4096]{1,0:T(8,128)(2,1)S(1)} %slice.29), channel_id=1, source_target_pairs={{0,6},{1,7},{2,0},{3,1},{4,2},{5,3},{6,4},{7,5},{8,14},{9,15},{10,... | collective-permute-start | bytes 786440 | tf_op jit(solution)/shard_map/ppermute | solution.py:413
  107.2 6.8 %collective-permute-start.24 = (bf16[16,4096]{1,0:T(8,128)(2,1)S(1)}, bf16[16,4096]{1,0:T(8,128)(2,1)S(1)}, u32[]{:S(2)}, u32[]{:S(2)}) collective-permute-start(bf16[16,4096]{1,0:T(8,128)(2,1)S(1)} %collective-permute-done.18.refs_8_), channel_id=1, source_target_pairs={{0,8},{1,9},{2,10},{3,11},{4,12},{5,13},{6,14},{7,15},{8,0},{9,1},... | collective-permute-start | bytes 393224 | tf_op jit(solution)/shard_map/ppermute | solution.py:413
  107.7 6.3 %collective-permute-start.25 = (bf16[16,4096]{1,0:T(8,128)(2,1)S(1)}, bf16[16,4096]{1,0:T(8,128)(2,1)S(1)}, u32[]{:S(2)}, u32[]{:S(2)}) collective-permute-start(bf16[16,4096]{1,0:T(8,128)(2,1)S(1)} %collective-permute-done.19.refs_9_), channel_id=1, source_target_pairs={{0,8},{1,9},{2,10},{3,11},{4,12},{5,13},{6,14},{7,15},{8,0},{9,1},... | collective-permute-start | bytes 393224 | tf_op jit(solution)/shard_map/ppermute | solution.py:413
  108.7 5.4 %collective-permute-start.20 = (bf16[16,256]{1,0:T(8,128)(2,1)S(1)}, bf16[16,256]{1,0:T(8,128)(2,1)S(1)}, u32[]{:S(2)}, u32[]{:S(2)}) collective-permute-start(bf16[16,256]{1,0:T(8,128)(2,1)S(1)} %shard_map.132.mine_ref), channel_id=1, source_target_pairs={{0,1},{1,0},{2,3},{3,2},{4,5},{5,4},{6,7},{7,6},{8,9},{9,8},{10,11... | collective-permute-start | bytes 24584 | tf_op jit(solution)/shard_map/ppermute | solution.py:413
  119.6 43.3 %copy-start = (bf16[256,4096]{1,0:T(8,128)(2,1)}, bf16[256,4096]{1,0:T(8,128)(2,1)S(1)}, u32[]{:S(2)}) copy-start(bf16[256,4096]{1,0:T(8,128)(2,1)S(1)} %get-tuple-element.108.second_ref.refs_2_.refs_3_) | copy-start | bytes 6291460
  119.6 11.3 %collective-permute-start.26 = (f32[16,4096]{1,0:T(8,128)S(1)}, f32[16,4096]{1,0:T(8,128)S(1)}, u32[]{:S(2)}, u32[]{:S(2)}) collective-permute-start(f32[16,4096]{1,0:T(8,128)S(1)} %get-tuple-element.105.x_ref.refs_0_), channel_id=1, source_target_pairs={{0,1},{1,0},{2,3},{3,2},{4,5},{5,4},{6,7},{7,6},{8,9},{9,8},{10,11... | collective-permute-start | bytes 786440 | tf_op jit(solution)/shard_map/ppermute | solution.py:413
  123.1 7.8 %collective-permute-start.27 = (bf16[16,4096]{1,0:T(8,128)(2,1)S(1)}, bf16[16,4096]{1,0:T(8,128)(2,1)S(1)}, u32[]{:S(2)}, u32[]{:S(2)}) collective-permute-start(bf16[16,4096]{1,0:T(8,128)(2,1)S(1)} %get-tuple-element.106), channel_id=1, source_target_pairs={{1,16},{16,1},{3,18},{18,3},{5,20},{20,5},{7,22},{22,7},{9,24},{24... | collective-permute-start | bytes 393224 | tf_op jit(solution)/shard_map/ppermute | solution.py:570
  132.1 1.2 collective-permute-start.28
  151.2 2.8 %collective-permute-start.29 = (bf16[16,256]{1,0:T(8,128)(2,1)S(1)}, bf16[16,256]{1,0:T(8,128)(2,1)S(1)}, u32[]{:S(2)}, u32[]{:S(2)}) collective-permute-start(bf16[16,256]{1,0:T(8,128)(2,1)S(1)} %shard_map.136.mine_ref), channel_id=1, source_target_pairs={{0,1},{1,0},{2,3},{3,2},{4,5},{5,4},{6,7},{7,6},{8,9},{9,8},{10,11... | collective-permute-start | bytes 24584 | tf_op jit(solution)/shard_map/ppermute | solution.py:413
  154.7 16.1 %copy-start.10 = (bf16[8,2,32,128]{3,2,1,0:T(8,128)(2,1)S(1)}, bf16[8,2,32,128]{3,2,1,0:T(8,128)(2,1)}, u32[]{:S(2)}) copy-start(bf16[8,2,32,128]{3,2,1,0:T(8,128)(2,1)} %param.18) | copy-start | bytes 393220
  154.7 8.2 %collective-permute-start.30 = (f32[16,4096]{1,0:T(8,128)S(1)}, f32[16,4096]{1,0:T(8,128)S(1)}, u32[]{:S(2)}, u32[]{:S(2)}) collective-permute-start(f32[16,4096]{1,0:T(8,128)S(1)} %get-tuple-element.112.x_ref.refs_0_), channel_id=1, source_target_pairs={{0,1},{1,0},{2,3},{3,2},{4,5},{5,4},{6,7},{7,6},{8,9},{9,8},{10,11... | collective-permute-start | bytes 786440 | tf_op jit(solution)/shard_map/ppermute | solution.py:413
  155.2 7.8 %collective-permute-start.31 = (bf16[16,4096]{1,0:T(8,128)(2,1)S(1)}, bf16[16,4096]{1,0:T(8,128)(2,1)S(1)}, u32[]{:S(2)}, u32[]{:S(2)}) collective-permute-start(bf16[16,4096]{1,0:T(8,128)(2,1)S(1)} %get-tuple-element.113), channel_id=1, source_target_pairs={{1,16},{16,1},{3,18},{18,3},{5,20},{20,5},{7,22},{22,7},{9,24},{24... | collective-permute-start | bytes 393224 | tf_op jit(solution)/shard_map/ppermute | solution.py:570
  164.2 1.4 collective-permute-start.32
  166.3 17.3 %all-to-all-start.5 = ((f32[16,8,512]{2,1,0:T(8,128)}), f32[16,8,512]{2,1,0:T(8,128)S(1)}, u32[]{:S(2)}, u32[]{:S(2)}) async-start(f32[16,8,512]{2,1,0:T(8,128)} %shard_map.139), calls=%async_computation.5 | async-start | bytes 524288 | tf_op jit(solution)/shard_map/all_to_all | solution.py:577
  171.0 15.2 %collective-permute-start.34 = (bf16[8,4096]{1,0:T(8,128)(2,1)S(1)}, bf16[8,4096]{1,0:T(8,128)(2,1)S(1)}, u32[]{:S(2)}, u32[]{:S(2)}) collective-permute-start(bf16[8,4096]{1,0:T(8,128)(2,1)S(1)} %convert_element_type.25), channel_id=1, source_target_pairs={{0,1},{1,0},{2,3},{3,2},{4,5},{5,4},{6,7},{7,6},{8,9},{9,8},{10,11... | collective-permute-start | bytes 196616 | tf_op jit(solution)/shard_map/ppermute | solution.py:413
  183.6 2.6 %collective-permute-start.33 = (bf16[16,256]{1,0:T(8,128)(2,1)S(1)}, bf16[16,256]{1,0:T(8,128)(2,1)S(1)}, u32[]{:S(2)}, u32[]{:S(2)}) collective-permute-start(bf16[16,256]{1,0:T(8,128)(2,1)S(1)} %get-tuple-element.116.mine_ref), channel_id=1, source_target_pairs={{0,1},{1,0},{2,3},{3,2},{4,5},{5,4},{6,7},{7,6},{8,9},{9,8},{10,11... | collective-permute-start | bytes 24584 | tf_op jit(solution)/shard_map/ppermute | solution.py:413
  186.3 1.6 copy-start.1
  189.3 7.0 %collective-permute-start.35 = (f32[8,4096]{1,0:T(8,128)S(1)}, f32[8,4096]{1,0:T(8,128)S(1)}, u32[]{:S(2)}, u32[]{:S(2)}) collective-permute-start(f32[8,4096]{1,0:T(8,128)S(1)} %get-tuple-element.121), channel_id=1, source_target_pairs={{0,1},{1,0},{2,3},{3,2},{4,5},{5,4},{6,7},{7,6},{8,9},{9,8},{10,11... | collective-permute-start | bytes 393224 | tf_op jit(solution)/shard_map/ppermute | solution.py:413
  189.5 20.7 %all-to-all-start.6 = ((f32[256,2,128]{2,1,0:T(2,128)}), f32[256,2,128]{2,1,0:T(2,128)S(1)}, u32[]{:S(2)}, u32[]{:S(2)}) async-start(f32[256,2,128]{2,1,0:T(2,128)} %bitcast.17), calls=%async_computation.6 | async-start | bytes 524288 | tf_op jit(solution)/shard_map/all_to_all | solution.py:602
  (4 other events, 3.9 us)

commit v3 on v2

--- a/solution.py
+++ b/solution.py
@@ -85,10 +85,14 @@
     run(copies(lambda at, n: occupied_ref.at[plan_ref[SLOT], pl.ds(at, n), 1 - core], offer_ref, sem))
 
 
-def fixed_kernel(plan_ref, occupied_ref, fixed_ref, sem):
-    core = plan_ref[DEV] % 2
+def fixed_kernel(n_orb, plan_ref, occupied_ref, fixed_ref, sem):
+    dev = plan_ref[DEV]
+    core = dev % 2
     slot = core * (occupied_ref.shape[0] - 1)
-    run(copies(lambda at, n: occupied_ref.at[slot, pl.ds(at, n), 1 - core], fixed_ref, sem))
+
+    @pl.when(jnp.logical_or(dev == 0, dev == n_orb - 1))
+    def _():
+        run(copies(lambda at, n: occupied_ref.at[slot, pl.ds(at, n), 1 - core], fixed_ref, sem))
 
 
 def pick_kernel(plan_ref, occupied_ref, offer_ref, out_ref, sem):
@@ -204,16 +208,15 @@
     chip = plan_ref[DEV] // 2
     y, x = chip % ring, chip // ring
     spare = lanes - ends_ref.shape[0] - mids_ref.shape[0]
-    for down, field_ref in zip(places, field_refs):
+    for place, field_ref in zip(places, field_refs):
         field = field_ref[...]
         got = [
             lax.dot_general(field, ref[...], NT, preferred_element_type=jnp.float32)
             for ref in (ends_ref, mids_ref)
         ]
         rows = jnp.concatenate(got + [jnp.zeros((field.shape[0], spare), jnp.float32)], axis=1) * scale
-        for k in range(rows.shape[0] // (2 * orbs)):
-            side = down[1] + k
-            to = 2 * ((x + side) % 2 * ring + (y + down[0]) % ring)
+        for k, (down, side) in enumerate(place):
+            to = 2 * ((x + side) % 2 * ring + (y + down) % ring)
             at = k * 2 * orbs
             out_ref[pl.ds(to, 1)] = rows[at : at + orbs][None]
             out_ref[pl.ds(to + 1, 1)] = rows[at + orbs : at + 2 * orbs][None]
@@ -356,14 +359,15 @@
 
 
 def finish_kernel(weights_ref, pick_ref, terms_ref, out_ref):
-    def product(one, two):
+    def product(one, two, dims):
         return lax.dot_general(
-            one, two, (((1,), (0,)), ((), ())),
+            one, two, (dims, ((), ())),
             precision=lax.Precision.HIGHEST, preferred_element_type=jnp.float32,
         )
 
     for k in range(terms_ref.shape[1]):
-        out_ref[:, k, :] = product(product(weights_ref[...], terms_ref[:, k, :]), pick_ref[...])
+        mine = product(pick_ref[...], terms_ref[:, k, :], ((1,), (1,)))
+        out_ref[k] = product(mine, weights_ref[...], ((1,), (1,)))
 
 
 def call(kernel, out_shape, in_specs=None, out_specs=None, scratch=()):
@@ -435,11 +439,10 @@
     rhs_wide, rhs_b = call(pair_kernel, (field_shape, shape((wide, cells), jnp.bfloat16)))(
         low_mask, rhs_mine, permute(rhs_other, swap_core)
     )
-    rhs_own = jnp.concatenate([rhs_b, permute(rhs_b, swap_x)], axis=0)
-    offer, rhs_own = lax.optimization_barrier((offer, rhs_own))
+    rhs_up, rhs_down = permute(rhs_b, up_y), permute(rhs_b, down_y)
 
     offer = call(pick_kernel, plane_shape, [SMEM, ANY, VMEM], VMEM, four)(plan, occupied, offer)
-    fixed = call(fixed_kernel, plane_shape, [SMEM, ANY], VMEM, four)(plan, occupied)
+    fixed = call(functools.partial(fixed_kernel, n_orb), plane_shape, [SMEM, ANY], VMEM, four)(plan, occupied)
     fixed = permute(fixed, [(0, 1), (n_orb - 1, n_orb - 2)])
     offer, fixed = lax.optimization_barrier((offer, fixed))
     pieces = call(
@@ -455,9 +458,13 @@
         pairs = [(c, 2 * s + c) for c in range(2)]
         pairs += [(n_orb - 2 + c, 2 * (ring + (ring - 1 + s) % ring) + c) for c in range(2)]
         got.append(permute(pieces[s], pairs))
-    rhs_up, rhs_down = permute(rhs_own, up_y), permute(rhs_own, down_y)
-    rhs_up, rhs_down, *got = lax.optimization_barrier((rhs_up, rhs_down, *got))
-    rhs_far_up, rhs_far_down = permute(rhs_up[:wide], up_y), permute(rhs_down[wide:], down_y)
+    rhs_up, rhs_down, got[1] = lax.optimization_barrier((rhs_up, rhs_down, got[1]))
+    rhs_line = jnp.concatenate([rhs_b, rhs_up, rhs_down], axis=0)
+    rhs_line_x = permute(rhs_line, swap_x)
+    rhs_far = jnp.concatenate(
+        [permute(rhs_up[:local_orbs], up_y), permute(rhs_down[local_orbs:], down_y)], axis=0
+    )
+    rhs_far_x = permute(rhs_far, swap_x)
     fixed = call(share_kernel, piece_shape, [SMEM] + [VMEM] * ring, VMEM)(plan, *got)
 
     def scatter(value):
@@ -496,14 +503,14 @@
     own_rows = 4 * share
     half_shape = shape((local_orbs, n_rows))
     spread_shape = shape((n_dom, local_orbs, n_rows))
-    rhs_places = ((0, 0), (ring - 1, 0), (1, 0), (2, 0), (2, 1))
+    rhs_places = [[(0, k), (ring - 1, k), (1, k)] for k in range(2)] + [[(2, k)] for k in range(2)]
     parts = call(
         functools.partial(shares_kernel, scale, rhs_places),
         shape((n_orb, local_orbs, 128)),
-        [SMEM] + [VMEM] * 7,
-    )(plan, rhs_own, rhs_up, rhs_down, rhs_far_up, rhs_far_down, xs, ys)
+        [SMEM] + [VMEM] * 6,
+    )(plan, rhs_line, rhs_line_x, rhs_far, rhs_far_x, xs, ys)
     parts = lax.all_to_all(parts, "orb", 0, 0, tiled=True)
-    xs_x, ys_up, ys_down, parts = lax.optimization_barrier((xs_x, ys_up, ys_down, parts))
+    xs_x, ys_up, ys_down = lax.optimization_barrier((xs_x, ys_up, ys_down))
     own, line = call(
         functools.partial(pack_kernel, (2, 3)),
         (shape((4 * share, cells), jnp.bfloat16), shape((6 * share, cells), jnp.bfloat16)),
@@ -513,11 +520,12 @@
     below = permute(own, down_y)
     far_up = permute(ys_up[:share], up_y)
     far_down = permute(ys_down[share:], down_y)
+    parts, _ = lax.optimization_barrier((parts, line))
     first_parts = lax.all_to_all(
         call(spread_shares_kernel, spread_shape)(parts), "dom", 0, 0, tiled=True
     )
-    line_x, above, below, far_up, far_down, first_parts = lax.optimization_barrier(
-        (line_x, above, below, far_up, far_down, first_parts)
+    line_x, above, below, far_up, far_down = lax.optimization_barrier(
+        (line_x, above, below, far_up, far_down)
     )
     far_up_x, far_down_x = permute(far_up, swap_x), permute(far_down, swap_x)
     own_up = permute(above[: 2 * share], up_y)
@@ -603,9 +611,10 @@
         raw.reshape((n_dom * n_orb,) + raw.shape[2:]), ("dom", "orb"), 0, 0, tiled=True
     )
     z_part = rows_z // n_orb
-    z_mine = o * z_part + jnp.arange(z_part)[None, :]
-    pick = (jnp.arange(rows_z)[:, None] == z_mine).astype(jnp.float32)
-    gradient = call(finish_kernel, shape((2 * n_dom, rows_y // n_dom, z_part)))(weights, pick, terms)
+    z_mine = o * z_part + jnp.arange(z_part)[:, None]
+    pick = (jnp.arange(rows_z)[None, :] == z_mine).astype(jnp.float32)
+    gradient = call(finish_kernel, shape((rows_y // n_dom, z_part, 2 * n_dom)))(weights, pick, terms)
+    gradient = jnp.transpose(gradient, (2, 0, 1))
 
     other = permute(other, swap_core)
     solution = jnp.stack([jnp.where(low, x, other), jnp.where(low, other, x)], axis=1)

time: 213 us -> 201 us (0.944)
  waiting for transfers between devices: 73.9 us -> 62.1 us
    ppermute x33 -> x34, waiting for transfers between devices: 27.1 us -> 16.9 us  [permute(): return lax.ppermute(value, 'orb', pairs)]
    all_to_all x1, waiting for transfers between devices: 4.98 us -> 0.83 us  [per_device(): parts = lax.all_to_all(parts, 'orb', 0, 0, tiled=True)]
    ppermute x33 -> x34, starting transfers between devices: 50 us -> 45.9 us  [permute(): return lax.ppermute(value, 'orb', pairs)]
    all_to_all x1, waiting for transfers between devices: 5.14 us -> 8.02 us  [per_device(): lax.all_to_all(call(spread_shares_kernel, spread_shape)(parts), 'dom', 0,...]
    unnamed x27 -> x37, local copies, waits for them, and re-layouts: 7.64 us -> 8.65 us
  transfers between devices with their start and end apart: 40 -> 41, of which waited for: 16 -> 13; matrix products, arithmetic and copies ran while one was open for 3% -> 4% of each run, Pallas kernels for 6% -> 5%
where the time goes in v3:
time: 201 us; the launch traced here: 199 us
  starting transfers between devices  79.5 us (40%)
  waiting for transfers between devices  62.1 us (31%)
  Pallas kernels  22.7 us (11%)
  blocking collectives  16.9 us (8%)
  local copies, waits for them, and re-layouts  11 us (5%)
  other arithmetic  4.82 us (2%)
    ppermute x34, starting transfers between devices, permute(): return lax.ppermute(value, 'orb', pairs)  45.9 us
    all_to_all x1, blocking collectives, per_device(): parts = lax.all_to_all(spread, 'dom', 0, 0, tiled=True)  16.9 us
    ppermute x34, waiting for transfers between devices, permute(): return lax.ppermute(value, 'orb', pairs)  16.9 us
    all_to_all x1, waiting for transfers between devices, per_device(): lax.all_to_all(raw.reshape((n_dom * n_orb,) + raw.shape[2:]), ('dom', 'or...  13.1 us
    all_to_all x1, waiting for transfers between devices, per_device(): parts = lax.all_to_all(spread, 'dom', 0, 0, tiled=True)  12.1 us
    ppermute x2, waiting for transfers between devices, per_device(): off = lax.ppermute(x_b, ('dom', 'orb'), across)  11.2 us
    all_to_all x1, starting transfers between devices, per_device(): lax.all_to_all(call(spread_shares_kernel, spread_shape)(parts), 'dom', 0,...  10.5 us
    unnamed x37, local copies, waits for them, and re-layouts  8.65 us
  transfers between devices with their start and end apart: 41, of which 13 were waited for; matrix products, arithmetic and copies ran while one was open for 4% of the time, Pallas kernels for 5%

profile of v3, /device:TPU:1, one launch (start us, length us, event | category | flops | bytes accessed | tf_op | source)
XLA Modules:
  0.0 199.1 jit_solution(4883439701497391176)
XLA Ops:
  1.3 2.9 %shard_map.121 = (s32[40]{0:T(128)S(1)}, s32[1]{0:T(128)}, bf16[128,32,128]{2,1,0:T(8,128)(2,1)}) custom-call(s32[4]{0:T(128)S(1)} %copy-done.11, s32[1]{0:T(128)} %bitcast.6.dev_ref, bf16[2,128,2,32,128]{4,3,2,1,0:T(8,128)(2,1)} %occupied_ref.7), custom_call_target="tpu_custom_call" | custom-call | tf_op jit(solution)/shard_map/pallas_call | solution.py:427
  4.2 3.3 %collective-permute-start.4 = (bf16[128,32,128]{2,1,0:T(8,128)(2,1)}, bf16[128,32,128]{2,1,0:T(8,128)(2,1)S(1)}, u32[]{:S(2)}, u32[]{:S(2)}) collective-permute-start(bf16[128,32,128]{2,1,0:T(8,128)(2,1)} %get-tuple-element.68), channel_id=1, source_target_pairs={{0,1},{1,0},{2,3},{3,2},{4,5},{5,4},{6,7},{7,6},{8,9},{9,8},{10,11... | collective-permute-start | bytes 3145736 | tf_op jit(solution)/shard_map/ppermute | solution.py:417
  7.5 1.6 shard_map.125
  9.1 1.3 collective-permute-start.5
  10.6 1.3 collective-permute-start.1
  12.7 1.2 collective-permute-done.1.other_ref
  14.0 2.7 %collective-permute-start.3 = (bf16[16,4096]{1,0:T(8,128)(2,1)S(1)}, bf16[16,4096]{1,0:T(8,128)(2,1)}, u32[]{:S(2)}, u32[]{:S(2)}) collective-permute-start(bf16[16,4096]{1,0:T(8,128)(2,1)S(1)} %get-tuple-element.67), channel_id=1, source_target_pairs={{0,6},{1,7},{2,0},{3,1},{4,2},{5,3},{6,4},{7,5},{8,14},{9,15},{10,... | collective-permute-start | bytes 393224 | tf_op jit(solution)/shard_map/ppermute | solution.py:417
  16.7 1.6 shard_map.124
  18.4 1.5 shard_map.126
  19.9 1.3 collective-permute-start.6
  21.2 1.3 collective-permute-start.11
  22.5 1.3 collective-permute-start.12
  23.8 4.0 %all-to-all-start.1 = ((bf16[8,16,32,128]{3,2,1,0:T(8,128)(2,1)}), bf16[8,16,32,128]{3,2,1,0:T(8,128)(2,1)S(1)}, u32[]{:S(2)}, u32[]{:S(2)}) async-start(bf16[8,16,32,128]{3,2,1,0:T(8,128)(2,1)} %bitcast.7), calls=%async_computation.1 | async-start | bytes 2097152 | tf_op jit(solution)/shard_map/all_to_all | solution.py:472
  27.8 1.5 collective-permute-start.8
  32.4 1.5 collective-permute-start.7
  36.2 7.3 %collective-permute-done.8 = bf16[8,4096]{1,0:T(8,128)(2,1)S(1)} collective-permute-done((bf16[8,4096]{1,0:T(8,128)(2,1)S(1)}, bf16[8,4096]{1,0:T(8,128)(2,1)S(1)}, u32[]{:S(2)}, u32[]{:S(2)}) %collective-permute-start.8) | collective-permute-done | bytes 65568 | tf_op jit(solution)/shard_map/ppermute | solution.py:417
  43.5 1.6 collective-permute-start.10
  47.0 1.7 collective-permute-start.15
  50.5 4.9 %collective-permute-start.17 = (f32[8,1]{0,1:T(1,128)S(1)}, f32[8,1]{0,1:T(1,128)S(1)}, u32[]{:S(2)}, u32[]{:S(2)}) collective-permute-start(f32[8,1]{0,1:T(1,128)S(1)} %bitcast.41), channel_id=1, source_target_pairs={{0,1},{1,0},{2,3},{3,2},{4,5},{5,4},{6,7},{7,6},{8,9},{9,8},{10,11... | collective-permute-start | bytes 104 | tf_op jit(solution)/shard_map/ppermute | solution.py:417
  55.5 2.1 %shard_map.129 = f32[16,8,128]{2,1,0:T(8,128)} custom-call(s32[40]{0:T(128)S(1)} %get-tuple-element.64.plan_ref, bf16[48,4096]{1,0:T(8,128)(2,1)S(1)} %constant_dynamic-update-slice_fusion.refs_0_, bf16[48,4096]{1,0:T(8,128)(2,1)S(1)} %collective-permute-done.7.refs_1_, bf16[16,4096]{1,0:T(8,128)(2,1)S(1)} %constant_dynamic-update-slice_fusion.3.refs_2_, ...), custom_call_target="tpu_custom_call" | custom-call | tf_op jit(solution)/shard_map/pallas_call | solution.py:507
  57.5 5.1 %all-to-all-start.2 = ((f32[16,8,128]{2,1,0:T(8,128)}), f32[16,8,128]{2,1,0:T(8,128)S(1)}, u32[]{:S(2)}, u32[]{:S(2)}) async-start(f32[16,8,128]{2,1,0:T(8,128)} %shard_map.129), calls=%async_computation.2 | async-start | bytes 131072 | tf_op jit(solution)/shard_map/all_to_all | solution.py:512
  63.5 1.4 collective-permute-start.18
  66.1 1.5 collective-permute-start.20
  69.2 10.5 %all-to-all-start.3 = ((f32[16,8,512]{2,1,0:T(8,128)}), f32[16,8,512]{2,1,0:T(8,128)S(1)}, u32[]{:S(2)}, u32[]{:S(2)}) async-start(f32[16,8,512]{2,1,0:T(8,128)} %shard_map.131), calls=%async_computation.3 | async-start | bytes 524288 | tf_op jit(solution)/shard_map/all_to_all | solution.py:524
  79.8 1.3 add_bitcast_fusion
  81.5 2.4 %collective-permute-start.22 = (bf16[16,4096]{1,0:T(8,128)(2,1)S(1)}, bf16[16,4096]{1,0:T(8,128)(2,1)S(1)}, u32[]{:S(2)}, u32[]{:S(2)}) collective-permute-start(bf16[16,4096]{1,0:T(8,128)(2,1)S(1)} %slice.27), channel_id=1, source_target_pairs={{0,6},{1,7},{2,0},{3,1},{4,2},{5,3},{6,4},{7,5},{8,14},{9,15},{10,... | collective-permute-start | bytes 393224 | tf_op jit(solution)/shard_map/ppermute | solution.py:417
  84.0 8.0 %all-to-all-done.3.parts_ref = f32[16,8,512]{2,1,0:T(8,128)S(1)} async-done(((f32[16,8,512]{2,1,0:T(8,128)}), f32[16,8,512]{2,1,0:T(8,128)S(1)}, u32[]{:S(2)}, u32[]{:S(2)}) %all-to-all-start.3) | async-done | bytes 262176 | tf_op jit(solution)/shard_map/all_to_all | solution.py:524
  92.1 2.2 %collective-permute-start.16 = (bf16[16,256]{1,0:T(8,128)(2,1)S(1)}, bf16[16,256]{1,0:T(8,128)(2,1)S(1)}, u32[]{:S(2)}, u32[]{:S(2)}) collective-permute-start(bf16[16,256]{1,0:T(8,128)(2,1)S(1)} %shard_map.132.mine_ref), channel_id=1, source_target_pairs={{0,1},{1,0},{2,3},{3,2},{4,5},{5,4},{6,7},{7,6},{8,9},{9,8},{10,11... | collective-permute-start | bytes 24584 | tf_op jit(solution)/shard_map/ppermute | solution.py:417
  94.7 2.5 %collective-permute-start.24 = (bf16[32,4096]{1,0:T(8,128)(2,1)S(1)}, bf16[32,4096]{1,0:T(8,128)(2,1)S(1)}, u32[]{:S(2)}, u32[]{:S(2)}) collective-permute-start(bf16[32,4096]{1,0:T(8,128)(2,1)S(1)} %slice.29), channel_id=1, source_target_pairs={{0,6},{1,7},{2,0},{3,1},{4,2},{5,3},{6,4},{7,5},{8,14},{9,15},{10,... | collective-permute-start | bytes 786440 | tf_op jit(solution)/shard_map/ppermute | solution.py:417
  97.2 1.5 collective-permute-start.26
  99.4 2.2 %collective-permute-done.25.refs_10_ = bf16[16,4096]{1,0:T(8,128)(2,1)S(1)} collective-permute-done((bf16[16,4096]{1,0:T(8,128)(2,1)S(1)}, bf16[16,4096]{1,0:T(8,128)(2,1)S(1)}, u32[]{:S(2)}, u32[]{:S(2)}) %collective-permute-start.25) | collective-permute-done | bytes 131104 | tf_op jit(solution)/shard_map/ppermute | solution.py:417
  101.6 2.8 %collective-permute-done.26.refs_11_ = bf16[16,4096]{1,0:T(8,128)(2,1)S(1)} collective-permute-done((bf16[16,4096]{1,0:T(8,128)(2,1)S(1)}, bf16[16,4096]{1,0:T(8,128)(2,1)S(1)}, u32[]{:S(2)}, u32[]{:S(2)}) %collective-permute-start.26) | collective-permute-done | bytes 131104 | tf_op jit(solution)/shard_map/ppermute | solution.py:417
  107.7 2.3 %shard_map.133 = (f32[16,4096]{1,0:T(8,128)S(1)}, bf16[16,4096]{1,0:T(8,128)(2,1)S(1)}, bf16[256,4096]{1,0:T(8,128)(2,1)S(1)}, bf16[256,4096]{1,0:T(8,128)(2,1)S(1)}) custom-call(f32[8,128]{1,0:T(8,128)S(1)} %broadcast_in_dim.41.low_ref, bf16[16,256]{1,0:T(8,128)(2,1)S(1)} %shard_map.132.mine_ref, bf16[16,256]{1,0:T(8,128)(2,1)S(1)} %collective-permute-done.16.other_ref, ...), custom_call_target="tpu_custom_call" | custom-call | tf_op jit(solution)/shard_map/pallas_call | solution.py:597
  110.0 1.5 collective-permute-start.27
  111.5 2.0 collective-permute-start.28
  113.5 5.8 %collective-permute-done.28.off_ref = bf16[16,4096]{1,0:T(8,128)(2,1)S(1)} collective-permute-done((bf16[16,4096]{1,0:T(8,128)(2,1)S(1)}, bf16[16,4096]{1,0:T(8,128)(2,1)S(1)}, u32[]{:S(2)}, u32[]{:S(2)}) %collective-permute-start.28) | collective-permute-done | bytes 131104 | tf_op jit(solution)/shard_map/ppermute | solution.py:578
  121.8 16.9 %all_to_all.34.parts_ref = f32[16,8,512]{2,1,0:T(8,128)S(1)} all-to-all(f32[16,8,512]{2,1,0:T(8,128)S(1)} %shard_map.135), channel_id=1, replica_groups=mesh['dom'=16,'orb'=16] {'dom'}, dimensions={0} | all-to-all | bytes 524288 | tf_op jit(solution)/shard_map/all_to_all | solution.py:585
  138.8 2.0 %collective-permute-start.30 = (bf16[16,256]{1,0:T(8,128)(2,1)S(1)}, bf16[16,256]{1,0:T(8,128)(2,1)S(1)}, u32[]{:S(2)}, u32[]{:S(2)}) collective-permute-start(bf16[16,256]{1,0:T(8,128)(2,1)S(1)} %shard_map.136.mine_ref), channel_id=1, source_target_pairs={{0,1},{1,0},{2,3},{3,2},{4,5},{5,4},{6,7},{7,6},{8,9},{9,8},{10,11... | collective-permute-start | bytes 24584 | tf_op jit(solution)/shard_map/ppermute | solution.py:417
  142.7 2.4 %collective-permute-start.32 = (bf16[16,4096]{1,0:T(8,128)(2,1)S(1)}, bf16[16,4096]{1,0:T(8,128)(2,1)S(1)}, u32[]{:S(2)}, u32[]{:S(2)}) collective-permute-start(bf16[16,4096]{1,0:T(8,128)(2,1)S(1)} %get-tuple-element.101), channel_id=1, source_target_pairs={{1,16},{16,1},{3,18},{18,3},{5,20},{20,5},{7,22},{22,7},{9,24},{24... | collective-permute-start | bytes 393224 | tf_op jit(solution)/shard_map/ppermute | solution.py:578
  145.1 5.4 %collective-permute-done.32.off_ref = bf16[16,4096]{1,0:T(8,128)(2,1)S(1)} collective-permute-done((bf16[16,4096]{1,0:T(8,128)(2,1)S(1)}, bf16[16,4096]{1,0:T(8,128)(2,1)S(1)}, u32[]{:S(2)}, u32[]{:S(2)}) %collective-permute-start.32) | collective-permute-done | bytes 131104 | tf_op jit(solution)/shard_map/ppermute | solution.py:578
  153.7 4.5 %all-to-all-start.5 = ((f32[16,8,512]{2,1,0:T(8,128)}), f32[16,8,512]{2,1,0:T(8,128)S(1)}, u32[]{:S(2)}, u32[]{:S(2)}) async-start(f32[16,8,512]{2,1,0:T(8,128)} %shard_map.139), calls=%async_computation.5 | async-start | bytes 524288 | tf_op jit(solution)/shard_map/all_to_all | solution.py:585
  158.9 12.1 %all-to-all-done.5.parts_ref = f32[16,8,512]{2,1,0:T(8,128)S(1)} async-done(((f32[16,8,512]{2,1,0:T(8,128)}), f32[16,8,512]{2,1,0:T(8,128)S(1)}, u32[]{:S(2)}, u32[]{:S(2)}) %all-to-all-start.5) | async-done | bytes 262176 | tf_op jit(solution)/shard_map/all_to_all | solution.py:585
  171.0 1.7 collective-permute-start.34
  173.7 1.6 copy-done.1
  175.2 1.4 shard_map.143
  176.9 5.3 %all-to-all-start.6 = ((f32[256,2,128]{2,1,0:T(2,128)}), f32[256,2,128]{2,1,0:T(2,128)S(1)}, u32[]{:S(2)}, u32[]{:S(2)}) async-start(f32[256,2,128]{2,1,0:T(2,128)} %bitcast.17), calls=%async_computation.6 | async-start | bytes 524288 | tf_op jit(solution)/shard_map/all_to_all | solution.py:610
  184.5 13.1 %all-to-all-done.6.terms_ref = f32[256,2,128]{2,1,0:T(2,128)S(1)} async-done(((f32[256,2,128]{2,1,0:T(2,128)}), f32[256,2,128]{2,1,0:T(2,128)S(1)}, u32[]{:S(2)}, u32[]{:S(2)}) %all-to-all-start.6) | async-done | bytes 262176 | tf_op jit(solution)/shard_map/all_to_all | solution.py:610
  197.6 1.5 shard_map.145
  (130 shorter events, 30.5 us)
Async XLA Ops:
  4.2 12.5 %collective-permute-start.4 = (bf16[128,32,128]{2,1,0:T(8,128)(2,1)}, bf16[128,32,128]{2,1,0:T(8,128)(2,1)S(1)}, u32[]{:S(2)}, u32[]{:S(2)}) collective-permute-start(bf16[128,32,128]{2,1,0:T(8,128)(2,1)} %get-tuple-element.68), channel_id=1, source_target_pairs={{0,1},{1,0},{2,3},{3,2},{4,5},{5,4},{6,7},{7,6},{8,9},{9,8},{10,11... | collective-permute-start | bytes 3145736 | tf_op jit(solution)/shard_map/ppermute | solution.py:417
  9.1 9.3 %collective-permute-start.5 = (bf16[128,32,128]{2,1,0:T(8,128)(2,1)}, bf16[128,32,128]{2,1,0:T(8,128)(2,1)S(1)}, u32[]{:S(2)}, u32[]{:S(2)}) collective-permute-start(bf16[128,32,128]{2,1,0:T(8,128)(2,1)} %shard_map.125), channel_id=1, source_target_pairs={{0,1},{15,14},{16,17},{31,30},{32,33},{47,46},{48,49},{63,62},{64,... | collective-permute-start | bytes 3145736 | tf_op jit(solution)/shard_map/ppermute | solution.py:417
  10.6 3.3 %collective-permute-start.1 = (f32[8,4096]{1,0:T(8,128)S(1)}, f32[8,4096]{1,0:T(8,128)S(1)}, u32[]{:S(2)}, u32[]{:S(2)}) collective-permute-start(f32[8,4096]{1,0:T(8,128)S(1)} %get-tuple-element.66), channel_id=1, source_target_pairs={{0,1},{1,0},{2,3},{3,2},{4,5},{5,4},{6,7},{7,6},{8,9},{9,8},{10,11... | collective-permute-start | bytes 393224 | tf_op jit(solution)/shard_map/ppermute | solution.py:417
  13.9 13.9 %collective-permute-start.2 = (bf16[16,4096]{1,0:T(8,128)(2,1)S(1)}, bf16[16,4096]{1,0:T(8,128)(2,1)S(1)}, u32[]{:S(2)}, u32[]{:S(2)}) collective-permute-start(bf16[16,4096]{1,0:T(8,128)(2,1)S(1)} %get-tuple-element.67), channel_id=1, source_target_pairs={{0,2},{1,3},{2,4},{3,5},{4,6},{5,7},{6,0},{7,1},{8,10},{9,11},{10,... | collective-permute-start | bytes 393224 | tf_op jit(solution)/shard_map/ppermute | solution.py:417
  14.0 13.8 %collective-permute-start.3 = (bf16[16,4096]{1,0:T(8,128)(2,1)S(1)}, bf16[16,4096]{1,0:T(8,128)(2,1)}, u32[]{:S(2)}, u32[]{:S(2)}) collective-permute-start(bf16[16,4096]{1,0:T(8,128)(2,1)S(1)} %get-tuple-element.67), channel_id=1, source_target_pairs={{0,6},{1,7},{2,0},{3,1},{4,2},{5,3},{6,4},{7,5},{8,14},{9,15},{10,... | collective-permute-start | bytes 393224 | tf_op jit(solution)/shard_map/ppermute | solution.py:417
  19.8 28.9 %copy-start.15 = (s32[16]{0:T(128)S(1)}, s32[16]{0:T(128)}, u32[]{:S(2)}) copy-start(s32[16]{0:T(128)} %constant.135.clone) | copy-start | bytes 196
  19.9 29.7 %copy-start.14 = (s32[8]{0:T(128)S(1)}, s32[8]{0:T(128)}, u32[]{:S(2)}) copy-start(s32[8]{0:T(128)} %param.15) | copy-start | bytes 100
  19.9 8.0 %collective-permute-start.6 = (bf16[32,32,128]{2,1,0:T(8,128)(2,1)S(1)}, bf16[32,32,128]{2,1,0:T(8,128)(2,1)S(1)}, u32[]{:S(2)}, u32[]{:S(2)}) collective-permute-start(bf16[32,32,128]{2,1,0:T(8,128)(2,1)S(1)} %get-tuple-element.70), channel_id=1, source_target_pairs={{0,2},{1,3},{14,8},{15,9},{16,18},{17,19},{30,24},{31,25},{32,34},... | collective-permute-start | bytes 786440 | tf_op jit(solution)/shard_map/ppermute | solution.py:417
  21.2 12.7 %collective-permute-start.11 = (bf16[32,32,128]{2,1,0:T(8,128)(2,1)}, bf16[32,32,128]{2,1,0:T(8,128)(2,1)S(1)}, u32[]{:S(2)}, u32[]{:S(2)}) collective-permute-start(bf16[32,32,128]{2,1,0:T(8,128)(2,1)} %get-tuple-element.75), channel_id=1, source_target_pairs={{0,4},{1,5},{14,10},{15,11},{16,20},{17,21},{30,26},{31,27},{32,36... | collective-permute-start | bytes 786440 | tf_op jit(solution)/shard_map/ppermute | solution.py:417
  22.5 11.4 %collective-permute-start.12 = (bf16[32,32,128]{2,1,0:T(8,128)(2,1)}, bf16[32,32,128]{2,1,0:T(8,128)(2,1)S(1)}, u32[]{:S(2)}, u32[]{:S(2)}) collective-permute-start(bf16[32,32,128]{2,1,0:T(8,128)(2,1)} %get-tuple-element.76), channel_id=1, source_target_pairs={{0,6},{1,7},{14,12},{15,13},{16,22},{17,23},{30,28},{31,29},{32,38... | collective-permute-start | bytes 786440 | tf_op jit(solution)/shard_map/ppermute | solution.py:417
  23.8 21.3 %all-to-all-start.1 = ((bf16[8,16,32,128]{3,2,1,0:T(8,128)(2,1)}), bf16[8,16,32,128]{3,2,1,0:T(8,128)(2,1)S(1)}, u32[]{:S(2)}, u32[]{:S(2)}) async-start(bf16[8,16,32,128]{3,2,1,0:T(8,128)(2,1)} %bitcast.7), calls=%async_computation.1 | async-start | bytes 2097152 | tf_op jit(solution)/shard_map/all_to_all | solution.py:472
  27.8 15.7 %collective-permute-start.8 = (bf16[8,4096]{1,0:T(8,128)(2,1)S(1)}, bf16[8,4096]{1,0:T(8,128)(2,1)S(1)}, u32[]{:S(2)}, u32[]{:S(2)}) collective-permute-start(bf16[8,4096]{1,0:T(8,128)(2,1)S(1)} %slice.24), channel_id=1, source_target_pairs={{0,2},{1,3},{2,4},{3,5},{4,6},{5,7},{6,0},{7,1},{8,10},{9,11},{10,... | collective-permute-start | bytes 196616 | tf_op jit(solution)/shard_map/ppermute | solution.py:417
  30.2 13.3 %collective-permute-start.9 = (bf16[8,4096]{1,0:T(8,128)(2,1)S(1)}, bf16[8,4096]{1,0:T(8,128)(2,1)S(1)}, u32[]{:S(2)}, u32[]{:S(2)}) collective-permute-start(bf16[8,4096]{1,0:T(8,128)(2,1)S(1)} %slice.25), channel_id=1, source_target_pairs={{0,6},{1,7},{2,0},{3,1},{4,2},{5,3},{6,4},{7,5},{8,14},{9,15},{10,... | collective-permute-start | bytes 196616 | tf_op jit(solution)/shard_map/ppermute | solution.py:417
  32.4 23.1 %collective-permute-start.7 = (bf16[48,4096]{1,0:T(8,128)(2,1)S(1)}, bf16[48,4096]{1,0:T(8,128)(2,1)S(1)}, u32[]{:S(2)}, u32[]{:S(2)}) collective-permute-start(bf16[48,4096]{1,0:T(8,128)(2,1)S(1)} %constant_dynamic-update-slice_fusion.refs_0_), channel_id=1, source_target_pairs={{0,8},{1,9},{2,10},{3,11},{4,12},{5,13},{6,14},{7,15},{8,0},{9,1},... | collective-permute-start | bytes 1179656 | tf_op jit(solution)/shard_map/ppermute | solution.py:417
  43.5 7.0 %collective-permute-start.10 = (bf16[16,4096]{1,0:T(8,128)(2,1)S(1)}, bf16[16,4096]{1,0:T(8,128)(2,1)S(1)}, u32[]{:S(2)}, u32[]{:S(2)}) collective-permute-start(bf16[16,4096]{1,0:T(8,128)(2,1)S(1)} %constant_dynamic-update-slice_fusion.3.refs_2_), channel_id=1, source_target_pairs={{0,8},{1,9},{2,10},{3,11},{4,12},{5,13},{6,14},{7,15},{8,0},{9,1},... | collective-permute-start | bytes 393224 | tf_op jit(solution)/shard_map/ppermute | solution.py:417
  45.9 16.7 %collective-permute-start.14 = (bf16[32,4096]{1,0:T(8,128)(2,1)S(1)}, bf16[32,4096]{1,0:T(8,128)(2,1)S(1)}, u32[]{:S(2)}, u32[]{:S(2)}) collective-permute-start(bf16[32,4096]{1,0:T(8,128)(2,1)S(1)} %get-tuple-element.80.refs_5_.refs_2_), channel_id=1, source_target_pairs={{0,2},{1,3},{2,4},{3,5},{4,6},{5,7},{6,0},{7,1},{8,10},{9,11},{10,... | collective-permute-start | bytes 786440 | tf_op jit(solution)/shard_map/ppermute | solution.py:417
  47.0 15.6 %collective-permute-start.15 = (bf16[32,4096]{1,0:T(8,128)(2,1)S(1)}, bf16[32,4096]{1,0:T(8,128)(2,1)S(1)}, u32[]{:S(2)}, u32[]{:S(2)}) collective-permute-start(bf16[32,4096]{1,0:T(8,128)(2,1)S(1)} %get-tuple-element.80.refs_5_.refs_2_), channel_id=1, source_target_pairs={{0,6},{1,7},{2,0},{3,1},{4,2},{5,3},{6,4},{7,5},{8,14},{9,15},{10,... | collective-permute-start | bytes 786440 | tf_op jit(solution)/shard_map/ppermute | solution.py:417
  48.7 13.9 %collective-permute-start.13 = (bf16[32,4096]{1,0:T(8,128)(2,1)S(1)}, bf16[32,4096]{1,0:T(8,128)(2,1)S(1)}, u32[]{:S(2)}, u32[]{:S(2)}) collective-permute-start(bf16[32,4096]{1,0:T(8,128)(2,1)S(1)} %get-tuple-element.79.refs_4_.refs_0_), channel_id=1, source_target_pairs={{0,8},{1,9},{2,10},{3,11},{4,12},{5,13},{6,14},{7,15},{8,0},{9,1},... | collective-permute-start | bytes 786440 | tf_op jit(solution)/shard_map/ppermute | solution.py:417
  50.5 31.0 %collective-permute-start.17 = (f32[8,1]{0,1:T(1,128)S(1)}, f32[8,1]{0,1:T(1,128)S(1)}, u32[]{:S(2)}, u32[]{:S(2)}) collective-permute-start(f32[8,1]{0,1:T(1,128)S(1)} %bitcast.41), channel_id=1, source_target_pairs={{0,1},{1,0},{2,3},{3,2},{4,5},{5,4},{6,7},{7,6},{8,9},{9,8},{10,11... | collective-permute-start | bytes 104 | tf_op jit(solution)/shard_map/ppermute | solution.py:417
  57.5 10.9 %all-to-all-start.2 = ((f32[16,8,128]{2,1,0:T(8,128)}), f32[16,8,128]{2,1,0:T(8,128)S(1)}, u32[]{:S(2)}, u32[]{:S(2)}) async-start(f32[16,8,128]{2,1,0:T(8,128)} %shard_map.129), calls=%async_computation.2 | async-start | bytes 131072 | tf_op jit(solution)/shard_map/all_to_all | solution.py:512
  63.5 40.9 %copy-start.6 = (bf16[96,4096]{1,0:T(8,128)(2,1)}, bf16[96,4096]{1,0:T(8,128)(2,1)S(1)}, u32[]{:S(2)}) copy-start(bf16[96,4096]{1,0:T(8,128)(2,1)S(1)} %get-tuple-element.84.refs_6_) | copy-start | bytes 2359300
  63.5 30.8 %collective-permute-start.18 = (bf16[96,4096]{1,0:T(8,128)(2,1)S(1)}, bf16[96,4096]{1,0:T(8,128)(2,1)}, u32[]{:S(2)}, u32[]{:S(2)}) collective-permute-start(bf16[96,4096]{1,0:T(8,128)(2,1)S(1)} %get-tuple-element.84.refs_6_), channel_id=1, source_target_pairs={{0,8},{1,9},{2,10},{3,11},{4,12},{5,13},{6,14},{7,15},{8,0},{9,1},... | collective-permute-start | bytes 2359304 | tf_op jit(solution)/shard_map/ppermute | solution.py:417
  64.9 29.3 %collective-permute-start.19 = (bf16[64,4096]{1,0:T(8,128)(2,1)}, bf16[64,4096]{1,0:T(8,128)(2,1)S(1)}, u32[]{:S(2)}, u32[]{:S(2)}) collective-permute-start(bf16[64,4096]{1,0:T(8,128)(2,1)} %get-tuple-element.87.refs_1_), channel_id=1, source_target_pairs={{0,2},{1,3},{2,4},{3,5},{4,6},{5,7},{6,0},{7,1},{8,10},{9,11},{10,... | collective-permute-start | bytes 1572872 | tf_op jit(solution)/shard_map/ppermute | solution.py:417
  66.1 28.2 %collective-permute-start.20 = (bf16[64,4096]{1,0:T(8,128)(2,1)}, bf16[64,4096]{1,0:T(8,128)(2,1)S(1)}, u32[]{:S(2)}, u32[]{:S(2)}) collective-permute-start(bf16[64,4096]{1,0:T(8,128)(2,1)} %get-tuple-element.87.refs_1_), channel_id=1, source_target_pairs={{0,6},{1,7},{2,0},{3,1},{4,2},{5,3},{6,4},{7,5},{8,14},{9,15},{10,... | collective-permute-start | bytes 1572872 | tf_op jit(solution)/shard_map/ppermute | solution.py:417
  69.2 22.8 %all-to-all-start.3 = ((f32[16,8,512]{2,1,0:T(8,128)}), f32[16,8,512]{2,1,0:T(8,128)S(1)}, u32[]{:S(2)}, u32[]{:S(2)}) async-start(f32[16,8,512]{2,1,0:T(8,128)} %shard_map.131), calls=%async_computation.3 | async-start | bytes 524288 | tf_op jit(solution)/shard_map/all_to_all | solution.py:524
  81.2 10.9 %collective-permute-start.21 = (bf16[16,4096]{1,0:T(8,128)(2,1)S(1)}, bf16[16,4096]{1,0:T(8,128)(2,1)S(1)}, u32[]{:S(2)}, u32[]{:S(2)}) collective-permute-start(bf16[16,4096]{1,0:T(8,128)(2,1)S(1)} %slice.26), channel_id=1, source_target_pairs={{0,2},{1,3},{2,4},{3,5},{4,6},{5,7},{6,0},{7,1},{8,10},{9,11},{10,... | collective-permute-start | bytes 393224 | tf_op jit(solution)/shard_map/ppermute | solution.py:417
  81.5 12.7 %collective-permute-start.22 = (bf16[16,4096]{1,0:T(8,128)(2,1)S(1)}, bf16[16,4096]{1,0:T(8,128)(2,1)S(1)}, u32[]{:S(2)}, u32[]{:S(2)}) collective-permute-start(bf16[16,4096]{1,0:T(8,128)(2,1)S(1)} %slice.27), channel_id=1, source_target_pairs={{0,6},{1,7},{2,0},{3,1},{4,2},{5,3},{6,4},{7,5},{8,14},{9,15},{10,... | collective-permute-start | bytes 393224 | tf_op jit(solution)/shard_map/ppermute | solution.py:417
  92.1 7.4 %collective-permute-start.16 = (bf16[16,256]{1,0:T(8,128)(2,1)S(1)}, bf16[16,256]{1,0:T(8,128)(2,1)S(1)}, u32[]{:S(2)}, u32[]{:S(2)}) collective-permute-start(bf16[16,256]{1,0:T(8,128)(2,1)S(1)} %shard_map.132.mine_ref), channel_id=1, source_target_pairs={{0,1},{1,0},{2,3},{3,2},{4,5},{5,4},{6,7},{7,6},{8,9},{9,8},{10,11... | collective-permute-start | bytes 24584 | tf_op jit(solution)/shard_map/ppermute | solution.py:417
  94.2 10.2 %copy-start.2 = (bf16[64,4096]{1,0:T(8,128)(2,1)}, bf16[64,4096]{1,0:T(8,128)(2,1)S(1)}, u32[]{:S(2)}) copy-start(bf16[64,4096]{1,0:T(8,128)(2,1)S(1)} %collective-permute-done.19.refs_3_) | copy-start | bytes 1572868
  94.2 10.2 %copy-start.4 = (bf16[64,4096]{1,0:T(8,128)(2,1)}, bf16[64,4096]{1,0:T(8,128)(2,1)S(1)}, u32[]{:S(2)}) copy-start(bf16[64,4096]{1,0:T(8,128)(2,1)S(1)} %collective-permute-done.20.refs_2_) | copy-start | bytes 1572868
  94.3 10.1 %collective-permute-start.23 = (bf16[32,4096]{1,0:T(8,128)(2,1)S(1)}, bf16[32,4096]{1,0:T(8,128)(2,1)S(1)}, u32[]{:S(2)}, u32[]{:S(2)}) collective-permute-start(bf16[32,4096]{1,0:T(8,128)(2,1)S(1)} %slice.28), channel_id=1, source_target_pairs={{0,2},{1,3},{2,4},{3,5},{4,6},{5,7},{6,0},{7,1},{8,10},{9,11},{10,... | collective-permute-start | bytes 786440 | tf_op jit(solution)/shard_map/ppermute | solution.py:417
  94.7 9.7 %collective-permute-start.24 = (bf16[32,4096]{1,0:T(8,128)(2,1)S(1)}, bf16[32,4096]{1,0:T(8,128)(2,1)S(1)}, u32[]{:S(2)}, u32[]{:S(2)}) collective-permute-start(bf16[32,4096]{1,0:T(8,128)(2,1)S(1)} %slice.29), channel_id=1, source_target_pairs={{0,6},{1,7},{2,0},{3,1},{4,2},{5,3},{6,4},{7,5},{8,14},{9,15},{10,... | collective-permute-start | bytes 786440 | tf_op jit(solution)/shard_map/ppermute | solution.py:417
  97.1 4.5 %collective-permute-start.25 = (bf16[16,4096]{1,0:T(8,128)(2,1)S(1)}, bf16[16,4096]{1,0:T(8,128)(2,1)S(1)}, u32[]{:S(2)}, u32[]{:S(2)}) collective-permute-start(bf16[16,4096]{1,0:T(8,128)(2,1)S(1)} %collective-permute-done.21.refs_8_), channel_id=1, source_target_pairs={{0,8},{1,9},{2,10},{3,11},{4,12},{5,13},{6,14},{7,15},{8,0},{9,1},... | collective-permute-start | bytes 393224 | tf_op jit(solution)/shard_map/ppermute | solution.py:417
  97.2 7.3 %collective-permute-start.26 = (bf16[16,4096]{1,0:T(8,128)(2,1)S(1)}, bf16[16,4096]{1,0:T(8,128)(2,1)S(1)}, u32[]{:S(2)}, u32[]{:S(2)}) collective-permute-start(bf16[16,4096]{1,0:T(8,128)(2,1)S(1)} %collective-permute-done.22.refs_9_), channel_id=1, source_target_pairs={{0,8},{1,9},{2,10},{3,11},{4,12},{5,13},{6,14},{7,15},{8,0},{9,1},... | collective-permute-start | bytes 393224 | tf_op jit(solution)/shard_map/ppermute | solution.py:417
  110.0 40.5 %copy-start = (bf16[256,4096]{1,0:T(8,128)(2,1)}, bf16[256,4096]{1,0:T(8,128)(2,1)S(1)}, u32[]{:S(2)}) copy-start(bf16[256,4096]{1,0:T(8,128)(2,1)S(1)} %get-tuple-element.96.second_ref.refs_2_.refs_3_) | copy-start | bytes 6291460
  110.0 9.3 %collective-permute-start.27 = (f32[16,4096]{1,0:T(8,128)S(1)}, f32[16,4096]{1,0:T(8,128)S(1)}, u32[]{:S(2)}, u32[]{:S(2)}) collective-permute-start(f32[16,4096]{1,0:T(8,128)S(1)} %get-tuple-element.93.x_ref.refs_0_), channel_id=1, source_target_pairs={{0,1},{1,0},{2,3},{3,2},{4,5},{5,4},{6,7},{7,6},{8,9},{9,8},{10,11... | collective-permute-start | bytes 786440 | tf_op jit(solution)/shard_map/ppermute | solution.py:417
  111.5 7.8 %collective-permute-start.28 = (bf16[16,4096]{1,0:T(8,128)(2,1)S(1)}, bf16[16,4096]{1,0:T(8,128)(2,1)S(1)}, u32[]{:S(2)}, u32[]{:S(2)}) collective-permute-start(bf16[16,4096]{1,0:T(8,128)(2,1)S(1)} %get-tuple-element.94), channel_id=1, source_target_pairs={{1,16},{16,1},{3,18},{18,3},{5,20},{20,5},{7,22},{22,7},{9,24},{24... | collective-permute-start | bytes 393224 | tf_op jit(solution)/shard_map/ppermute | solution.py:578
  120.5 1.2 collective-permute-start.29
  138.8 2.8 %collective-permute-start.30 = (bf16[16,256]{1,0:T(8,128)(2,1)S(1)}, bf16[16,256]{1,0:T(8,128)(2,1)S(1)}, u32[]{:S(2)}, u32[]{:S(2)}) collective-permute-start(bf16[16,256]{1,0:T(8,128)(2,1)S(1)} %shard_map.136.mine_ref), channel_id=1, source_target_pairs={{0,1},{1,0},{2,3},{3,2},{4,5},{5,4},{6,7},{7,6},{8,9},{9,8},{10,11... | collective-permute-start | bytes 24584 | tf_op jit(solution)/shard_map/ppermute | solution.py:417
  142.3 15.9 %copy-start.13 = (bf16[8,2,32,128]{3,2,1,0:T(8,128)(2,1)S(1)}, bf16[8,2,32,128]{3,2,1,0:T(8,128)(2,1)}, u32[]{:S(2)}) copy-start(bf16[8,2,32,128]{3,2,1,0:T(8,128)(2,1)} %param.18) | copy-start | bytes 393220
  142.3 8.2 %collective-permute-start.31 = (f32[16,4096]{1,0:T(8,128)S(1)}, f32[16,4096]{1,0:T(8,128)S(1)}, u32[]{:S(2)}, u32[]{:S(2)}) collective-permute-start(f32[16,4096]{1,0:T(8,128)S(1)} %get-tuple-element.100.x_ref.refs_0_), channel_id=1, source_target_pairs={{0,1},{1,0},{2,3},{3,2},{4,5},{5,4},{6,7},{7,6},{8,9},{9,8},{10,11... | collective-permute-start | bytes 786440 | tf_op jit(solution)/shard_map/ppermute | solution.py:417
  142.7 7.8 %collective-permute-start.32 = (bf16[16,4096]{1,0:T(8,128)(2,1)S(1)}, bf16[16,4096]{1,0:T(8,128)(2,1)S(1)}, u32[]{:S(2)}, u32[]{:S(2)}) collective-permute-start(bf16[16,4096]{1,0:T(8,128)(2,1)S(1)} %get-tuple-element.101), channel_id=1, source_target_pairs={{1,16},{16,1},{3,18},{18,3},{5,20},{20,5},{7,22},{22,7},{9,24},{24... | collective-permute-start | bytes 393224 | tf_op jit(solution)/shard_map/ppermute | solution.py:578
  151.7 1.2 collective-permute-start.33
  153.7 17.3 %all-to-all-start.5 = ((f32[16,8,512]{2,1,0:T(8,128)}), f32[16,8,512]{2,1,0:T(8,128)S(1)}, u32[]{:S(2)}, u32[]{:S(2)}) async-start(f32[16,8,512]{2,1,0:T(8,128)} %shard_map.139), calls=%async_computation.5 | async-start | bytes 524288 | tf_op jit(solution)/shard_map/all_to_all | solution.py:585
  158.4 15.2 %collective-permute-start.35 = (bf16[8,4096]{1,0:T(8,128)(2,1)S(1)}, bf16[8,4096]{1,0:T(8,128)(2,1)S(1)}, u32[]{:S(2)}, u32[]{:S(2)}) collective-permute-start(bf16[8,4096]{1,0:T(8,128)(2,1)S(1)} %convert_element_type.25), channel_id=1, source_target_pairs={{0,1},{1,0},{2,3},{3,2},{4,5},{5,4},{6,7},{7,6},{8,9},{9,8},{10,11... | collective-permute-start | bytes 196616 | tf_op jit(solution)/shard_map/ppermute | solution.py:417
  171.0 2.6 %collective-permute-start.34 = (bf16[16,256]{1,0:T(8,128)(2,1)S(1)}, bf16[16,256]{1,0:T(8,128)(2,1)S(1)}, u32[]{:S(2)}, u32[]{:S(2)}) collective-permute-start(bf16[16,256]{1,0:T(8,128)(2,1)S(1)} %get-tuple-element.104.mine_ref), channel_id=1, source_target_pairs={{0,1},{1,0},{2,3},{3,2},{4,5},{5,4},{6,7},{7,6},{8,9},{9,8},{10,11... | collective-permute-start | bytes 24584 | tf_op jit(solution)/shard_map/ppermute | solution.py:417
  176.7 7.0 %collective-permute-start.36 = (f32[8,4096]{1,0:T(8,128)S(1)}, f32[8,4096]{1,0:T(8,128)S(1)}, u32[]{:S(2)}, u32[]{:S(2)}) collective-permute-start(f32[8,4096]{1,0:T(8,128)S(1)} %get-tuple-element.109), channel_id=1, source_target_pairs={{0,1},{1,0},{2,3},{3,2},{4,5},{5,4},{6,7},{7,6},{8,9},{9,8},{10,11... | collective-permute-start | bytes 393224 | tf_op jit(solution)/shard_map/ppermute | solution.py:417
  176.9 20.7 %all-to-all-start.6 = ((f32[256,2,128]{2,1,0:T(2,128)}), f32[256,2,128]{2,1,0:T(2,128)S(1)}, u32[]{:S(2)}, u32[]{:S(2)}) async-start(f32[256,2,128]{2,1,0:T(2,128)} %bitcast.17), calls=%async_computation.6 | async-start | bytes 524288 | tf_op jit(solution)/shard_map/all_to_all | solution.py:610
  (9 other events, 22.0 us)

commit v4 on v3

--- a/solution.py
+++ b/solution.py
@@ -78,21 +78,21 @@
         copy.wait()
 
 
-def offer_kernel(per_dev, n_orb, ids_ref, dev_ref, occupied_ref, plan_ref, same_ref, offer_ref, sem):
+def offer_kernel(per_dev, n_orb, ids_ref, dev_ref, occupied_ref, *refs):
+    plan_ref, same_ref, offer_ref, fixed_ref, sem, fixed_sem = refs
     plan(per_dev, n_orb, ids_ref, dev_ref, plan_ref)
     same_ref[0] = plan_ref[SAME]
-    core = plan_ref[DEV] % 2
-    run(copies(lambda at, n: occupied_ref.at[plan_ref[SLOT], pl.ds(at, n), 1 - core], offer_ref, sem))
-
-
-def fixed_kernel(n_orb, plan_ref, occupied_ref, fixed_ref, sem):
     dev = plan_ref[DEV]
     core = dev % 2
-    slot = core * (occupied_ref.shape[0] - 1)
+
+    def plane(slot):
+        return lambda at, n: occupied_ref.at[slot, pl.ds(at, n), 1 - core]
 
     @pl.when(jnp.logical_or(dev == 0, dev == n_orb - 1))
     def _():
-        run(copies(lambda at, n: occupied_ref.at[slot, pl.ds(at, n), 1 - core], fixed_ref, sem))
+        run(copies(plane(core * (occupied_ref.shape[0] - 1)), fixed_ref, fixed_sem))
+
+    run(copies(plane(plan_ref[SLOT]), offer_ref, sem))
 
 
 def pick_kernel(plan_ref, occupied_ref, offer_ref, out_ref, sem):
@@ -289,30 +289,12 @@
         pieces = pieces[count:]
 
 
-def packed(splits, *refs):
-    *refs, sem = refs
-    pieces, outs = refs[: sum(splits)], refs[sum(splits) :]
-    moves = []
-    for count, out_ref in zip(splits, outs):
-        at = 0
-        for ref in pieces[:count]:
-            rows = ref.shape[0]
-            moves.append(pltpu.make_async_copy(ref, out_ref.at[pl.ds(at, rows)], sem.at[len(moves)]))
-            at += rows
-        pieces = pieces[count:]
-    return moves
-
-
-def update_kernel(scale, tile, has_x, last, root, splits, low_ref, mine_ref, other_ref, resid_ref, diag_ref, *refs):
+def update_kernel(scale, tile, has_x, last, root, low_ref, mine_ref, other_ref, resid_ref, diag_ref, *refs):
     refs = list(refs)
     x_ref = refs.pop(0) if has_x else None
     move_ref = None if has_x else refs.pop(0)
     psi_ref = refs.pop(0) if last else None
-    if has_x:
-        first_ref, second_ref, *outs = refs
-    else:
-        *refs, x_out, x_b_out, first_ref, second_ref, sem = refs
-        outs = [x_out, x_b_out]
+    first_ref, second_ref, *outs = refs
     low = core_mask(low_ref, 2 * mine_ref.shape[1])
     mine = unstacked(mine_ref[...].astype(jnp.float32))
     other = unstacked(other_ref[...].astype(jnp.float32))
@@ -320,7 +302,6 @@
     coeff = coeff.astype(jnp.bfloat16)
     if not has_x:
         coeff = jnp.dot(coeff, move_ref[...], preferred_element_type=jnp.float32).astype(jnp.bfloat16)
-        run(packed(splits, *refs, first_ref, second_ref, sem))
     cells = resid_ref.shape[1]
     for at in range(0, cells, tile):
         here = slice(at, at + tile)
@@ -424,12 +405,12 @@
 
     plane_shape = shape((blk_rows, rows_y, rows_z), jnp.bfloat16)
     piece_shape = shape((2 * share, rows_y, rows_z), jnp.bfloat16)
-    plan, same, offer = call(
+    plan, same, offer, fixed = call(
         functools.partial(offer_kernel, per_dev, n_orb),
-        (shape((TABLE + nproj * chips,), jnp.int32), shape((1,), jnp.int32), plane_shape),
+        (shape((TABLE + nproj * chips,), jnp.int32), shape((1,), jnp.int32), plane_shape, plane_shape),
         [SMEM, SMEM, ANY],
-        (SMEM, SMEM, VMEM),
-        four,
+        (SMEM, SMEM, VMEM, VMEM),
+        four * 2,
     )(block_ids, o.astype(jnp.int32).reshape(1), occupied)
     offer = permute(offer, swap_core)
 
@@ -442,7 +423,6 @@
     rhs_up, rhs_down = permute(rhs_b, up_y), permute(rhs_b, down_y)
 
     offer = call(pick_kernel, plane_shape, [SMEM, ANY, VMEM], VMEM, four)(plan, occupied, offer)
-    fixed = call(functools.partial(fixed_kernel, n_orb), plane_shape, [SMEM, ANY], VMEM, four)(plan, occupied)
     fixed = permute(fixed, [(0, 1), (n_orb - 1, n_orb - 2)])
     offer, fixed = lax.optimization_barrier((offer, fixed))
     pieces = call(
@@ -498,6 +478,7 @@
     ys = mids.reshape(2 * share, cells)
     xs, ys = lax.optimization_barrier((xs, ys))
     xs_x = permute(xs, swap_x)
+    ys_x = permute(ys, swap_x)
     ys_up = permute(ys, up_y)
     ys_down = permute(ys, down_y)
     own_rows = 4 * share
@@ -510,11 +491,10 @@
         [SMEM] + [VMEM] * 6,
     )(plan, rhs_line, rhs_line_x, rhs_far, rhs_far_x, xs, ys)
     parts = lax.all_to_all(parts, "orb", 0, 0, tiled=True)
-    xs_x, ys_up, ys_down = lax.optimization_barrier((xs_x, ys_up, ys_down))
+    xs_x, ys_x, ys_up, ys_down = lax.optimization_barrier((xs_x, ys_x, ys_up, ys_down))
     own, line = call(
-        functools.partial(pack_kernel, (2, 3)),
-        (shape((4 * share, cells), jnp.bfloat16), shape((6 * share, cells), jnp.bfloat16)),
-    )(xs, xs_x, ys, ys_up, ys_down)
+        functools.partial(pack_kernel, (2, 2)), (shape((4 * share, cells), jnp.bfloat16),) * 2
+    )(xs, xs_x, ys_up, ys_down)
     line_x = permute(line, swap_x)
     above = permute(own, up_y)
     below = permute(own, down_y)
@@ -530,9 +510,17 @@
     far_up_x, far_down_x = permute(far_up, swap_x), permute(far_down, swap_x)
     own_up = permute(above[: 2 * share], up_y)
     own_down = permute(below[2 * share :], down_y)
-    pieces = [own, below, above, own_up, own_down]
-    pieces += [line, line_x, far_up, far_down, far_up_x, far_down_x]
-    blocks_shape = [shape((n_rows // 2, cells), jnp.bfloat16)] * 2
+    block_shape = shape((n_rows // 2, cells), jnp.bfloat16)
+    blocks = call(functools.partial(pack_kernel, (3, 5)), [block_shape] * 2)(
+        own, below, above, ys, line, ys_x, line_x, jnp.concatenate([far_up, far_down], axis=0)
+    )
+    blocks = list(blocks)
+    late = ((own_up, own_down), (far_up_x, far_down_x))
+    for k, pair_of in enumerate(late):
+        at = n_rows // 2 - sum(piece.shape[0] for piece in pair_of)
+        for piece in pair_of:
+            blocks[k] = lax.dynamic_update_slice(blocks[k], piece, (at, 0))
+            at += piece.shape[0]
 
     picks = win_index[:, None] == jnp.arange(n_occ, dtype=jnp.int32)[None, :]
     eps = jnp.sum(jnp.where(picks, eigen_table[None, :], 0.0), axis=1)[:, None]
@@ -588,20 +576,9 @@
         outs = [field_shape, shape((wide, cells), jnp.bfloat16)]
         if final:
             outs = [shape((local_orbs, cells))] * 2 + [shape((n_dom, n_orb, rows_y // n_dom, rows_z))]
-        if step == 0:
-            outs, blocks = outs + blocks_shape, pieces
-            specs = [VMEM] * 6 + [HBM] * len(pieces), [VMEM] * 4
-            sems = (pltpu.SemaphoreType.DMA((len(pieces),)),)
-        else:
-            specs, sems = (None, None), ()
         x, x_b, *rest = call(
-            functools.partial(update_kernel, scale, 512, step > 0, final, math.sqrt(width), (5, 6)),
-            outs,
-            *specs,
-            sems,
+            functools.partial(update_kernel, scale, 512, step > 0, final, math.sqrt(width)), outs
         )(low_mask, coeff_b, coeff_o, resid, diag, *extra, *blocks)
-        if step == 0:
-            blocks = rest
     other, raw = x_b, rest[0]
 
     weights = jnp.broadcast_to(

time: 201 us -> 204 us (1.015)
  starting transfers between devices: 79.5 us -> 82.8 us
  local copies, waits for them, and re-layouts: 11 us -> 14.1 us
  waiting for transfers between devices: 62.1 us -> 59.7 us
    all_to_all x1, starting transfers between devices: 5.06 us -> 8.2 us  [per_device(): parts = lax.all_to_all(parts, 'orb', 0, 0, tiled=True)]
    unnamed x37 -> x53, local copies, waits for them, and re-layouts: 8.65 us -> 10.9 us
    ppermute x34 -> x35, waiting for transfers between devices: 16.9 us -> 15.7 us  [permute(): return lax.ppermute(value, 'orb', pairs)]
    ppermute x34 -> x35, starting transfers between devices: 45.9 us -> 45.5 us  [permute(): return lax.ppermute(value, 'orb', pairs)]
  transfers between devices with their start and end apart: 41 -> 42, of which waited for: 13 -> 12; matrix products, arithmetic and copies ran while one was open for 4% -> 5% of each run, Pallas kernels for 5% -> 6%
where the time goes in v4:
time: 204 us; the launch traced here: 202 us
  starting transfers between devices  82.8 us (41%)
  waiting for transfers between devices  59.7 us (29%)
  Pallas kernels  22.9 us (11%)
  blocking collectives  16.9 us (8%)
  local copies, waits for them, and re-layouts  14.1 us (7%)
  other arithmetic  3.97 us (2%)
    ppermute x35, starting transfers between devices, permute(): return lax.ppermute(value, 'orb', pairs)  45.5 us
    all_to_all x1, blocking collectives, per_device(): parts = lax.all_to_all(spread, 'dom', 0, 0, tiled=True)  16.9 us
    ppermute x35, waiting for transfers between devices, permute(): return lax.ppermute(value, 'orb', pairs)  15.7 us
    all_to_all x1, waiting for transfers between devices, per_device(): lax.all_to_all(raw.reshape((n_dom * n_orb,) + raw.shape[2:]), ('dom', 'or...  12.9 us
    all_to_all x1, waiting for transfers between devices, per_device(): parts = lax.all_to_all(spread, 'dom', 0, 0, tiled=True)  12.1 us
    ppermute x2, waiting for transfers between devices, per_device(): off = lax.ppermute(x_b, ('dom', 'orb'), across)  11.2 us
    unnamed x53, local copies, waits for them, and re-layouts  10.9 us
    all_to_all x1, starting transfers between devices, per_device(): lax.all_to_all(call(spread_shares_kernel, spread_shape)(parts), 'dom', 0,...  10.5 us
  transfers between devices with their start and end apart: 42, of which 12 were waited for; matrix products, arithmetic and copies ran while one was open for 5% of the time, Pallas kernels for 6%

profile of v4, /device:TPU:1, one launch (start us, length us, event | category | flops | bytes accessed | tf_op | source)
XLA Modules:
  0.0 202.5 jit_solution(14731315204072063873)
XLA Ops:
  1.3 3.3 %shard_map.121 = (s32[40]{0:T(128)S(1)}, s32[1]{0:T(128)}, bf16[128,32,128]{2,1,0:T(8,128)(2,1)}, bf16[128,32,128]{2,1,0:T(8,128)(2,1)}) custom-call(s32[4]{0:T(128)S(1)} %copy-done.11, s32[1]{0:T(128)} %bitcast.6.dev_ref, bf16[2,128,2,32,128]{4,3,2,1,0:T(8,128)(2,1)} %occupied_ref.5), custom_call_target="tpu_custom_call" | custom-call | tf_op jit(solution)/shard_map/pallas_call | solution.py:408
  4.6 4.5 %collective-permute-start.4 = (bf16[128,32,128]{2,1,0:T(8,128)(2,1)}, bf16[128,32,128]{2,1,0:T(8,128)(2,1)S(1)}, u32[]{:S(2)}, u32[]{:S(2)}) collective-permute-start(bf16[128,32,128]{2,1,0:T(8,128)(2,1)} %get-tuple-element.70), channel_id=1, source_target_pairs={{0,1},{1,0},{2,3},{3,2},{4,5},{5,4},{6,7},{7,6},{8,9},{9,8},{10,11... | collective-permute-start | bytes 3145736 | tf_op jit(solution)/shard_map/ppermute | solution.py:398
  9.1 1.3 collective-permute-start.5
  10.6 1.3 collective-permute-start.1
  14.7 2.7 %collective-permute-start.3 = (bf16[16,4096]{1,0:T(8,128)(2,1)S(1)}, bf16[16,4096]{1,0:T(8,128)(2,1)}, u32[]{:S(2)}, u32[]{:S(2)}) collective-permute-start(bf16[16,4096]{1,0:T(8,128)(2,1)S(1)} %get-tuple-element.69), channel_id=1, source_target_pairs={{0,6},{1,7},{2,0},{3,1},{4,2},{5,3},{6,4},{7,5},{8,14},{9,15},{10,... | collective-permute-start | bytes 393224 | tf_op jit(solution)/shard_map/ppermute | solution.py:398
  17.4 2.8 %shard_map.124 = bf16[128,32,128]{2,1,0:T(8,128)(2,1)} custom-call(s32[40]{0:T(128)S(1)} %get-tuple-element.66.plan_ref, bf16[2,128,2,32,128]{4,3,2,1,0:T(8,128)(2,1)} %occupied_ref.5, bf16[128,32,128]{2,1,0:T(8,128)(2,1)S(1)} %collective-permute-done.4.offer_ref), custom_call_target="tpu_custom_call" | custom-call | tf_op jit(solution)/shard_map/pallas_call | solution.py:425
  20.1 1.4 shard_map.125
  22.2 1.4 collective-permute-start.6
  23.7 3.7 %all-to-all-start.1 = ((bf16[8,16,32,128]{3,2,1,0:T(8,128)(2,1)}), bf16[8,16,32,128]{3,2,1,0:T(8,128)(2,1)S(1)}, u32[]{:S(2)}, u32[]{:S(2)}) async-start(bf16[8,16,32,128]{3,2,1,0:T(8,128)(2,1)} %bitcast.7), calls=%async_computation.1 | async-start | bytes 2097152 | tf_op jit(solution)/shard_map/all_to_all | solution.py:452
  27.5 4.9 %collective-permute-start.11 = (bf16[32,32,128]{2,1,0:T(8,128)(2,1)S(1)}, bf16[32,32,128]{2,1,0:T(8,128)(2,1)S(1)}, u32[]{:S(2)}, u32[]{:S(2)}) collective-permute-start(bf16[32,32,128]{2,1,0:T(8,128)(2,1)S(1)} %copy-done.14), channel_id=1, source_target_pairs={{0,4},{1,5},{14,10},{15,11},{16,20},{17,21},{30,26},{31,27},{32,36... | collective-permute-start | bytes 786440 | tf_op jit(solution)/shard_map/ppermute | solution.py:398
  32.4 1.3 collective-permute-start.12
  37.3 9.4 %collective-permute-done.11.refs_2_ = bf16[32,32,128]{2,1,0:T(8,128)(2,1)S(1)} collective-permute-done((bf16[32,32,128]{2,1,0:T(8,128)(2,1)S(1)}, bf16[32,32,128]{2,1,0:T(8,128)(2,1)S(1)}, u32[]{:S(2)}, u32[]{:S(2)}) %collective-permute-start.11) | collective-permute-done | bytes 262176 | tf_op jit(solution)/shard_map/ppermute | solution.py:398
  48.2 2.0 %collective-permute-done.9 = bf16[8,4096]{1,0:T(8,128)(2,1)S(1)} collective-permute-done((bf16[8,4096]{1,0:T(8,128)(2,1)S(1)}, bf16[8,4096]{1,0:T(8,128)(2,1)S(1)}, u32[]{:S(2)}, u32[]{:S(2)}) %collective-permute-start.9) | collective-permute-done | bytes 65568 | tf_op jit(solution)/shard_map/ppermute | solution.py:398
  50.2 2.0 collective-permute-start.10
  54.2 2.7 %collective-permute-start.16 = (bf16[32,4096]{1,0:T(8,128)(2,1)S(1)}, bf16[32,4096]{1,0:T(8,128)(2,1)S(1)}, u32[]{:S(2)}, u32[]{:S(2)}) collective-permute-start(bf16[32,4096]{1,0:T(8,128)(2,1)S(1)} %get-tuple-element.83.refs_5_.refs_3_), channel_id=1, source_target_pairs={{0,6},{1,7},{2,0},{3,1},{4,2},{5,3},{6,4},{7,5},{8,14},{9,15},{10,... | collective-permute-start | bytes 786440 | tf_op jit(solution)/shard_map/ppermute | solution.py:398
  56.9 1.3 collective-permute-start.13
  58.2 2.5 %shard_map.128 = f32[16,8,128]{2,1,0:T(8,128)} custom-call(s32[40]{0:T(128)S(1)} %get-tuple-element.66.plan_ref, bf16[48,4096]{1,0:T(8,128)(2,1)S(1)} %constant_dynamic-update-slice_fusion.refs_0_, bf16[48,4096]{1,0:T(8,128)(2,1)} %collective-permute-done.7.refs_1_, bf16[16,4096]{1,0:T(8,128)(2,1)S(1)} %constant_dynamic-update-slice_fusion.3.refs_2_, ...), custom_call_target="tpu_custom_call" | custom-call | tf_op jit(solution)/shard_map/pallas_call | solution.py:488
  60.7 8.2 %all-to-all-start.2 = ((f32[16,8,128]{2,1,0:T(8,128)}), f32[16,8,128]{2,1,0:T(8,128)S(1)}, u32[]{:S(2)}, u32[]{:S(2)}) async-start(f32[16,8,128]{2,1,0:T(8,128)} %shard_map.128), calls=%async_computation.2 | async-start | bytes 131072 | tf_op jit(solution)/shard_map/all_to_all | solution.py:493
  70.6 1.4 collective-permute-start.20
  72.0 1.3 collective-permute-start.21
  73.3 1.5 collective-permute-start.19
  75.6 10.5 %all-to-all-start.3 = ((f32[16,8,512]{2,1,0:T(8,128)}), f32[16,8,512]{2,1,0:T(8,128)S(1)}, u32[]{:S(2)}, u32[]{:S(2)}) async-start(f32[16,8,512]{2,1,0:T(8,128)} %shard_map.130), calls=%async_computation.3 | async-start | bytes 524288 | tf_op jit(solution)/shard_map/all_to_all | solution.py:504
  86.4 2.4 %collective-permute-start.23 = (bf16[16,4096]{1,0:T(8,128)(2,1)S(1)}, bf16[16,4096]{1,0:T(8,128)(2,1)}, u32[]{:S(2)}, u32[]{:S(2)}) collective-permute-start(bf16[16,4096]{1,0:T(8,128)(2,1)S(1)} %slice.27), channel_id=1, source_target_pairs={{0,6},{1,7},{2,0},{3,1},{4,2},{5,3},{6,4},{7,5},{8,14},{9,15},{10,... | collective-permute-start | bytes 393224 | tf_op jit(solution)/shard_map/ppermute | solution.py:398
  89.6 7.8 %all-to-all-done.3.parts_ref = f32[16,8,512]{2,1,0:T(8,128)S(1)} async-done(((f32[16,8,512]{2,1,0:T(8,128)}), f32[16,8,512]{2,1,0:T(8,128)S(1)}, u32[]{:S(2)}, u32[]{:S(2)}) %all-to-all-start.3) | async-done | bytes 262176 | tf_op jit(solution)/shard_map/all_to_all | solution.py:504
  97.4 3.3 %collective-permute-start.17 = (bf16[16,256]{1,0:T(8,128)(2,1)S(1)}, bf16[16,256]{1,0:T(8,128)(2,1)S(1)}, u32[]{:S(2)}, u32[]{:S(2)}) collective-permute-start(bf16[16,256]{1,0:T(8,128)(2,1)S(1)} %shard_map.131.mine_ref), channel_id=1, source_target_pairs={{0,1},{1,0},{2,3},{3,2},{4,5},{5,4},{6,7},{7,6},{8,9},{9,8},{10,11... | collective-permute-start | bytes 24584 | tf_op jit(solution)/shard_map/ppermute | solution.py:398
  100.9 1.2 pad_maximum_fusion.refs_7_
  102.2 1.3 collective-permute-start.27
  103.9 2.5 %collective-permute-start.25 = (bf16[32,4096]{1,0:T(8,128)(2,1)S(1)}, bf16[32,4096]{1,0:T(8,128)(2,1)S(1)}, u32[]{:S(2)}, u32[]{:S(2)}) collective-permute-start(bf16[32,4096]{1,0:T(8,128)(2,1)S(1)} %slice.29), channel_id=1, source_target_pairs={{0,6},{1,7},{2,0},{3,1},{4,2},{5,3},{6,4},{7,5},{8,14},{9,15},{10,... | collective-permute-start | bytes 786440 | tf_op jit(solution)/shard_map/ppermute | solution.py:398
  110.4 1.4 shard_map.132
  112.9 1.5 collective-permute-start.28
  114.4 2.0 collective-permute-start.29
  116.4 5.8 %collective-permute-done.29.off_ref = bf16[16,4096]{1,0:T(8,128)(2,1)S(1)} collective-permute-done((bf16[16,4096]{1,0:T(8,128)(2,1)S(1)}, bf16[16,4096]{1,0:T(8,128)(2,1)S(1)}, u32[]{:S(2)}, u32[]{:S(2)}) %collective-permute-start.29) | collective-permute-done | bytes 131104 | tf_op jit(solution)/shard_map/ppermute | solution.py:566
  122.2 1.2 shard_map.134
  123.5 1.2 collective-permute-done.30.other_ref
  124.7 16.9 %all_to_all.34.parts_ref = f32[16,8,512]{2,1,0:T(8,128)S(1)} all-to-all(f32[16,8,512]{2,1,0:T(8,128)S(1)} %shard_map.135), channel_id=1, replica_groups=mesh['dom'=16,'orb'=16] {'dom'}, dimensions={0} | all-to-all | bytes 524288 | tf_op jit(solution)/shard_map/all_to_all | solution.py:573
  141.7 1.9 collective-permute-start.31
  145.4 2.5 %collective-permute-start.33 = (bf16[16,4096]{1,0:T(8,128)(2,1)S(1)}, bf16[16,4096]{1,0:T(8,128)(2,1)S(1)}, u32[]{:S(2)}, u32[]{:S(2)}) collective-permute-start(bf16[16,4096]{1,0:T(8,128)(2,1)S(1)} %get-tuple-element.105), channel_id=1, source_target_pairs={{1,16},{16,1},{3,18},{18,3},{5,20},{20,5},{7,22},{22,7},{9,24},{24... | collective-permute-start | bytes 393224 | tf_op jit(solution)/shard_map/ppermute | solution.py:566
  147.9 5.4 %collective-permute-done.33.off_ref = bf16[16,4096]{1,0:T(8,128)(2,1)S(1)} collective-permute-done((bf16[16,4096]{1,0:T(8,128)(2,1)S(1)}, bf16[16,4096]{1,0:T(8,128)(2,1)S(1)}, u32[]{:S(2)}, u32[]{:S(2)}) %collective-permute-start.33) | collective-permute-done | bytes 131104 | tf_op jit(solution)/shard_map/ppermute | solution.py:566
  153.4 1.2 shard_map.138
  154.6 1.2 collective-permute-done.34.other_ref
  156.6 4.5 %all-to-all-start.5 = ((f32[16,8,512]{2,1,0:T(8,128)}), f32[16,8,512]{2,1,0:T(8,128)S(1)}, u32[]{:S(2)}, u32[]{:S(2)}) async-start(f32[16,8,512]{2,1,0:T(8,128)} %shard_map.139), calls=%async_computation.5 | async-start | bytes 524288 | tf_op jit(solution)/shard_map/all_to_all | solution.py:573
  161.8 12.1 %all-to-all-done.5.parts_ref = f32[16,8,512]{2,1,0:T(8,128)S(1)} async-done(((f32[16,8,512]{2,1,0:T(8,128)}), f32[16,8,512]{2,1,0:T(8,128)S(1)}, u32[]{:S(2)}, u32[]{:S(2)}) %all-to-all-start.5) | async-done | bytes 262176 | tf_op jit(solution)/shard_map/all_to_all | solution.py:573
  173.9 1.7 collective-permute-start.35
  176.6 1.6 copy-done.1
  178.2 1.4 shard_map.143
  179.8 6.0 %all-to-all-start.6 = ((f32[256,2,128]{2,1,0:T(2,128)}), f32[256,2,128]{2,1,0:T(2,128)S(1)}, u32[]{:S(2)}, u32[]{:S(2)}) async-start(f32[256,2,128]{2,1,0:T(2,128)} %bitcast.17), calls=%async_computation.6 | async-start | bytes 524288 | tf_op jit(solution)/shard_map/all_to_all | solution.py:587
  188.1 12.9 %all-to-all-done.6.terms_ref = f32[256,2,128]{2,1,0:T(2,128)S(1)} async-done(((f32[256,2,128]{2,1,0:T(2,128)}), f32[256,2,128]{2,1,0:T(2,128)S(1)}, u32[]{:S(2)}, u32[]{:S(2)}) %all-to-all-start.6) | async-done | bytes 262176 | tf_op jit(solution)/shard_map/all_to_all | solution.py:587
  201.0 1.5 shard_map.145
  (153 shorter events, 26.7 us)
Async XLA Ops:
  1.3 10.9 %copy-start.22 = (s32[16]{0:T(128)S(1)}, s32[16]{0:T(128)}, u32[]{:S(2)}) copy-start(s32[16]{0:T(128)} %constant.141.clone) | copy-start | bytes 196
  1.3 10.9 %copy-start.23 = (s32[16]{0:T(128)S(1)}, s32[16]{0:T(128)}, u32[]{:S(2)}) copy-start(s32[16]{0:T(128)} %constant.142.clone) | copy-start | bytes 196
  4.6 12.8 %collective-permute-start.4 = (bf16[128,32,128]{2,1,0:T(8,128)(2,1)}, bf16[128,32,128]{2,1,0:T(8,128)(2,1)S(1)}, u32[]{:S(2)}, u32[]{:S(2)}) collective-permute-start(bf16[128,32,128]{2,1,0:T(8,128)(2,1)} %get-tuple-element.70), channel_id=1, source_target_pairs={{0,1},{1,0},{2,3},{3,2},{4,5},{5,4},{6,7},{7,6},{8,9},{9,8},{10,11... | collective-permute-start | bytes 3145736 | tf_op jit(solution)/shard_map/ppermute | solution.py:398
  9.1 11.0 %collective-permute-start.5 = (bf16[128,32,128]{2,1,0:T(8,128)(2,1)}, bf16[128,32,128]{2,1,0:T(8,128)(2,1)S(1)}, u32[]{:S(2)}, u32[]{:S(2)}) collective-permute-start(bf16[128,32,128]{2,1,0:T(8,128)(2,1)} %get-tuple-element.71), channel_id=1, source_target_pairs={{0,1},{15,14},{16,17},{31,30},{32,33},{47,46},{48,49},{63,62},{64,... | collective-permute-start | bytes 3145736 | tf_op jit(solution)/shard_map/ppermute | solution.py:398
  10.6 4.0 %collective-permute-start.1 = (f32[8,4096]{1,0:T(8,128)S(1)}, f32[8,4096]{1,0:T(8,128)S(1)}, u32[]{:S(2)}, u32[]{:S(2)}) collective-permute-start(f32[8,4096]{1,0:T(8,128)S(1)} %get-tuple-element.68), channel_id=1, source_target_pairs={{0,1},{1,0},{2,3},{3,2},{4,5},{5,4},{6,7},{7,6},{8,9},{9,8},{10,11... | collective-permute-start | bytes 393224 | tf_op jit(solution)/shard_map/ppermute | solution.py:398
  12.0 42.2 %collective-permute-start.18 = (f32[8,1]{0,1:T(1,128)S(1)}, f32[8,1]{0,1:T(1,128)S(1)}, u32[]{:S(2)}, u32[]{:S(2)}) collective-permute-start(f32[8,1]{0,1:T(1,128)S(1)} %bitcast.41), channel_id=1, source_target_pairs={{0,1},{1,0},{2,3},{3,2},{4,5},{5,4},{6,7},{7,6},{8,9},{9,8},{10,11... | collective-permute-start | bytes 104 | tf_op jit(solution)/shard_map/ppermute | solution.py:398
  14.6 17.8 %collective-permute-start.2 = (bf16[16,4096]{1,0:T(8,128)(2,1)S(1)}, bf16[16,4096]{1,0:T(8,128)(2,1)}, u32[]{:S(2)}, u32[]{:S(2)}) collective-permute-start(bf16[16,4096]{1,0:T(8,128)(2,1)S(1)} %get-tuple-element.69), channel_id=1, source_target_pairs={{0,2},{1,3},{2,4},{3,5},{4,6},{5,7},{6,0},{7,1},{8,10},{9,11},{10,... | collective-permute-start | bytes 393224 | tf_op jit(solution)/shard_map/ppermute | solution.py:398
  14.7 19.0 %collective-permute-start.3 = (bf16[16,4096]{1,0:T(8,128)(2,1)S(1)}, bf16[16,4096]{1,0:T(8,128)(2,1)}, u32[]{:S(2)}, u32[]{:S(2)}) collective-permute-start(bf16[16,4096]{1,0:T(8,128)(2,1)S(1)} %get-tuple-element.69), channel_id=1, source_target_pairs={{0,6},{1,7},{2,0},{3,1},{4,2},{5,3},{6,4},{7,5},{8,14},{9,15},{10,... | collective-permute-start | bytes 393224 | tf_op jit(solution)/shard_map/ppermute | solution.py:398
  22.2 11.5 %collective-permute-start.6 = (bf16[32,32,128]{2,1,0:T(8,128)(2,1)}, bf16[32,32,128]{2,1,0:T(8,128)(2,1)S(1)}, u32[]{:S(2)}, u32[]{:S(2)}) collective-permute-start(bf16[32,32,128]{2,1,0:T(8,128)(2,1)} %get-tuple-element.73), channel_id=1, source_target_pairs={{0,2},{1,3},{14,8},{15,9},{16,18},{17,19},{30,24},{31,25},{32,34},... | collective-permute-start | bytes 786440 | tf_op jit(solution)/shard_map/ppermute | solution.py:398
  23.7 28.6 %copy-start.17 = (bf16[16,32,128]{2,1,0:T(8,128)(2,1)S(1)}, bf16[16,32,128]{2,1,0:T(8,128)(2,1)}, u32[]{:S(2)}) copy-start(bf16[16,32,128]{2,1,0:T(8,128)(2,1)} %copy-done.16) | copy-start | bytes 393220
  23.7 28.5 %all-to-all-start.1 = ((bf16[8,16,32,128]{3,2,1,0:T(8,128)(2,1)}), bf16[8,16,32,128]{3,2,1,0:T(8,128)(2,1)S(1)}, u32[]{:S(2)}, u32[]{:S(2)}) async-start(bf16[8,16,32,128]{3,2,1,0:T(8,128)(2,1)} %bitcast.7), calls=%async_computation.1 | async-start | bytes 2097152 | tf_op jit(solution)/shard_map/all_to_all | solution.py:452
  27.5 19.3 %collective-permute-start.11 = (bf16[32,32,128]{2,1,0:T(8,128)(2,1)S(1)}, bf16[32,32,128]{2,1,0:T(8,128)(2,1)S(1)}, u32[]{:S(2)}, u32[]{:S(2)}) collective-permute-start(bf16[32,32,128]{2,1,0:T(8,128)(2,1)S(1)} %copy-done.14), channel_id=1, source_target_pairs={{0,4},{1,5},{14,10},{15,11},{16,20},{17,21},{30,26},{31,27},{32,36... | collective-permute-start | bytes 786440 | tf_op jit(solution)/shard_map/ppermute | solution.py:398
  32.4 14.4 %collective-permute-start.12 = (bf16[32,32,128]{2,1,0:T(8,128)(2,1)}, bf16[32,32,128]{2,1,0:T(8,128)(2,1)S(1)}, u32[]{:S(2)}, u32[]{:S(2)}) collective-permute-start(bf16[32,32,128]{2,1,0:T(8,128)(2,1)} %copy-done.12), channel_id=1, source_target_pairs={{0,6},{1,7},{14,12},{15,13},{16,22},{17,23},{30,28},{31,29},{32,38... | collective-permute-start | bytes 786440 | tf_op jit(solution)/shard_map/ppermute | solution.py:398
  35.5 12.7 %collective-permute-start.8 = (bf16[8,4096]{1,0:T(8,128)(2,1)S(1)}, bf16[8,4096]{1,0:T(8,128)(2,1)S(1)}, u32[]{:S(2)}, u32[]{:S(2)}) collective-permute-start(bf16[8,4096]{1,0:T(8,128)(2,1)S(1)} %slice.24), channel_id=1, source_target_pairs={{0,2},{1,3},{2,4},{3,5},{4,6},{5,7},{6,0},{7,1},{8,10},{9,11},{10,... | collective-permute-start | bytes 196616 | tf_op jit(solution)/shard_map/ppermute | solution.py:398
  37.3 20.9 %collective-permute-start.7 = (bf16[48,4096]{1,0:T(8,128)(2,1)S(1)}, bf16[48,4096]{1,0:T(8,128)(2,1)}, u32[]{:S(2)}, u32[]{:S(2)}) collective-permute-start(bf16[48,4096]{1,0:T(8,128)(2,1)S(1)} %constant_dynamic-update-slice_fusion.refs_0_), channel_id=1, source_target_pairs={{0,8},{1,9},{2,10},{3,11},{4,12},{5,13},{6,14},{7,15},{8,0},{9,1},... | collective-permute-start | bytes 1179656 | tf_op jit(solution)/shard_map/ppermute | solution.py:398
  46.7 3.5 %collective-permute-start.9 = (bf16[8,4096]{1,0:T(8,128)(2,1)S(1)}, bf16[8,4096]{1,0:T(8,128)(2,1)S(1)}, u32[]{:S(2)}, u32[]{:S(2)}) collective-permute-start(bf16[8,4096]{1,0:T(8,128)(2,1)S(1)} %slice.25), channel_id=1, source_target_pairs={{0,6},{1,7},{2,0},{3,1},{4,2},{5,3},{6,4},{7,5},{8,14},{9,15},{10,... | collective-permute-start | bytes 196616 | tf_op jit(solution)/shard_map/ppermute | solution.py:398
  50.2 6.7 %collective-permute-start.10 = (bf16[16,4096]{1,0:T(8,128)(2,1)S(1)}, bf16[16,4096]{1,0:T(8,128)(2,1)S(1)}, u32[]{:S(2)}, u32[]{:S(2)}) collective-permute-start(bf16[16,4096]{1,0:T(8,128)(2,1)S(1)} %constant_dynamic-update-slice_fusion.3.refs_2_), channel_id=1, source_target_pairs={{0,8},{1,9},{2,10},{3,11},{4,12},{5,13},{6,14},{7,15},{8,0},{9,1},... | collective-permute-start | bytes 393224 | tf_op jit(solution)/shard_map/ppermute | solution.py:398
  53.0 16.0 %collective-permute-start.14 = (bf16[32,4096]{1,0:T(8,128)(2,1)S(1)}, bf16[32,4096]{1,0:T(8,128)(2,1)S(1)}, u32[]{:S(2)}, u32[]{:S(2)}) collective-permute-start(bf16[32,4096]{1,0:T(8,128)(2,1)S(1)} %get-tuple-element.83.refs_5_.refs_3_), channel_id=1, source_target_pairs={{0,8},{1,9},{2,10},{3,11},{4,12},{5,13},{6,14},{7,15},{8,0},{9,1},... | collective-permute-start | bytes 786440 | tf_op jit(solution)/shard_map/ppermute | solution.py:398
  53.1 16.6 %collective-permute-start.15 = (bf16[32,4096]{1,0:T(8,128)(2,1)S(1)}, bf16[32,4096]{1,0:T(8,128)(2,1)S(1)}, u32[]{:S(2)}, u32[]{:S(2)}) collective-permute-start(bf16[32,4096]{1,0:T(8,128)(2,1)S(1)} %get-tuple-element.83.refs_5_.refs_3_), channel_id=1, source_target_pairs={{0,2},{1,3},{2,4},{3,5},{4,6},{5,7},{6,0},{7,1},{8,10},{9,11},{10,... | collective-permute-start | bytes 786440 | tf_op jit(solution)/shard_map/ppermute | solution.py:398
  54.2 15.5 %collective-permute-start.16 = (bf16[32,4096]{1,0:T(8,128)(2,1)S(1)}, bf16[32,4096]{1,0:T(8,128)(2,1)S(1)}, u32[]{:S(2)}, u32[]{:S(2)}) collective-permute-start(bf16[32,4096]{1,0:T(8,128)(2,1)S(1)} %get-tuple-element.83.refs_5_.refs_3_), channel_id=1, source_target_pairs={{0,6},{1,7},{2,0},{3,1},{4,2},{5,3},{6,4},{7,5},{8,14},{9,15},{10,... | collective-permute-start | bytes 786440 | tf_op jit(solution)/shard_map/ppermute | solution.py:398
  56.9 12.1 %collective-permute-start.13 = (bf16[32,4096]{1,0:T(8,128)(2,1)S(1)}, bf16[32,4096]{1,0:T(8,128)(2,1)S(1)}, u32[]{:S(2)}, u32[]{:S(2)}) collective-permute-start(bf16[32,4096]{1,0:T(8,128)(2,1)S(1)} %get-tuple-element.82.refs_4_.refs_0_), channel_id=1, source_target_pairs={{0,8},{1,9},{2,10},{3,11},{4,12},{5,13},{6,14},{7,15},{8,0},{9,1},... | collective-permute-start | bytes 786440 | tf_op jit(solution)/shard_map/ppermute | solution.py:398
  60.7 14.1 %all-to-all-start.2 = ((f32[16,8,128]{2,1,0:T(8,128)}), f32[16,8,128]{2,1,0:T(8,128)S(1)}, u32[]{:S(2)}, u32[]{:S(2)}) async-start(f32[16,8,128]{2,1,0:T(8,128)} %shard_map.128), calls=%async_computation.2 | async-start | bytes 131072 | tf_op jit(solution)/shard_map/all_to_all | solution.py:493
  70.6 33.3 %copy-start.6 = (bf16[64,4096]{1,0:T(8,128)(2,1)}, bf16[64,4096]{1,0:T(8,128)(2,1)S(1)}, u32[]{:S(2)}) copy-start(bf16[64,4096]{1,0:T(8,128)(2,1)S(1)} %get-tuple-element.90.refs_0_) | copy-start | bytes 1572868
  70.6 30.2 %collective-permute-start.20 = (bf16[64,4096]{1,0:T(8,128)(2,1)S(1)}, bf16[64,4096]{1,0:T(8,128)(2,1)S(1)}, u32[]{:S(2)}, u32[]{:S(2)}) collective-permute-start(bf16[64,4096]{1,0:T(8,128)(2,1)S(1)} %get-tuple-element.90.refs_0_), channel_id=1, source_target_pairs={{0,2},{1,3},{2,4},{3,5},{4,6},{5,7},{6,0},{7,1},{8,10},{9,11},{10,... | collective-permute-start | bytes 1572872 | tf_op jit(solution)/shard_map/ppermute | solution.py:398
  72.0 28.8 %collective-permute-start.21 = (bf16[64,4096]{1,0:T(8,128)(2,1)S(1)}, bf16[64,4096]{1,0:T(8,128)(2,1)S(1)}, u32[]{:S(2)}, u32[]{:S(2)}) collective-permute-start(bf16[64,4096]{1,0:T(8,128)(2,1)S(1)} %get-tuple-element.90.refs_0_), channel_id=1, source_target_pairs={{0,6},{1,7},{2,0},{3,1},{4,2},{5,3},{6,4},{7,5},{8,14},{9,15},{10,... | collective-permute-start | bytes 1572872 | tf_op jit(solution)/shard_map/ppermute | solution.py:398
  73.3 27.5 %collective-permute-start.19 = (bf16[64,4096]{1,0:T(8,128)(2,1)}, bf16[64,4096]{1,0:T(8,128)(2,1)}, u32[]{:S(2)}, u32[]{:S(2)}) collective-permute-start(bf16[64,4096]{1,0:T(8,128)(2,1)} %get-tuple-element.87.refs_4_), channel_id=1, source_target_pairs={{0,8},{1,9},{2,10},{3,11},{4,12},{5,13},{6,14},{7,15},{8,0},{9,1},... | collective-permute-start | bytes 1572872 | tf_op jit(solution)/shard_map/ppermute | solution.py:398
  75.6 21.8 %all-to-all-start.3 = ((f32[16,8,512]{2,1,0:T(8,128)}), f32[16,8,512]{2,1,0:T(8,128)S(1)}, u32[]{:S(2)}, u32[]{:S(2)}) async-start(f32[16,8,512]{2,1,0:T(8,128)} %shard_map.130), calls=%async_computation.3 | async-start | bytes 524288 | tf_op jit(solution)/shard_map/all_to_all | solution.py:504
  86.0 11.4 %collective-permute-start.22 = (bf16[16,4096]{1,0:T(8,128)(2,1)S(1)}, bf16[16,4096]{1,0:T(8,128)(2,1)}, u32[]{:S(2)}, u32[]{:S(2)}) collective-permute-start(bf16[16,4096]{1,0:T(8,128)(2,1)S(1)} %slice.26), channel_id=1, source_target_pairs={{0,2},{1,3},{2,4},{3,5},{4,6},{5,7},{6,0},{7,1},{8,10},{9,11},{10,... | collective-permute-start | bytes 393224 | tf_op jit(solution)/shard_map/ppermute | solution.py:398
  86.4 14.4 %collective-permute-start.23 = (bf16[16,4096]{1,0:T(8,128)(2,1)S(1)}, bf16[16,4096]{1,0:T(8,128)(2,1)}, u32[]{:S(2)}, u32[]{:S(2)}) collective-permute-start(bf16[16,4096]{1,0:T(8,128)(2,1)S(1)} %slice.27), channel_id=1, source_target_pairs={{0,6},{1,7},{2,0},{3,1},{4,2},{5,3},{6,4},{7,5},{8,14},{9,15},{10,... | collective-permute-start | bytes 393224 | tf_op jit(solution)/shard_map/ppermute | solution.py:398
  97.4 14.7 %collective-permute-start.17 = (bf16[16,256]{1,0:T(8,128)(2,1)S(1)}, bf16[16,256]{1,0:T(8,128)(2,1)S(1)}, u32[]{:S(2)}, u32[]{:S(2)}) collective-permute-start(bf16[16,256]{1,0:T(8,128)(2,1)S(1)} %shard_map.131.mine_ref), channel_id=1, source_target_pairs={{0,1},{1,0},{2,3},{3,2},{4,5},{5,4},{6,7},{7,6},{8,9},{9,8},{10,11... | collective-permute-start | bytes 24584 | tf_op jit(solution)/shard_map/ppermute | solution.py:398
  100.8 11.0 %collective-permute-start.26 = (bf16[16,4096]{1,0:T(8,128)(2,1)}, bf16[16,4096]{1,0:T(8,128)(2,1)S(1)}, u32[]{:S(2)}, u32[]{:S(2)}) collective-permute-start(bf16[16,4096]{1,0:T(8,128)(2,1)} %collective-permute-done.22), channel_id=1, source_target_pairs={{0,8},{1,9},{2,10},{3,11},{4,12},{5,13},{6,14},{7,15},{8,0},{9,1},... | collective-permute-start | bytes 393224 | tf_op jit(solution)/shard_map/ppermute | solution.py:398
  102.2 9.7 %collective-permute-start.27 = (bf16[16,4096]{1,0:T(8,128)(2,1)}, bf16[16,4096]{1,0:T(8,128)(2,1)S(1)}, u32[]{:S(2)}, u32[]{:S(2)}) collective-permute-start(bf16[16,4096]{1,0:T(8,128)(2,1)} %collective-permute-done.23), channel_id=1, source_target_pairs={{0,8},{1,9},{2,10},{3,11},{4,12},{5,13},{6,14},{7,15},{8,0},{9,1},... | collective-permute-start | bytes 393224 | tf_op jit(solution)/shard_map/ppermute | solution.py:398
  103.5 8.6 %collective-permute-start.24 = (bf16[32,4096]{1,0:T(8,128)(2,1)S(1)}, bf16[32,4096]{1,0:T(8,128)(2,1)S(1)}, u32[]{:S(2)}, u32[]{:S(2)}) collective-permute-start(bf16[32,4096]{1,0:T(8,128)(2,1)S(1)} %slice.28), channel_id=1, source_target_pairs={{0,2},{1,3},{2,4},{3,5},{4,6},{5,7},{6,0},{7,1},{8,10},{9,11},{10,... | collective-permute-start | bytes 786440 | tf_op jit(solution)/shard_map/ppermute | solution.py:398
  103.9 8.2 %collective-permute-start.25 = (bf16[32,4096]{1,0:T(8,128)(2,1)S(1)}, bf16[32,4096]{1,0:T(8,128)(2,1)S(1)}, u32[]{:S(2)}, u32[]{:S(2)}) collective-permute-start(bf16[32,4096]{1,0:T(8,128)(2,1)S(1)} %slice.29), channel_id=1, source_target_pairs={{0,6},{1,7},{2,0},{3,1},{4,2},{5,3},{6,4},{7,5},{8,14},{9,15},{10,... | collective-permute-start | bytes 786440 | tf_op jit(solution)/shard_map/ppermute | solution.py:398
  111.9 41.4 %copy-start = (bf16[256,4096]{1,0:T(8,128)(2,1)}, bf16[256,4096]{1,0:T(8,128)(2,1)S(1)}, u32[]{:S(2)}) copy-start(bf16[256,4096]{1,0:T(8,128)(2,1)S(1)} %constant_dynamic-update-slice_fusion.5.refs_2_.second_ref.refs_3_) | copy-start | bytes 6291460
  112.9 9.3 %collective-permute-start.28 = (f32[16,4096]{1,0:T(8,128)S(1)}, f32[16,4096]{1,0:T(8,128)S(1)}, u32[]{:S(2)}, u32[]{:S(2)}) collective-permute-start(f32[16,4096]{1,0:T(8,128)S(1)} %get-tuple-element.99.x_ref.refs_0_), channel_id=1, source_target_pairs={{0,1},{1,0},{2,3},{3,2},{4,5},{5,4},{6,7},{7,6},{8,9},{9,8},{10,11... | collective-permute-start | bytes 786440 | tf_op jit(solution)/shard_map/ppermute | solution.py:398
  114.4 7.8 %collective-permute-start.29 = (bf16[16,4096]{1,0:T(8,128)(2,1)S(1)}, bf16[16,4096]{1,0:T(8,128)(2,1)S(1)}, u32[]{:S(2)}, u32[]{:S(2)}) collective-permute-start(bf16[16,4096]{1,0:T(8,128)(2,1)S(1)} %get-tuple-element.100), channel_id=1, source_target_pairs={{1,16},{16,1},{3,18},{18,3},{5,20},{20,5},{7,22},{22,7},{9,24},{24... | collective-permute-start | bytes 393224 | tf_op jit(solution)/shard_map/ppermute | solution.py:566
  123.4 1.2 collective-permute-start.30
  141.7 2.7 %collective-permute-start.31 = (bf16[16,256]{1,0:T(8,128)(2,1)S(1)}, bf16[16,256]{1,0:T(8,128)(2,1)S(1)}, u32[]{:S(2)}, u32[]{:S(2)}) collective-permute-start(bf16[16,256]{1,0:T(8,128)(2,1)S(1)} %shard_map.136.mine_ref), channel_id=1, source_target_pairs={{0,1},{1,0},{2,3},{3,2},{4,5},{5,4},{6,7},{7,6},{8,9},{9,8},{10,11... | collective-permute-start | bytes 24584 | tf_op jit(solution)/shard_map/ppermute | solution.py:398
  145.0 8.3 %collective-permute-start.32 = (f32[16,4096]{1,0:T(8,128)S(1)}, f32[16,4096]{1,0:T(8,128)S(1)}, u32[]{:S(2)}, u32[]{:S(2)}) collective-permute-start(f32[16,4096]{1,0:T(8,128)S(1)} %get-tuple-element.104.x_ref.refs_0_), channel_id=1, source_target_pairs={{0,1},{1,0},{2,3},{3,2},{4,5},{5,4},{6,7},{7,6},{8,9},{9,8},{10,11... | collective-permute-start | bytes 786440 | tf_op jit(solution)/shard_map/ppermute | solution.py:398
  145.4 15.6 %copy-start.18 = (bf16[8,2,32,128]{3,2,1,0:T(8,128)(2,1)S(1)}, bf16[8,2,32,128]{3,2,1,0:T(8,128)(2,1)}, u32[]{:S(2)}) copy-start(bf16[8,2,32,128]{3,2,1,0:T(8,128)(2,1)} %param.18) | copy-start | bytes 393220
  145.4 7.9 %collective-permute-start.33 = (bf16[16,4096]{1,0:T(8,128)(2,1)S(1)}, bf16[16,4096]{1,0:T(8,128)(2,1)S(1)}, u32[]{:S(2)}, u32[]{:S(2)}) collective-permute-start(bf16[16,4096]{1,0:T(8,128)(2,1)S(1)} %get-tuple-element.105), channel_id=1, source_target_pairs={{1,16},{16,1},{3,18},{18,3},{5,20},{20,5},{7,22},{22,7},{9,24},{24... | collective-permute-start | bytes 393224 | tf_op jit(solution)/shard_map/ppermute | solution.py:566
  154.6 1.2 collective-permute-start.34
  156.6 17.3 %all-to-all-start.5 = ((f32[16,8,512]{2,1,0:T(8,128)}), f32[16,8,512]{2,1,0:T(8,128)S(1)}, u32[]{:S(2)}, u32[]{:S(2)}) async-start(f32[16,8,512]{2,1,0:T(8,128)} %shard_map.139), calls=%async_computation.5 | async-start | bytes 524288 | tf_op jit(solution)/shard_map/all_to_all | solution.py:573
  161.3 15.2 %collective-permute-start.36 = (bf16[8,4096]{1,0:T(8,128)(2,1)S(1)}, bf16[8,4096]{1,0:T(8,128)(2,1)S(1)}, u32[]{:S(2)}, u32[]{:S(2)}) collective-permute-start(bf16[8,4096]{1,0:T(8,128)(2,1)S(1)} %convert_element_type.25), channel_id=1, source_target_pairs={{0,1},{1,0},{2,3},{3,2},{4,5},{5,4},{6,7},{7,6},{8,9},{9,8},{10,11... | collective-permute-start | bytes 196616 | tf_op jit(solution)/shard_map/ppermute | solution.py:398
  173.9 2.6 %collective-permute-start.35 = (bf16[16,256]{1,0:T(8,128)(2,1)S(1)}, bf16[16,256]{1,0:T(8,128)(2,1)S(1)}, u32[]{:S(2)}, u32[]{:S(2)}) collective-permute-start(bf16[16,256]{1,0:T(8,128)(2,1)S(1)} %get-tuple-element.108.mine_ref), channel_id=1, source_target_pairs={{0,1},{1,0},{2,3},{3,2},{4,5},{5,4},{6,7},{7,6},{8,9},{9,8},{10,11... | collective-permute-start | bytes 24584 | tf_op jit(solution)/shard_map/ppermute | solution.py:398
  179.6 7.6 %collective-permute-start.37 = (f32[8,4096]{1,0:T(8,128)S(1)}, f32[8,4096]{1,0:T(8,128)S(1)}, u32[]{:S(2)}, u32[]{:S(2)}) collective-permute-start(f32[8,4096]{1,0:T(8,128)S(1)} %get-tuple-element.113), channel_id=1, source_target_pairs={{0,1},{1,0},{2,3},{3,2},{4,5},{5,4},{6,7},{7,6},{8,9},{9,8},{10,11... | collective-permute-start | bytes 393224 | tf_op jit(solution)/shard_map/ppermute | solution.py:398
  179.8 21.2 %all-to-all-start.6 = ((f32[256,2,128]{2,1,0:T(2,128)}), f32[256,2,128]{2,1,0:T(2,128)S(1)}, u32[]{:S(2)}, u32[]{:S(2)}) async-start(f32[256,2,128]{2,1,0:T(2,128)} %bitcast.17), calls=%async_computation.6 | async-start | bytes 524288 | tf_op jit(solution)/shard_map/all_to_all | solution.py:587
  (18 other events, 62.1 us)

commit v5 on v4

--- a/solution.py
+++ b/solution.py
@@ -78,21 +78,21 @@
         copy.wait()
 
 
-def offer_kernel(per_dev, n_orb, ids_ref, dev_ref, occupied_ref, *refs):
-    plan_ref, same_ref, offer_ref, fixed_ref, sem, fixed_sem = refs
+def offer_kernel(per_dev, n_orb, ids_ref, dev_ref, occupied_ref, plan_ref, same_ref, offer_ref, sem):
     plan(per_dev, n_orb, ids_ref, dev_ref, plan_ref)
     same_ref[0] = plan_ref[SAME]
+    core = plan_ref[DEV] % 2
+    run(copies(lambda at, n: occupied_ref.at[plan_ref[SLOT], pl.ds(at, n), 1 - core], offer_ref, sem))
+
+
+def fixed_kernel(n_orb, plan_ref, occupied_ref, fixed_ref, sem):
     dev = plan_ref[DEV]
     core = dev % 2
-
-    def plane(slot):
-        return lambda at, n: occupied_ref.at[slot, pl.ds(at, n), 1 - core]
+    slot = core * (occupied_ref.shape[0] - 1)
 
     @pl.when(jnp.logical_or(dev == 0, dev == n_orb - 1))
     def _():
-        run(copies(plane(core * (occupied_ref.shape[0] - 1)), fixed_ref, fixed_sem))
-
-    run(copies(plane(plan_ref[SLOT]), offer_ref, sem))
+        run(copies(lambda at, n: occupied_ref.at[slot, pl.ds(at, n), 1 - core], fixed_ref, sem))
 
 
 def pick_kernel(plan_ref, occupied_ref, offer_ref, out_ref, sem):
@@ -405,12 +405,12 @@
 
     plane_shape = shape((blk_rows, rows_y, rows_z), jnp.bfloat16)
     piece_shape = shape((2 * share, rows_y, rows_z), jnp.bfloat16)
-    plan, same, offer, fixed = call(
+    plan, same, offer = call(
         functools.partial(offer_kernel, per_dev, n_orb),
-        (shape((TABLE + nproj * chips,), jnp.int32), shape((1,), jnp.int32), plane_shape, plane_shape),
+        (shape((TABLE + nproj * chips,), jnp.int32), shape((1,), jnp.int32), plane_shape),
         [SMEM, SMEM, ANY],
-        (SMEM, SMEM, VMEM, VMEM),
-        four * 2,
+        (SMEM, SMEM, VMEM),
+        four,
     )(block_ids, o.astype(jnp.int32).reshape(1), occupied)
     offer = permute(offer, swap_core)
 
@@ -422,9 +422,8 @@
     )
     rhs_up, rhs_down = permute(rhs_b, up_y), permute(rhs_b, down_y)
 
-    offer = call(pick_kernel, plane_shape, [SMEM, ANY, VMEM], VMEM, four)(plan, occupied, offer)
+    fixed = call(functools.partial(fixed_kernel, n_orb), plane_shape, [SMEM, ANY], VMEM, four)(plan, occupied)
     fixed = permute(fixed, [(0, 1), (n_orb - 1, n_orb - 2)])
-    offer, fixed = lax.optimization_barrier((offer, fixed))
     pieces = call(
         functools.partial(pieces_kernel, n_orb),
         [piece_shape] * ring,
@@ -432,6 +431,8 @@
         [VMEM] * ring,
         (pltpu.SemaphoreType.DMA((ring,)),),
     )(plan, occupied, fixed)
+    offer, *pieces = lax.optimization_barrier((offer, *pieces))
+    offer = call(pick_kernel, plane_shape, [SMEM, ANY, VMEM], VMEM, four)(plan, occupied, offer)
 
     got = [pieces[0]]
     for s in range(1, ring):

time: 204 us -> 202 us (level)
  waiting for transfers between devices: 59.7 us -> 56.7 us
  starting transfers between devices: 82.8 us -> 84.9 us
    ppermute x35, waiting for transfers between devices: 15.7 us -> 12.6 us  [permute(): return lax.ppermute(value, 'orb', pairs)]
    unnamed x53 -> x55, local copies, waits for them, and re-layouts: 10.9 us -> 10.2 us
  transfers between devices with their start and end apart: 42 -> 42, of which waited for: 12 -> 13; matrix products, arithmetic and copies ran while one was open for 5% -> 5% of each run, Pallas kernels for 6% -> 5%
where the time goes in v5:
time: 202 us; the launch traced here: 201 us
  starting transfers between devices  84.9 us (42%)
  waiting for transfers between devices  56.7 us (28%)
  Pallas kernels  23.2 us (11%)
  blocking collectives  16.9 us (8%)
  local copies, waits for them, and re-layouts  13.4 us (7%)
  other arithmetic  3.97 us (2%)
    ppermute x35, starting transfers between devices, permute(): return lax.ppermute(value, 'orb', pairs)  46.6 us
    all_to_all x1, blocking collectives, per_device(): parts = lax.all_to_all(spread, 'dom', 0, 0, tiled=True)  16.9 us
    all_to_all x1, waiting for transfers between devices, per_device(): lax.all_to_all(raw.reshape((n_dom * n_orb,) + raw.shape[2:]), ('dom', 'or...  13 us
    ppermute x35, waiting for transfers between devices, permute(): return lax.ppermute(value, 'orb', pairs)  12.6 us
    all_to_all x1, waiting for transfers between devices, per_device(): parts = lax.all_to_all(spread, 'dom', 0, 0, tiled=True)  12.1 us
    ppermute x2, waiting for transfers between devices, per_device(): off = lax.ppermute(x_b, ('dom', 'orb'), across)  11.2 us
    all_to_all x1, starting transfers between devices, per_device(): lax.all_to_all(call(spread_shares_kernel, spread_shape)(parts), 'dom', 0,...  10.5 us
    unnamed x55, local copies, waits for them, and re-layouts  10.2 us
  transfers between devices with their start and end apart: 42, of which 13 were waited for; matrix products, arithmetic and copies ran while one was open for 5% of the time, Pallas kernels for 5%

profile of v5, /device:TPU:1, one launch (start us, length us, event | category | flops | bytes accessed | tf_op | source)
XLA Modules:
  0.0 201.2 jit_solution(9208623941080138903)
XLA Ops:
  1.3 3.2 %shard_map.121 = (s32[40]{0:T(128)S(1)}, s32[1]{0:T(128)}, bf16[128,32,128]{2,1,0:T(8,128)(2,1)}) custom-call(s32[4]{0:T(128)S(1)} %copy-done.11, s32[1]{0:T(128)} %bitcast.6.dev_ref, bf16[2,128,2,32,128]{4,3,2,1,0:T(8,128)(2,1)} %occupied_ref.7), custom_call_target="tpu_custom_call" | custom-call | tf_op jit(solution)/shard_map/pallas_call | solution.py:408
  4.6 1.6 shard_map.124
  6.1 1.3 collective-permute-start.5
  7.4 3.5 %collective-permute-start.4 = (bf16[128,32,128]{2,1,0:T(8,128)(2,1)}, bf16[128,32,128]{2,1,0:T(8,128)(2,1)S(1)}, u32[]{:S(2)}, u32[]{:S(2)}) collective-permute-start(bf16[128,32,128]{2,1,0:T(8,128)(2,1)} %get-tuple-element.72), channel_id=1, source_target_pairs={{0,1},{1,0},{2,3},{3,2},{4,5},{5,4},{6,7},{7,6},{8,9},{9,8},{10,11... | collective-permute-start | bytes 3145736 | tf_op jit(solution)/shard_map/ppermute | solution.py:398
  14.5 2.7 %collective-permute-start.3 = (bf16[16,4096]{1,0:T(8,128)(2,1)S(1)}, bf16[16,4096]{1,0:T(8,128)(2,1)}, u32[]{:S(2)}, u32[]{:S(2)}) collective-permute-start(bf16[16,4096]{1,0:T(8,128)(2,1)S(1)} %get-tuple-element.71), channel_id=1, source_target_pairs={{0,6},{1,7},{2,0},{3,1},{4,2},{5,3},{6,4},{7,5},{8,14},{9,15},{10,... | collective-permute-start | bytes 393224 | tf_op jit(solution)/shard_map/ppermute | solution.py:398
  17.1 1.4 shard_map.125
  18.5 1.3 collective-permute-start.6
  19.9 1.6 shard_map.127
  21.6 4.6 %all-to-all-start.1 = ((bf16[8,16,32,128]{3,2,1,0:T(8,128)(2,1)}), bf16[8,16,32,128]{3,2,1,0:T(8,128)(2,1)S(1)}, u32[]{:S(2)}, u32[]{:S(2)}) async-start(bf16[8,16,32,128]{3,2,1,0:T(8,128)(2,1)} %bitcast.7), calls=%async_computation.1 | async-start | bytes 2097152 | tf_op jit(solution)/shard_map/all_to_all | solution.py:453
  26.1 4.9 %collective-permute-start.11 = (bf16[32,32,128]{2,1,0:T(8,128)(2,1)}, bf16[32,32,128]{2,1,0:T(8,128)(2,1)S(1)}, u32[]{:S(2)}, u32[]{:S(2)}) collective-permute-start(bf16[32,32,128]{2,1,0:T(8,128)(2,1)} %copy-done.14), channel_id=1, source_target_pairs={{0,4},{1,5},{14,10},{15,11},{16,20},{17,21},{30,26},{31,27},{32,36... | collective-permute-start | bytes 786440 | tf_op jit(solution)/shard_map/ppermute | solution.py:398
  31.1 1.3 collective-permute-start.12
  36.0 6.3 %collective-permute-done.11.refs_2_ = bf16[32,32,128]{2,1,0:T(8,128)(2,1)S(1)} collective-permute-done((bf16[32,32,128]{2,1,0:T(8,128)(2,1)}, bf16[32,32,128]{2,1,0:T(8,128)(2,1)S(1)}, u32[]{:S(2)}, u32[]{:S(2)}) %collective-permute-start.11) | collective-permute-done | bytes 262176 | tf_op jit(solution)/shard_map/ppermute | solution.py:398
  43.6 2.2 %collective-permute-done.9 = bf16[8,4096]{1,0:T(8,128)(2,1)S(1)} collective-permute-done((bf16[8,4096]{1,0:T(8,128)(2,1)S(1)}, bf16[8,4096]{1,0:T(8,128)(2,1)S(1)}, u32[]{:S(2)}, u32[]{:S(2)}) %collective-permute-start.9) | collective-permute-done | bytes 65568 | tf_op jit(solution)/shard_map/ppermute | solution.py:398
  45.8 4.6 %collective-permute-start.10 = (bf16[16,4096]{1,0:T(8,128)(2,1)S(1)}, bf16[16,4096]{1,0:T(8,128)(2,1)S(1)}, u32[]{:S(2)}, u32[]{:S(2)}) collective-permute-start(bf16[16,4096]{1,0:T(8,128)(2,1)S(1)} %constant_dynamic-update-slice_fusion.3.refs_2_), channel_id=1, source_target_pairs={{0,8},{1,9},{2,10},{3,11},{4,12},{5,13},{6,14},{7,15},{8,0},{9,1},... | collective-permute-start | bytes 393224 | tf_op jit(solution)/shard_map/ppermute | solution.py:398
  51.3 1.5 collective-permute-start.15
  52.9 2.7 %collective-permute-start.16 = (bf16[32,4096]{1,0:T(8,128)(2,1)S(1)}, bf16[32,4096]{1,0:T(8,128)(2,1)S(1)}, u32[]{:S(2)}, u32[]{:S(2)}) collective-permute-start(bf16[32,4096]{1,0:T(8,128)(2,1)S(1)} %get-tuple-element.87.refs_5_.refs_3_), channel_id=1, source_target_pairs={{0,6},{1,7},{2,0},{3,1},{4,2},{5,3},{6,4},{7,5},{8,14},{9,15},{10,... | collective-permute-start | bytes 786440 | tf_op jit(solution)/shard_map/ppermute | solution.py:398
  55.6 1.3 collective-permute-start.13
  56.8 2.5 %shard_map.129 = f32[16,8,128]{2,1,0:T(8,128)} custom-call(s32[40]{0:T(128)S(1)} %get-tuple-element.68.plan_ref, bf16[48,4096]{1,0:T(8,128)(2,1)S(1)} %constant_dynamic-update-slice_fusion.refs_0_, bf16[48,4096]{1,0:T(8,128)(2,1)} %collective-permute-done.7.refs_1_, bf16[16,4096]{1,0:T(8,128)(2,1)S(1)} %constant_dynamic-update-slice_fusion.3.refs_2_, ...), custom_call_target="tpu_custom_call" | custom-call | tf_op jit(solution)/shard_map/pallas_call | solution.py:489
  59.4 8.3 %all-to-all-start.2 = ((f32[16,8,128]{2,1,0:T(8,128)}), f32[16,8,128]{2,1,0:T(8,128)S(1)}, u32[]{:S(2)}, u32[]{:S(2)}) async-start(f32[16,8,128]{2,1,0:T(8,128)} %shard_map.129), calls=%async_computation.2 | async-start | bytes 131072 | tf_op jit(solution)/shard_map/all_to_all | solution.py:494
  69.3 1.4 collective-permute-start.20
  70.7 1.3 collective-permute-start.21
  72.0 1.5 collective-permute-start.19
  74.3 10.5 %all-to-all-start.3 = ((f32[16,8,512]{2,1,0:T(8,128)}), f32[16,8,512]{2,1,0:T(8,128)S(1)}, u32[]{:S(2)}, u32[]{:S(2)}) async-start(f32[16,8,512]{2,1,0:T(8,128)} %shard_map.131), calls=%async_computation.3 | async-start | bytes 524288 | tf_op jit(solution)/shard_map/all_to_all | solution.py:505
  85.1 2.4 %collective-permute-start.23 = (bf16[16,4096]{1,0:T(8,128)(2,1)S(1)}, bf16[16,4096]{1,0:T(8,128)(2,1)}, u32[]{:S(2)}, u32[]{:S(2)}) collective-permute-start(bf16[16,4096]{1,0:T(8,128)(2,1)S(1)} %slice.27), channel_id=1, source_target_pairs={{0,6},{1,7},{2,0},{3,1},{4,2},{5,3},{6,4},{7,5},{8,14},{9,15},{10,... | collective-permute-start | bytes 393224 | tf_op jit(solution)/shard_map/ppermute | solution.py:398
  88.3 7.8 %all-to-all-done.3.parts_ref = f32[16,8,512]{2,1,0:T(8,128)S(1)} async-done(((f32[16,8,512]{2,1,0:T(8,128)}), f32[16,8,512]{2,1,0:T(8,128)S(1)}, u32[]{:S(2)}, u32[]{:S(2)}) %all-to-all-start.3) | async-done | bytes 262176 | tf_op jit(solution)/shard_map/all_to_all | solution.py:505
  96.1 3.3 %collective-permute-start.17 = (bf16[16,256]{1,0:T(8,128)(2,1)S(1)}, bf16[16,256]{1,0:T(8,128)(2,1)S(1)}, u32[]{:S(2)}, u32[]{:S(2)}) collective-permute-start(bf16[16,256]{1,0:T(8,128)(2,1)S(1)} %shard_map.132.mine_ref), channel_id=1, source_target_pairs={{0,1},{1,0},{2,3},{3,2},{4,5},{5,4},{6,7},{7,6},{8,9},{9,8},{10,11... | collective-permute-start | bytes 24584 | tf_op jit(solution)/shard_map/ppermute | solution.py:398
  99.6 1.2 pad_maximum_fusion.refs_7_
  100.9 1.3 collective-permute-start.27
  102.6 2.5 %collective-permute-start.25 = (bf16[32,4096]{1,0:T(8,128)(2,1)S(1)}, bf16[32,4096]{1,0:T(8,128)(2,1)S(1)}, u32[]{:S(2)}, u32[]{:S(2)}) collective-permute-start(bf16[32,4096]{1,0:T(8,128)(2,1)S(1)} %slice.29), channel_id=1, source_target_pairs={{0,6},{1,7},{2,0},{3,1},{4,2},{5,3},{6,4},{7,5},{8,14},{9,15},{10,... | collective-permute-start | bytes 786440 | tf_op jit(solution)/shard_map/ppermute | solution.py:398
  109.1 1.4 shard_map.133
  111.6 1.5 collective-permute-start.28
  113.1 2.0 collective-permute-start.29
  115.1 5.8 %collective-permute-done.29.off_ref = bf16[16,4096]{1,0:T(8,128)(2,1)S(1)} collective-permute-done((bf16[16,4096]{1,0:T(8,128)(2,1)S(1)}, bf16[16,4096]{1,0:T(8,128)(2,1)S(1)}, u32[]{:S(2)}, u32[]{:S(2)}) %collective-permute-start.29) | collective-permute-done | bytes 131104 | tf_op jit(solution)/shard_map/ppermute | solution.py:567
  120.9 1.2 shard_map.135
  123.4 16.9 %all_to_all.34.parts_ref = f32[16,8,512]{2,1,0:T(8,128)S(1)} all-to-all(f32[16,8,512]{2,1,0:T(8,128)S(1)} %shard_map.136), channel_id=1, replica_groups=mesh['dom'=16,'orb'=16] {'dom'}, dimensions={0} | all-to-all | bytes 524288 | tf_op jit(solution)/shard_map/all_to_all | solution.py:574
  140.4 1.9 collective-permute-start.31
  144.2 2.5 %collective-permute-start.33 = (bf16[16,4096]{1,0:T(8,128)(2,1)S(1)}, bf16[16,4096]{1,0:T(8,128)(2,1)S(1)}, u32[]{:S(2)}, u32[]{:S(2)}) collective-permute-start(bf16[16,4096]{1,0:T(8,128)(2,1)S(1)} %get-tuple-element.109), channel_id=1, source_target_pairs={{1,16},{16,1},{3,18},{18,3},{5,20},{20,5},{7,22},{22,7},{9,24},{24... | collective-permute-start | bytes 393224 | tf_op jit(solution)/shard_map/ppermute | solution.py:567
  146.6 5.4 %collective-permute-done.33.off_ref = bf16[16,4096]{1,0:T(8,128)(2,1)S(1)} collective-permute-done((bf16[16,4096]{1,0:T(8,128)(2,1)S(1)}, bf16[16,4096]{1,0:T(8,128)(2,1)S(1)}, u32[]{:S(2)}, u32[]{:S(2)}) %collective-permute-start.33) | collective-permute-done | bytes 131104 | tf_op jit(solution)/shard_map/ppermute | solution.py:567
  152.1 1.2 shard_map.139
  153.3 1.2 collective-permute-done.34.other_ref
  155.3 4.5 %all-to-all-start.5 = ((f32[16,8,512]{2,1,0:T(8,128)}), f32[16,8,512]{2,1,0:T(8,128)S(1)}, u32[]{:S(2)}, u32[]{:S(2)}) async-start(f32[16,8,512]{2,1,0:T(8,128)} %shard_map.140), calls=%async_computation.5 | async-start | bytes 524288 | tf_op jit(solution)/shard_map/all_to_all | solution.py:574
  160.5 12.1 %all-to-all-done.5.parts_ref = f32[16,8,512]{2,1,0:T(8,128)S(1)} async-done(((f32[16,8,512]{2,1,0:T(8,128)}), f32[16,8,512]{2,1,0:T(8,128)S(1)}, u32[]{:S(2)}, u32[]{:S(2)}) %all-to-all-start.5) | async-done | bytes 262176 | tf_op jit(solution)/shard_map/all_to_all | solution.py:574
  172.6 1.7 collective-permute-start.35
  175.3 1.6 copy-done.1
  176.9 1.4 shard_map.144
  178.5 6.0 %all-to-all-start.6 = ((f32[256,2,128]{2,1,0:T(2,128)}), f32[256,2,128]{2,1,0:T(2,128)S(1)}, u32[]{:S(2)}, u32[]{:S(2)}) async-start(f32[256,2,128]{2,1,0:T(2,128)} %bitcast.17), calls=%async_computation.6 | async-start | bytes 524288 | tf_op jit(solution)/shard_map/all_to_all | solution.py:588
  186.7 13.0 %all-to-all-done.6.terms_ref = f32[256,2,128]{2,1,0:T(2,128)S(1)} async-done(((f32[256,2,128]{2,1,0:T(2,128)}), f32[256,2,128]{2,1,0:T(2,128)S(1)}, u32[]{:S(2)}, u32[]{:S(2)}) %all-to-all-start.6) | async-done | bytes 262176 | tf_op jit(solution)/shard_map/all_to_all | solution.py:588
  199.7 1.5 shard_map.146
  (156 shorter events, 26.6 us)
Async XLA Ops:
  4.5 7.4 %copy-start.23 = (s32[16]{0:T(128)S(1)}, s32[16]{0:T(128)}, u32[]{:S(2)}) copy-start(s32[16]{0:T(128)} %constant.141.clone) | copy-start | bytes 196
  6.1 11.0 %collective-permute-start.5 = (bf16[128,32,128]{2,1,0:T(8,128)(2,1)}, bf16[128,32,128]{2,1,0:T(8,128)(2,1)S(1)}, u32[]{:S(2)}, u32[]{:S(2)}) collective-permute-start(bf16[128,32,128]{2,1,0:T(8,128)(2,1)} %shard_map.124), channel_id=1, source_target_pairs={{0,1},{15,14},{16,17},{31,30},{32,33},{47,46},{48,49},{63,62},{64,... | collective-permute-start | bytes 3145736 | tf_op jit(solution)/shard_map/ppermute | solution.py:398
  7.4 11.1 %collective-permute-start.4 = (bf16[128,32,128]{2,1,0:T(8,128)(2,1)}, bf16[128,32,128]{2,1,0:T(8,128)(2,1)S(1)}, u32[]{:S(2)}, u32[]{:S(2)}) collective-permute-start(bf16[128,32,128]{2,1,0:T(8,128)(2,1)} %get-tuple-element.72), channel_id=1, source_target_pairs={{0,1},{1,0},{2,3},{3,2},{4,5},{5,4},{6,7},{7,6},{8,9},{9,8},{10,11... | collective-permute-start | bytes 3145736 | tf_op jit(solution)/shard_map/ppermute | solution.py:398
  11.1 3.3 %collective-permute-start.1 = (f32[8,4096]{1,0:T(8,128)S(1)}, f32[8,4096]{1,0:T(8,128)S(1)}, u32[]{:S(2)}, u32[]{:S(2)}) collective-permute-start(f32[8,4096]{1,0:T(8,128)S(1)} %get-tuple-element.70), channel_id=1, source_target_pairs={{0,1},{1,0},{2,3},{3,2},{4,5},{5,4},{6,7},{7,6},{8,9},{9,8},{10,11... | collective-permute-start | bytes 393224 | tf_op jit(solution)/shard_map/ppermute | solution.py:398
  11.4 41.4 %collective-permute-start.18 = (f32[8,1]{0,1:T(1,128)S(1)}, f32[8,1]{0,1:T(1,128)S(1)}, u32[]{:S(2)}, u32[]{:S(2)}) collective-permute-start(f32[8,1]{0,1:T(1,128)S(1)} %bitcast.41), channel_id=1, source_target_pairs={{0,1},{1,0},{2,3},{3,2},{4,5},{5,4},{6,7},{7,6},{8,9},{9,8},{10,11... | collective-permute-start | bytes 104 | tf_op jit(solution)/shard_map/ppermute | solution.py:398
  14.4 16.7 %collective-permute-start.2 = (bf16[16,4096]{1,0:T(8,128)(2,1)S(1)}, bf16[16,4096]{1,0:T(8,128)(2,1)}, u32[]{:S(2)}, u32[]{:S(2)}) collective-permute-start(bf16[16,4096]{1,0:T(8,128)(2,1)S(1)} %get-tuple-element.71), channel_id=1, source_target_pairs={{0,2},{1,3},{2,4},{3,5},{4,6},{5,7},{6,0},{7,1},{8,10},{9,11},{10,... | collective-permute-start | bytes 393224 | tf_op jit(solution)/shard_map/ppermute | solution.py:398
  14.5 17.9 %collective-permute-start.3 = (bf16[16,4096]{1,0:T(8,128)(2,1)S(1)}, bf16[16,4096]{1,0:T(8,128)(2,1)}, u32[]{:S(2)}, u32[]{:S(2)}) collective-permute-start(bf16[16,4096]{1,0:T(8,128)(2,1)S(1)} %get-tuple-element.71), channel_id=1, source_target_pairs={{0,6},{1,7},{2,0},{3,1},{4,2},{5,3},{6,4},{7,5},{8,14},{9,15},{10,... | collective-permute-start | bytes 393224 | tf_op jit(solution)/shard_map/ppermute | solution.py:398
  18.5 13.8 %collective-permute-start.6 = (bf16[32,32,128]{2,1,0:T(8,128)(2,1)}, bf16[32,32,128]{2,1,0:T(8,128)(2,1)S(1)}, u32[]{:S(2)}, u32[]{:S(2)}) collective-permute-start(bf16[32,32,128]{2,1,0:T(8,128)(2,1)} %get-tuple-element.77), channel_id=1, source_target_pairs={{0,2},{1,3},{14,8},{15,9},{16,18},{17,19},{30,24},{31,25},{32,34},... | collective-permute-start | bytes 786440 | tf_op jit(solution)/shard_map/ppermute | solution.py:398
  21.5 9.5 %copy-start.13 = (bf16[32,32,128]{2,1,0:T(8,128)(2,1)S(1)}, bf16[32,32,128]{2,1,0:T(8,128)(2,1)}, u32[]{:S(2)}) copy-start(bf16[32,32,128]{2,1,0:T(8,128)(2,1)} %copy-done.12) | copy-start | bytes 786436
  21.5 28.9 %copy-start.18 = (bf16[16,32,128]{2,1,0:T(8,128)(2,1)S(1)}, bf16[16,32,128]{2,1,0:T(8,128)(2,1)}, u32[]{:S(2)}) copy-start(bf16[16,32,128]{2,1,0:T(8,128)(2,1)} %copy-done.17) | copy-start | bytes 393220
  21.6 28.9 %all-to-all-start.1 = ((bf16[8,16,32,128]{3,2,1,0:T(8,128)(2,1)}), bf16[8,16,32,128]{3,2,1,0:T(8,128)(2,1)S(1)}, u32[]{:S(2)}, u32[]{:S(2)}) async-start(bf16[8,16,32,128]{3,2,1,0:T(8,128)(2,1)} %bitcast.7), calls=%async_computation.1 | async-start | bytes 2097152 | tf_op jit(solution)/shard_map/all_to_all | solution.py:453
  26.1 16.2 %collective-permute-start.11 = (bf16[32,32,128]{2,1,0:T(8,128)(2,1)}, bf16[32,32,128]{2,1,0:T(8,128)(2,1)S(1)}, u32[]{:S(2)}, u32[]{:S(2)}) collective-permute-start(bf16[32,32,128]{2,1,0:T(8,128)(2,1)} %copy-done.14), channel_id=1, source_target_pairs={{0,4},{1,5},{14,10},{15,11},{16,20},{17,21},{30,26},{31,27},{32,36... | collective-permute-start | bytes 786440 | tf_op jit(solution)/shard_map/ppermute | solution.py:398
  31.1 11.8 %collective-permute-start.12 = (bf16[32,32,128]{2,1,0:T(8,128)(2,1)S(1)}, bf16[32,32,128]{2,1,0:T(8,128)(2,1)S(1)}, u32[]{:S(2)}, u32[]{:S(2)}) collective-permute-start(bf16[32,32,128]{2,1,0:T(8,128)(2,1)S(1)} %copy-done.13), channel_id=1, source_target_pairs={{0,6},{1,7},{14,12},{15,13},{16,22},{17,23},{30,28},{31,29},{32,38... | collective-permute-start | bytes 786440 | tf_op jit(solution)/shard_map/ppermute | solution.py:398
  34.1 9.5 %collective-permute-start.8 = (bf16[8,4096]{1,0:T(8,128)(2,1)S(1)}, bf16[8,4096]{1,0:T(8,128)(2,1)S(1)}, u32[]{:S(2)}, u32[]{:S(2)}) collective-permute-start(bf16[8,4096]{1,0:T(8,128)(2,1)S(1)} %slice.24), channel_id=1, source_target_pairs={{0,2},{1,3},{2,4},{3,5},{4,6},{5,7},{6,0},{7,1},{8,10},{9,11},{10,... | collective-permute-start | bytes 196616 | tf_op jit(solution)/shard_map/ppermute | solution.py:398
  36.0 20.8 %collective-permute-start.7 = (bf16[48,4096]{1,0:T(8,128)(2,1)S(1)}, bf16[48,4096]{1,0:T(8,128)(2,1)}, u32[]{:S(2)}, u32[]{:S(2)}) collective-permute-start(bf16[48,4096]{1,0:T(8,128)(2,1)S(1)} %constant_dynamic-update-slice_fusion.refs_0_), channel_id=1, source_target_pairs={{0,8},{1,9},{2,10},{3,11},{4,12},{5,13},{6,14},{7,15},{8,0},{9,1},... | collective-permute-start | bytes 1179656 | tf_op jit(solution)/shard_map/ppermute | solution.py:398
  42.3 3.5 %collective-permute-start.9 = (bf16[8,4096]{1,0:T(8,128)(2,1)S(1)}, bf16[8,4096]{1,0:T(8,128)(2,1)S(1)}, u32[]{:S(2)}, u32[]{:S(2)}) collective-permute-start(bf16[8,4096]{1,0:T(8,128)(2,1)S(1)} %slice.25), channel_id=1, source_target_pairs={{0,6},{1,7},{2,0},{3,1},{4,2},{5,3},{6,4},{7,5},{8,14},{9,15},{10,... | collective-permute-start | bytes 196616 | tf_op jit(solution)/shard_map/ppermute | solution.py:398
  45.8 9.7 %collective-permute-start.10 = (bf16[16,4096]{1,0:T(8,128)(2,1)S(1)}, bf16[16,4096]{1,0:T(8,128)(2,1)S(1)}, u32[]{:S(2)}, u32[]{:S(2)}) collective-permute-start(bf16[16,4096]{1,0:T(8,128)(2,1)S(1)} %constant_dynamic-update-slice_fusion.3.refs_2_), channel_id=1, source_target_pairs={{0,8},{1,9},{2,10},{3,11},{4,12},{5,13},{6,14},{7,15},{8,0},{9,1},... | collective-permute-start | bytes 393224 | tf_op jit(solution)/shard_map/ppermute | solution.py:398
  51.2 16.5 %collective-permute-start.14 = (bf16[32,4096]{1,0:T(8,128)(2,1)S(1)}, bf16[32,4096]{1,0:T(8,128)(2,1)S(1)}, u32[]{:S(2)}, u32[]{:S(2)}) collective-permute-start(bf16[32,4096]{1,0:T(8,128)(2,1)S(1)} %get-tuple-element.87.refs_5_.refs_3_), channel_id=1, source_target_pairs={{0,8},{1,9},{2,10},{3,11},{4,12},{5,13},{6,14},{7,15},{8,0},{9,1},... | collective-permute-start | bytes 786440 | tf_op jit(solution)/shard_map/ppermute | solution.py:398
  51.3 17.1 %collective-permute-start.15 = (bf16[32,4096]{1,0:T(8,128)(2,1)S(1)}, bf16[32,4096]{1,0:T(8,128)(2,1)S(1)}, u32[]{:S(2)}, u32[]{:S(2)}) collective-permute-start(bf16[32,4096]{1,0:T(8,128)(2,1)S(1)} %get-tuple-element.87.refs_5_.refs_3_), channel_id=1, source_target_pairs={{0,2},{1,3},{2,4},{3,5},{4,6},{5,7},{6,0},{7,1},{8,10},{9,11},{10,... | collective-permute-start | bytes 786440 | tf_op jit(solution)/shard_map/ppermute | solution.py:398
  52.9 15.6 %collective-permute-start.16 = (bf16[32,4096]{1,0:T(8,128)(2,1)S(1)}, bf16[32,4096]{1,0:T(8,128)(2,1)S(1)}, u32[]{:S(2)}, u32[]{:S(2)}) collective-permute-start(bf16[32,4096]{1,0:T(8,128)(2,1)S(1)} %get-tuple-element.87.refs_5_.refs_3_), channel_id=1, source_target_pairs={{0,6},{1,7},{2,0},{3,1},{4,2},{5,3},{6,4},{7,5},{8,14},{9,15},{10,... | collective-permute-start | bytes 786440 | tf_op jit(solution)/shard_map/ppermute | solution.py:398
  55.6 12.2 %collective-permute-start.13 = (bf16[32,4096]{1,0:T(8,128)(2,1)S(1)}, bf16[32,4096]{1,0:T(8,128)(2,1)S(1)}, u32[]{:S(2)}, u32[]{:S(2)}) collective-permute-start(bf16[32,4096]{1,0:T(8,128)(2,1)S(1)} %get-tuple-element.86.refs_4_.refs_0_), channel_id=1, source_target_pairs={{0,8},{1,9},{2,10},{3,11},{4,12},{5,13},{6,14},{7,15},{8,0},{9,1},... | collective-permute-start | bytes 786440 | tf_op jit(solution)/shard_map/ppermute | solution.py:398
  59.4 14.1 %all-to-all-start.2 = ((f32[16,8,128]{2,1,0:T(8,128)}), f32[16,8,128]{2,1,0:T(8,128)S(1)}, u32[]{:S(2)}, u32[]{:S(2)}) async-start(f32[16,8,128]{2,1,0:T(8,128)} %shard_map.129), calls=%async_computation.2 | async-start | bytes 131072 | tf_op jit(solution)/shard_map/all_to_all | solution.py:494
  69.3 33.3 %copy-start.6 = (bf16[64,4096]{1,0:T(8,128)(2,1)}, bf16[64,4096]{1,0:T(8,128)(2,1)S(1)}, u32[]{:S(2)}) copy-start(bf16[64,4096]{1,0:T(8,128)(2,1)S(1)} %get-tuple-element.94.refs_0_) | copy-start | bytes 1572868
  69.3 30.2 %collective-permute-start.20 = (bf16[64,4096]{1,0:T(8,128)(2,1)S(1)}, bf16[64,4096]{1,0:T(8,128)(2,1)S(1)}, u32[]{:S(2)}, u32[]{:S(2)}) collective-permute-start(bf16[64,4096]{1,0:T(8,128)(2,1)S(1)} %get-tuple-element.94.refs_0_), channel_id=1, source_target_pairs={{0,2},{1,3},{2,4},{3,5},{4,6},{5,7},{6,0},{7,1},{8,10},{9,11},{10,... | collective-permute-start | bytes 1572872 | tf_op jit(solution)/shard_map/ppermute | solution.py:398
  70.7 28.8 %collective-permute-start.21 = (bf16[64,4096]{1,0:T(8,128)(2,1)S(1)}, bf16[64,4096]{1,0:T(8,128)(2,1)S(1)}, u32[]{:S(2)}, u32[]{:S(2)}) collective-permute-start(bf16[64,4096]{1,0:T(8,128)(2,1)S(1)} %get-tuple-element.94.refs_0_), channel_id=1, source_target_pairs={{0,6},{1,7},{2,0},{3,1},{4,2},{5,3},{6,4},{7,5},{8,14},{9,15},{10,... | collective-permute-start | bytes 1572872 | tf_op jit(solution)/shard_map/ppermute | solution.py:398
  72.0 27.5 %collective-permute-start.19 = (bf16[64,4096]{1,0:T(8,128)(2,1)}, bf16[64,4096]{1,0:T(8,128)(2,1)}, u32[]{:S(2)}, u32[]{:S(2)}) collective-permute-start(bf16[64,4096]{1,0:T(8,128)(2,1)} %get-tuple-element.91.refs_4_), channel_id=1, source_target_pairs={{0,8},{1,9},{2,10},{3,11},{4,12},{5,13},{6,14},{7,15},{8,0},{9,1},... | collective-permute-start | bytes 1572872 | tf_op jit(solution)/shard_map/ppermute | solution.py:398
  74.3 21.8 %all-to-all-start.3 = ((f32[16,8,512]{2,1,0:T(8,128)}), f32[16,8,512]{2,1,0:T(8,128)S(1)}, u32[]{:S(2)}, u32[]{:S(2)}) async-start(f32[16,8,512]{2,1,0:T(8,128)} %shard_map.131), calls=%async_computation.3 | async-start | bytes 524288 | tf_op jit(solution)/shard_map/all_to_all | solution.py:505
  84.8 11.4 %collective-permute-start.22 = (bf16[16,4096]{1,0:T(8,128)(2,1)S(1)}, bf16[16,4096]{1,0:T(8,128)(2,1)}, u32[]{:S(2)}, u32[]{:S(2)}) collective-permute-start(bf16[16,4096]{1,0:T(8,128)(2,1)S(1)} %slice.26), channel_id=1, source_target_pairs={{0,2},{1,3},{2,4},{3,5},{4,6},{5,7},{6,0},{7,1},{8,10},{9,11},{10,... | collective-permute-start | bytes 393224 | tf_op jit(solution)/shard_map/ppermute | solution.py:398
  85.1 14.4 %collective-permute-start.23 = (bf16[16,4096]{1,0:T(8,128)(2,1)S(1)}, bf16[16,4096]{1,0:T(8,128)(2,1)}, u32[]{:S(2)}, u32[]{:S(2)}) collective-permute-start(bf16[16,4096]{1,0:T(8,128)(2,1)S(1)} %slice.27), channel_id=1, source_target_pairs={{0,6},{1,7},{2,0},{3,1},{4,2},{5,3},{6,4},{7,5},{8,14},{9,15},{10,... | collective-permute-start | bytes 393224 | tf_op jit(solution)/shard_map/ppermute | solution.py:398
  96.1 14.7 %collective-permute-start.17 = (bf16[16,256]{1,0:T(8,128)(2,1)S(1)}, bf16[16,256]{1,0:T(8,128)(2,1)S(1)}, u32[]{:S(2)}, u32[]{:S(2)}) collective-permute-start(bf16[16,256]{1,0:T(8,128)(2,1)S(1)} %shard_map.132.mine_ref), channel_id=1, source_target_pairs={{0,1},{1,0},{2,3},{3,2},{4,5},{5,4},{6,7},{7,6},{8,9},{9,8},{10,11... | collective-permute-start | bytes 24584 | tf_op jit(solution)/shard_map/ppermute | solution.py:398
  99.5 11.0 %collective-permute-start.26 = (bf16[16,4096]{1,0:T(8,128)(2,1)}, bf16[16,4096]{1,0:T(8,128)(2,1)S(1)}, u32[]{:S(2)}, u32[]{:S(2)}) collective-permute-start(bf16[16,4096]{1,0:T(8,128)(2,1)} %collective-permute-done.22), channel_id=1, source_target_pairs={{0,8},{1,9},{2,10},{3,11},{4,12},{5,13},{6,14},{7,15},{8,0},{9,1},... | collective-permute-start | bytes 393224 | tf_op jit(solution)/shard_map/ppermute | solution.py:398
  100.9 9.7 %collective-permute-start.27 = (bf16[16,4096]{1,0:T(8,128)(2,1)}, bf16[16,4096]{1,0:T(8,128)(2,1)S(1)}, u32[]{:S(2)}, u32[]{:S(2)}) collective-permute-start(bf16[16,4096]{1,0:T(8,128)(2,1)} %collective-permute-done.23), channel_id=1, source_target_pairs={{0,8},{1,9},{2,10},{3,11},{4,12},{5,13},{6,14},{7,15},{8,0},{9,1},... | collective-permute-start | bytes 393224 | tf_op jit(solution)/shard_map/ppermute | solution.py:398
  102.2 8.6 %collective-permute-start.24 = (bf16[32,4096]{1,0:T(8,128)(2,1)S(1)}, bf16[32,4096]{1,0:T(8,128)(2,1)S(1)}, u32[]{:S(2)}, u32[]{:S(2)}) collective-permute-start(bf16[32,4096]{1,0:T(8,128)(2,1)S(1)} %slice.28), channel_id=1, source_target_pairs={{0,2},{1,3},{2,4},{3,5},{4,6},{5,7},{6,0},{7,1},{8,10},{9,11},{10,... | collective-permute-start | bytes 786440 | tf_op jit(solution)/shard_map/ppermute | solution.py:398
  102.6 8.2 %collective-permute-start.25 = (bf16[32,4096]{1,0:T(8,128)(2,1)S(1)}, bf16[32,4096]{1,0:T(8,128)(2,1)S(1)}, u32[]{:S(2)}, u32[]{:S(2)}) collective-permute-start(bf16[32,4096]{1,0:T(8,128)(2,1)S(1)} %slice.29), channel_id=1, source_target_pairs={{0,6},{1,7},{2,0},{3,1},{4,2},{5,3},{6,4},{7,5},{8,14},{9,15},{10,... | collective-permute-start | bytes 786440 | tf_op jit(solution)/shard_map/ppermute | solution.py:398
  110.6 41.4 %copy-start = (bf16[256,4096]{1,0:T(8,128)(2,1)}, bf16[256,4096]{1,0:T(8,128)(2,1)S(1)}, u32[]{:S(2)}) copy-start(bf16[256,4096]{1,0:T(8,128)(2,1)S(1)} %constant_dynamic-update-slice_fusion.5.refs_2_.second_ref.refs_3_) | copy-start | bytes 6291460
  111.6 9.3 %collective-permute-start.28 = (f32[16,4096]{1,0:T(8,128)S(1)}, f32[16,4096]{1,0:T(8,128)S(1)}, u32[]{:S(2)}, u32[]{:S(2)}) collective-permute-start(f32[16,4096]{1,0:T(8,128)S(1)} %get-tuple-element.103.x_ref.refs_0_), channel_id=1, source_target_pairs={{0,1},{1,0},{2,3},{3,2},{4,5},{5,4},{6,7},{7,6},{8,9},{9,8},{10,11... | collective-permute-start | bytes 786440 | tf_op jit(solution)/shard_map/ppermute | solution.py:398
  113.1 7.8 %collective-permute-start.29 = (bf16[16,4096]{1,0:T(8,128)(2,1)S(1)}, bf16[16,4096]{1,0:T(8,128)(2,1)S(1)}, u32[]{:S(2)}, u32[]{:S(2)}) collective-permute-start(bf16[16,4096]{1,0:T(8,128)(2,1)S(1)} %get-tuple-element.104), channel_id=1, source_target_pairs={{1,16},{16,1},{3,18},{18,3},{5,20},{20,5},{7,22},{22,7},{9,24},{24... | collective-permute-start | bytes 393224 | tf_op jit(solution)/shard_map/ppermute | solution.py:567
  122.2 1.2 collective-permute-start.30
  140.4 2.7 %collective-permute-start.31 = (bf16[16,256]{1,0:T(8,128)(2,1)S(1)}, bf16[16,256]{1,0:T(8,128)(2,1)S(1)}, u32[]{:S(2)}, u32[]{:S(2)}) collective-permute-start(bf16[16,256]{1,0:T(8,128)(2,1)S(1)} %shard_map.137.mine_ref), channel_id=1, source_target_pairs={{0,1},{1,0},{2,3},{3,2},{4,5},{5,4},{6,7},{7,6},{8,9},{9,8},{10,11... | collective-permute-start | bytes 24584 | tf_op jit(solution)/shard_map/ppermute | solution.py:398
  143.7 8.3 %collective-permute-start.32 = (f32[16,4096]{1,0:T(8,128)S(1)}, f32[16,4096]{1,0:T(8,128)S(1)}, u32[]{:S(2)}, u32[]{:S(2)}) collective-permute-start(f32[16,4096]{1,0:T(8,128)S(1)} %get-tuple-element.108.x_ref.refs_0_), channel_id=1, source_target_pairs={{0,1},{1,0},{2,3},{3,2},{4,5},{5,4},{6,7},{7,6},{8,9},{9,8},{10,11... | collective-permute-start | bytes 786440 | tf_op jit(solution)/shard_map/ppermute | solution.py:398
  144.1 15.6 %copy-start.19 = (bf16[8,2,32,128]{3,2,1,0:T(8,128)(2,1)S(1)}, bf16[8,2,32,128]{3,2,1,0:T(8,128)(2,1)}, u32[]{:S(2)}) copy-start(bf16[8,2,32,128]{3,2,1,0:T(8,128)(2,1)} %param.18) | copy-start | bytes 393220
  144.2 7.9 %collective-permute-start.33 = (bf16[16,4096]{1,0:T(8,128)(2,1)S(1)}, bf16[16,4096]{1,0:T(8,128)(2,1)S(1)}, u32[]{:S(2)}, u32[]{:S(2)}) collective-permute-start(bf16[16,4096]{1,0:T(8,128)(2,1)S(1)} %get-tuple-element.109), channel_id=1, source_target_pairs={{1,16},{16,1},{3,18},{18,3},{5,20},{20,5},{7,22},{22,7},{9,24},{24... | collective-permute-start | bytes 393224 | tf_op jit(solution)/shard_map/ppermute | solution.py:567
  153.3 1.2 collective-permute-start.34
  155.3 17.3 %all-to-all-start.5 = ((f32[16,8,512]{2,1,0:T(8,128)}), f32[16,8,512]{2,1,0:T(8,128)S(1)}, u32[]{:S(2)}, u32[]{:S(2)}) async-start(f32[16,8,512]{2,1,0:T(8,128)} %shard_map.140), calls=%async_computation.5 | async-start | bytes 524288 | tf_op jit(solution)/shard_map/all_to_all | solution.py:574
  160.0 15.2 %collective-permute-start.36 = (bf16[8,4096]{1,0:T(8,128)(2,1)S(1)}, bf16[8,4096]{1,0:T(8,128)(2,1)S(1)}, u32[]{:S(2)}, u32[]{:S(2)}) collective-permute-start(bf16[8,4096]{1,0:T(8,128)(2,1)S(1)} %convert_element_type.25), channel_id=1, source_target_pairs={{0,1},{1,0},{2,3},{3,2},{4,5},{5,4},{6,7},{7,6},{8,9},{9,8},{10,11... | collective-permute-start | bytes 196616 | tf_op jit(solution)/shard_map/ppermute | solution.py:398
  172.6 2.6 %collective-permute-start.35 = (bf16[16,256]{1,0:T(8,128)(2,1)S(1)}, bf16[16,256]{1,0:T(8,128)(2,1)S(1)}, u32[]{:S(2)}, u32[]{:S(2)}) collective-permute-start(bf16[16,256]{1,0:T(8,128)(2,1)S(1)} %get-tuple-element.112.mine_ref), channel_id=1, source_target_pairs={{0,1},{1,0},{2,3},{3,2},{4,5},{5,4},{6,7},{7,6},{8,9},{9,8},{10,11... | collective-permute-start | bytes 24584 | tf_op jit(solution)/shard_map/ppermute | solution.py:398
  178.3 7.6 %collective-permute-start.37 = (f32[8,4096]{1,0:T(8,128)S(1)}, f32[8,4096]{1,0:T(8,128)S(1)}, u32[]{:S(2)}, u32[]{:S(2)}) collective-permute-start(f32[8,4096]{1,0:T(8,128)S(1)} %get-tuple-element.117), channel_id=1, source_target_pairs={{0,1},{1,0},{2,3},{3,2},{4,5},{5,4},{6,7},{7,6},{8,9},{9,8},{10,11... | collective-permute-start | bytes 393224 | tf_op jit(solution)/shard_map/ppermute | solution.py:398
  178.5 21.2 %all-to-all-start.6 = ((f32[256,2,128]{2,1,0:T(2,128)}), f32[256,2,128]{2,1,0:T(2,128)S(1)}, u32[]{:S(2)}, u32[]{:S(2)}) async-start(f32[256,2,128]{2,1,0:T(2,128)} %bitcast.17), calls=%async_computation.6 | async-start | bytes 524288 | tf_op jit(solution)/shard_map/all_to_all | solution.py:588
  (19 other events, 57.2 us)

commit v6 on v5

--- a/solution.py
+++ b/solution.py
@@ -439,7 +439,7 @@
         pairs = [(c, 2 * s + c) for c in range(2)]
         pairs += [(n_orb - 2 + c, 2 * (ring + (ring - 1 + s) % ring) + c) for c in range(2)]
         got.append(permute(pieces[s], pairs))
-    rhs_up, rhs_down, got[1] = lax.optimization_barrier((rhs_up, rhs_down, got[1]))
+    rhs_up, rhs_down, *got[1:] = lax.optimization_barrier((rhs_up, rhs_down, *got[1:]))
     rhs_line = jnp.concatenate([rhs_b, rhs_up, rhs_down], axis=0)
     rhs_line_x = permute(rhs_line, swap_x)
     rhs_far = jnp.concatenate(
@@ -511,6 +511,7 @@
     far_up_x, far_down_x = permute(far_up, swap_x), permute(far_down, swap_x)
     own_up = permute(above[: 2 * share], up_y)
     own_down = permute(below[2 * share :], down_y)
+    first_parts, own_up, own_down = lax.optimization_barrier((first_parts, own_up, own_down))
     block_shape = shape((n_rows // 2, cells), jnp.bfloat16)
     blocks = call(functools.partial(pack_kernel, (3, 5)), [block_shape] * 2)(
         own, below, above, ys, line, ys_x, line_x, jnp.concatenate([far_up, far_down], axis=0)

time: 202 us -> 210 us (1.040)
  waiting for transfers between devices: 56.7 us -> 40.2 us
  local copies, waits for them, and re-layouts: 13.4 us -> 21.9 us
  starting transfers between devices: 84.9 us -> 93.3 us
  blocking collectives: 16.9 us -> 22.9 us
    all_to_all x1, waiting for transfers between devices: 7.79 us -> 0.01 us  [per_device(): lax.all_to_all(call(spread_shares_kernel, spread_shape)(parts), 'dom', 0,...]
    all_to_all x1, blocking collectives: 16.9 us -> 22.9 us  [per_device(): parts = lax.all_to_all(spread, 'dom', 0, 0, tiled=True)]
    ppermute x35, waiting for transfers between devices: 12.6 us -> 6.75 us  [permute(): return lax.ppermute(value, 'orb', pairs)]
    unnamed x55 -> x57, local copies, waits for them, and re-layouts: 10.2 us -> 14 us
    ppermute x2, starting transfers between devices: 4.46 us -> 7.76 us  [per_device(): off = lax.ppermute(x_b, ('dom', 'orb'), across)]
    dynamic_update_slice x4, local copies, waits for them, and re-layouts: 0.06 us -> 3.26 us  [per_device(): blocks[k] = lax.dynamic_update_slice(blocks[k], piece, (at, 0))]
    ppermute x2, waiting for transfers between devices: 11.2 us -> 8.28 us  [per_device(): off = lax.ppermute(x_b, ('dom', 'orb'), across)]
    all_to_all x1, starting transfers between devices: 8.28 us -> 11.2 us  [per_device(): parts = lax.all_to_all(parts, 'orb', 0, 0, tiled=True)]
  transfers between devices with their start and end apart: 42 -> 42, of which waited for: 13 -> 8; matrix products, arithmetic and copies ran while one was open for 5% -> 7% of each run, Pallas kernels for 5% -> 5%
where the time goes in v6:
time: 210 us; the launch traced here: 209 us
  starting transfers between devices  93.3 us (44%)
  waiting for transfers between devices  40.2 us (19%)
  Pallas kernels  24.4 us (12%)
  blocking collectives  22.9 us (11%)
  local copies, waits for them, and re-layouts  21.9 us (10%)
  other arithmetic  3.98 us (2%)
    ppermute x35, starting transfers between devices, permute(): return lax.ppermute(value, 'orb', pairs)  49.1 us
    all_to_all x1, blocking collectives, per_device(): parts = lax.all_to_all(spread, 'dom', 0, 0, tiled=True)  22.9 us
    unnamed x57, local copies, waits for them, and re-layouts  14 us
    all_to_all x1, waiting for transfers between devices, per_device(): lax.all_to_all(raw.reshape((n_dom * n_orb,) + raw.shape[2:]), ('dom', 'or...  13.1 us
    all_to_all x1, waiting for transfers between devices, per_device(): parts = lax.all_to_all(spread, 'dom', 0, 0, tiled=True)  12.1 us
    all_to_all x1, starting transfers between devices, per_device(): parts = lax.all_to_all(parts, 'orb', 0, 0, tiled=True)  11.2 us
    all_to_all x1, starting transfers between devices, per_device(): lax.all_to_all(call(spread_shares_kernel, spread_shape)(parts), 'dom', 0,...  10.5 us
    ppermute x2, waiting for transfers between devices, per_device(): off = lax.ppermute(x_b, ('dom', 'orb'), across)  8.28 us
  transfers between devices with their start and end apart: 42, of which 8 were waited for; matrix products, arithmetic and copies ran while one was open for 7% of the time, Pallas kernels for 5%

profile of v6, /device:TPU:1, one launch (start us, length us, event | category | flops | bytes accessed | tf_op | source)
XLA Modules:
  0.0 208.7 jit_solution(18173895751571406389)
XLA Ops:
  1.3 3.2 %shard_map.121 = (s32[40]{0:T(128)S(1)}, s32[1]{0:T(128)}, bf16[128,32,128]{2,1,0:T(8,128)(2,1)}) custom-call(s32[4]{0:T(128)S(1)} %copy-done.15, s32[1]{0:T(128)} %bitcast.6.dev_ref, bf16[2,128,2,32,128]{4,3,2,1,0:T(8,128)(2,1)} %occupied_ref.7), custom_call_target="tpu_custom_call" | custom-call | tf_op jit(solution)/shard_map/pallas_call | solution.py:408
  4.6 1.6 shard_map.124
  6.1 1.3 collective-permute-start.5
  7.4 3.5 %collective-permute-start.4 = (bf16[128,32,128]{2,1,0:T(8,128)(2,1)}, bf16[128,32,128]{2,1,0:T(8,128)(2,1)S(1)}, u32[]{:S(2)}, u32[]{:S(2)}) collective-permute-start(bf16[128,32,128]{2,1,0:T(8,128)(2,1)} %get-tuple-element.77), channel_id=1, source_target_pairs={{0,1},{1,0},{2,3},{3,2},{4,5},{5,4},{6,7},{7,6},{8,9},{9,8},{10,11... | collective-permute-start | bytes 3145736 | tf_op jit(solution)/shard_map/ppermute | solution.py:398
  13.9 2.7 %collective-permute-start.3 = (bf16[16,4096]{1,0:T(8,128)(2,1)S(1)}, bf16[16,4096]{1,0:T(8,128)(2,1)}, u32[]{:S(2)}, u32[]{:S(2)}) collective-permute-start(bf16[16,4096]{1,0:T(8,128)(2,1)S(1)} %get-tuple-element.76), channel_id=1, source_target_pairs={{0,6},{1,7},{2,0},{3,1},{4,2},{5,3},{6,4},{7,5},{8,14},{9,15},{10,... | collective-permute-start | bytes 393224 | tf_op jit(solution)/shard_map/ppermute | solution.py:398
  16.6 1.6 shard_map.125
  18.1 1.3 collective-permute-start.6
  19.5 1.3 collective-permute-start.7
  20.8 1.3 collective-permute-start.8
  22.1 1.6 shard_map.127
  23.8 5.0 %all-to-all-start.1 = ((bf16[8,16,32,128]{3,2,1,0:T(8,128)(2,1)}), bf16[8,16,32,128]{3,2,1,0:T(8,128)(2,1)S(1)}, u32[]{:S(2)}, u32[]{:S(2)}) async-start(bf16[8,16,32,128]{3,2,1,0:T(8,128)(2,1)} %bitcast.7), calls=%async_computation.1 | async-start | bytes 2097152 | tf_op jit(solution)/shard_map/all_to_all | solution.py:453
  30.7 1.7 collective-permute-start.10
  33.2 1.2 collective-permute-start.11
  36.2 8.9 %collective-permute-start.9 = (bf16[48,4096]{1,0:T(8,128)(2,1)S(1)}, bf16[48,4096]{1,0:T(8,128)(2,1)}, u32[]{:S(2)}, u32[]{:S(2)}) collective-permute-start(bf16[48,4096]{1,0:T(8,128)(2,1)S(1)} %constant_dynamic-update-slice_fusion.refs_0_), channel_id=1, source_target_pairs={{0,8},{1,9},{2,10},{3,11},{4,12},{5,13},{6,14},{7,15},{8,0},{9,1},... | collective-permute-start | bytes 1179656 | tf_op jit(solution)/shard_map/ppermute | solution.py:398
  47.6 1.5 collective-permute-start.14
  49.1 1.5 collective-permute-start.15
  51.8 3.4 %collective-permute-done.12.refs_3_ = bf16[16,4096]{1,0:T(8,128)(2,1)S(1)} collective-permute-done((bf16[16,4096]{1,0:T(8,128)(2,1)S(1)}, bf16[16,4096]{1,0:T(8,128)(2,1)S(1)}, u32[]{:S(2)}, u32[]{:S(2)}) %collective-permute-start.12) | collective-permute-done | bytes 131104 | tf_op jit(solution)/shard_map/ppermute | solution.py:398
  56.5 2.5 %shard_map.129 = f32[16,8,128]{2,1,0:T(8,128)} custom-call(s32[40]{0:T(128)S(1)} %get-tuple-element.73.plan_ref, bf16[48,4096]{1,0:T(8,128)(2,1)S(1)} %constant_dynamic-update-slice_fusion.refs_0_, bf16[48,4096]{1,0:T(8,128)(2,1)} %collective-permute-done.9.refs_1_, bf16[16,4096]{1,0:T(8,128)(2,1)S(1)} %constant_dynamic-update-slice_fusion.3.refs_2_, ...), custom_call_target="tpu_custom_call" | custom-call | tf_op jit(solution)/shard_map/pallas_call | solution.py:489
  59.0 11.2 %all-to-all-start.2 = ((f32[16,8,128]{2,1,0:T(8,128)}), f32[16,8,128]{2,1,0:T(8,128)S(1)}, u32[]{:S(2)}, u32[]{:S(2)}) async-start(f32[16,8,128]{2,1,0:T(8,128)} %shard_map.129), calls=%async_computation.2 | async-start | bytes 131072 | tf_op jit(solution)/shard_map/all_to_all | solution.py:494
  71.8 1.4 collective-permute-start.18
  73.2 1.3 collective-permute-start.19
  74.6 1.5 collective-permute-start.17
  76.0 2.7 %collective-permute-start.21 = (bf16[16,4096]{1,0:T(8,128)(2,1)S(1)}, bf16[16,4096]{1,0:T(8,128)(2,1)}, u32[]{:S(2)}, u32[]{:S(2)}) collective-permute-start(bf16[16,4096]{1,0:T(8,128)(2,1)S(1)} %slice.27), channel_id=1, source_target_pairs={{0,6},{1,7},{2,0},{3,1},{4,2},{5,3},{6,4},{7,5},{8,14},{9,15},{10,... | collective-permute-start | bytes 393224 | tf_op jit(solution)/shard_map/ppermute | solution.py:398
  80.3 10.5 %all-to-all-start.3 = ((f32[16,8,512]{2,1,0:T(8,128)}), f32[16,8,512]{2,1,0:T(8,128)}, u32[]{:S(2)}, u32[]{:S(2)}) async-start(f32[16,8,512]{2,1,0:T(8,128)} %shard_map.131), calls=%async_computation.3 | async-start | bytes 524288 | tf_op jit(solution)/shard_map/all_to_all | solution.py:505
  91.0 1.2 pad_maximum_fusion.refs_7_
  92.2 1.3 collective-permute-start.27
  95.0 2.7 %collective-permute-start.23 = (bf16[32,4096]{1,0:T(8,128)(2,1)}, bf16[32,4096]{1,0:T(8,128)(2,1)}, u32[]{:S(2)}, u32[]{:S(2)}) collective-permute-start(bf16[32,4096]{1,0:T(8,128)(2,1)} %slice.29), channel_id=1, source_target_pairs={{0,6},{1,7},{2,0},{3,1},{4,2},{5,3},{6,4},{7,5},{8,14},{9,15},{10,... | collective-permute-start | bytes 786440 | tf_op jit(solution)/shard_map/ppermute | solution.py:398
  101.8 1.4 shard_map.133
  103.3 1.3 copy-done
  106.9 3.2 %collective-permute-start.24 = (bf16[16,256]{1,0:T(8,128)(2,1)S(1)}, bf16[16,256]{1,0:T(8,128)(2,1)S(1)}, u32[]{:S(2)}, u32[]{:S(2)}) collective-permute-start(bf16[16,256]{1,0:T(8,128)(2,1)S(1)} %shard_map.132.mine_ref), channel_id=1, source_target_pairs={{0,1},{1,0},{2,3},{3,2},{4,5},{5,4},{6,7},{7,6},{8,9},{9,8},{10,11... | collective-permute-start | bytes 24584 | tf_op jit(solution)/shard_map/ppermute | solution.py:398
  112.1 1.6 copy-done.1
  114.5 5.5 %collective-permute-start.29 = (bf16[16,4096]{1,0:T(8,128)(2,1)S(1)}, bf16[16,4096]{1,0:T(8,128)(2,1)S(1)}, u32[]{:S(2)}, u32[]{:S(2)}) collective-permute-start(bf16[16,4096]{1,0:T(8,128)(2,1)S(1)} %get-tuple-element.114), channel_id=1, source_target_pairs={{1,16},{16,1},{3,18},{18,3},{5,20},{20,5},{7,22},{22,7},{9,24},{24... | collective-permute-start | bytes 393224 | tf_op jit(solution)/shard_map/ppermute | solution.py:568
  120.0 2.6 %collective-permute-done.29.off_ref = bf16[16,4096]{1,0:T(8,128)(2,1)S(1)} collective-permute-done((bf16[16,4096]{1,0:T(8,128)(2,1)S(1)}, bf16[16,4096]{1,0:T(8,128)(2,1)S(1)}, u32[]{:S(2)}, u32[]{:S(2)}) %collective-permute-start.29) | collective-permute-done | bytes 131104 | tf_op jit(solution)/shard_map/ppermute | solution.py:568
  122.7 1.2 shard_map.135
  125.1 22.9 %all_to_all.34.parts_ref = f32[16,8,512]{2,1,0:T(8,128)S(1)} all-to-all(f32[16,8,512]{2,1,0:T(8,128)S(1)} %shard_map.136), channel_id=1, replica_groups=mesh['dom'=16,'orb'=16] {'dom'}, dimensions={0} | all-to-all | bytes 524288 | tf_op jit(solution)/shard_map/all_to_all | solution.py:575
  148.1 2.2 %collective-permute-start.31 = (bf16[16,256]{1,0:T(8,128)(2,1)S(1)}, bf16[16,256]{1,0:T(8,128)(2,1)S(1)}, u32[]{:S(2)}, u32[]{:S(2)}) collective-permute-start(bf16[16,256]{1,0:T(8,128)(2,1)S(1)} %shard_map.137.mine_ref), channel_id=1, source_target_pairs={{0,1},{1,0},{2,3},{3,2},{4,5},{5,4},{6,7},{7,6},{8,9},{9,8},{10,11... | collective-permute-start | bytes 24584 | tf_op jit(solution)/shard_map/ppermute | solution.py:398
  152.3 2.3 %collective-permute-start.33 = (bf16[16,4096]{1,0:T(8,128)(2,1)S(1)}, bf16[16,4096]{1,0:T(8,128)(2,1)S(1)}, u32[]{:S(2)}, u32[]{:S(2)}) collective-permute-start(bf16[16,4096]{1,0:T(8,128)(2,1)S(1)} %get-tuple-element.119), channel_id=1, source_target_pairs={{1,16},{16,1},{3,18},{18,3},{5,20},{20,5},{7,22},{22,7},{9,24},{24... | collective-permute-start | bytes 393224 | tf_op jit(solution)/shard_map/ppermute | solution.py:568
  154.5 5.6 %collective-permute-done.33.off_ref = bf16[16,4096]{1,0:T(8,128)(2,1)S(1)} collective-permute-done((bf16[16,4096]{1,0:T(8,128)(2,1)S(1)}, bf16[16,4096]{1,0:T(8,128)(2,1)S(1)}, u32[]{:S(2)}, u32[]{:S(2)}) %collective-permute-start.33) | collective-permute-done | bytes 131104 | tf_op jit(solution)/shard_map/ppermute | solution.py:568
  160.2 1.2 shard_map.139
  161.4 1.2 collective-permute-done.34.other_ref
  163.4 4.5 %all-to-all-start.5 = ((f32[16,8,512]{2,1,0:T(8,128)}), f32[16,8,512]{2,1,0:T(8,128)S(1)}, u32[]{:S(2)}, u32[]{:S(2)}) async-start(f32[16,8,512]{2,1,0:T(8,128)} %shard_map.140), calls=%async_computation.5 | async-start | bytes 524288 | tf_op jit(solution)/shard_map/all_to_all | solution.py:575
  168.6 12.1 %all-to-all-done.5.parts_ref = f32[16,8,512]{2,1,0:T(8,128)S(1)} async-done(((f32[16,8,512]{2,1,0:T(8,128)}), f32[16,8,512]{2,1,0:T(8,128)S(1)}, u32[]{:S(2)}, u32[]{:S(2)}) %all-to-all-start.5) | async-done | bytes 262176 | tf_op jit(solution)/shard_map/all_to_all | solution.py:575
  180.7 1.7 collective-permute-start.35
  183.3 1.6 copy-done.3
  184.9 1.4 shard_map.144
  186.6 5.3 %all-to-all-start.6 = ((f32[256,2,128]{2,1,0:T(2,128)}), f32[256,2,128]{2,1,0:T(2,128)S(1)}, u32[]{:S(2)}, u32[]{:S(2)}) async-start(f32[256,2,128]{2,1,0:T(2,128)} %bitcast.17), calls=%async_computation.6 | async-start | bytes 524288 | tf_op jit(solution)/shard_map/all_to_all | solution.py:589
  194.2 13.1 %all-to-all-done.6.terms_ref = f32[256,2,128]{2,1,0:T(2,128)S(1)} async-done(((f32[256,2,128]{2,1,0:T(2,128)}), f32[256,2,128]{2,1,0:T(2,128)S(1)}, u32[]{:S(2)}, u32[]{:S(2)}) %all-to-all-start.6) | async-done | bytes 262176 | tf_op jit(solution)/shard_map/all_to_all | solution.py:589
  207.3 1.5 shard_map.146
  (158 shorter events, 34.4 us)
Async XLA Ops:
  4.5 7.0 %copy-start.22 = (f32[2,32,128]{2,1,0:T(8,128)S(1)}, f32[2,32,128]{2,1,0:T(8,128)}, u32[]{:S(2)}) copy-start(f32[2,32,128]{2,1,0:T(8,128)} %param.13) | copy-start | bytes 98308
  6.1 10.4 %collective-permute-start.5 = (bf16[128,32,128]{2,1,0:T(8,128)(2,1)}, bf16[128,32,128]{2,1,0:T(8,128)(2,1)S(1)}, u32[]{:S(2)}, u32[]{:S(2)}) collective-permute-start(bf16[128,32,128]{2,1,0:T(8,128)(2,1)} %shard_map.124), channel_id=1, source_target_pairs={{0,1},{15,14},{16,17},{31,30},{32,33},{47,46},{48,49},{63,62},{64,... | collective-permute-start | bytes 3145736 | tf_op jit(solution)/shard_map/ppermute | solution.py:398
  7.4 10.7 %collective-permute-start.4 = (bf16[128,32,128]{2,1,0:T(8,128)(2,1)}, bf16[128,32,128]{2,1,0:T(8,128)(2,1)S(1)}, u32[]{:S(2)}, u32[]{:S(2)}) collective-permute-start(bf16[128,32,128]{2,1,0:T(8,128)(2,1)} %get-tuple-element.77), channel_id=1, source_target_pairs={{0,1},{1,0},{2,3},{3,2},{4,5},{5,4},{6,7},{7,6},{8,9},{9,8},{10,11... | collective-permute-start | bytes 3145736 | tf_op jit(solution)/shard_map/ppermute | solution.py:398
  11.1 2.7 %collective-permute-start.1 = (f32[8,4096]{1,0:T(8,128)S(1)}, f32[8,4096]{1,0:T(8,128)S(1)}, u32[]{:S(2)}, u32[]{:S(2)}) collective-permute-start(f32[8,4096]{1,0:T(8,128)S(1)} %get-tuple-element.75), channel_id=1, source_target_pairs={{0,1},{1,0},{2,3},{3,2},{4,5},{5,4},{6,7},{7,6},{8,9},{9,8},{10,11... | collective-permute-start | bytes 393224 | tf_op jit(solution)/shard_map/ppermute | solution.py:398
  13.8 8.3 %copy-start.17 = (bf16[2,128,2,32,128]{4,3,2,1,0:T(8,128)(2,1)S(1)}, bf16[2,128,2,32,128]{4,3,2,1,0:T(8,128)(2,1)}, u32[]{:S(2)}) copy-start(bf16[2,128,2,32,128]{4,3,2,1,0:T(8,128)(2,1)} %occupied_ref.7) | copy-start | bytes 12582916
  13.8 14.9 %collective-permute-start.2 = (bf16[16,4096]{1,0:T(8,128)(2,1)S(1)}, bf16[16,4096]{1,0:T(8,128)(2,1)}, u32[]{:S(2)}, u32[]{:S(2)}) collective-permute-start(bf16[16,4096]{1,0:T(8,128)(2,1)S(1)} %get-tuple-element.76), channel_id=1, source_target_pairs={{0,2},{1,3},{2,4},{3,5},{4,6},{5,7},{6,0},{7,1},{8,10},{9,11},{10,... | collective-permute-start | bytes 393224 | tf_op jit(solution)/shard_map/ppermute | solution.py:398
  13.9 15.8 %collective-permute-start.3 = (bf16[16,4096]{1,0:T(8,128)(2,1)S(1)}, bf16[16,4096]{1,0:T(8,128)(2,1)}, u32[]{:S(2)}, u32[]{:S(2)}) collective-permute-start(bf16[16,4096]{1,0:T(8,128)(2,1)S(1)} %get-tuple-element.76), channel_id=1, source_target_pairs={{0,6},{1,7},{2,0},{3,1},{4,2},{5,3},{6,4},{7,5},{8,14},{9,15},{10,... | collective-permute-start | bytes 393224 | tf_op jit(solution)/shard_map/ppermute | solution.py:398
  18.1 11.6 %collective-permute-start.6 = (bf16[32,32,128]{2,1,0:T(8,128)(2,1)}, bf16[32,32,128]{2,1,0:T(8,128)(2,1)S(1)}, u32[]{:S(2)}, u32[]{:S(2)}) collective-permute-start(bf16[32,32,128]{2,1,0:T(8,128)(2,1)} %get-tuple-element.82), channel_id=1, source_target_pairs={{0,2},{1,3},{14,8},{15,9},{16,18},{17,19},{30,24},{31,25},{32,34},... | collective-permute-start | bytes 786440 | tf_op jit(solution)/shard_map/ppermute | solution.py:398
  19.5 10.3 %collective-permute-start.7 = (bf16[32,32,128]{2,1,0:T(8,128)(2,1)}, bf16[32,32,128]{2,1,0:T(8,128)(2,1)S(1)}, u32[]{:S(2)}, u32[]{:S(2)}) collective-permute-start(bf16[32,32,128]{2,1,0:T(8,128)(2,1)} %get-tuple-element.83), channel_id=1, source_target_pairs={{0,4},{1,5},{14,10},{15,11},{16,20},{17,21},{30,26},{31,27},{32,36... | collective-permute-start | bytes 786440 | tf_op jit(solution)/shard_map/ppermute | solution.py:398
  20.8 9.0 %collective-permute-start.8 = (bf16[32,32,128]{2,1,0:T(8,128)(2,1)}, bf16[32,32,128]{2,1,0:T(8,128)(2,1)S(1)}, u32[]{:S(2)}, u32[]{:S(2)}) collective-permute-start(bf16[32,32,128]{2,1,0:T(8,128)(2,1)} %get-tuple-element.84), channel_id=1, source_target_pairs={{0,6},{1,7},{14,12},{15,13},{16,22},{17,23},{30,28},{31,29},{32,38... | collective-permute-start | bytes 786440 | tf_op jit(solution)/shard_map/ppermute | solution.py:398
  23.8 23.1 %copy-start.19 = (bf16[16,32,128]{2,1,0:T(8,128)(2,1)S(1)}, bf16[16,32,128]{2,1,0:T(8,128)(2,1)}, u32[]{:S(2)}) copy-start(bf16[16,32,128]{2,1,0:T(8,128)(2,1)} %copy-done.18) | copy-start | bytes 393220
  23.8 23.1 %all-to-all-start.1 = ((bf16[8,16,32,128]{3,2,1,0:T(8,128)(2,1)}), bf16[8,16,32,128]{3,2,1,0:T(8,128)(2,1)S(1)}, u32[]{:S(2)}, u32[]{:S(2)}) async-start(bf16[8,16,32,128]{3,2,1,0:T(8,128)(2,1)} %bitcast.7), calls=%async_computation.1 | async-start | bytes 2097152 | tf_op jit(solution)/shard_map/all_to_all | solution.py:453
  28.7 21.9 %collective-permute-start.25 = (f32[8,1]{0,1:T(1,128)S(1)}, f32[8,1]{0,1:T(1,128)S(1)}, u32[]{:S(2)}, u32[]{:S(2)}) collective-permute-start(f32[8,1]{0,1:T(1,128)S(1)} %bitcast.41), channel_id=1, source_target_pairs={{0,1},{1,0},{2,3},{3,2},{4,5},{5,4},{6,7},{7,6},{8,9},{9,8},{10,11... | collective-permute-start | bytes 104 | tf_op jit(solution)/shard_map/ppermute | solution.py:398
  30.7 16.0 %collective-permute-start.10 = (bf16[8,4096]{1,0:T(8,128)(2,1)S(1)}, bf16[8,4096]{1,0:T(8,128)(2,1)S(1)}, u32[]{:S(2)}, u32[]{:S(2)}) collective-permute-start(bf16[8,4096]{1,0:T(8,128)(2,1)S(1)} %slice.24), channel_id=1, source_target_pairs={{0,2},{1,3},{2,4},{3,5},{4,6},{5,7},{6,0},{7,1},{8,10},{9,11},{10,... | collective-permute-start | bytes 196616 | tf_op jit(solution)/shard_map/ppermute | solution.py:398
  33.2 13.5 %collective-permute-start.11 = (bf16[8,4096]{1,0:T(8,128)(2,1)S(1)}, bf16[8,4096]{1,0:T(8,128)(2,1)S(1)}, u32[]{:S(2)}, u32[]{:S(2)}) collective-permute-start(bf16[8,4096]{1,0:T(8,128)(2,1)S(1)} %slice.25), channel_id=1, source_target_pairs={{0,6},{1,7},{2,0},{3,1},{4,2},{5,3},{6,4},{7,5},{8,14},{9,15},{10,... | collective-permute-start | bytes 196616 | tf_op jit(solution)/shard_map/ppermute | solution.py:398
  36.2 20.3 %collective-permute-start.9 = (bf16[48,4096]{1,0:T(8,128)(2,1)S(1)}, bf16[48,4096]{1,0:T(8,128)(2,1)}, u32[]{:S(2)}, u32[]{:S(2)}) collective-permute-start(bf16[48,4096]{1,0:T(8,128)(2,1)S(1)} %constant_dynamic-update-slice_fusion.refs_0_), channel_id=1, source_target_pairs={{0,8},{1,9},{2,10},{3,11},{4,12},{5,13},{6,14},{7,15},{8,0},{9,1},... | collective-permute-start | bytes 1179656 | tf_op jit(solution)/shard_map/ppermute | solution.py:398
  46.7 8.5 %collective-permute-start.12 = (bf16[16,4096]{1,0:T(8,128)(2,1)S(1)}, bf16[16,4096]{1,0:T(8,128)(2,1)S(1)}, u32[]{:S(2)}, u32[]{:S(2)}) collective-permute-start(bf16[16,4096]{1,0:T(8,128)(2,1)S(1)} %constant_dynamic-update-slice_fusion.3.refs_2_), channel_id=1, source_target_pairs={{0,8},{1,9},{2,10},{3,11},{4,12},{5,13},{6,14},{7,15},{8,0},{9,1},... | collective-permute-start | bytes 393224 | tf_op jit(solution)/shard_map/ppermute | solution.py:398
  47.6 22.6 %collective-permute-start.14 = (bf16[32,4096]{1,0:T(8,128)(2,1)S(1)}, bf16[32,4096]{1,0:T(8,128)(2,1)S(1)}, u32[]{:S(2)}, u32[]{:S(2)}) collective-permute-start(bf16[32,4096]{1,0:T(8,128)(2,1)S(1)} %get-tuple-element.94.refs_5_.refs_3_), channel_id=1, source_target_pairs={{0,8},{1,9},{2,10},{3,11},{4,12},{5,13},{6,14},{7,15},{8,0},{9,1},... | collective-permute-start | bytes 786440 | tf_op jit(solution)/shard_map/ppermute | solution.py:398
  49.1 21.8 %collective-permute-start.15 = (bf16[32,4096]{1,0:T(8,128)(2,1)S(1)}, bf16[32,4096]{1,0:T(8,128)(2,1)S(1)}, u32[]{:S(2)}, u32[]{:S(2)}) collective-permute-start(bf16[32,4096]{1,0:T(8,128)(2,1)S(1)} %get-tuple-element.94.refs_5_.refs_3_), channel_id=1, source_target_pairs={{0,2},{1,3},{2,4},{3,5},{4,6},{5,7},{6,0},{7,1},{8,10},{9,11},{10,... | collective-permute-start | bytes 786440 | tf_op jit(solution)/shard_map/ppermute | solution.py:398
  50.7 20.3 %collective-permute-start.16 = (bf16[32,4096]{1,0:T(8,128)(2,1)S(1)}, bf16[32,4096]{1,0:T(8,128)(2,1)S(1)}, u32[]{:S(2)}, u32[]{:S(2)}) collective-permute-start(bf16[32,4096]{1,0:T(8,128)(2,1)S(1)} %get-tuple-element.94.refs_5_.refs_3_), channel_id=1, source_target_pairs={{0,6},{1,7},{2,0},{3,1},{4,2},{5,3},{6,4},{7,5},{8,14},{9,15},{10,... | collective-permute-start | bytes 786440 | tf_op jit(solution)/shard_map/ppermute | solution.py:398
  55.3 15.0 %collective-permute-start.13 = (bf16[32,4096]{1,0:T(8,128)(2,1)S(1)}, bf16[32,4096]{1,0:T(8,128)(2,1)S(1)}, u32[]{:S(2)}, u32[]{:S(2)}) collective-permute-start(bf16[32,4096]{1,0:T(8,128)(2,1)S(1)} %get-tuple-element.93.refs_4_.refs_0_), channel_id=1, source_target_pairs={{0,8},{1,9},{2,10},{3,11},{4,12},{5,13},{6,14},{7,15},{8,0},{9,1},... | collective-permute-start | bytes 786440 | tf_op jit(solution)/shard_map/ppermute | solution.py:398
  59.0 20.5 %all-to-all-start.2 = ((f32[16,8,128]{2,1,0:T(8,128)}), f32[16,8,128]{2,1,0:T(8,128)S(1)}, u32[]{:S(2)}, u32[]{:S(2)}) async-start(f32[16,8,128]{2,1,0:T(8,128)} %shard_map.129), calls=%async_computation.2 | async-start | bytes 131072 | tf_op jit(solution)/shard_map/all_to_all | solution.py:494
  71.8 23.2 %copy-start.8 = (bf16[64,4096]{1,0:T(8,128)(2,1)}, bf16[64,4096]{1,0:T(8,128)(2,1)S(1)}, u32[]{:S(2)}) copy-start(bf16[64,4096]{1,0:T(8,128)(2,1)S(1)} %get-tuple-element.100.refs_0_) | copy-start | bytes 1572868
  71.8 19.0 %collective-permute-start.18 = (bf16[64,4096]{1,0:T(8,128)(2,1)S(1)}, bf16[64,4096]{1,0:T(8,128)(2,1)S(1)}, u32[]{:S(2)}, u32[]{:S(2)}) collective-permute-start(bf16[64,4096]{1,0:T(8,128)(2,1)S(1)} %get-tuple-element.100.refs_0_), channel_id=1, source_target_pairs={{0,2},{1,3},{2,4},{3,5},{4,6},{5,7},{6,0},{7,1},{8,10},{9,11},{10,... | collective-permute-start | bytes 1572872 | tf_op jit(solution)/shard_map/ppermute | solution.py:398
  73.2 17.7 %collective-permute-start.19 = (bf16[64,4096]{1,0:T(8,128)(2,1)S(1)}, bf16[64,4096]{1,0:T(8,128)(2,1)S(1)}, u32[]{:S(2)}, u32[]{:S(2)}) collective-permute-start(bf16[64,4096]{1,0:T(8,128)(2,1)S(1)} %get-tuple-element.100.refs_0_), channel_id=1, source_target_pairs={{0,6},{1,7},{2,0},{3,1},{4,2},{5,3},{6,4},{7,5},{8,14},{9,15},{10,... | collective-permute-start | bytes 1572872 | tf_op jit(solution)/shard_map/ppermute | solution.py:398
  74.6 16.3 %collective-permute-start.17 = (bf16[64,4096]{1,0:T(8,128)(2,1)}, bf16[64,4096]{1,0:T(8,128)(2,1)}, u32[]{:S(2)}, u32[]{:S(2)}) collective-permute-start(bf16[64,4096]{1,0:T(8,128)(2,1)} %get-tuple-element.98.refs_4_), channel_id=1, source_target_pairs={{0,8},{1,9},{2,10},{3,11},{4,12},{5,13},{6,14},{7,15},{8,0},{9,1},... | collective-permute-start | bytes 1572872 | tf_op jit(solution)/shard_map/ppermute | solution.py:398
  76.0 14.8 %collective-permute-start.20 = (bf16[16,4096]{1,0:T(8,128)(2,1)S(1)}, bf16[16,4096]{1,0:T(8,128)(2,1)}, u32[]{:S(2)}, u32[]{:S(2)}) collective-permute-start(bf16[16,4096]{1,0:T(8,128)(2,1)S(1)} %slice.26), channel_id=1, source_target_pairs={{0,2},{1,3},{2,4},{3,5},{4,6},{5,7},{6,0},{7,1},{8,10},{9,11},{10,... | collective-permute-start | bytes 393224 | tf_op jit(solution)/shard_map/ppermute | solution.py:398
  76.0 14.8 %collective-permute-start.21 = (bf16[16,4096]{1,0:T(8,128)(2,1)S(1)}, bf16[16,4096]{1,0:T(8,128)(2,1)}, u32[]{:S(2)}, u32[]{:S(2)}) collective-permute-start(bf16[16,4096]{1,0:T(8,128)(2,1)S(1)} %slice.27), channel_id=1, source_target_pairs={{0,6},{1,7},{2,0},{3,1},{4,2},{5,3},{6,4},{7,5},{8,14},{9,15},{10,... | collective-permute-start | bytes 393224 | tf_op jit(solution)/shard_map/ppermute | solution.py:398
  80.3 25.6 %all-to-all-start.3 = ((f32[16,8,512]{2,1,0:T(8,128)}), f32[16,8,512]{2,1,0:T(8,128)}, u32[]{:S(2)}, u32[]{:S(2)}) async-start(f32[16,8,512]{2,1,0:T(8,128)} %shard_map.131), calls=%async_computation.3 | async-start | bytes 524288 | tf_op jit(solution)/shard_map/all_to_all | solution.py:505
  90.9 13.7 %collective-permute-start.26 = (bf16[16,4096]{1,0:T(8,128)(2,1)}, bf16[16,4096]{1,0:T(8,128)(2,1)S(1)}, u32[]{:S(2)}, u32[]{:S(2)}) collective-permute-start(bf16[16,4096]{1,0:T(8,128)(2,1)} %collective-permute-done.20), channel_id=1, source_target_pairs={{0,8},{1,9},{2,10},{3,11},{4,12},{5,13},{6,14},{7,15},{8,0},{9,1},... | collective-permute-start | bytes 393224 | tf_op jit(solution)/shard_map/ppermute | solution.py:398
  92.2 13.0 %collective-permute-start.27 = (bf16[16,4096]{1,0:T(8,128)(2,1)}, bf16[16,4096]{1,0:T(8,128)(2,1)S(1)}, u32[]{:S(2)}, u32[]{:S(2)}) collective-permute-start(bf16[16,4096]{1,0:T(8,128)(2,1)} %collective-permute-done.21), channel_id=1, source_target_pairs={{0,8},{1,9},{2,10},{3,11},{4,12},{5,13},{6,14},{7,15},{8,0},{9,1},... | collective-permute-start | bytes 393224 | tf_op jit(solution)/shard_map/ppermute | solution.py:398
  94.3 11.6 %collective-permute-start.22 = (bf16[32,4096]{1,0:T(8,128)(2,1)}, bf16[32,4096]{1,0:T(8,128)(2,1)}, u32[]{:S(2)}, u32[]{:S(2)}) collective-permute-start(bf16[32,4096]{1,0:T(8,128)(2,1)} %slice.28), channel_id=1, source_target_pairs={{0,2},{1,3},{2,4},{3,5},{4,6},{5,7},{6,0},{7,1},{8,10},{9,11},{10,... | collective-permute-start | bytes 786440 | tf_op jit(solution)/shard_map/ppermute | solution.py:398
  95.0 10.9 %collective-permute-start.23 = (bf16[32,4096]{1,0:T(8,128)(2,1)}, bf16[32,4096]{1,0:T(8,128)(2,1)}, u32[]{:S(2)}, u32[]{:S(2)}) collective-permute-start(bf16[32,4096]{1,0:T(8,128)(2,1)} %slice.29), channel_id=1, source_target_pairs={{0,6},{1,7},{2,0},{3,1},{4,2},{5,3},{6,4},{7,5},{8,14},{9,15},{10,... | collective-permute-start | bytes 786440 | tf_op jit(solution)/shard_map/ppermute | solution.py:398
  106.9 5.2 %collective-permute-start.24 = (bf16[16,256]{1,0:T(8,128)(2,1)S(1)}, bf16[16,256]{1,0:T(8,128)(2,1)S(1)}, u32[]{:S(2)}, u32[]{:S(2)}) collective-permute-start(bf16[16,256]{1,0:T(8,128)(2,1)S(1)} %shard_map.132.mine_ref), channel_id=1, source_target_pairs={{0,1},{1,0},{2,3},{3,2},{4,5},{5,4},{6,7},{7,6},{8,9},{9,8},{10,11... | collective-permute-start | bytes 24584 | tf_op jit(solution)/shard_map/ppermute | solution.py:398
  114.5 8.2 %collective-permute-start.28 = (f32[16,4096]{1,0:T(8,128)S(1)}, f32[16,4096]{1,0:T(8,128)S(1)}, u32[]{:S(2)}, u32[]{:S(2)}) collective-permute-start(f32[16,4096]{1,0:T(8,128)S(1)} %get-tuple-element.113.x_ref.refs_0_), channel_id=1, source_target_pairs={{0,1},{1,0},{2,3},{3,2},{4,5},{5,4},{6,7},{7,6},{8,9},{9,8},{10,11... | collective-permute-start | bytes 786440 | tf_op jit(solution)/shard_map/ppermute | solution.py:398
  114.5 36.6 %copy-start.2 = (bf16[256,4096]{1,0:T(8,128)(2,1)S(1)}, bf16[256,4096]{1,0:T(8,128)(2,1)}, u32[]{:S(2)}) copy-start(bf16[256,4096]{1,0:T(8,128)(2,1)} %constant_dynamic-update-slice_fusion.5.refs_2_.second_ref.refs_3_) | copy-start | bytes 6291460
  114.5 8.1 %collective-permute-start.29 = (bf16[16,4096]{1,0:T(8,128)(2,1)S(1)}, bf16[16,4096]{1,0:T(8,128)(2,1)S(1)}, u32[]{:S(2)}, u32[]{:S(2)}) collective-permute-start(bf16[16,4096]{1,0:T(8,128)(2,1)S(1)} %get-tuple-element.114), channel_id=1, source_target_pairs={{1,16},{16,1},{3,18},{18,3},{5,20},{20,5},{7,22},{22,7},{9,24},{24... | collective-permute-start | bytes 393224 | tf_op jit(solution)/shard_map/ppermute | solution.py:568
  123.9 1.2 collective-permute-start.30
  148.1 3.0 %collective-permute-start.31 = (bf16[16,256]{1,0:T(8,128)(2,1)S(1)}, bf16[16,256]{1,0:T(8,128)(2,1)S(1)}, u32[]{:S(2)}, u32[]{:S(2)}) collective-permute-start(bf16[16,256]{1,0:T(8,128)(2,1)S(1)} %shard_map.137.mine_ref), channel_id=1, source_target_pairs={{0,1},{1,0},{2,3},{3,2},{4,5},{5,4},{6,7},{7,6},{8,9},{9,8},{10,11... | collective-permute-start | bytes 24584 | tf_op jit(solution)/shard_map/ppermute | solution.py:398
  151.8 8.3 %collective-permute-start.32 = (f32[16,4096]{1,0:T(8,128)S(1)}, f32[16,4096]{1,0:T(8,128)S(1)}, u32[]{:S(2)}, u32[]{:S(2)}) collective-permute-start(f32[16,4096]{1,0:T(8,128)S(1)} %get-tuple-element.118.x_ref.refs_0_), channel_id=1, source_target_pairs={{0,1},{1,0},{2,3},{3,2},{4,5},{5,4},{6,7},{7,6},{8,9},{9,8},{10,11... | collective-permute-start | bytes 786440 | tf_op jit(solution)/shard_map/ppermute | solution.py:398
  152.2 15.6 %copy-start.20 = (bf16[8,2,32,128]{3,2,1,0:T(8,128)(2,1)S(1)}, bf16[8,2,32,128]{3,2,1,0:T(8,128)(2,1)}, u32[]{:S(2)}) copy-start(bf16[8,2,32,128]{3,2,1,0:T(8,128)(2,1)} %param.18) | copy-start | bytes 393220
  152.3 7.9 %collective-permute-start.33 = (bf16[16,4096]{1,0:T(8,128)(2,1)S(1)}, bf16[16,4096]{1,0:T(8,128)(2,1)S(1)}, u32[]{:S(2)}, u32[]{:S(2)}) collective-permute-start(bf16[16,4096]{1,0:T(8,128)(2,1)S(1)} %get-tuple-element.119), channel_id=1, source_target_pairs={{1,16},{16,1},{3,18},{18,3},{5,20},{20,5},{7,22},{22,7},{9,24},{24... | collective-permute-start | bytes 393224 | tf_op jit(solution)/shard_map/ppermute | solution.py:568
  161.4 1.2 collective-permute-start.34
  163.4 17.3 %all-to-all-start.5 = ((f32[16,8,512]{2,1,0:T(8,128)}), f32[16,8,512]{2,1,0:T(8,128)S(1)}, u32[]{:S(2)}, u32[]{:S(2)}) async-start(f32[16,8,512]{2,1,0:T(8,128)} %shard_map.140), calls=%async_computation.5 | async-start | bytes 524288 | tf_op jit(solution)/shard_map/all_to_all | solution.py:575
  168.0 15.2 %collective-permute-start.36 = (bf16[8,4096]{1,0:T(8,128)(2,1)S(1)}, bf16[8,4096]{1,0:T(8,128)(2,1)S(1)}, u32[]{:S(2)}, u32[]{:S(2)}) collective-permute-start(bf16[8,4096]{1,0:T(8,128)(2,1)S(1)} %convert_element_type.25), channel_id=1, source_target_pairs={{0,1},{1,0},{2,3},{3,2},{4,5},{5,4},{6,7},{7,6},{8,9},{9,8},{10,11... | collective-permute-start | bytes 196616 | tf_op jit(solution)/shard_map/ppermute | solution.py:398
  180.7 2.6 %collective-permute-start.35 = (bf16[16,256]{1,0:T(8,128)(2,1)S(1)}, bf16[16,256]{1,0:T(8,128)(2,1)S(1)}, u32[]{:S(2)}, u32[]{:S(2)}) collective-permute-start(bf16[16,256]{1,0:T(8,128)(2,1)S(1)} %get-tuple-element.122.mine_ref), channel_id=1, source_target_pairs={{0,1},{1,0},{2,3},{3,2},{4,5},{5,4},{6,7},{7,6},{8,9},{9,8},{10,11... | collective-permute-start | bytes 24584 | tf_op jit(solution)/shard_map/ppermute | solution.py:398
  186.4 7.0 %collective-permute-start.37 = (f32[8,4096]{1,0:T(8,128)S(1)}, f32[8,4096]{1,0:T(8,128)S(1)}, u32[]{:S(2)}, u32[]{:S(2)}) collective-permute-start(f32[8,4096]{1,0:T(8,128)S(1)} %get-tuple-element.127), channel_id=1, source_target_pairs={{0,1},{1,0},{2,3},{3,2},{4,5},{5,4},{6,7},{7,6},{8,9},{9,8},{10,11... | collective-permute-start | bytes 393224 | tf_op jit(solution)/shard_map/ppermute | solution.py:398
  186.6 20.7 %all-to-all-start.6 = ((f32[256,2,128]{2,1,0:T(2,128)}), f32[256,2,128]{2,1,0:T(2,128)S(1)}, u32[]{:S(2)}, u32[]{:S(2)}) async-start(f32[256,2,128]{2,1,0:T(2,128)} %bitcast.17), calls=%async_computation.6 | async-start | bytes 524288 | tf_op jit(solution)/shard_map/all_to_all | solution.py:589
  (20 other events, 50.9 us)

commit v7 on v3

--- a/solution.py
+++ b/solution.py
@@ -358,16 +358,23 @@
         out_ref[j * share : (j + 1) * share] = rows_ref[pl.ds(at, share)]
 
 
-def finish_kernel(weights_ref, pick_ref, terms_ref, out_ref):
+def finish_kernel(smoother_ref, pick_ref, terms_ref, out_ref):
     def product(one, two, dims):
         return lax.dot_general(
             one, two, (dims, ((), ())),
             precision=lax.Precision.HIGHEST, preferred_element_type=jnp.float32,
         )
 
+    sources, planes = terms_ref.shape[0], smoother_ref.shape[1]
+    chips = sources // planes
+    row = lax.broadcasted_iota(jnp.int32, (sources, planes), 0)
+    plane = lax.broadcasted_iota(jnp.int32, (sources, planes), 1)
+    same = jnp.logical_and(row // (2 * chips) == plane // 2, row % 2 == plane % 2)
+    gather = jnp.where(same, 1.0, 0.0)
     for k in range(terms_ref.shape[1]):
         mine = product(pick_ref[...], terms_ref[:, k, :], ((1,), (1,)))
-        out_ref[k] = product(mine, weights_ref[...], ((1,), (1,)))
+        raw = product(mine, gather, ((1,), (0,)))
+        out_ref[k] = product(raw, smoother_ref[...], ((1,), (1,)))
 
 
 def call(kernel, out_shape, in_specs=None, out_specs=None, scratch=()):
@@ -413,6 +420,8 @@
     up_y = chip_perm(lambda k: k // ring * ring + (k + 1) % ring)
     down_y = chip_perm(lambda k: k // ring * ring + (k - 1) % ring)
 
+    over_y = chip_perm(lambda k: k // ring * ring + (k + 2) % ring)
+
     def permute(value, pairs):
         return lax.ppermute(value, "orb", pairs)
 
@@ -439,7 +448,7 @@
     rhs_wide, rhs_b = call(pair_kernel, (field_shape, shape((wide, cells), jnp.bfloat16)))(
         low_mask, rhs_mine, permute(rhs_other, swap_core)
     )
-    rhs_up, rhs_down = permute(rhs_b, up_y), permute(rhs_b, down_y)
+    rhs_up, rhs_down, rhs_far = permute(rhs_b, up_y), permute(rhs_b, down_y), permute(rhs_b, over_y)
 
     offer = call(pick_kernel, plane_shape, [SMEM, ANY, VMEM], VMEM, four)(plan, occupied, offer)
     fixed = call(functools.partial(fixed_kernel, n_orb), plane_shape, [SMEM, ANY], VMEM, four)(plan, occupied)
@@ -458,13 +467,9 @@
         pairs = [(c, 2 * s + c) for c in range(2)]
         pairs += [(n_orb - 2 + c, 2 * (ring + (ring - 1 + s) % ring) + c) for c in range(2)]
         got.append(permute(pieces[s], pairs))
-    rhs_up, rhs_down, got[1] = lax.optimization_barrier((rhs_up, rhs_down, got[1]))
-    rhs_line = jnp.concatenate([rhs_b, rhs_up, rhs_down], axis=0)
+    rhs_up, rhs_down, rhs_far, got[1] = lax.optimization_barrier((rhs_up, rhs_down, rhs_far, got[1]))
+    rhs_line = jnp.concatenate([rhs_b, rhs_up, rhs_down, rhs_far], axis=0)
     rhs_line_x = permute(rhs_line, swap_x)
-    rhs_far = jnp.concatenate(
-        [permute(rhs_up[:local_orbs], up_y), permute(rhs_down[local_orbs:], down_y)], axis=0
-    )
-    rhs_far_x = permute(rhs_far, swap_x)
     fixed = call(share_kernel, piece_shape, [SMEM] + [VMEM] * ring, VMEM)(plan, *got)
 
     def scatter(value):
@@ -503,12 +508,12 @@
     own_rows = 4 * share
     half_shape = shape((local_orbs, n_rows))
     spread_shape = shape((n_dom, local_orbs, n_rows))
-    rhs_places = [[(0, k), (ring - 1, k), (1, k)] for k in range(2)] + [[(2, k)] for k in range(2)]
+    rhs_places = [[(0, k), (ring - 1, k), (1, k), (2, k)] for k in range(2)]
     parts = call(
         functools.partial(shares_kernel, scale, rhs_places),
         shape((n_orb, local_orbs, 128)),
-        [SMEM] + [VMEM] * 6,
-    )(plan, rhs_line, rhs_line_x, rhs_far, rhs_far_x, xs, ys)
+        [SMEM] + [VMEM] * 4,
+    )(plan, rhs_line, rhs_line_x, xs, ys)
     parts = lax.all_to_all(parts, "orb", 0, 0, tiled=True)
     xs_x, ys_up, ys_down = lax.optimization_barrier((xs_x, ys_up, ys_down))
     own, line = call(
@@ -604,16 +609,13 @@
             blocks = rest
     other, raw = x_b, rest[0]
 
-    weights = jnp.broadcast_to(
-        smoother.reshape(2 * n_dom, n_dom, 1, 2), (2 * n_dom, n_dom, chips, 2)
-    ).reshape(2 * n_dom, n_dom * n_orb)
     terms = lax.all_to_all(
         raw.reshape((n_dom * n_orb,) + raw.shape[2:]), ("dom", "orb"), 0, 0, tiled=True
     )
     z_part = rows_z // n_orb
     z_mine = o * z_part + jnp.arange(z_part)[:, None]
     pick = (jnp.arange(rows_z)[None, :] == z_mine).astype(jnp.float32)
-    gradient = call(finish_kernel, shape((rows_y // n_dom, z_part, 2 * n_dom)))(weights, pick, terms)
+    gradient = call(finish_kernel, shape((rows_y // n_dom, z_part, 2 * n_dom)))(smoother, pick, terms)
     gradient = jnp.transpose(gradient, (2, 0, 1))
 
     other = permute(other, swap_core)

time: 201 us -> 199 us (0.990)
  local copies, waits for them, and re-layouts: 11 us -> 8.51 us
    ppermute x34 -> x32, waiting for transfers between devices: 16.9 us -> 18.5 us  [permute(): return lax.ppermute(value, 'orb', pairs)]
    unnamed x37 -> x32, local copies, waits for them, and re-layouts: 8.65 us -> 7.13 us
    ppermute x34 -> x32, starting transfers between devices: 45.9 us -> 47 us  [permute(): return lax.ppermute(value, 'orb', pairs)]
  transfers between devices with their start and end apart: 41 -> 39, of which waited for: 13 -> 14; matrix products, arithmetic and copies ran while one was open for 4% -> 4% of each run, Pallas kernels for 5% -> 5%
where the time goes in v7:
time: 199 us; the launch traced here: 198 us
  starting transfers between devices  79.2 us (40%)
  waiting for transfers between devices  63.7 us (32%)
  Pallas kernels  23 us (12%)
  blocking collectives  16.9 us (8%)
  local copies, waits for them, and re-layouts  8.51 us (4%)
  other arithmetic  4.83 us (2%)
    ppermute x32, starting transfers between devices, permute(): return lax.ppermute(value, 'orb', pairs)  47 us
    ppermute x32, waiting for transfers between devices, permute(): return lax.ppermute(value, 'orb', pairs)  18.5 us
    all_to_all x1, blocking collectives, per_device(): parts = lax.all_to_all(spread, 'dom', 0, 0, tiled=True)  16.9 us
    all_to_all x1, waiting for transfers between devices, per_device(): lax.all_to_all(raw.reshape((n_dom * n_orb,) + raw.shape[2:]), ('dom', 'or...  13.1 us
    all_to_all x1, waiting for transfers between devices, per_device(): parts = lax.all_to_all(spread, 'dom', 0, 0, tiled=True)  11.9 us
    ppermute x2, waiting for transfers between devices, per_device(): off = lax.ppermute(x_b, ('dom', 'orb'), across)  11.4 us
    all_to_all x1, starting transfers between devices, per_device(): lax.all_to_all(call(spread_shares_kernel, spread_shape)(parts), 'dom', 0,...  10.5 us
    all_to_all x1, waiting for transfers between devices, per_device(): lax.all_to_all(call(spread_shares_kernel, spread_shape)(parts), 'dom', 0,...  8.02 us
  transfers between devices with their start and end apart: 39, of which 14 were waited for; matrix products, arithmetic and copies ran while one was open for 4% of the time, Pallas kernels for 5%

profile of v7, /device:TPU:1, one launch (start us, length us, event | category | flops | bytes accessed | tf_op | source)
XLA Modules:
  0.0 198.1 jit_solution(5952541952423267893)
XLA Ops:
  1.3 2.9 %shard_map.121 = (s32[40]{0:T(128)S(1)}, s32[1]{0:T(128)}, bf16[128,32,128]{2,1,0:T(8,128)(2,1)}) custom-call(s32[4]{0:T(128)S(1)} %copy-done.10, s32[1]{0:T(128)} %bitcast.6.dev_ref, bf16[2,128,2,32,128]{4,3,2,1,0:T(8,128)(2,1)} %occupied_ref.7), custom_call_target="tpu_custom_call" | custom-call | tf_op jit(solution)/shard_map/pallas_call | solution.py:436
  4.2 3.3 %collective-permute-start.5 = (bf16[128,32,128]{2,1,0:T(8,128)(2,1)}, bf16[128,32,128]{2,1,0:T(8,128)(2,1)S(1)}, u32[]{:S(2)}, u32[]{:S(2)}) collective-permute-start(bf16[128,32,128]{2,1,0:T(8,128)(2,1)} %get-tuple-element.69), channel_id=1, source_target_pairs={{0,1},{1,0},{2,3},{3,2},{4,5},{5,4},{6,7},{7,6},{8,9},{9,8},{10,11... | collective-permute-start | bytes 3145736 | tf_op jit(solution)/shard_map/ppermute | solution.py:426
  7.5 1.6 shard_map.125
  9.1 1.3 collective-permute-start.6
  10.6 1.3 collective-permute-start.1
  12.7 1.3 collective-permute-done.1.other_ref
  14.0 2.7 %collective-permute-start.3 = (bf16[16,4096]{1,0:T(8,128)(2,1)S(1)}, bf16[16,4096]{1,0:T(8,128)(2,1)}, u32[]{:S(2)}, u32[]{:S(2)}) collective-permute-start(bf16[16,4096]{1,0:T(8,128)(2,1)S(1)} %get-tuple-element.68), channel_id=1, source_target_pairs={{0,6},{1,7},{2,0},{3,1},{4,2},{5,3},{6,4},{7,5},{8,14},{9,15},{10,... | collective-permute-start | bytes 393224 | tf_op jit(solution)/shard_map/ppermute | solution.py:426
  16.7 1.7 shard_map.124
  18.4 1.5 shard_map.126
  19.9 2.4 %collective-permute-start.7 = (bf16[32,32,128]{2,1,0:T(8,128)(2,1)S(1)}, bf16[32,32,128]{2,1,0:T(8,128)(2,1)S(1)}, u32[]{:S(2)}, u32[]{:S(2)}) collective-permute-start(bf16[32,32,128]{2,1,0:T(8,128)(2,1)S(1)} %get-tuple-element.71), channel_id=1, source_target_pairs={{0,2},{1,3},{14,8},{15,9},{16,18},{17,19},{30,24},{31,25},{32,34},... | collective-permute-start | bytes 786440 | tf_op jit(solution)/shard_map/ppermute | solution.py:426
  22.3 1.4 collective-permute-start.10
  23.7 3.9 %all-to-all-start.1 = ((bf16[8,16,32,128]{3,2,1,0:T(8,128)(2,1)}), bf16[8,16,32,128]{3,2,1,0:T(8,128)(2,1)S(1)}, u32[]{:S(2)}, u32[]{:S(2)}) async-start(bf16[8,16,32,128]{3,2,1,0:T(8,128)(2,1)} %bitcast.7), calls=%async_computation.1 | async-start | bytes 2097152 | tf_op jit(solution)/shard_map/all_to_all | solution.py:477
  27.6 4.9 %collective-permute-start.9 = (bf16[32,32,128]{2,1,0:T(8,128)(2,1)}, bf16[32,32,128]{2,1,0:T(8,128)(2,1)S(1)}, u32[]{:S(2)}, u32[]{:S(2)}) collective-permute-start(bf16[32,32,128]{2,1,0:T(8,128)(2,1)} %get-tuple-element.77), channel_id=1, source_target_pairs={{0,4},{1,5},{14,10},{15,11},{16,20},{17,21},{30,26},{31,27},{32,36... | collective-permute-start | bytes 786440 | tf_op jit(solution)/shard_map/ppermute | solution.py:426
  34.5 8.2 %collective-permute-done.9.refs_2_ = bf16[32,32,128]{2,1,0:T(8,128)(2,1)S(1)} collective-permute-done((bf16[32,32,128]{2,1,0:T(8,128)(2,1)}, bf16[32,32,128]{2,1,0:T(8,128)(2,1)S(1)}, u32[]{:S(2)}, u32[]{:S(2)}) %collective-permute-start.9) | collective-permute-done | bytes 262176 | tf_op jit(solution)/shard_map/ppermute | solution.py:426
  44.1 2.7 %collective-permute-start.13 = (bf16[32,4096]{1,0:T(8,128)(2,1)S(1)}, bf16[32,4096]{1,0:T(8,128)(2,1)S(1)}, u32[]{:S(2)}, u32[]{:S(2)}) collective-permute-start(bf16[32,4096]{1,0:T(8,128)(2,1)S(1)} %get-tuple-element.82.refs_3_.refs_2_), channel_id=1, source_target_pairs={{0,6},{1,7},{2,0},{3,1},{4,2},{5,3},{6,4},{7,5},{8,14},{9,15},{10,... | collective-permute-start | bytes 786440 | tf_op jit(solution)/shard_map/ppermute | solution.py:426
  46.8 5.0 %collective-permute-start.11 = (bf16[32,4096]{1,0:T(8,128)(2,1)S(1)}, bf16[32,4096]{1,0:T(8,128)(2,1)S(1)}, u32[]{:S(2)}, u32[]{:S(2)}) collective-permute-start(bf16[32,4096]{1,0:T(8,128)(2,1)S(1)} %get-tuple-element.81.refs_2_.refs_0_), channel_id=1, source_target_pairs={{0,8},{1,9},{2,10},{3,11},{4,12},{5,13},{6,14},{7,15},{8,0},{9,1},... | collective-permute-start | bytes 786440 | tf_op jit(solution)/shard_map/ppermute | solution.py:426
  52.8 1.7 collective-permute-start.15
  55.3 1.9 shard_map.129
  57.2 4.1 %all-to-all-start.2 = ((f32[16,8,128]{2,1,0:T(8,128)}), f32[16,8,128]{2,1,0:T(8,128)S(1)}, u32[]{:S(2)}, u32[]{:S(2)}) async-start(f32[16,8,128]{2,1,0:T(8,128)} %shard_map.129), calls=%async_computation.2 | async-start | bytes 131072 | tf_op jit(solution)/shard_map/all_to_all | solution.py:517
  62.2 1.4 collective-permute-start.16
  64.8 1.5 collective-permute-start.18
  67.9 10.5 %all-to-all-start.3 = ((f32[16,8,512]{2,1,0:T(8,128)}), f32[16,8,512]{2,1,0:T(8,128)S(1)}, u32[]{:S(2)}, u32[]{:S(2)}) async-start(f32[16,8,512]{2,1,0:T(8,128)} %shard_map.131), calls=%async_computation.3 | async-start | bytes 524288 | tf_op jit(solution)/shard_map/all_to_all | solution.py:529
  78.5 1.3 add_bitcast_fusion
  80.3 2.4 %collective-permute-start.20 = (bf16[16,4096]{1,0:T(8,128)(2,1)S(1)}, bf16[16,4096]{1,0:T(8,128)(2,1)S(1)}, u32[]{:S(2)}, u32[]{:S(2)}) collective-permute-start(bf16[16,4096]{1,0:T(8,128)(2,1)S(1)} %slice.19), channel_id=1, source_target_pairs={{0,6},{1,7},{2,0},{3,1},{4,2},{5,3},{6,4},{7,5},{8,14},{9,15},{10,... | collective-permute-start | bytes 393224 | tf_op jit(solution)/shard_map/ppermute | solution.py:426
  82.7 8.0 %all-to-all-done.3.parts_ref = f32[16,8,512]{2,1,0:T(8,128)S(1)} async-done(((f32[16,8,512]{2,1,0:T(8,128)}), f32[16,8,512]{2,1,0:T(8,128)S(1)}, u32[]{:S(2)}, u32[]{:S(2)}) %all-to-all-start.3) | async-done | bytes 262176 | tf_op jit(solution)/shard_map/all_to_all | solution.py:529
  90.8 2.2 %collective-permute-start.14 = (bf16[16,256]{1,0:T(8,128)(2,1)S(1)}, bf16[16,256]{1,0:T(8,128)(2,1)S(1)}, u32[]{:S(2)}, u32[]{:S(2)}) collective-permute-start(bf16[16,256]{1,0:T(8,128)(2,1)S(1)} %shard_map.132.mine_ref), channel_id=1, source_target_pairs={{0,1},{1,0},{2,3},{3,2},{4,5},{5,4},{6,7},{7,6},{8,9},{9,8},{10,11... | collective-permute-start | bytes 24584 | tf_op jit(solution)/shard_map/ppermute | solution.py:426
  93.4 2.5 %collective-permute-start.22 = (bf16[32,4096]{1,0:T(8,128)(2,1)S(1)}, bf16[32,4096]{1,0:T(8,128)(2,1)S(1)}, u32[]{:S(2)}, u32[]{:S(2)}) collective-permute-start(bf16[32,4096]{1,0:T(8,128)(2,1)S(1)} %slice.21), channel_id=1, source_target_pairs={{0,6},{1,7},{2,0},{3,1},{4,2},{5,3},{6,4},{7,5},{8,14},{9,15},{10,... | collective-permute-start | bytes 786440 | tf_op jit(solution)/shard_map/ppermute | solution.py:426
  95.9 1.5 collective-permute-start.24
  98.2 2.2 %collective-permute-done.23.refs_10_ = bf16[16,4096]{1,0:T(8,128)(2,1)S(1)} collective-permute-done((bf16[16,4096]{1,0:T(8,128)(2,1)S(1)}, bf16[16,4096]{1,0:T(8,128)(2,1)S(1)}, u32[]{:S(2)}, u32[]{:S(2)}) %collective-permute-start.23) | collective-permute-done | bytes 131104 | tf_op jit(solution)/shard_map/ppermute | solution.py:426
  100.3 2.8 %collective-permute-done.24.refs_11_ = bf16[16,4096]{1,0:T(8,128)(2,1)S(1)} collective-permute-done((bf16[16,4096]{1,0:T(8,128)(2,1)S(1)}, bf16[16,4096]{1,0:T(8,128)(2,1)S(1)}, u32[]{:S(2)}, u32[]{:S(2)}) %collective-permute-start.24) | collective-permute-done | bytes 131104 | tf_op jit(solution)/shard_map/ppermute | solution.py:426
  106.4 2.3 %shard_map.133 = (f32[16,4096]{1,0:T(8,128)S(1)}, bf16[16,4096]{1,0:T(8,128)(2,1)S(1)}, bf16[256,4096]{1,0:T(8,128)(2,1)S(1)}, bf16[256,4096]{1,0:T(8,128)(2,1)S(1)}) custom-call(f32[8,128]{1,0:T(8,128)S(1)} %broadcast_in_dim.34.low_ref, bf16[16,256]{1,0:T(8,128)(2,1)S(1)} %shard_map.132.mine_ref, bf16[16,256]{1,0:T(8,128)(2,1)S(1)} %collective-permute-done.14.other_ref, ...), custom_call_target="tpu_custom_call" | custom-call | tf_op jit(solution)/shard_map/pallas_call | solution.py:602
  108.7 1.5 collective-permute-start.25
  110.3 2.0 %collective-permute-start.26 = (bf16[16,4096]{1,0:T(8,128)(2,1)S(1)}, bf16[16,4096]{1,0:T(8,128)(2,1)S(1)}, u32[]{:S(2)}, u32[]{:S(2)}) collective-permute-start(bf16[16,4096]{1,0:T(8,128)(2,1)S(1)} %get-tuple-element.96), channel_id=1, source_target_pairs={{1,16},{16,1},{3,18},{18,3},{5,20},{20,5},{7,22},{22,7},{9,24},{24... | collective-permute-start | bytes 393224 | tf_op jit(solution)/shard_map/ppermute | solution.py:583
  112.3 5.8 %collective-permute-done.26.off_ref = bf16[16,4096]{1,0:T(8,128)(2,1)S(1)} collective-permute-done((bf16[16,4096]{1,0:T(8,128)(2,1)S(1)}, bf16[16,4096]{1,0:T(8,128)(2,1)S(1)}, u32[]{:S(2)}, u32[]{:S(2)}) %collective-permute-start.26) | collective-permute-done | bytes 131104 | tf_op jit(solution)/shard_map/ppermute | solution.py:583
  118.0 1.2 shard_map.134
  120.5 16.9 %all_to_all.34.parts_ref = f32[16,8,512]{2,1,0:T(8,128)S(1)} all-to-all(f32[16,8,512]{2,1,0:T(8,128)S(1)} %shard_map.135), channel_id=1, replica_groups=mesh['dom'=16,'orb'=16] {'dom'}, dimensions={0} | all-to-all | bytes 524288 | tf_op jit(solution)/shard_map/all_to_all | solution.py:590
  137.5 2.0 %collective-permute-start.28 = (bf16[16,256]{1,0:T(8,128)(2,1)S(1)}, bf16[16,256]{1,0:T(8,128)(2,1)S(1)}, u32[]{:S(2)}, u32[]{:S(2)}) collective-permute-start(bf16[16,256]{1,0:T(8,128)(2,1)S(1)} %shard_map.136.mine_ref), channel_id=1, source_target_pairs={{0,1},{1,0},{2,3},{3,2},{4,5},{5,4},{6,7},{7,6},{8,9},{9,8},{10,11... | collective-permute-start | bytes 24584 | tf_op jit(solution)/shard_map/ppermute | solution.py:426
  141.4 2.1 %collective-permute-start.30 = (bf16[16,4096]{1,0:T(8,128)(2,1)S(1)}, bf16[16,4096]{1,0:T(8,128)(2,1)S(1)}, u32[]{:S(2)}, u32[]{:S(2)}) collective-permute-start(bf16[16,4096]{1,0:T(8,128)(2,1)S(1)} %get-tuple-element.103), channel_id=1, source_target_pairs={{1,16},{16,1},{3,18},{18,3},{5,20},{20,5},{7,22},{22,7},{9,24},{24... | collective-permute-start | bytes 393224 | tf_op jit(solution)/shard_map/ppermute | solution.py:583
  143.6 5.6 %collective-permute-done.30.off_ref = bf16[16,4096]{1,0:T(8,128)(2,1)S(1)} collective-permute-done((bf16[16,4096]{1,0:T(8,128)(2,1)S(1)}, bf16[16,4096]{1,0:T(8,128)(2,1)S(1)}, u32[]{:S(2)}, u32[]{:S(2)}) %collective-permute-start.30) | collective-permute-done | bytes 131104 | tf_op jit(solution)/shard_map/ppermute | solution.py:583
  149.2 1.2 shard_map.138
  152.4 4.5 %all-to-all-start.5 = ((f32[16,8,512]{2,1,0:T(8,128)}), f32[16,8,512]{2,1,0:T(8,128)S(1)}, u32[]{:S(2)}, u32[]{:S(2)}) async-start(f32[16,8,512]{2,1,0:T(8,128)} %shard_map.139), calls=%async_computation.5 | async-start | bytes 524288 | tf_op jit(solution)/shard_map/all_to_all | solution.py:590
  157.9 11.9 %all-to-all-done.5.parts_ref = f32[16,8,512]{2,1,0:T(8,128)S(1)} async-done(((f32[16,8,512]{2,1,0:T(8,128)}), f32[16,8,512]{2,1,0:T(8,128)S(1)}, u32[]{:S(2)}, u32[]{:S(2)}) %all-to-all-start.5) | async-done | bytes 262176 | tf_op jit(solution)/shard_map/all_to_all | solution.py:590
  169.8 1.7 collective-permute-start.32
  172.3 1.6 copy-done.1
  173.8 1.4 shard_map.143
  175.6 5.2 %all-to-all-start.6 = ((f32[256,2,128]{2,1,0:T(2,128)}), f32[256,2,128]{2,1,0:T(2,128)S(1)}, u32[]{:S(2)}, u32[]{:S(2)}) async-start(f32[256,2,128]{2,1,0:T(2,128)} %bitcast.15), calls=%async_computation.6 | async-start | bytes 524288 | tf_op jit(solution)/shard_map/all_to_all | solution.py:612
  183.1 13.1 %all-to-all-done.6.terms_ref = f32[256,2,128]{2,1,0:T(2,128)S(1)} async-done(((f32[256,2,128]{2,1,0:T(2,128)}), f32[256,2,128]{2,1,0:T(2,128)S(1)}, u32[]{:S(2)}, u32[]{:S(2)}) %all-to-all-start.6) | async-done | bytes 262176 | tf_op jit(solution)/shard_map/all_to_all | solution.py:612
  196.2 1.9 shard_map.145
  (116 shorter events, 24.4 us)
Async XLA Ops:
  1.3 9.2 %copy-start.8 = (f32[8,2,32,128]{3,2,1,0:T(8,128)S(1)}, f32[8,2,32,128]{3,2,1,0:T(8,128)}, u32[]{:S(2)}) copy-start(f32[8,2,32,128]{3,2,1,0:T(8,128)} %field_ref.1) | copy-start | bytes 786436
  4.2 12.5 %collective-permute-start.5 = (bf16[128,32,128]{2,1,0:T(8,128)(2,1)}, bf16[128,32,128]{2,1,0:T(8,128)(2,1)S(1)}, u32[]{:S(2)}, u32[]{:S(2)}) collective-permute-start(bf16[128,32,128]{2,1,0:T(8,128)(2,1)} %get-tuple-element.69), channel_id=1, source_target_pairs={{0,1},{1,0},{2,3},{3,2},{4,5},{5,4},{6,7},{7,6},{8,9},{9,8},{10,11... | collective-permute-start | bytes 3145736 | tf_op jit(solution)/shard_map/ppermute | solution.py:426
  9.1 9.3 %collective-permute-start.6 = (bf16[128,32,128]{2,1,0:T(8,128)(2,1)}, bf16[128,32,128]{2,1,0:T(8,128)(2,1)S(1)}, u32[]{:S(2)}, u32[]{:S(2)}) collective-permute-start(bf16[128,32,128]{2,1,0:T(8,128)(2,1)} %shard_map.125), channel_id=1, source_target_pairs={{0,1},{15,14},{16,17},{31,30},{32,33},{47,46},{48,49},{63,62},{64,... | collective-permute-start | bytes 3145736 | tf_op jit(solution)/shard_map/ppermute | solution.py:426
  10.6 3.3 %collective-permute-start.1 = (f32[8,4096]{1,0:T(8,128)S(1)}, f32[8,4096]{1,0:T(8,128)S(1)}, u32[]{:S(2)}, u32[]{:S(2)}) collective-permute-start(f32[8,4096]{1,0:T(8,128)S(1)} %get-tuple-element.67), channel_id=1, source_target_pairs={{0,1},{1,0},{2,3},{3,2},{4,5},{5,4},{6,7},{7,6},{8,9},{9,8},{10,11... | collective-permute-start | bytes 393224 | tf_op jit(solution)/shard_map/ppermute | solution.py:426
  12.6 5.7 %copy-start.11 = (bf16[2,128,2,32,128]{4,3,2,1,0:T(8,128)(2,1)S(1)}, bf16[2,128,2,32,128]{4,3,2,1,0:T(8,128)(2,1)}, u32[]{:S(2)}) copy-start(bf16[2,128,2,32,128]{4,3,2,1,0:T(8,128)(2,1)} %occupied_ref.7) | copy-start | bytes 12582916
  14.0 13.6 %collective-permute-start.2 = (bf16[16,4096]{1,0:T(8,128)(2,1)S(1)}, bf16[16,4096]{1,0:T(8,128)(2,1)S(1)}, u32[]{:S(2)}, u32[]{:S(2)}) collective-permute-start(bf16[16,4096]{1,0:T(8,128)(2,1)S(1)} %get-tuple-element.68), channel_id=1, source_target_pairs={{0,2},{1,3},{2,4},{3,5},{4,6},{5,7},{6,0},{7,1},{8,10},{9,11},{10,... | collective-permute-start | bytes 393224 | tf_op jit(solution)/shard_map/ppermute | solution.py:426
  14.0 18.4 %collective-permute-start.3 = (bf16[16,4096]{1,0:T(8,128)(2,1)S(1)}, bf16[16,4096]{1,0:T(8,128)(2,1)}, u32[]{:S(2)}, u32[]{:S(2)}) collective-permute-start(bf16[16,4096]{1,0:T(8,128)(2,1)S(1)} %get-tuple-element.68), channel_id=1, source_target_pairs={{0,6},{1,7},{2,0},{3,1},{4,2},{5,3},{6,4},{7,5},{8,14},{9,15},{10,... | collective-permute-start | bytes 393224 | tf_op jit(solution)/shard_map/ppermute | solution.py:426
  16.7 15.8 %collective-permute-start.4 = (bf16[16,4096]{1,0:T(8,128)(2,1)S(1)}, bf16[16,4096]{1,0:T(8,128)(2,1)}, u32[]{:S(2)}, u32[]{:S(2)}) collective-permute-start(bf16[16,4096]{1,0:T(8,128)(2,1)S(1)} %get-tuple-element.68), channel_id=1, source_target_pairs={{0,4},{1,5},{2,6},{3,7},{4,0},{5,1},{6,2},{7,3},{8,12},{9,13},{10,... | collective-permute-start | bytes 393224 | tf_op jit(solution)/shard_map/ppermute | solution.py:426
  19.9 32.0 %copy-start.13 = (s32[8]{0:T(128)S(1)}, s32[8]{0:T(128)}, u32[]{:S(2)}) copy-start(s32[8]{0:T(128)} %param.15) | copy-start | bytes 100
  19.9 12.6 %collective-permute-start.7 = (bf16[32,32,128]{2,1,0:T(8,128)(2,1)S(1)}, bf16[32,32,128]{2,1,0:T(8,128)(2,1)S(1)}, u32[]{:S(2)}, u32[]{:S(2)}) collective-permute-start(bf16[32,32,128]{2,1,0:T(8,128)(2,1)S(1)} %get-tuple-element.71), channel_id=1, source_target_pairs={{0,2},{1,3},{14,8},{15,9},{16,18},{17,19},{30,24},{31,25},{32,34},... | collective-permute-start | bytes 786440 | tf_op jit(solution)/shard_map/ppermute | solution.py:426
  22.3 12.1 %collective-permute-start.10 = (bf16[32,32,128]{2,1,0:T(8,128)(2,1)}, bf16[32,32,128]{2,1,0:T(8,128)(2,1)S(1)}, u32[]{:S(2)}, u32[]{:S(2)}) collective-permute-start(bf16[32,32,128]{2,1,0:T(8,128)(2,1)} %get-tuple-element.78), channel_id=1, source_target_pairs={{0,6},{1,7},{14,12},{15,13},{16,22},{17,23},{30,28},{31,29},{32,38... | collective-permute-start | bytes 786440 | tf_op jit(solution)/shard_map/ppermute | solution.py:426
  23.7 19.6 %all-to-all-start.1 = ((bf16[8,16,32,128]{3,2,1,0:T(8,128)(2,1)}), bf16[8,16,32,128]{3,2,1,0:T(8,128)(2,1)S(1)}, u32[]{:S(2)}, u32[]{:S(2)}) async-start(bf16[8,16,32,128]{3,2,1,0:T(8,128)(2,1)} %bitcast.7), calls=%async_computation.1 | async-start | bytes 2097152 | tf_op jit(solution)/shard_map/all_to_all | solution.py:477
  27.6 15.1 %collective-permute-start.9 = (bf16[32,32,128]{2,1,0:T(8,128)(2,1)}, bf16[32,32,128]{2,1,0:T(8,128)(2,1)S(1)}, u32[]{:S(2)}, u32[]{:S(2)}) collective-permute-start(bf16[32,32,128]{2,1,0:T(8,128)(2,1)} %get-tuple-element.77), channel_id=1, source_target_pairs={{0,4},{1,5},{14,10},{15,11},{16,20},{17,21},{30,26},{31,27},{32,36... | collective-permute-start | bytes 786440 | tf_op jit(solution)/shard_map/ppermute | solution.py:426
  34.4 21.0 %collective-permute-start.8 = (bf16[64,4096]{1,0:T(8,128)(2,1)S(1)}, bf16[64,4096]{1,0:T(8,128)(2,1)S(1)}, u32[]{:S(2)}, u32[]{:S(2)}) collective-permute-start(bf16[64,4096]{1,0:T(8,128)(2,1)S(1)} %constant_dynamic-update-slice_fusion.refs_0_), channel_id=1, source_target_pairs={{0,8},{1,9},{2,10},{3,11},{4,12},{5,13},{6,14},{7,15},{8,0},{9,1},... | collective-permute-start | bytes 1572872 | tf_op jit(solution)/shard_map/ppermute | solution.py:426
  44.1 17.3 %collective-permute-start.12 = (bf16[32,4096]{1,0:T(8,128)(2,1)S(1)}, bf16[32,4096]{1,0:T(8,128)(2,1)S(1)}, u32[]{:S(2)}, u32[]{:S(2)}) collective-permute-start(bf16[32,4096]{1,0:T(8,128)(2,1)S(1)} %get-tuple-element.82.refs_3_.refs_2_), channel_id=1, source_target_pairs={{0,2},{1,3},{2,4},{3,5},{4,6},{5,7},{6,0},{7,1},{8,10},{9,11},{10,... | collective-permute-start | bytes 786440 | tf_op jit(solution)/shard_map/ppermute | solution.py:426
  44.1 17.2 %collective-permute-start.13 = (bf16[32,4096]{1,0:T(8,128)(2,1)S(1)}, bf16[32,4096]{1,0:T(8,128)(2,1)S(1)}, u32[]{:S(2)}, u32[]{:S(2)}) collective-permute-start(bf16[32,4096]{1,0:T(8,128)(2,1)S(1)} %get-tuple-element.82.refs_3_.refs_2_), channel_id=1, source_target_pairs={{0,6},{1,7},{2,0},{3,1},{4,2},{5,3},{6,4},{7,5},{8,14},{9,15},{10,... | collective-permute-start | bytes 786440 | tf_op jit(solution)/shard_map/ppermute | solution.py:426
  46.8 14.5 %collective-permute-start.11 = (bf16[32,4096]{1,0:T(8,128)(2,1)S(1)}, bf16[32,4096]{1,0:T(8,128)(2,1)S(1)}, u32[]{:S(2)}, u32[]{:S(2)}) collective-permute-start(bf16[32,4096]{1,0:T(8,128)(2,1)S(1)} %get-tuple-element.81.refs_2_.refs_0_), channel_id=1, source_target_pairs={{0,8},{1,9},{2,10},{3,11},{4,12},{5,13},{6,14},{7,15},{8,0},{9,1},... | collective-permute-start | bytes 786440 | tf_op jit(solution)/shard_map/ppermute | solution.py:426
  52.8 27.5 %collective-permute-start.15 = (f32[8,1]{0,1:T(1,128)S(1)}, f32[8,1]{0,1:T(1,128)S(1)}, u32[]{:S(2)}, u32[]{:S(2)}) collective-permute-start(f32[8,1]{0,1:T(1,128)S(1)} %bitcast.37), channel_id=1, source_target_pairs={{0,1},{1,0},{2,3},{3,2},{4,5},{5,4},{6,7},{7,6},{8,9},{9,8},{10,11... | collective-permute-start | bytes 104 | tf_op jit(solution)/shard_map/ppermute | solution.py:426
  57.2 9.9 %all-to-all-start.2 = ((f32[16,8,128]{2,1,0:T(8,128)}), f32[16,8,128]{2,1,0:T(8,128)S(1)}, u32[]{:S(2)}, u32[]{:S(2)}) async-start(f32[16,8,128]{2,1,0:T(8,128)} %shard_map.129), calls=%async_computation.2 | async-start | bytes 131072 | tf_op jit(solution)/shard_map/all_to_all | solution.py:517
  62.2 40.9 %copy-start.6 = (bf16[96,4096]{1,0:T(8,128)(2,1)}, bf16[96,4096]{1,0:T(8,128)(2,1)S(1)}, u32[]{:S(2)}) copy-start(bf16[96,4096]{1,0:T(8,128)(2,1)S(1)} %get-tuple-element.86.refs_6_) | copy-start | bytes 2359300
  62.2 30.8 %collective-permute-start.16 = (bf16[96,4096]{1,0:T(8,128)(2,1)S(1)}, bf16[96,4096]{1,0:T(8,128)(2,1)}, u32[]{:S(2)}, u32[]{:S(2)}) collective-permute-start(bf16[96,4096]{1,0:T(8,128)(2,1)S(1)} %get-tuple-element.86.refs_6_), channel_id=1, source_target_pairs={{0,8},{1,9},{2,10},{3,11},{4,12},{5,13},{6,14},{7,15},{8,0},{9,1},... | collective-permute-start | bytes 2359304 | tf_op jit(solution)/shard_map/ppermute | solution.py:426
  63.6 29.3 %collective-permute-start.17 = (bf16[64,4096]{1,0:T(8,128)(2,1)}, bf16[64,4096]{1,0:T(8,128)(2,1)S(1)}, u32[]{:S(2)}, u32[]{:S(2)}) collective-permute-start(bf16[64,4096]{1,0:T(8,128)(2,1)} %get-tuple-element.89.refs_1_), channel_id=1, source_target_pairs={{0,2},{1,3},{2,4},{3,5},{4,6},{5,7},{6,0},{7,1},{8,10},{9,11},{10,... | collective-permute-start | bytes 1572872 | tf_op jit(solution)/shard_map/ppermute | solution.py:426
  64.8 28.2 %collective-permute-start.18 = (bf16[64,4096]{1,0:T(8,128)(2,1)}, bf16[64,4096]{1,0:T(8,128)(2,1)S(1)}, u32[]{:S(2)}, u32[]{:S(2)}) collective-permute-start(bf16[64,4096]{1,0:T(8,128)(2,1)} %get-tuple-element.89.refs_1_), channel_id=1, source_target_pairs={{0,6},{1,7},{2,0},{3,1},{4,2},{5,3},{6,4},{7,5},{8,14},{9,15},{10,... | collective-permute-start | bytes 1572872 | tf_op jit(solution)/shard_map/ppermute | solution.py:426
  67.9 22.8 %all-to-all-start.3 = ((f32[16,8,512]{2,1,0:T(8,128)}), f32[16,8,512]{2,1,0:T(8,128)S(1)}, u32[]{:S(2)}, u32[]{:S(2)}) async-start(f32[16,8,512]{2,1,0:T(8,128)} %shard_map.131), calls=%async_computation.3 | async-start | bytes 524288 | tf_op jit(solution)/shard_map/all_to_all | solution.py:529
  79.9 10.9 %collective-permute-start.19 = (bf16[16,4096]{1,0:T(8,128)(2,1)S(1)}, bf16[16,4096]{1,0:T(8,128)(2,1)S(1)}, u32[]{:S(2)}, u32[]{:S(2)}) collective-permute-start(bf16[16,4096]{1,0:T(8,128)(2,1)S(1)} %slice.18), channel_id=1, source_target_pairs={{0,2},{1,3},{2,4},{3,5},{4,6},{5,7},{6,0},{7,1},{8,10},{9,11},{10,... | collective-permute-start | bytes 393224 | tf_op jit(solution)/shard_map/ppermute | solution.py:426
  80.3 12.7 %collective-permute-start.20 = (bf16[16,4096]{1,0:T(8,128)(2,1)S(1)}, bf16[16,4096]{1,0:T(8,128)(2,1)S(1)}, u32[]{:S(2)}, u32[]{:S(2)}) collective-permute-start(bf16[16,4096]{1,0:T(8,128)(2,1)S(1)} %slice.19), channel_id=1, source_target_pairs={{0,6},{1,7},{2,0},{3,1},{4,2},{5,3},{6,4},{7,5},{8,14},{9,15},{10,... | collective-permute-start | bytes 393224 | tf_op jit(solution)/shard_map/ppermute | solution.py:426
  90.8 7.4 %collective-permute-start.14 = (bf16[16,256]{1,0:T(8,128)(2,1)S(1)}, bf16[16,256]{1,0:T(8,128)(2,1)S(1)}, u32[]{:S(2)}, u32[]{:S(2)}) collective-permute-start(bf16[16,256]{1,0:T(8,128)(2,1)S(1)} %shard_map.132.mine_ref), channel_id=1, source_target_pairs={{0,1},{1,0},{2,3},{3,2},{4,5},{5,4},{6,7},{7,6},{8,9},{9,8},{10,11... | collective-permute-start | bytes 24584 | tf_op jit(solution)/shard_map/ppermute | solution.py:426
  93.0 10.2 %copy-start.2 = (bf16[64,4096]{1,0:T(8,128)(2,1)}, bf16[64,4096]{1,0:T(8,128)(2,1)S(1)}, u32[]{:S(2)}) copy-start(bf16[64,4096]{1,0:T(8,128)(2,1)S(1)} %collective-permute-done.17.refs_3_) | copy-start | bytes 1572868
  93.0 10.2 %copy-start.4 = (bf16[64,4096]{1,0:T(8,128)(2,1)}, bf16[64,4096]{1,0:T(8,128)(2,1)S(1)}, u32[]{:S(2)}) copy-start(bf16[64,4096]{1,0:T(8,128)(2,1)S(1)} %collective-permute-done.18.refs_2_) | copy-start | bytes 1572868
  93.0 10.1 %collective-permute-start.21 = (bf16[32,4096]{1,0:T(8,128)(2,1)S(1)}, bf16[32,4096]{1,0:T(8,128)(2,1)S(1)}, u32[]{:S(2)}, u32[]{:S(2)}) collective-permute-start(bf16[32,4096]{1,0:T(8,128)(2,1)S(1)} %slice.20), channel_id=1, source_target_pairs={{0,2},{1,3},{2,4},{3,5},{4,6},{5,7},{6,0},{7,1},{8,10},{9,11},{10,... | collective-permute-start | bytes 786440 | tf_op jit(solution)/shard_map/ppermute | solution.py:426
  93.4 9.7 %collective-permute-start.22 = (bf16[32,4096]{1,0:T(8,128)(2,1)S(1)}, bf16[32,4096]{1,0:T(8,128)(2,1)S(1)}, u32[]{:S(2)}, u32[]{:S(2)}) collective-permute-start(bf16[32,4096]{1,0:T(8,128)(2,1)S(1)} %slice.21), channel_id=1, source_target_pairs={{0,6},{1,7},{2,0},{3,1},{4,2},{5,3},{6,4},{7,5},{8,14},{9,15},{10,... | collective-permute-start | bytes 786440 | tf_op jit(solution)/shard_map/ppermute | solution.py:426
  95.9 4.5 %collective-permute-start.23 = (bf16[16,4096]{1,0:T(8,128)(2,1)S(1)}, bf16[16,4096]{1,0:T(8,128)(2,1)S(1)}, u32[]{:S(2)}, u32[]{:S(2)}) collective-permute-start(bf16[16,4096]{1,0:T(8,128)(2,1)S(1)} %collective-permute-done.19.refs_8_), channel_id=1, source_target_pairs={{0,8},{1,9},{2,10},{3,11},{4,12},{5,13},{6,14},{7,15},{8,0},{9,1},... | collective-permute-start | bytes 393224 | tf_op jit(solution)/shard_map/ppermute | solution.py:426
  95.9 7.3 %collective-permute-start.24 = (bf16[16,4096]{1,0:T(8,128)(2,1)S(1)}, bf16[16,4096]{1,0:T(8,128)(2,1)S(1)}, u32[]{:S(2)}, u32[]{:S(2)}) collective-permute-start(bf16[16,4096]{1,0:T(8,128)(2,1)S(1)} %collective-permute-done.20.refs_9_), channel_id=1, source_target_pairs={{0,8},{1,9},{2,10},{3,11},{4,12},{5,13},{6,14},{7,15},{8,0},{9,1},... | collective-permute-start | bytes 393224 | tf_op jit(solution)/shard_map/ppermute | solution.py:426
  108.7 40.5 %copy-start = (bf16[256,4096]{1,0:T(8,128)(2,1)}, bf16[256,4096]{1,0:T(8,128)(2,1)S(1)}, u32[]{:S(2)}) copy-start(bf16[256,4096]{1,0:T(8,128)(2,1)S(1)} %get-tuple-element.98.second_ref.refs_2_.refs_3_) | copy-start | bytes 6291460
  108.7 9.3 %collective-permute-start.25 = (f32[16,4096]{1,0:T(8,128)S(1)}, f32[16,4096]{1,0:T(8,128)S(1)}, u32[]{:S(2)}, u32[]{:S(2)}) collective-permute-start(f32[16,4096]{1,0:T(8,128)S(1)} %get-tuple-element.95.x_ref.refs_0_), channel_id=1, source_target_pairs={{0,1},{1,0},{2,3},{3,2},{4,5},{5,4},{6,7},{7,6},{8,9},{9,8},{10,11... | collective-permute-start | bytes 786440 | tf_op jit(solution)/shard_map/ppermute | solution.py:426
  110.3 7.8 %collective-permute-start.26 = (bf16[16,4096]{1,0:T(8,128)(2,1)S(1)}, bf16[16,4096]{1,0:T(8,128)(2,1)S(1)}, u32[]{:S(2)}, u32[]{:S(2)}) collective-permute-start(bf16[16,4096]{1,0:T(8,128)(2,1)S(1)} %get-tuple-element.96), channel_id=1, source_target_pairs={{1,16},{16,1},{3,18},{18,3},{5,20},{20,5},{7,22},{22,7},{9,24},{24... | collective-permute-start | bytes 393224 | tf_op jit(solution)/shard_map/ppermute | solution.py:583
  119.3 1.2 collective-permute-start.27
  137.5 2.8 %collective-permute-start.28 = (bf16[16,256]{1,0:T(8,128)(2,1)S(1)}, bf16[16,256]{1,0:T(8,128)(2,1)S(1)}, u32[]{:S(2)}, u32[]{:S(2)}) collective-permute-start(bf16[16,256]{1,0:T(8,128)(2,1)S(1)} %shard_map.136.mine_ref), channel_id=1, source_target_pairs={{0,1},{1,0},{2,3},{3,2},{4,5},{5,4},{6,7},{7,6},{8,9},{9,8},{10,11... | collective-permute-start | bytes 24584 | tf_op jit(solution)/shard_map/ppermute | solution.py:426
  141.0 15.9 %copy-start.12 = (bf16[8,2,32,128]{3,2,1,0:T(8,128)(2,1)S(1)}, bf16[8,2,32,128]{3,2,1,0:T(8,128)(2,1)}, u32[]{:S(2)}) copy-start(bf16[8,2,32,128]{3,2,1,0:T(8,128)(2,1)} %param.18) | copy-start | bytes 393220
  141.0 8.2 %collective-permute-start.29 = (f32[16,4096]{1,0:T(8,128)S(1)}, f32[16,4096]{1,0:T(8,128)S(1)}, u32[]{:S(2)}, u32[]{:S(2)}) collective-permute-start(f32[16,4096]{1,0:T(8,128)S(1)} %get-tuple-element.102.x_ref.refs_0_), channel_id=1, source_target_pairs={{0,1},{1,0},{2,3},{3,2},{4,5},{5,4},{6,7},{7,6},{8,9},{9,8},{10,11... | collective-permute-start | bytes 786440 | tf_op jit(solution)/shard_map/ppermute | solution.py:426
  141.4 7.8 %collective-permute-start.30 = (bf16[16,4096]{1,0:T(8,128)(2,1)S(1)}, bf16[16,4096]{1,0:T(8,128)(2,1)S(1)}, u32[]{:S(2)}, u32[]{:S(2)}) collective-permute-start(bf16[16,4096]{1,0:T(8,128)(2,1)S(1)} %get-tuple-element.103), channel_id=1, source_target_pairs={{1,16},{16,1},{3,18},{18,3},{5,20},{20,5},{7,22},{22,7},{9,24},{24... | collective-permute-start | bytes 393224 | tf_op jit(solution)/shard_map/ppermute | solution.py:583
  150.5 1.2 collective-permute-start.31
  152.4 17.3 %all-to-all-start.5 = ((f32[16,8,512]{2,1,0:T(8,128)}), f32[16,8,512]{2,1,0:T(8,128)S(1)}, u32[]{:S(2)}, u32[]{:S(2)}) async-start(f32[16,8,512]{2,1,0:T(8,128)} %shard_map.139), calls=%async_computation.5 | async-start | bytes 524288 | tf_op jit(solution)/shard_map/all_to_all | solution.py:590
  157.1 14.3 %collective-permute-start.33 = (bf16[8,4096]{1,0:T(8,128)(2,1)S(1)}, bf16[8,4096]{1,0:T(8,128)(2,1)S(1)}, u32[]{:S(2)}, u32[]{:S(2)}) collective-permute-start(bf16[8,4096]{1,0:T(8,128)(2,1)S(1)} %convert_element_type.25), channel_id=1, source_target_pairs={{0,1},{1,0},{2,3},{3,2},{4,5},{5,4},{6,7},{7,6},{8,9},{9,8},{10,11... | collective-permute-start | bytes 196616 | tf_op jit(solution)/shard_map/ppermute | solution.py:426
  169.8 2.5 %collective-permute-start.32 = (bf16[16,256]{1,0:T(8,128)(2,1)S(1)}, bf16[16,256]{1,0:T(8,128)(2,1)S(1)}, u32[]{:S(2)}, u32[]{:S(2)}) collective-permute-start(bf16[16,256]{1,0:T(8,128)(2,1)S(1)} %get-tuple-element.106.mine_ref), channel_id=1, source_target_pairs={{0,1},{1,0},{2,3},{3,2},{4,5},{5,4},{6,7},{7,6},{8,9},{9,8},{10,11... | collective-permute-start | bytes 24584 | tf_op jit(solution)/shard_map/ppermute | solution.py:426
  171.4 24.8 %copy-start.9 = (f32[32,32]{1,0:T(8,128)S(1)}, f32[32,32]{1,0:T(8,128)}, u32[]{:S(2)}) copy-start(f32[32,32]{1,0:T(8,128)} %smoother_ref.1) | copy-start | bytes 12292
  175.3 7.0 %collective-permute-start.34 = (f32[8,4096]{1,0:T(8,128)S(1)}, f32[8,4096]{1,0:T(8,128)S(1)}, u32[]{:S(2)}, u32[]{:S(2)}) collective-permute-start(f32[8,4096]{1,0:T(8,128)S(1)} %get-tuple-element.111), channel_id=1, source_target_pairs={{0,1},{1,0},{2,3},{3,2},{4,5},{5,4},{6,7},{7,6},{8,9},{9,8},{10,11... | collective-permute-start | bytes 393224 | tf_op jit(solution)/shard_map/ppermute | solution.py:426
  175.6 20.6 %all-to-all-start.6 = ((f32[256,2,128]{2,1,0:T(2,128)}), f32[256,2,128]{2,1,0:T(2,128)S(1)}, u32[]{:S(2)}, u32[]{:S(2)}) async-start(f32[256,2,128]{2,1,0:T(2,128)} %bitcast.15), calls=%async_computation.6 | async-start | bytes 524288 | tf_op jit(solution)/shard_map/all_to_all | solution.py:612
  (5 other events, 5.5 us)

commit v8 on v7

--- a/solution.py
+++ b/solution.py
@@ -467,7 +467,7 @@
         pairs = [(c, 2 * s + c) for c in range(2)]
         pairs += [(n_orb - 2 + c, 2 * (ring + (ring - 1 + s) % ring) + c) for c in range(2)]
         got.append(permute(pieces[s], pairs))
-    rhs_up, rhs_down, rhs_far, got[1] = lax.optimization_barrier((rhs_up, rhs_down, rhs_far, got[1]))
+    rhs_up, rhs_down, rhs_far, got[2] = lax.optimization_barrier((rhs_up, rhs_down, rhs_far, got[2]))
     rhs_line = jnp.concatenate([rhs_b, rhs_up, rhs_down, rhs_far], axis=0)
     rhs_line_x = permute(rhs_line, swap_x)
     fixed = call(share_kernel, piece_shape, [SMEM] + [VMEM] * ring, VMEM)(plan, *got)

time: 199 us -> 201 us (1.010)
  waiting for transfers between devices: 63.7 us -> 66.3 us
    ppermute x32, waiting for transfers between devices: 18.5 us -> 21.1 us  [permute(): return lax.ppermute(value, 'orb', pairs)]
where the time goes in v8:
time: 201 us; the launch traced here: 200 us
  starting transfers between devices  78.3 us (39%)
  waiting for transfers between devices  66.3 us (33%)
  Pallas kernels  23 us (11%)
  blocking collectives  16.9 us (8%)
  local copies, waits for them, and re-layouts  8.51 us (4%)
  other arithmetic  4.83 us (2%)
    ppermute x32, starting transfers between devices, permute(): return lax.ppermute(value, 'orb', pairs)  48.3 us
    ppermute x32, waiting for transfers between devices, permute(): return lax.ppermute(value, 'orb', pairs)  21.1 us
    all_to_all x1, blocking collectives, per_device(): parts = lax.all_to_all(spread, 'dom', 0, 0, tiled=True)  16.9 us
    all_to_all x1, waiting for transfers between devices, per_device(): lax.all_to_all(raw.reshape((n_dom * n_orb,) + raw.shape[2:]), ('dom', 'or...  13.1 us
    all_to_all x1, waiting for transfers between devices, per_device(): parts = lax.all_to_all(spread, 'dom', 0, 0, tiled=True)  11.9 us
    ppermute x2, waiting for transfers between devices, per_device(): off = lax.ppermute(x_b, ('dom', 'orb'), across)  11.4 us
    all_to_all x1, starting transfers between devices, per_device(): lax.all_to_all(call(spread_shares_kernel, spread_shape)(parts), 'dom', 0,...  9.1 us
    all_to_all x1, waiting for transfers between devices, per_device(): lax.all_to_all(call(spread_shares_kernel, spread_shape)(parts), 'dom', 0,...  8.02 us
  transfers between devices with their start and end apart: 39, of which 14 were waited for; matrix products, arithmetic and copies ran while one was open for 4% of the time, Pallas kernels for 5%

profile of v8, /device:TPU:1, one launch (start us, length us, event | category | flops | bytes accessed | tf_op | source)
XLA Modules:
  0.0 199.8 jit_solution(10946512040146072379)
XLA Ops:
  1.3 2.9 %shard_map.121 = (s32[40]{0:T(128)S(1)}, s32[1]{0:T(128)}, bf16[128,32,128]{2,1,0:T(8,128)(2,1)}) custom-call(s32[4]{0:T(128)S(1)} %copy-done.10, s32[1]{0:T(128)} %bitcast.6.dev_ref, bf16[2,128,2,32,128]{4,3,2,1,0:T(8,128)(2,1)} %occupied_ref.7), custom_call_target="tpu_custom_call" | custom-call | tf_op jit(solution)/shard_map/pallas_call | solution.py:436
  4.2 3.3 %collective-permute-start.5 = (bf16[128,32,128]{2,1,0:T(8,128)(2,1)}, bf16[128,32,128]{2,1,0:T(8,128)(2,1)S(1)}, u32[]{:S(2)}, u32[]{:S(2)}) collective-permute-start(bf16[128,32,128]{2,1,0:T(8,128)(2,1)} %get-tuple-element.69), channel_id=1, source_target_pairs={{0,1},{1,0},{2,3},{3,2},{4,5},{5,4},{6,7},{7,6},{8,9},{9,8},{10,11... | collective-permute-start | bytes 3145736 | tf_op jit(solution)/shard_map/ppermute | solution.py:426
  7.5 1.6 shard_map.125
  9.1 1.3 collective-permute-start.6
  10.6 1.3 collective-permute-start.1
  12.7 1.3 collective-permute-done.1.other_ref
  14.0 2.7 %collective-permute-start.3 = (bf16[16,4096]{1,0:T(8,128)(2,1)S(1)}, bf16[16,4096]{1,0:T(8,128)(2,1)}, u32[]{:S(2)}, u32[]{:S(2)}) collective-permute-start(bf16[16,4096]{1,0:T(8,128)(2,1)S(1)} %get-tuple-element.68), channel_id=1, source_target_pairs={{0,6},{1,7},{2,0},{3,1},{4,2},{5,3},{6,4},{7,5},{8,14},{9,15},{10,... | collective-permute-start | bytes 393224 | tf_op jit(solution)/shard_map/ppermute | solution.py:426
  16.7 1.7 shard_map.124
  18.4 1.5 shard_map.126
  19.9 4.8 %collective-permute-start.7 = (bf16[32,32,128]{2,1,0:T(8,128)(2,1)S(1)}, bf16[32,32,128]{2,1,0:T(8,128)(2,1)S(1)}, u32[]{:S(2)}, u32[]{:S(2)}) collective-permute-start(bf16[32,32,128]{2,1,0:T(8,128)(2,1)S(1)} %get-tuple-element.71), channel_id=1, source_target_pairs={{0,4},{1,5},{14,10},{15,11},{16,20},{17,21},{30,26},{31,27},{32,36... | collective-permute-start | bytes 786440 | tf_op jit(solution)/shard_map/ppermute | solution.py:426
  24.7 1.3 collective-permute-start.10
  26.0 3.6 %all-to-all-start.1 = ((bf16[8,16,32,128]{3,2,1,0:T(8,128)(2,1)}), bf16[8,16,32,128]{3,2,1,0:T(8,128)(2,1)S(1)}, u32[]{:S(2)}, u32[]{:S(2)}) async-start(bf16[8,16,32,128]{3,2,1,0:T(8,128)(2,1)} %bitcast.7), calls=%async_computation.1 | async-start | bytes 2097152 | tf_op jit(solution)/shard_map/all_to_all | solution.py:477
  29.6 3.3 %collective-permute-start.9 = (bf16[32,32,128]{2,1,0:T(8,128)(2,1)}, bf16[32,32,128]{2,1,0:T(8,128)(2,1)S(1)}, u32[]{:S(2)}, u32[]{:S(2)}) collective-permute-start(bf16[32,32,128]{2,1,0:T(8,128)(2,1)} %get-tuple-element.76), channel_id=1, source_target_pairs={{0,2},{1,3},{14,8},{15,9},{16,18},{17,19},{30,24},{31,25},{32,34},... | collective-permute-start | bytes 786440 | tf_op jit(solution)/shard_map/ppermute | solution.py:426
  34.9 10.8 %collective-permute-done.9.refs_1_ = bf16[32,32,128]{2,1,0:T(8,128)(2,1)S(1)} collective-permute-done((bf16[32,32,128]{2,1,0:T(8,128)(2,1)}, bf16[32,32,128]{2,1,0:T(8,128)(2,1)S(1)}, u32[]{:S(2)}, u32[]{:S(2)}) %collective-permute-start.9) | collective-permute-done | bytes 262176 | tf_op jit(solution)/shard_map/ppermute | solution.py:426
  47.1 2.2 %collective-permute-start.12 = (bf16[32,4096]{1,0:T(8,128)(2,1)S(1)}, bf16[32,4096]{1,0:T(8,128)(2,1)S(1)}, u32[]{:S(2)}, u32[]{:S(2)}) collective-permute-start(bf16[32,4096]{1,0:T(8,128)(2,1)S(1)} %get-tuple-element.82.refs_3_.refs_2_), channel_id=1, source_target_pairs={{0,2},{1,3},{2,4},{3,5},{4,6},{5,7},{6,0},{7,1},{8,10},{9,11},{10,... | collective-permute-start | bytes 786440 | tf_op jit(solution)/shard_map/ppermute | solution.py:426
  49.8 5.3 %collective-permute-start.11 = (bf16[32,4096]{1,0:T(8,128)(2,1)S(1)}, bf16[32,4096]{1,0:T(8,128)(2,1)S(1)}, u32[]{:S(2)}, u32[]{:S(2)}) collective-permute-start(bf16[32,4096]{1,0:T(8,128)(2,1)S(1)} %get-tuple-element.81.refs_2_.refs_0_), channel_id=1, source_target_pairs={{0,8},{1,9},{2,10},{3,11},{4,12},{5,13},{6,14},{7,15},{8,0},{9,1},... | collective-permute-start | bytes 786440 | tf_op jit(solution)/shard_map/ppermute | solution.py:426
  56.1 2.0 %collective-permute-start.15 = (f32[8,1]{0,1:T(1,128)S(1)}, f32[8,1]{0,1:T(1,128)S(1)}, u32[]{:S(2)}, u32[]{:S(2)}) collective-permute-start(f32[8,1]{0,1:T(1,128)S(1)} %bitcast.37), channel_id=1, source_target_pairs={{0,1},{1,0},{2,3},{3,2},{4,5},{5,4},{6,7},{7,6},{8,9},{9,8},{10,11... | collective-permute-start | bytes 104 | tf_op jit(solution)/shard_map/ppermute | solution.py:426
  58.9 1.9 shard_map.129
  60.9 3.5 %all-to-all-start.2 = ((f32[16,8,128]{2,1,0:T(8,128)}), f32[16,8,128]{2,1,0:T(8,128)S(1)}, u32[]{:S(2)}, u32[]{:S(2)}) async-start(f32[16,8,128]{2,1,0:T(8,128)} %shard_map.129), calls=%async_computation.2 | async-start | bytes 131072 | tf_op jit(solution)/shard_map/all_to_all | solution.py:517
  65.3 1.4 collective-permute-start.16
  67.9 1.5 collective-permute-start.18
  71.0 9.1 %all-to-all-start.3 = ((f32[16,8,512]{2,1,0:T(8,128)}), f32[16,8,512]{2,1,0:T(8,128)S(1)}, u32[]{:S(2)}, u32[]{:S(2)}) async-start(f32[16,8,512]{2,1,0:T(8,128)} %shard_map.131), calls=%async_computation.3 | async-start | bytes 524288 | tf_op jit(solution)/shard_map/all_to_all | solution.py:529
  80.3 1.3 add_bitcast_fusion
  82.0 2.4 %collective-permute-start.20 = (bf16[16,4096]{1,0:T(8,128)(2,1)S(1)}, bf16[16,4096]{1,0:T(8,128)(2,1)S(1)}, u32[]{:S(2)}, u32[]{:S(2)}) collective-permute-start(bf16[16,4096]{1,0:T(8,128)(2,1)S(1)} %slice.19), channel_id=1, source_target_pairs={{0,6},{1,7},{2,0},{3,1},{4,2},{5,3},{6,4},{7,5},{8,14},{9,15},{10,... | collective-permute-start | bytes 393224 | tf_op jit(solution)/shard_map/ppermute | solution.py:426
  84.5 8.0 %all-to-all-done.3.parts_ref = f32[16,8,512]{2,1,0:T(8,128)S(1)} async-done(((f32[16,8,512]{2,1,0:T(8,128)}), f32[16,8,512]{2,1,0:T(8,128)S(1)}, u32[]{:S(2)}, u32[]{:S(2)}) %all-to-all-start.3) | async-done | bytes 262176 | tf_op jit(solution)/shard_map/all_to_all | solution.py:529
  92.5 2.2 %collective-permute-start.14 = (bf16[16,256]{1,0:T(8,128)(2,1)S(1)}, bf16[16,256]{1,0:T(8,128)(2,1)S(1)}, u32[]{:S(2)}, u32[]{:S(2)}) collective-permute-start(bf16[16,256]{1,0:T(8,128)(2,1)S(1)} %shard_map.132.mine_ref), channel_id=1, source_target_pairs={{0,1},{1,0},{2,3},{3,2},{4,5},{5,4},{6,7},{7,6},{8,9},{9,8},{10,11... | collective-permute-start | bytes 24584 | tf_op jit(solution)/shard_map/ppermute | solution.py:426
  95.1 2.5 %collective-permute-start.22 = (bf16[32,4096]{1,0:T(8,128)(2,1)S(1)}, bf16[32,4096]{1,0:T(8,128)(2,1)S(1)}, u32[]{:S(2)}, u32[]{:S(2)}) collective-permute-start(bf16[32,4096]{1,0:T(8,128)(2,1)S(1)} %slice.21), channel_id=1, source_target_pairs={{0,6},{1,7},{2,0},{3,1},{4,2},{5,3},{6,4},{7,5},{8,14},{9,15},{10,... | collective-permute-start | bytes 786440 | tf_op jit(solution)/shard_map/ppermute | solution.py:426
  97.6 1.5 collective-permute-start.24
  99.9 2.2 %collective-permute-done.23.refs_10_ = bf16[16,4096]{1,0:T(8,128)(2,1)S(1)} collective-permute-done((bf16[16,4096]{1,0:T(8,128)(2,1)S(1)}, bf16[16,4096]{1,0:T(8,128)(2,1)S(1)}, u32[]{:S(2)}, u32[]{:S(2)}) %collective-permute-start.23) | collective-permute-done | bytes 131104 | tf_op jit(solution)/shard_map/ppermute | solution.py:426
  102.1 2.8 %collective-permute-done.24.refs_11_ = bf16[16,4096]{1,0:T(8,128)(2,1)S(1)} collective-permute-done((bf16[16,4096]{1,0:T(8,128)(2,1)S(1)}, bf16[16,4096]{1,0:T(8,128)(2,1)S(1)}, u32[]{:S(2)}, u32[]{:S(2)}) %collective-permute-start.24) | collective-permute-done | bytes 131104 | tf_op jit(solution)/shard_map/ppermute | solution.py:426
  108.1 2.3 %shard_map.133 = (f32[16,4096]{1,0:T(8,128)S(1)}, bf16[16,4096]{1,0:T(8,128)(2,1)S(1)}, bf16[256,4096]{1,0:T(8,128)(2,1)S(1)}, bf16[256,4096]{1,0:T(8,128)(2,1)S(1)}) custom-call(f32[8,128]{1,0:T(8,128)S(1)} %broadcast_in_dim.34.low_ref, bf16[16,256]{1,0:T(8,128)(2,1)S(1)} %shard_map.132.mine_ref, bf16[16,256]{1,0:T(8,128)(2,1)S(1)} %collective-permute-done.14.other_ref, ...), custom_call_target="tpu_custom_call" | custom-call | tf_op jit(solution)/shard_map/pallas_call | solution.py:602
  110.4 1.5 collective-permute-start.25
  112.0 2.0 collective-permute-start.26
  114.0 5.8 %collective-permute-done.26.off_ref = bf16[16,4096]{1,0:T(8,128)(2,1)S(1)} collective-permute-done((bf16[16,4096]{1,0:T(8,128)(2,1)S(1)}, bf16[16,4096]{1,0:T(8,128)(2,1)S(1)}, u32[]{:S(2)}, u32[]{:S(2)}) %collective-permute-start.26) | collective-permute-done | bytes 131104 | tf_op jit(solution)/shard_map/ppermute | solution.py:583
  119.8 1.2 shard_map.134
  122.3 16.9 %all_to_all.34.parts_ref = f32[16,8,512]{2,1,0:T(8,128)S(1)} all-to-all(f32[16,8,512]{2,1,0:T(8,128)S(1)} %shard_map.135), channel_id=1, replica_groups=mesh['dom'=16,'orb'=16] {'dom'}, dimensions={0} | all-to-all | bytes 524288 | tf_op jit(solution)/shard_map/all_to_all | solution.py:590
  139.2 2.0 %collective-permute-start.28 = (bf16[16,256]{1,0:T(8,128)(2,1)S(1)}, bf16[16,256]{1,0:T(8,128)(2,1)S(1)}, u32[]{:S(2)}, u32[]{:S(2)}) collective-permute-start(bf16[16,256]{1,0:T(8,128)(2,1)S(1)} %shard_map.136.mine_ref), channel_id=1, source_target_pairs={{0,1},{1,0},{2,3},{3,2},{4,5},{5,4},{6,7},{7,6},{8,9},{9,8},{10,11... | collective-permute-start | bytes 24584 | tf_op jit(solution)/shard_map/ppermute | solution.py:426
  143.2 2.1 %collective-permute-start.30 = (bf16[16,4096]{1,0:T(8,128)(2,1)S(1)}, bf16[16,4096]{1,0:T(8,128)(2,1)S(1)}, u32[]{:S(2)}, u32[]{:S(2)}) collective-permute-start(bf16[16,4096]{1,0:T(8,128)(2,1)S(1)} %get-tuple-element.103), channel_id=1, source_target_pairs={{1,16},{16,1},{3,18},{18,3},{5,20},{20,5},{7,22},{22,7},{9,24},{24... | collective-permute-start | bytes 393224 | tf_op jit(solution)/shard_map/ppermute | solution.py:583
  145.3 5.6 %collective-permute-done.30.off_ref = bf16[16,4096]{1,0:T(8,128)(2,1)S(1)} collective-permute-done((bf16[16,4096]{1,0:T(8,128)(2,1)S(1)}, bf16[16,4096]{1,0:T(8,128)(2,1)S(1)}, u32[]{:S(2)}, u32[]{:S(2)}) %collective-permute-start.30) | collective-permute-done | bytes 131104 | tf_op jit(solution)/shard_map/ppermute | solution.py:583
  150.9 1.2 shard_map.138
  154.1 4.5 %all-to-all-start.5 = ((f32[16,8,512]{2,1,0:T(8,128)}), f32[16,8,512]{2,1,0:T(8,128)S(1)}, u32[]{:S(2)}, u32[]{:S(2)}) async-start(f32[16,8,512]{2,1,0:T(8,128)} %shard_map.139), calls=%async_computation.5 | async-start | bytes 524288 | tf_op jit(solution)/shard_map/all_to_all | solution.py:590
  159.6 11.9 %all-to-all-done.5.parts_ref = f32[16,8,512]{2,1,0:T(8,128)S(1)} async-done(((f32[16,8,512]{2,1,0:T(8,128)}), f32[16,8,512]{2,1,0:T(8,128)S(1)}, u32[]{:S(2)}, u32[]{:S(2)}) %all-to-all-start.5) | async-done | bytes 262176 | tf_op jit(solution)/shard_map/all_to_all | solution.py:590
  171.5 1.7 collective-permute-start.32
  174.0 1.6 copy-done.1
  175.6 1.4 shard_map.143
  177.4 5.2 %all-to-all-start.6 = ((f32[256,2,128]{2,1,0:T(2,128)}), f32[256,2,128]{2,1,0:T(2,128)S(1)}, u32[]{:S(2)}, u32[]{:S(2)}) async-start(f32[256,2,128]{2,1,0:T(2,128)} %bitcast.15), calls=%async_computation.6 | async-start | bytes 524288 | tf_op jit(solution)/shard_map/all_to_all | solution.py:612
  184.8 13.1 %all-to-all-done.6.terms_ref = f32[256,2,128]{2,1,0:T(2,128)S(1)} async-done(((f32[256,2,128]{2,1,0:T(2,128)}), f32[256,2,128]{2,1,0:T(2,128)S(1)}, u32[]{:S(2)}, u32[]{:S(2)}) %all-to-all-start.6) | async-done | bytes 262176 | tf_op jit(solution)/shard_map/all_to_all | solution.py:612
  197.9 1.9 shard_map.145
  (116 shorter events, 24.9 us)
Async XLA Ops:
  1.3 9.2 %copy-start.8 = (f32[8,2,32,128]{3,2,1,0:T(8,128)S(1)}, f32[8,2,32,128]{3,2,1,0:T(8,128)}, u32[]{:S(2)}) copy-start(f32[8,2,32,128]{3,2,1,0:T(8,128)} %field_ref.1) | copy-start | bytes 786436
  4.2 12.5 %collective-permute-start.5 = (bf16[128,32,128]{2,1,0:T(8,128)(2,1)}, bf16[128,32,128]{2,1,0:T(8,128)(2,1)S(1)}, u32[]{:S(2)}, u32[]{:S(2)}) collective-permute-start(bf16[128,32,128]{2,1,0:T(8,128)(2,1)} %get-tuple-element.69), channel_id=1, source_target_pairs={{0,1},{1,0},{2,3},{3,2},{4,5},{5,4},{6,7},{7,6},{8,9},{9,8},{10,11... | collective-permute-start | bytes 3145736 | tf_op jit(solution)/shard_map/ppermute | solution.py:426
  9.1 9.3 %collective-permute-start.6 = (bf16[128,32,128]{2,1,0:T(8,128)(2,1)}, bf16[128,32,128]{2,1,0:T(8,128)(2,1)S(1)}, u32[]{:S(2)}, u32[]{:S(2)}) collective-permute-start(bf16[128,32,128]{2,1,0:T(8,128)(2,1)} %shard_map.125), channel_id=1, source_target_pairs={{0,1},{15,14},{16,17},{31,30},{32,33},{47,46},{48,49},{63,62},{64,... | collective-permute-start | bytes 3145736 | tf_op jit(solution)/shard_map/ppermute | solution.py:426
  10.6 3.3 %collective-permute-start.1 = (f32[8,4096]{1,0:T(8,128)S(1)}, f32[8,4096]{1,0:T(8,128)S(1)}, u32[]{:S(2)}, u32[]{:S(2)}) collective-permute-start(f32[8,4096]{1,0:T(8,128)S(1)} %get-tuple-element.67), channel_id=1, source_target_pairs={{0,1},{1,0},{2,3},{3,2},{4,5},{5,4},{6,7},{7,6},{8,9},{9,8},{10,11... | collective-permute-start | bytes 393224 | tf_op jit(solution)/shard_map/ppermute | solution.py:426
  12.6 5.7 %copy-start.11 = (bf16[2,128,2,32,128]{4,3,2,1,0:T(8,128)(2,1)S(1)}, bf16[2,128,2,32,128]{4,3,2,1,0:T(8,128)(2,1)}, u32[]{:S(2)}) copy-start(bf16[2,128,2,32,128]{4,3,2,1,0:T(8,128)(2,1)} %occupied_ref.7) | copy-start | bytes 12582916
  14.0 15.7 %collective-permute-start.2 = (bf16[16,4096]{1,0:T(8,128)(2,1)S(1)}, bf16[16,4096]{1,0:T(8,128)(2,1)S(1)}, u32[]{:S(2)}, u32[]{:S(2)}) collective-permute-start(bf16[16,4096]{1,0:T(8,128)(2,1)S(1)} %get-tuple-element.68), channel_id=1, source_target_pairs={{0,2},{1,3},{2,4},{3,5},{4,6},{5,7},{6,0},{7,1},{8,10},{9,11},{10,... | collective-permute-start | bytes 393224 | tf_op jit(solution)/shard_map/ppermute | solution.py:426
  14.0 18.9 %collective-permute-start.3 = (bf16[16,4096]{1,0:T(8,128)(2,1)S(1)}, bf16[16,4096]{1,0:T(8,128)(2,1)}, u32[]{:S(2)}, u32[]{:S(2)}) collective-permute-start(bf16[16,4096]{1,0:T(8,128)(2,1)S(1)} %get-tuple-element.68), channel_id=1, source_target_pairs={{0,6},{1,7},{2,0},{3,1},{4,2},{5,3},{6,4},{7,5},{8,14},{9,15},{10,... | collective-permute-start | bytes 393224 | tf_op jit(solution)/shard_map/ppermute | solution.py:426
  16.7 16.2 %collective-permute-start.4 = (bf16[16,4096]{1,0:T(8,128)(2,1)S(1)}, bf16[16,4096]{1,0:T(8,128)(2,1)}, u32[]{:S(2)}, u32[]{:S(2)}) collective-permute-start(bf16[16,4096]{1,0:T(8,128)(2,1)S(1)} %get-tuple-element.68), channel_id=1, source_target_pairs={{0,4},{1,5},{2,6},{3,7},{4,0},{5,1},{6,2},{7,3},{8,12},{9,13},{10,... | collective-permute-start | bytes 393224 | tf_op jit(solution)/shard_map/ppermute | solution.py:426
  19.9 35.3 %copy-start.13 = (s32[8]{0:T(128)S(1)}, s32[8]{0:T(128)}, u32[]{:S(2)}) copy-start(s32[8]{0:T(128)} %param.15) | copy-start | bytes 100
  19.9 13.0 %collective-permute-start.7 = (bf16[32,32,128]{2,1,0:T(8,128)(2,1)S(1)}, bf16[32,32,128]{2,1,0:T(8,128)(2,1)S(1)}, u32[]{:S(2)}, u32[]{:S(2)}) collective-permute-start(bf16[32,32,128]{2,1,0:T(8,128)(2,1)S(1)} %get-tuple-element.71), channel_id=1, source_target_pairs={{0,4},{1,5},{14,10},{15,11},{16,20},{17,21},{30,26},{31,27},{32,36... | collective-permute-start | bytes 786440 | tf_op jit(solution)/shard_map/ppermute | solution.py:426
  24.7 10.2 %collective-permute-start.10 = (bf16[32,32,128]{2,1,0:T(8,128)(2,1)}, bf16[32,32,128]{2,1,0:T(8,128)(2,1)S(1)}, u32[]{:S(2)}, u32[]{:S(2)}) collective-permute-start(bf16[32,32,128]{2,1,0:T(8,128)(2,1)} %get-tuple-element.78), channel_id=1, source_target_pairs={{0,6},{1,7},{14,12},{15,13},{16,22},{17,23},{30,28},{31,29},{32,38... | collective-permute-start | bytes 786440 | tf_op jit(solution)/shard_map/ppermute | solution.py:426
  26.0 20.3 %all-to-all-start.1 = ((bf16[8,16,32,128]{3,2,1,0:T(8,128)(2,1)}), bf16[8,16,32,128]{3,2,1,0:T(8,128)(2,1)S(1)}, u32[]{:S(2)}, u32[]{:S(2)}) async-start(bf16[8,16,32,128]{3,2,1,0:T(8,128)(2,1)} %bitcast.7), calls=%async_computation.1 | async-start | bytes 2097152 | tf_op jit(solution)/shard_map/all_to_all | solution.py:477
  29.6 16.1 %collective-permute-start.9 = (bf16[32,32,128]{2,1,0:T(8,128)(2,1)}, bf16[32,32,128]{2,1,0:T(8,128)(2,1)S(1)}, u32[]{:S(2)}, u32[]{:S(2)}) collective-permute-start(bf16[32,32,128]{2,1,0:T(8,128)(2,1)} %get-tuple-element.76), channel_id=1, source_target_pairs={{0,2},{1,3},{14,8},{15,9},{16,18},{17,19},{30,24},{31,25},{32,34},... | collective-permute-start | bytes 786440 | tf_op jit(solution)/shard_map/ppermute | solution.py:426
  34.8 24.2 %collective-permute-start.8 = (bf16[64,4096]{1,0:T(8,128)(2,1)S(1)}, bf16[64,4096]{1,0:T(8,128)(2,1)S(1)}, u32[]{:S(2)}, u32[]{:S(2)}) collective-permute-start(bf16[64,4096]{1,0:T(8,128)(2,1)S(1)} %constant_dynamic-update-slice_fusion.refs_0_), channel_id=1, source_target_pairs={{0,8},{1,9},{2,10},{3,11},{4,12},{5,13},{6,14},{7,15},{8,0},{9,1},... | collective-permute-start | bytes 1572872 | tf_op jit(solution)/shard_map/ppermute | solution.py:426
  47.1 17.3 %collective-permute-start.12 = (bf16[32,4096]{1,0:T(8,128)(2,1)S(1)}, bf16[32,4096]{1,0:T(8,128)(2,1)S(1)}, u32[]{:S(2)}, u32[]{:S(2)}) collective-permute-start(bf16[32,4096]{1,0:T(8,128)(2,1)S(1)} %get-tuple-element.82.refs_3_.refs_2_), channel_id=1, source_target_pairs={{0,2},{1,3},{2,4},{3,5},{4,6},{5,7},{6,0},{7,1},{8,10},{9,11},{10,... | collective-permute-start | bytes 786440 | tf_op jit(solution)/shard_map/ppermute | solution.py:426
  49.2 15.2 %collective-permute-start.13 = (bf16[32,4096]{1,0:T(8,128)(2,1)S(1)}, bf16[32,4096]{1,0:T(8,128)(2,1)S(1)}, u32[]{:S(2)}, u32[]{:S(2)}) collective-permute-start(bf16[32,4096]{1,0:T(8,128)(2,1)S(1)} %get-tuple-element.82.refs_3_.refs_2_), channel_id=1, source_target_pairs={{0,6},{1,7},{2,0},{3,1},{4,2},{5,3},{6,4},{7,5},{8,14},{9,15},{10,... | collective-permute-start | bytes 786440 | tf_op jit(solution)/shard_map/ppermute | solution.py:426
  49.8 14.6 %collective-permute-start.11 = (bf16[32,4096]{1,0:T(8,128)(2,1)S(1)}, bf16[32,4096]{1,0:T(8,128)(2,1)S(1)}, u32[]{:S(2)}, u32[]{:S(2)}) collective-permute-start(bf16[32,4096]{1,0:T(8,128)(2,1)S(1)} %get-tuple-element.81.refs_2_.refs_0_), channel_id=1, source_target_pairs={{0,8},{1,9},{2,10},{3,11},{4,12},{5,13},{6,14},{7,15},{8,0},{9,1},... | collective-permute-start | bytes 786440 | tf_op jit(solution)/shard_map/ppermute | solution.py:426
  56.1 25.9 %collective-permute-start.15 = (f32[8,1]{0,1:T(1,128)S(1)}, f32[8,1]{0,1:T(1,128)S(1)}, u32[]{:S(2)}, u32[]{:S(2)}) collective-permute-start(f32[8,1]{0,1:T(1,128)S(1)} %bitcast.37), channel_id=1, source_target_pairs={{0,1},{1,0},{2,3},{3,2},{4,5},{5,4},{6,7},{7,6},{8,9},{9,8},{10,11... | collective-permute-start | bytes 104 | tf_op jit(solution)/shard_map/ppermute | solution.py:426
  60.9 9.4 %all-to-all-start.2 = ((f32[16,8,128]{2,1,0:T(8,128)}), f32[16,8,128]{2,1,0:T(8,128)S(1)}, u32[]{:S(2)}, u32[]{:S(2)}) async-start(f32[16,8,128]{2,1,0:T(8,128)} %shard_map.129), calls=%async_computation.2 | async-start | bytes 131072 | tf_op jit(solution)/shard_map/all_to_all | solution.py:517
  65.3 39.6 %copy-start.6 = (bf16[96,4096]{1,0:T(8,128)(2,1)}, bf16[96,4096]{1,0:T(8,128)(2,1)S(1)}, u32[]{:S(2)}) copy-start(bf16[96,4096]{1,0:T(8,128)(2,1)S(1)} %get-tuple-element.86.refs_6_) | copy-start | bytes 2359300
  65.3 29.4 %collective-permute-start.16 = (bf16[96,4096]{1,0:T(8,128)(2,1)S(1)}, bf16[96,4096]{1,0:T(8,128)(2,1)}, u32[]{:S(2)}, u32[]{:S(2)}) collective-permute-start(bf16[96,4096]{1,0:T(8,128)(2,1)S(1)} %get-tuple-element.86.refs_6_), channel_id=1, source_target_pairs={{0,8},{1,9},{2,10},{3,11},{4,12},{5,13},{6,14},{7,15},{8,0},{9,1},... | collective-permute-start | bytes 2359304 | tf_op jit(solution)/shard_map/ppermute | solution.py:426
  66.7 28.0 %collective-permute-start.17 = (bf16[64,4096]{1,0:T(8,128)(2,1)}, bf16[64,4096]{1,0:T(8,128)(2,1)S(1)}, u32[]{:S(2)}, u32[]{:S(2)}) collective-permute-start(bf16[64,4096]{1,0:T(8,128)(2,1)} %get-tuple-element.89.refs_1_), channel_id=1, source_target_pairs={{0,2},{1,3},{2,4},{3,5},{4,6},{5,7},{6,0},{7,1},{8,10},{9,11},{10,... | collective-permute-start | bytes 1572872 | tf_op jit(solution)/shard_map/ppermute | solution.py:426
  67.9 26.8 %collective-permute-start.18 = (bf16[64,4096]{1,0:T(8,128)(2,1)}, bf16[64,4096]{1,0:T(8,128)(2,1)S(1)}, u32[]{:S(2)}, u32[]{:S(2)}) collective-permute-start(bf16[64,4096]{1,0:T(8,128)(2,1)} %get-tuple-element.89.refs_1_), channel_id=1, source_target_pairs={{0,6},{1,7},{2,0},{3,1},{4,2},{5,3},{6,4},{7,5},{8,14},{9,15},{10,... | collective-permute-start | bytes 1572872 | tf_op jit(solution)/shard_map/ppermute | solution.py:426
  71.0 21.5 %all-to-all-start.3 = ((f32[16,8,512]{2,1,0:T(8,128)}), f32[16,8,512]{2,1,0:T(8,128)S(1)}, u32[]{:S(2)}, u32[]{:S(2)}) async-start(f32[16,8,512]{2,1,0:T(8,128)} %shard_map.131), calls=%async_computation.3 | async-start | bytes 524288 | tf_op jit(solution)/shard_map/all_to_all | solution.py:529
  81.6 10.9 %collective-permute-start.19 = (bf16[16,4096]{1,0:T(8,128)(2,1)S(1)}, bf16[16,4096]{1,0:T(8,128)(2,1)S(1)}, u32[]{:S(2)}, u32[]{:S(2)}) collective-permute-start(bf16[16,4096]{1,0:T(8,128)(2,1)S(1)} %slice.18), channel_id=1, source_target_pairs={{0,2},{1,3},{2,4},{3,5},{4,6},{5,7},{6,0},{7,1},{8,10},{9,11},{10,... | collective-permute-start | bytes 393224 | tf_op jit(solution)/shard_map/ppermute | solution.py:426
  82.0 12.7 %collective-permute-start.20 = (bf16[16,4096]{1,0:T(8,128)(2,1)S(1)}, bf16[16,4096]{1,0:T(8,128)(2,1)S(1)}, u32[]{:S(2)}, u32[]{:S(2)}) collective-permute-start(bf16[16,4096]{1,0:T(8,128)(2,1)S(1)} %slice.19), channel_id=1, source_target_pairs={{0,6},{1,7},{2,0},{3,1},{4,2},{5,3},{6,4},{7,5},{8,14},{9,15},{10,... | collective-permute-start | bytes 393224 | tf_op jit(solution)/shard_map/ppermute | solution.py:426
  92.5 7.4 %collective-permute-start.14 = (bf16[16,256]{1,0:T(8,128)(2,1)S(1)}, bf16[16,256]{1,0:T(8,128)(2,1)S(1)}, u32[]{:S(2)}, u32[]{:S(2)}) collective-permute-start(bf16[16,256]{1,0:T(8,128)(2,1)S(1)} %shard_map.132.mine_ref), channel_id=1, source_target_pairs={{0,1},{1,0},{2,3},{3,2},{4,5},{5,4},{6,7},{7,6},{8,9},{9,8},{10,11... | collective-permute-start | bytes 24584 | tf_op jit(solution)/shard_map/ppermute | solution.py:426
  94.7 10.2 %copy-start.2 = (bf16[64,4096]{1,0:T(8,128)(2,1)}, bf16[64,4096]{1,0:T(8,128)(2,1)S(1)}, u32[]{:S(2)}) copy-start(bf16[64,4096]{1,0:T(8,128)(2,1)S(1)} %collective-permute-done.17.refs_3_) | copy-start | bytes 1572868
  94.7 10.2 %copy-start.4 = (bf16[64,4096]{1,0:T(8,128)(2,1)}, bf16[64,4096]{1,0:T(8,128)(2,1)S(1)}, u32[]{:S(2)}) copy-start(bf16[64,4096]{1,0:T(8,128)(2,1)S(1)} %collective-permute-done.18.refs_2_) | copy-start | bytes 1572868
  94.8 10.1 %collective-permute-start.21 = (bf16[32,4096]{1,0:T(8,128)(2,1)S(1)}, bf16[32,4096]{1,0:T(8,128)(2,1)S(1)}, u32[]{:S(2)}, u32[]{:S(2)}) collective-permute-start(bf16[32,4096]{1,0:T(8,128)(2,1)S(1)} %slice.20), channel_id=1, source_target_pairs={{0,2},{1,3},{2,4},{3,5},{4,6},{5,7},{6,0},{7,1},{8,10},{9,11},{10,... | collective-permute-start | bytes 786440 | tf_op jit(solution)/shard_map/ppermute | solution.py:426
  95.1 9.7 %collective-permute-start.22 = (bf16[32,4096]{1,0:T(8,128)(2,1)S(1)}, bf16[32,4096]{1,0:T(8,128)(2,1)S(1)}, u32[]{:S(2)}, u32[]{:S(2)}) collective-permute-start(bf16[32,4096]{1,0:T(8,128)(2,1)S(1)} %slice.21), channel_id=1, source_target_pairs={{0,6},{1,7},{2,0},{3,1},{4,2},{5,3},{6,4},{7,5},{8,14},{9,15},{10,... | collective-permute-start | bytes 786440 | tf_op jit(solution)/shard_map/ppermute | solution.py:426
  97.6 4.5 %collective-permute-start.23 = (bf16[16,4096]{1,0:T(8,128)(2,1)S(1)}, bf16[16,4096]{1,0:T(8,128)(2,1)S(1)}, u32[]{:S(2)}, u32[]{:S(2)}) collective-permute-start(bf16[16,4096]{1,0:T(8,128)(2,1)S(1)} %collective-permute-done.19.refs_8_), channel_id=1, source_target_pairs={{0,8},{1,9},{2,10},{3,11},{4,12},{5,13},{6,14},{7,15},{8,0},{9,1},... | collective-permute-start | bytes 393224 | tf_op jit(solution)/shard_map/ppermute | solution.py:426
  97.6 7.3 %collective-permute-start.24 = (bf16[16,4096]{1,0:T(8,128)(2,1)S(1)}, bf16[16,4096]{1,0:T(8,128)(2,1)S(1)}, u32[]{:S(2)}, u32[]{:S(2)}) collective-permute-start(bf16[16,4096]{1,0:T(8,128)(2,1)S(1)} %collective-permute-done.20.refs_9_), channel_id=1, source_target_pairs={{0,8},{1,9},{2,10},{3,11},{4,12},{5,13},{6,14},{7,15},{8,0},{9,1},... | collective-permute-start | bytes 393224 | tf_op jit(solution)/shard_map/ppermute | solution.py:426
  110.4 40.5 %copy-start = (bf16[256,4096]{1,0:T(8,128)(2,1)}, bf16[256,4096]{1,0:T(8,128)(2,1)S(1)}, u32[]{:S(2)}) copy-start(bf16[256,4096]{1,0:T(8,128)(2,1)S(1)} %get-tuple-element.98.second_ref.refs_2_.refs_3_) | copy-start | bytes 6291460
  110.4 9.3 %collective-permute-start.25 = (f32[16,4096]{1,0:T(8,128)S(1)}, f32[16,4096]{1,0:T(8,128)S(1)}, u32[]{:S(2)}, u32[]{:S(2)}) collective-permute-start(f32[16,4096]{1,0:T(8,128)S(1)} %get-tuple-element.95.x_ref.refs_0_), channel_id=1, source_target_pairs={{0,1},{1,0},{2,3},{3,2},{4,5},{5,4},{6,7},{7,6},{8,9},{9,8},{10,11... | collective-permute-start | bytes 786440 | tf_op jit(solution)/shard_map/ppermute | solution.py:426
  112.0 7.8 %collective-permute-start.26 = (bf16[16,4096]{1,0:T(8,128)(2,1)S(1)}, bf16[16,4096]{1,0:T(8,128)(2,1)S(1)}, u32[]{:S(2)}, u32[]{:S(2)}) collective-permute-start(bf16[16,4096]{1,0:T(8,128)(2,1)S(1)} %get-tuple-element.96), channel_id=1, source_target_pairs={{1,16},{16,1},{3,18},{18,3},{5,20},{20,5},{7,22},{22,7},{9,24},{24... | collective-permute-start | bytes 393224 | tf_op jit(solution)/shard_map/ppermute | solution.py:583
  121.0 1.2 collective-permute-start.27
  139.2 2.8 %collective-permute-start.28 = (bf16[16,256]{1,0:T(8,128)(2,1)S(1)}, bf16[16,256]{1,0:T(8,128)(2,1)S(1)}, u32[]{:S(2)}, u32[]{:S(2)}) collective-permute-start(bf16[16,256]{1,0:T(8,128)(2,1)S(1)} %shard_map.136.mine_ref), channel_id=1, source_target_pairs={{0,1},{1,0},{2,3},{3,2},{4,5},{5,4},{6,7},{7,6},{8,9},{9,8},{10,11... | collective-permute-start | bytes 24584 | tf_op jit(solution)/shard_map/ppermute | solution.py:426
  142.7 15.9 %copy-start.12 = (bf16[8,2,32,128]{3,2,1,0:T(8,128)(2,1)S(1)}, bf16[8,2,32,128]{3,2,1,0:T(8,128)(2,1)}, u32[]{:S(2)}) copy-start(bf16[8,2,32,128]{3,2,1,0:T(8,128)(2,1)} %param.18) | copy-start | bytes 393220
  142.7 8.2 %collective-permute-start.29 = (f32[16,4096]{1,0:T(8,128)S(1)}, f32[16,4096]{1,0:T(8,128)S(1)}, u32[]{:S(2)}, u32[]{:S(2)}) collective-permute-start(f32[16,4096]{1,0:T(8,128)S(1)} %get-tuple-element.102.x_ref.refs_0_), channel_id=1, source_target_pairs={{0,1},{1,0},{2,3},{3,2},{4,5},{5,4},{6,7},{7,6},{8,9},{9,8},{10,11... | collective-permute-start | bytes 786440 | tf_op jit(solution)/shard_map/ppermute | solution.py:426
  143.2 7.8 %collective-permute-start.30 = (bf16[16,4096]{1,0:T(8,128)(2,1)S(1)}, bf16[16,4096]{1,0:T(8,128)(2,1)S(1)}, u32[]{:S(2)}, u32[]{:S(2)}) collective-permute-start(bf16[16,4096]{1,0:T(8,128)(2,1)S(1)} %get-tuple-element.103), channel_id=1, source_target_pairs={{1,16},{16,1},{3,18},{18,3},{5,20},{20,5},{7,22},{22,7},{9,24},{24... | collective-permute-start | bytes 393224 | tf_op jit(solution)/shard_map/ppermute | solution.py:583
  152.2 1.2 collective-permute-start.31
  154.1 17.3 %all-to-all-start.5 = ((f32[16,8,512]{2,1,0:T(8,128)}), f32[16,8,512]{2,1,0:T(8,128)S(1)}, u32[]{:S(2)}, u32[]{:S(2)}) async-start(f32[16,8,512]{2,1,0:T(8,128)} %shard_map.139), calls=%async_computation.5 | async-start | bytes 524288 | tf_op jit(solution)/shard_map/all_to_all | solution.py:590
  158.8 14.3 %collective-permute-start.33 = (bf16[8,4096]{1,0:T(8,128)(2,1)S(1)}, bf16[8,4096]{1,0:T(8,128)(2,1)S(1)}, u32[]{:S(2)}, u32[]{:S(2)}) collective-permute-start(bf16[8,4096]{1,0:T(8,128)(2,1)S(1)} %convert_element_type.25), channel_id=1, source_target_pairs={{0,1},{1,0},{2,3},{3,2},{4,5},{5,4},{6,7},{7,6},{8,9},{9,8},{10,11... | collective-permute-start | bytes 196616 | tf_op jit(solution)/shard_map/ppermute | solution.py:426
  171.5 2.5 %collective-permute-start.32 = (bf16[16,256]{1,0:T(8,128)(2,1)S(1)}, bf16[16,256]{1,0:T(8,128)(2,1)S(1)}, u32[]{:S(2)}, u32[]{:S(2)}) collective-permute-start(bf16[16,256]{1,0:T(8,128)(2,1)S(1)} %get-tuple-element.106.mine_ref), channel_id=1, source_target_pairs={{0,1},{1,0},{2,3},{3,2},{4,5},{5,4},{6,7},{7,6},{8,9},{9,8},{10,11... | collective-permute-start | bytes 24584 | tf_op jit(solution)/shard_map/ppermute | solution.py:426
  173.2 24.8 %copy-start.9 = (f32[32,32]{1,0:T(8,128)S(1)}, f32[32,32]{1,0:T(8,128)}, u32[]{:S(2)}) copy-start(f32[32,32]{1,0:T(8,128)} %smoother_ref.1) | copy-start | bytes 12292
  177.0 7.0 %collective-permute-start.34 = (f32[8,4096]{1,0:T(8,128)S(1)}, f32[8,4096]{1,0:T(8,128)S(1)}, u32[]{:S(2)}, u32[]{:S(2)}) collective-permute-start(f32[8,4096]{1,0:T(8,128)S(1)} %get-tuple-element.111), channel_id=1, source_target_pairs={{0,1},{1,0},{2,3},{3,2},{4,5},{5,4},{6,7},{7,6},{8,9},{9,8},{10,11... | collective-permute-start | bytes 393224 | tf_op jit(solution)/shard_map/ppermute | solution.py:426
  177.4 20.6 %all-to-all-start.6 = ((f32[256,2,128]{2,1,0:T(2,128)}), f32[256,2,128]{2,1,0:T(2,128)S(1)}, u32[]{:S(2)}, u32[]{:S(2)}) async-start(f32[256,2,128]{2,1,0:T(2,128)} %bitcast.15), calls=%async_computation.6 | async-start | bytes 524288 | tf_op jit(solution)/shard_map/all_to_all | solution.py:612
  (5 other events, 5.5 us)
